TPU v7x, 128 devices: a whole 4x4x4 slice. The times are simulated.
128 devices in a mesh: gx: 16 (over x, z), gy: 8 (over y, core).
Axes of the slice: x: 4, y: 4, z: 4, core: 2. Of those that a mesh axis runs over, the one named last changes fastest.
Arguments:
- mean_field: float32 [16, 256, 2048], P(None, 'gx', 'gy'), may hold values from -6 to 6
- mode_fields: float32 [16, 16, 256, 2048], P(None, None, 'gx', 'gy'), may hold values from -6 to 6
- velocity_east: float32 [16, 256, 2048], P(None, 'gx', 'gy'), may hold values from -6 to 6
- velocity_north: float32 [16, 256, 2048], P(None, 'gx', 'gy'), may hold values from -6 to 6
- flag_east: int32 [16, 256, 2048], P(None, 'gx', 'gy'), may hold values 0 or 1
- flag_north: int32 [16, 256, 2048], P(None, 'gx', 'gy'), may hold values 0 or 1
- ocean_mask: int32 [16, 256, 2048], P(None, 'gx', 'gy'), may hold values 0 or 1
Outputs:
- mean_next: float32 [16, 256, 2048], P(None, 'gx', 'gy')
- modes_next: float32 [16, 16, 256, 2048], P(None, None, 'gx', 'gy')
- factor: float32 [16, 16], replicated
Inputs may be any that keep to these rules, and one draw needn't show every extreme that they name: `flag_east`: 1 takes the five-point upwind value biased to the cell of lower index beside the face, 0 the one biased to the higher. `flag_north`: as for the first dimension. `ocean_mask`: 1 marks ocean, 0 land.
All inputs are finite; a program needn't handle non-finite values. No bound on the sum of `flag_east` or of `flag_north` or of `ocean_mask` on one device may be relied on, other than what follows from the above.
Results may differ from a plain program's by a relative error of at most 0.0003.
Values sent between devices are 32-bit elements; how exact they have to be, the bound alone decides.
No kernel may reach another device: no remote copies, remote signals or barrier semaphores. Data moves between devices by JAX's collectives and lax.ppermute only.
A program may use at most 128 MiB of HBM per device.

v0:
```python
import jax
import jax.numpy as jnp
from jax import lax
from jax.sharding import PartitionSpec as P

time_step = 0.1
horiz_diff = 0.05
vert_diff = 0.2


def extended(value, sides, width):
    for axis, dim in sides:
        size, length = (lax.axis_size(axis), value.shape[dim])
        up = [(i, (i + 1) % size) for i in range(size - 1)]
        down = [(j, i) for i, j in up]
        last = lax.slice_in_dim(value, length - width, length, axis=dim)
        leading = lax.slice_in_dim(value, 0, width, axis=dim)
        before = lax.ppermute(last, axis, up)
        after = lax.ppermute(leading, axis, down)
        value = jnp.concatenate([before, value, after], axis=dim)
    return value


def passed_along(block, axis, distance):
    devices = range(lax.axis_size(axis))
    route = [(i - distance, i) for i in devices if i - distance in devices]
    return lax.ppermute(block, axis, route)


def cells_at(values, axis_dim, first_face, face_count, offset):
    start_index = first_face + offset + 3
    return lax.slice_in_dim(values, start_index, start_index + face_count, axis=axis_dim)


def face_fluxes(values, openness, pos_speed, neg_speed, axis_dim, first_face, face_count):
    centre = cells_at(values, axis_dim, first_face, face_count, 0)
    upper_one = cells_at(values, axis_dim, first_face, face_count, 1)
    lower_one = cells_at(values, axis_dim, first_face, face_count, -1)
    upper_two = cells_at(values, axis_dim, first_face, face_count, 2)
    left_side = (
        2.0 * cells_at(values, axis_dim, first_face, face_count, -2)
        - 13.0 * lower_one
        + 47.0 * centre
        + 27.0 * upper_one
        - 3.0 * upper_two
    ) / 60.0
    right_side = (
        2.0 * cells_at(values, axis_dim, first_face, face_count, 3)
        - 13.0 * upper_two
        + 47.0 * upper_one
        + 27.0 * centre
        - 3.0 * lower_one
    ) / 60.0
    return openness * (
        pos_speed * left_side + neg_speed * right_side - horiz_diff * (upper_one - centre)
    )


def direction_fluxes(channels, pos_speed, neg_speed, axis_dim, first_face, face_count):
    mask_part = channels[-1]
    field_part = channels[:-1]
    openness = cells_at(mask_part, axis_dim - 1, first_face, face_count, 0) * cells_at(
        mask_part, axis_dim - 1, first_face, face_count, 1
    )
    return face_fluxes(field_part, openness, pos_speed, neg_speed, axis_dim, first_face, face_count)


def lower_inverse(lower_factor):
    order_size = lower_factor.shape[0]
    identity = jnp.eye(order_size, dtype=lower_factor.dtype)
    rows_out = []
    for row_index in range(order_size):
        partial_value = identity[row_index]
        for col_index in range(row_index):
            partial_value = partial_value - lower_factor[row_index, col_index] * rows_out[col_index]
        rows_out.append(partial_value / lower_factor[row_index, row_index])
    return jnp.stack(rows_out)


def shards(
    mean_field, mode_fields, velocity_east, velocity_north, flag_east, flag_north, ocean_mask
):
    fields = jnp.concatenate([mean_field[None], mode_fields], axis=0)
    wet_cells = ocean_mask.astype(jnp.float32)
    east_flag = flag_east.astype(jnp.float32)
    north_flag = flag_north.astype(jnp.float32)
    pos_east = velocity_east * east_flag
    neg_east = velocity_east * (1.0 - east_flag)
    pos_north = velocity_north * north_flag
    neg_north = velocity_north * (1.0 - north_flag)
    width_x = fields.shape[2]
    width_y = fields.shape[3]
    stacked = jnp.concatenate([fields, wet_cells[None]], axis=0)
    padded = extended(stacked, (("gx", 2), ("gy", 3)), 3)
    across_x = padded[:, :, :, 3:-3]
    flux_east = direction_fluxes(across_x, pos_east, neg_east, 2, 0, width_x)
    west_flux = passed_along(flux_east[:, :, width_x - 1], "gx", 1)
    joined = jnp.concatenate([west_flux[:, :, None], flux_east], axis=2)
    tend_x = joined[:, :, :-1] - joined[:, :, 1:]
    across_y = padded[:, :, 3:-3, :]
    flux_north = direction_fluxes(across_y, pos_north, neg_north, 3, 0, width_y)
    south_flux = passed_along(flux_north[:, :, :, width_y - 1], "gy", 1)
    joined_y = jnp.concatenate([south_flux[:, :, :, None], flux_north], axis=3)
    tend_y = joined_y[:, :, :, :-1] - joined_y[:, :, :, 1:]
    vertical_flux = vert_diff * (fields[:, 1:] - fields[:, :-1])
    zero_level = jnp.zeros_like(fields[:, :1])
    vertical = jnp.concatenate([vertical_flux, zero_level], axis=1) - jnp.concatenate(
        [zero_level, vertical_flux], axis=1
    )
    tendency = wet_cells * (tend_x + tend_y + vertical)
    mean_next = mean_field + time_step * tendency[0]
    mode_count = mode_fields.shape[0]
    flat_modes = mode_fields.reshape(mode_count, -1)
    flat_tend = tendency[1:].reshape(mode_count, -1)
    cell_count = float(flat_modes.shape[1] * lax.axis_size("gx") * lax.axis_size("gy"))
    highest = lax.Precision.HIGHEST
    projection = (
        lax.psum(jnp.dot(flat_modes, flat_tend.T, precision=highest), ("gx", "gy")) / cell_count
    )
    growth = flat_tend - jnp.dot(projection.T, flat_modes, precision=highest)
    updated = flat_modes + time_step * growth
    gram_matrix = (
        lax.psum(jnp.dot(updated, updated.T, precision=highest), ("gx", "gy")) / cell_count
    )
    lower_factor = jnp.linalg.cholesky(gram_matrix)
    inverse = lower_inverse(lower_factor)
    modes_next = jnp.dot(inverse, updated, precision=highest).reshape(mode_fields.shape)
    return (mean_next, modes_next, lower_factor.T)


def solution(mesh):
    return jax.shard_map(
        shards,
        mesh=mesh,
        in_specs=(
            P(None, "gx", "gy"),
            P(None, None, "gx", "gy"),
            P(None, "gx", "gy"),
            P(None, "gx", "gy"),
            P(None, "gx", "gy"),
            P(None, "gx", "gy"),
            P(None, "gx", "gy"),
        ),
        out_specs=(P(None, "gx", "gy"), P(None, None, "gx", "gy"), P()),
        check_vma=False,
    )
```

profile of v0, /device:TPU:0, one launch (start us, length us, event | category | flops | bytes accessed | tf_op | source)
XLA Modules:
  0.0 429.4 jit_solution(251561628221567672)
XLA Ops:
  0.7 5.5 %copy.59 = f32[16,16,16,256]{3,0,2,1:T(8,128)S(1)} copy(f32[16,16,16,256]{3,2,1,0:T(8,128)} %param.8) | data formatting | bytes 8388608 | tf_op args[1]
  6.5 0.7 fusion.79
  7.5 0.4 pad_maximum_fusion.13
  8.2 4.0 collective-permute-start
  12.5 1.5 collective-permute-start.1
  14.0 0.9 multiply_multiply_fusion.1
  14.9 0.9 multiply_multiply_fusion.3
  15.8 3.4 fusion.36
  19.2 11.8 %collective-permute-done = f32[18,16,3,256]{3,1,2,0:T(8,128)S(1)} collective-permute-done((f32[18,16,3,256]{3,1,2,0:T(8,128)S(1)}, f32[18,16,3,256]{3,1,2,0:T(8,128)S(1)}, u32[]{:S(2)}, u32[]{:S(2)}) %collective-permute-start) | collective-permute-done | bytes 884768 | tf_op jit(solution)/shard_map/ppermute | solution.py:18
  31.0 0.5 copy.63
  31.5 4.1 collective-permute-done.1
  35.6 0.5 copy.64
  36.1 1.4 pad_maximum_fusion.2
  37.6 6.5 %maximum_maximum_fusion = (f32[18,16,19,256]{3,0,2,1:T(8,128)}, f32[18,16,19,256]{3,0,2,1:T(8,128)}) fusion(f32[1,16,16,256]{3,0,2,1:T(1,128)S(1)} %copy.60, f32[16,16,16,256]{3,0,2,1:T(8,128)S(1)} %copy.59, f32[1,16,16,256]{3,0,2,1:T(1,128)S(1)} %copy.58, f32[18,16,3,256]{3,0,2,1:T(8,128)S(1)} %copy.63, f32[18,16,3,256]{3,0,2,1:T(8,128)S(1)} %copy.64), kind=kLoop, calls=%fused_computation.10 | loop fusion | flops 8404992 | bytes 17694720 | tf_op jit(solution)/shard_map/concatenate | solution.py:20
  44.0 1.1 pad_maximum_fusion.20
  45.2 4.7 %fusion.78 = (f32[18,16,22,3]{3,0,2,1:T(8,128)}, f32[18,16,22,3]{3,0,2,1:T(8,128)}) fusion(f32[18,16,22,256]{3,0,2,1:T(8,128)S(1)} %pad_maximum_fusion.2), kind=kLoop, calls=%fused_computation.155 | loop fusion | bytes 304128 | tf_op jit(solution)/shard_map/slice | solution.py:16
  49.9 4.2 copy.72
  54.1 2.1 collective-permute-start.3
  56.2 4.2 copy.73
  60.4 1.3 collective-permute-start.4
  61.7 1.0 copy.99
  62.9 13.8 %fusion.27 = f32[17,16,16,256]{3,0,2,1:T(8,128)S(1)} fusion(f32[18,16,19,256]{3,0,2,1:T(8,128)} %get-tuple-element.37, f32[18,16,19,256]{3,0,2,1:T(8,128)} %get-tuple-element.36, f32[16,16,16,256]{3,0,2,1:T(8,128)} %copy-done, f32[1,16,16,256]{3,0,2,1:T(1,128)S(1)} %copy.58, f32[16,16,256]{2,1,0:T(8,128)} %get-tuple-element.41, ...), kind=kLoop, calls=%fused_computation.47 | loop fusion | flops 28966912 | bytes 31981568 | tf_op jit(solution)/shard_map/mul | solution.py:54
  76.8 2.6 copy-done.7
  79.4 0.8 slice_bitcast_fusion
  80.2 4.6 %collective-permute-start.2 = (f32[17,16,256]{2,0,1:T(8,128)}, f32[17,16,256]{2,0,1:T(8,128)}, u32[]{:S(2)}, u32[]{:S(2)}) collective-permute-start(f32[17,16,256]{2,0,1:T(8,128)} %slice_bitcast_fusion), channel_id=1, source_target_pairs={{0,8},{8,16},{16,24},{24,32},{32,40},{40,48},{48,56},{56,64},{64,7... | collective-permute-start | bytes 835592 | tf_op jit(solution)/shard_map/ppermute | solution.py:27
  84.8 5.0 %copy.75 = f32[18,16,22,3]{3,0,2,1:T(8,128)} copy(f32[18,16,22,3]{2,1,3,0:T(8,128)} %collective-permute-done.4) | data formatting | bytes 152064 | tf_op jit(solution)/shard_map/ppermute | solution.py:19
  89.8 8.8 %pad_maximum_fusion = f32[18,16,22,259]{3,0,2,1:T(8,128)} fusion(f32[18,16,22,3]{3,0,2,1:T(8,128)} %copy.75, f32[18,16,3,256]{3,0,2,1:T(8,128)S(1)} %copy.64, f32[1,16,16,256]{3,0,2,1:T(1,128)S(1)} %copy.60, f32[16,16,16,256]{3,0,2,1:T(8,128)} %copy-done, f32[1,16,16,256]{3,0,2,1:T(1,128)S(1)} %copy.58, f32[18,16,3,256]{3,0,2,1:T(8,128)S(1)} %copy.63), kind=kLoop, calls=%fused_computation.3 | loop fusion | flops 8205120 | bytes 13128192 | tf_op jit(solution)/shard_map/concatenate | solution.py:20
  98.6 5.0 %copy.74 = f32[18,16,22,3]{3,0,2,1:T(8,128)} copy(f32[18,16,22,3]{2,1,3,0:T(8,128)} %collective-permute-done.3) | data formatting | bytes 152064 | tf_op jit(solution)/shard_map/ppermute | solution.py:18
  103.6 3.8 pad_maximum_fusion.14
  107.5 0.9 slice_multiply_fusion.4
  108.4 2.0 copy-done.2
  110.4 16.9 %fusion.13 = f32[17,16,16,256]{3,0,2,1:T(8,128)} fusion(f32[18,16,22,259]{3,0,2,1:T(8,128)S(1)} %copy-done.2, f32[18,16,22,3]{3,0,2,1:T(8,128)} %copy.74, f32[18,16,3,256]{3,0,2,1:T(8,128)} %copy-done.5, f32[18,16,3,256]{3,0,2,1:T(8,128)} %copy-done.4, f32[1,16,16,256]{3,0,2,1:T(1,128)S(1)} %copy.60, f32[16,16,16,256]{3,0,2,1:T(8,128)S(1)} %copy-done.1, ...), kind=kLoop, calls=%fused_computation.25 | loop fusion | flops 40108032 | bytes 25176320 | tf_op jit(solution)/shard_map/mul | solution.py:54
  127.2 3.6 slice_reduce_fusion
  130.8 4.4 %collective-permute-start.5 = (f32[17,16,16]{0,2,1:T(8,128)S(1)}, f32[17,16,16]{0,2,1:T(8,128)S(1)}, u32[]{:S(2)}, u32[]{:S(2)}) collective-permute-start(f32[17,16,16]{0,2,1:T(8,128)S(1)} %slice_reduce_fusion), channel_id=1, source_target_pairs={{0,1},{1,2},{2,3},{3,4},{4,5},{5,6},{6,7},{8,9},{9,10},{10,11},{11... | collective-permute-start | bytes 52232 | tf_op jit(solution)/shard_map/ppermute | solution.py:27
  135.2 6.6 %copy.89 = f32[2,8,256,256]{3,1,2,0:T(8,128)} copy(f32[2,8,256,256]{3,2,1,0:T(8,128)} %bitcast.180) | data formatting | bytes 8388608
  141.8 1.8 copy.78
  143.7 17.4 %fusion.5 = f32[17,16,16,256]{3,0,2,1:T(8,128)} fusion(f32[17,16,16,256]{3,0,2,1:T(8,128)} %fusion.13, f32[17,16,16,1]{3,0,2,1:T(8,128)S(1)} %copy.78, f32[17,16,16,256]{3,0,2,1:T(8,128)} %copy-done.7, f32[17,16,1,256]{3,0,2,1:T(8,128)} %bitcast.4, f32[17,15,16,256]{3,0,2,1:T(8,128)} %fusion.36, f32[16,16,256]{2,1,0:T(8,128)S(1)} %copy-done.8), kind=kLoop, calls=%fused_computation.16 | loop fusion | flops 8912896 | bytes 18105344 | tf_op jit(solution)/shard_map/mul | solution.py:110
  161.1 3.5 slice.782
  164.7 0.5 copy-done.6
  165.1 8.4 %convolution_bitcast_fusion = f32[16,16]{0,1:T(8,128)S(1)} fusion(f32[17,16,16,256]{3,0,2,1:T(8,128)} %fusion.5, f32[16,16,16,256]{3,2,1,0:T(8,128)S(1)} %copy-done.6), kind=kOutput, calls=%fused_computation.63 | convolution fusion | flops 201326592 | bytes 8389632 | tf_op jit(solution)/shard_map/dot_general | solution.py:118
  173.6 2.3 copy.90
  175.9 66.4 %psum.14 = f32[16,16]{0,1:T(8,128)S(1)} all-reduce(f32[16,16]{0,1:T(8,128)S(1)} %convolution_bitcast_fusion), channel_id=1, replica_groups=mesh['gx'=16,'gy'=8] {'gx','gy'}, use_global_device_ids=true, to_apply=%region_0.0 | all-reduce | flops 256 | bytes 2048 | tf_op jit(solution)/shard_map/psum | solution.py:118
  242.3 8.9 %fusion.1 = f32[16,65536]{1,0:T(8,128)S(1)} fusion(f32[16,65536]{1,0:T(8,128)} %bitcast.183, f32[16,65536]{1,0:T(8,128)} %bitcast.184, f32[16,16]{0,1:T(8,128)S(1)} %psum.14), kind=kOutput, calls=%fused_computation.2 | convolution fusion | flops 204472576 | bytes 12583936 | tf_op jit(solution)/shard_map/dot_general | solution.py:120
  251.2 2.0 copy-done.3
  253.2 5.6 %fusion.88 = f32[16,16]{0,1:T(8,128)S(1)} fusion(f32[16,65536]{1,0:T(8,128)S(1)} %fusion.1), kind=kOutput, calls=%fused_computation.165 | convolution fusion | flops 201326592 | bytes 4195328 | tf_op jit(solution)/shard_map/dot_general | solution.py:123
  258.9 63.7 %psum.15 = f32[16,16]{0,1:T(8,128)S(1)} all-reduce(f32[16,16]{0,1:T(8,128)S(1)} %fusion.88), channel_id=1, replica_groups=mesh['gx'=16,'gy'=8] {'gx','gy'}, use_global_device_ids=true, to_apply=%region_1.0 | all-reduce | flops 256 | bytes 2048 | tf_op jit(solution)/shard_map/psum | solution.py:123
  322.7 1.5 cholesky.14
  324.1 0.6 compare_reduce_fusion
  324.8 0.6 fusion.95
  325.4 0.7 select_select_fusion
  326.1 0.7 fusion.80
  326.8 0.7 fusion.82
  327.6 0.7 fusion.81
  328.3 0.7 fusion.83
  329.0 0.7 fusion.84
  329.7 0.7 fusion.85
  330.5 0.7 fusion.86
  331.2 0.7 fusion.87
  331.8 1.9 slice_multiply_fusion.3
  333.7 0.7 copy.83
  334.4 85.3 %subtract_divide_fusion = (f32[1,16]{1,0:T(1,128)S(1)}, f32[1,16]{1,0:T(1,128)S(1)}, f32[1,16]{1,0:T(1,128)S(1)}, f32[1,16]{1,0:T(1,128)S(1)}, f32[1,16]{1,0:T(1...) fusion(f32[16,16]{1,0:T(8,128)S(1)} %fusion.40, ...), kind=kLoop, calls=%fused_computation.137 | loop fusion | flops 4096 | bytes 2592 | tf_op jit(solution)/shard_map/div | solution.py:76
  419.8 5.4 %fusion.89 = f32[16,65536]{1,0:T(8,128)S(1)} fusion(f32[16,16]{1,0:T(8,128)S(1)} %stack.2, f32[16,65536]{1,0:T(8,128)} %copy-done.3), kind=kOutput, calls=%fused_computation.166 | convolution fusion | flops 201326592 | bytes 8389632 | tf_op jit(solution)/shard_map/dot_general | solution.py:127
  425.1 3.3 copy.91
  428.4 0.7 bitcast_add_fusion
  (45 shorter events, 1.6 us)
Async XLA Ops:
  0.6 5.5 %copy-start.9 = (f32[16,16,256]{2,1,0:T(8,128)S(1)}, f32[16,16,256]{2,1,0:T(8,128)}, u32[]{:S(2)}) copy-start(f32[16,16,256]{2,1,0:T(8,128)} %param.7) | copy-start | bytes 786436
  0.6 5.8 %copy-start.11 = (s32[16,16,256]{2,1,0:T(8,128)S(1)}, s32[16,16,256]{2,1,0:T(8,128)}, u32[]{:S(2)}) copy-start(s32[16,16,256]{2,1,0:T(8,128)} %param.13) | copy-start | bytes 786436
  6.2 37.9 %copy-start = (f32[16,16,16,256]{3,0,2,1:T(8,128)}, f32[16,16,16,256]{3,0,2,1:T(8,128)S(1)}, u32[]{:S(2)}) copy-start(f32[16,16,16,256]{3,0,2,1:T(8,128)S(1)} %copy.59) | copy-start | bytes 12582916
  6.5 7.5 %copy-start.12 = (f32[16,16,256]{2,1,0:T(8,128)S(1)}, f32[16,16,256]{2,1,0:T(8,128)}, u32[]{:S(2)}) copy-start(f32[16,16,256]{2,1,0:T(8,128)} %param.10) | copy-start | bytes 786436
  6.5 7.5 %copy-start.13 = (s32[16,16,256]{2,1,0:T(8,128)S(1)}, s32[16,16,256]{2,1,0:T(8,128)}, u32[]{:S(2)}) copy-start(s32[16,16,256]{2,1,0:T(8,128)} %param.12) | copy-start | bytes 786436
  7.2 7.6 %copy-start.14 = (f32[16,16,256]{2,1,0:T(8,128)S(1)}, f32[16,16,256]{2,1,0:T(8,128)}, u32[]{:S(2)}) copy-start(f32[16,16,256]{2,1,0:T(8,128)} %param.9) | copy-start | bytes 786436
  7.2 7.6 %copy-start.15 = (s32[16,16,256]{2,1,0:T(8,128)S(1)}, s32[16,16,256]{2,1,0:T(8,128)}, u32[]{:S(2)}) copy-start(s32[16,16,256]{2,1,0:T(8,128)} %param.11) | copy-start | bytes 786436
  8.2 22.8 %collective-permute-start = (f32[18,16,3,256]{3,1,2,0:T(8,128)S(1)}, f32[18,16,3,256]{3,1,2,0:T(8,128)S(1)}, u32[]{:S(2)}, u32[]{:S(2)}) collective-permute-start(f32[18,16,3,256]{3,1,2,0:T(8,128)S(1)} %copy.61), channel_id=1, source_target_pairs={{0,8},{8,16},{16,24},{24,32},{32,40},{40,48},{48,56},{56,64},{64,7... | collective-permute-start | bytes 2654216 | tf_op jit(solution)/shard_map/ppermute | solution.py:18
  12.5 23.1 %collective-permute-start.1 = (f32[18,16,3,256]{3,1,2,0:T(8,128)S(1)}, f32[18,16,3,256]{3,1,2,0:T(8,128)S(1)}, u32[]{:S(2)}, u32[]{:S(2)}) collective-permute-start(f32[18,16,3,256]{3,1,2,0:T(8,128)S(1)} %copy.62), channel_id=1, source_target_pairs={{8,0},{16,8},{24,16},{32,24},{40,32},{48,40},{56,48},{64,56},{72,6... | collective-permute-start | bytes 2654216 | tf_op jit(solution)/shard_map/ppermute | solution.py:19
  31.5 58.3 %copy-start.4 = (f32[18,16,3,256]{3,0,2,1:T(8,128)}, f32[18,16,3,256]{3,0,2,1:T(8,128)S(1)}, u32[]{:S(2)}) copy-start(f32[18,16,3,256]{3,0,2,1:T(8,128)S(1)} %copy.63) | copy-start | bytes 2654212
  36.1 53.7 %copy-start.5 = (f32[18,16,3,256]{3,0,2,1:T(8,128)}, f32[18,16,3,256]{3,0,2,1:T(8,128)S(1)}, u32[]{:S(2)}) copy-start(f32[18,16,3,256]{3,0,2,1:T(8,128)S(1)} %copy.64) | copy-start | bytes 2654212
  54.1 44.5 %collective-permute-start.3 = (f32[18,16,22,3]{2,1,3,0:T(8,128)}, f32[18,16,22,3]{2,1,3,0:T(8,128)}, u32[]{:S(2)}, u32[]{:S(2)}) collective-permute-start(f32[18,16,22,3]{2,1,3,0:T(8,128)} %copy.72), channel_id=1, source_target_pairs={{0,1},{1,2},{2,3},{3,4},{4,5},{5,6},{6,7},{8,9},{9,10},{10,11},{11... | collective-permute-start | bytes 228104 | tf_op jit(solution)/shard_map/ppermute | solution.py:18
  60.4 24.4 %collective-permute-start.4 = (f32[18,16,22,3]{2,1,3,0:T(8,128)}, f32[18,16,22,3]{2,1,3,0:T(8,128)}, u32[]{:S(2)}, u32[]{:S(2)}) collective-permute-start(f32[18,16,22,3]{2,1,3,0:T(8,128)} %copy.73), channel_id=1, source_target_pairs={{1,0},{2,1},{3,2},{4,3},{5,4},{6,5},{7,6},{9,8},{10,9},{11,10},{12... | collective-permute-start | bytes 228104 | tf_op jit(solution)/shard_map/ppermute | solution.py:19
  76.8 2.6 copy-start.7
  80.2 63.5 %collective-permute-start.2 = (f32[17,16,256]{2,0,1:T(8,128)}, f32[17,16,256]{2,0,1:T(8,128)}, u32[]{:S(2)}, u32[]{:S(2)}) collective-permute-start(f32[17,16,256]{2,0,1:T(8,128)} %slice_bitcast_fusion), channel_id=1, source_target_pairs={{0,8},{8,16},{16,24},{24,32},{32,40},{40,48},{48,56},{56,64},{64,7... | collective-permute-start | bytes 835592 | tf_op jit(solution)/shard_map/ppermute | solution.py:27
  103.6 4.8 %copy-start.1 = (f32[16,16,16,256]{3,0,2,1:T(8,128)S(1)}, f32[16,16,16,256]{3,0,2,1:T(8,128)}, u32[]{:S(2)}) copy-start(f32[16,16,16,256]{3,0,2,1:T(8,128)} %copy-done) | copy-start | bytes 12582916
  103.6 6.7 %copy-start.2 = (f32[18,16,22,259]{3,0,2,1:T(8,128)S(1)}, f32[18,16,22,259]{3,0,2,1:T(8,128)}, u32[]{:S(2)}) copy-start(f32[18,16,22,259]{3,0,2,1:T(8,128)} %pad_maximum_fusion) | copy-start | bytes 19692292
  130.8 12.8 %copy-start.8 = (f32[16,16,256]{2,1,0:T(8,128)S(1)}, f32[16,16,256]{2,1,0:T(8,128)}, u32[]{:S(2)}) copy-start(f32[16,16,256]{2,1,0:T(8,128)} %get-tuple-element.44) | copy-start | bytes 786436
  130.8 11.0 %collective-permute-start.5 = (f32[17,16,16]{0,2,1:T(8,128)S(1)}, f32[17,16,16]{0,2,1:T(8,128)S(1)}, u32[]{:S(2)}, u32[]{:S(2)}) collective-permute-start(f32[17,16,16]{0,2,1:T(8,128)S(1)} %slice_reduce_fusion), channel_id=1, source_target_pairs={{0,1},{1,2},{2,3},{3,4},{4,5},{5,6},{6,7},{8,9},{9,10},{10,11},{11... | collective-permute-start | bytes 52232 | tf_op jit(solution)/shard_map/ppermute | solution.py:27
  161.1 4.0 copy-start.6
  251.2 2.0 copy-start.3
  425.1 3.3 copy-start.10
where the time goes:
time: 436 us; the launch traced here: 429 us
  other arithmetic  168 us (39%)
  blocking collectives  130 us (30%)
  local copies, waits for them, and re-layouts  67.6 us (16%)
  matrix products  28.3 us (6%)
  starting transfers between devices  17.8 us (4%)
  waiting for transfers between devices  15.9 us (4%)
    div x1, other arithmetic, lower_inverse(): rows_out.append(partial_value / lower_factor[row_index, row_index])  85.3 us
    psum x1, blocking collectives, shards(): lax.psum(jnp.dot(flat_modes, flat_tend.T, precision=highest), ('gx', 'gy'))  66.4 us
    psum x1, blocking collectives, shards(): lax.psum(jnp.dot(updated, updated.T, precision=highest), ('gx', 'gy'))  63.7 us
    mul x2, other arithmetic, face_fluxes(): openness * (pos_speed * left_side + neg_speed * right_side - horiz_diff *...  30.7 us
    unnamed x38, local copies, waits for them, and re-layouts  25.5 us
    concatenate x4, other arithmetic, extended(): value = jnp.concatenate([before, value, after], axis=dim)  20.5 us
    mul x1, other arithmetic, shards(): tendency = wet_cells * (tend_x + tend_y + vertical)  17.4 us
    ppermute x2, waiting for transfers between devices, extended(): before = lax.ppermute(last, axis, up)  11.8 us
  transfers between devices with their start and end apart: 6, of which 2 were waited for; matrix products, arithmetic and copies ran while one was open for 18% of the time, Pallas kernels for 0%

commit v1 on v0

v1 whole, which is shorter than its diff:
```python
import jax
import jax.numpy as jnp
from jax import lax
from jax.experimental import pallas as pl
from jax.experimental.pallas import tpu as pltpu
from jax.sharding import PartitionSpec as P

time_step = 0.1
horiz_diff = 0.05
vert_diff = 0.2

M = 16
F = 17
NZ = 16
BX = 16
LANES = 128
ROWS = 3 * NZ
ZG = 2
HIGH = lax.Precision.HIGHEST
f32 = jnp.float32
bf16 = jnp.bfloat16

ANY = pl.BlockSpec(memory_space=pl.ANY)
VMEM = pl.BlockSpec(memory_space=pltpu.VMEM)


def params():
    return pltpu.CompilerParams(vmem_limit_bytes=56 * 1024 * 1024)


def cost(flops, nbytes):
    return pl.CostEstimate(flops=flops, bytes_accessed=nbytes, transcendentals=0)


def rolled(value, shift, axis):
    shift = shift % value.shape[axis]
    return value if shift == 0 else pltpu.roll(value, shift, axis)


def lane_ids():
    return lax.broadcasted_iota(jnp.int32, (8, LANES), 1)


def row_ids():
    return lax.broadcasted_iota(jnp.int32, (8, LANES), 0)


def lane_half(ref, half):
    where = (slice(None),) * (len(ref.shape) - 1) + (pl.ds(LANES * half, LANES),)
    return ref.at[where]


def pack_rows(get, first_row):
    rows = row_ids()
    tiles = []
    for out in range(3):
        tile = None
        for z in range(8):
            low, high = max(3 * z, 8 * out), min(3 * z + 3, 8 * out + 8)
            if low >= high:
                continue
            piece = rolled(get(z), 3 * z - 8 * out - first_row, 0)
            tile = piece if tile is None else jnp.where(rows >= low - 8 * out, piece, tile)
        tiles.append(tile)
    return tiles


def pack_columns(get, shift_of):
    slot = lane_ids() // 4
    parts = [jnp.zeros((8, LANES), f32) for _ in range(4)]
    for k in range(2 * NZ):
        moved = rolled(get(k), shift_of(k), 1)
        parts[k % 4] = jnp.where(slot == k, moved, parts[k % 4])
    out = parts[0]
    for k in range(1, 4):
        out = jnp.where(slot % 4 == k, parts[k], out)
    return out


def pack_kernel(modes, mean, vn, fn, mask, up, down, east, west, X, V, I, sems):
    copies = []
    for chunk in range(4):
        for half in range(2):
            copies.append(
                pltpu.make_async_copy(
                    lane_half(modes, half).at[pl.ds(4 * chunk, 4)],
                    X.at[half, pl.ds(4 * chunk, 4)],
                    sems.at[len(copies)],
                )
            )
    for source, target in (
        (mean, lambda half: X.at[half, M]),
        (vn, lambda half: V.at[half]),
        (fn, lambda half: I.at[0, half]),
        (mask, lambda half: I.at[1, half]),
    ):
        for half in range(2):
            copies.append(
                pltpu.make_async_copy(lane_half(source, half), target(half), sems.at[len(copies)])
            )
    for copy in copies:
        copy.start()

    def field(f, carry):
        for half in range(2):
            for zh in range(2):
                for target, tile, first in ((up, 1, 5), (down, 0, 0)):
                    tiles = pack_rows(
                        lambda z: X[half, f, 8 * zh + z, 8 * tile : 8 * tile + 8, :], first
                    )
                    for t in range(3):
                        target[half, f, 24 * zh + 8 * t : 24 * zh + 8 * t + 8, :] = tiles[t]
        def tile_of(half):
            return lambda k: X[half, f, k // 2, 8 * (k % 2) : 8 * (k % 2) + 8, :]
        east[f] = pack_columns(tile_of(1), lambda k: 4 * k - 125)
        west[f] = pack_columns(tile_of(0), lambda k: 4 * k)
        return carry

    for chunk in range(4):
        copies[2 * chunk].wait()
        copies[2 * chunk + 1].wait()
        lax.fori_loop(4 * chunk, 4 * chunk + 4, field, 0)
    for copy in copies[8:]:
        copy.wait()
    lax.fori_loop(M, F, field, 0)
    for index, plane in enumerate(
        (
            lambda half, k: V[half, k // 2, 8 * (k % 2) : 8 * (k % 2) + 8, :],
            lambda half, k: I[0, half, k // 2, 8 * (k % 2) : 8 * (k % 2) + 8, :].astype(f32),
            lambda half, k: I[1, half, k // 2, 8 * (k % 2) : 8 * (k % 2) + 8, :].astype(f32),
        )
    ):
        east[F + index] = pack_columns(lambda k: plane(1, k), lambda k: 4 * k - 125)
        west[F + index] = pack_columns(lambda k: plane(0, k), lambda k: 4 * k)


def pack(modes, mean, vn, fn, mask):
    rows = jax.ShapeDtypeStruct((2, F, ROWS, LANES), f32)
    columns = jax.ShapeDtypeStruct((F + 3, 8, LANES), f32)
    return pl.pallas_call(
        pack_kernel,
        out_shape=(rows, rows, columns, columns),
        in_specs=[ANY] * 5,
        out_specs=(VMEM,) * 4,
        scratch_shapes=[
            pltpu.VMEM((2, F, NZ, BX, LANES), f32),
            pltpu.VMEM((2, NZ, BX, LANES), f32),
            pltpu.VMEM((2, 2, NZ, BX, LANES), jnp.int32),
            pltpu.SemaphoreType.DMA((16,)),
        ],
        compiler_params=params(),
        cost_estimate=cost(10**7, 7 * 10**6),
        name="pack",
    )(modes, mean, vn, fn, mask)


def along_lanes(first, second, outer, offset):
    lanes = lane_ids()
    a, b, c = (rolled(v, -offset, 1) for v in (first, second, outer))
    if offset > 0:
        inside = lanes < LANES - offset
        return jnp.where(inside, a, b), jnp.where(inside, b, c)
    outside = lanes < -offset
    return jnp.where(outside, c, a), jnp.where(outside, a, b)


def cell_weights(a_low, b_low, d_low, a_high, b_high, d_high):
    return (
        2.0 * a_low,
        -13.0 * a_low - 3.0 * b_low - 2.0 * a_high,
        47.0 * a_low + 27.0 * b_low + d_low + 13.0 * a_high + 3.0 * b_high,
        27.0 * a_low + 47.0 * b_low - d_low - 47.0 * a_high - 27.0 * b_high - d_high,
        -3.0 * a_low - 13.0 * b_low - 27.0 * a_high - 47.0 * b_high + d_high,
        2.0 * b_low + 3.0 * a_high + 13.0 * b_high,
        -2.0 * b_high,
    )


def face_parts(openness, speed, flag):
    scaled = openness * speed * (1.0 / 60.0)
    return scaled * flag, scaled * (1.0 - flag), horiz_diff * openness


def split(value):
    high = value.astype(bf16)
    return high, (value - high.astype(f32)).astype(bf16)


def add_products(acc, high, low):
    dims = (((1,), (1,)), ((), ()))
    acc[0:256, :] += lax.dot_general(high, high, dims, preferred_element_type=f32)
    acc[256:512, :] += lax.dot_general(low, high, dims, preferred_element_type=f32)


def field_sums(acc):
    rows = lax.broadcasted_iota(jnp.int32, (512, 256), 0)
    columns = lax.broadcasted_iota(jnp.int32, (512, 256), 1)
    kept = jnp.where(rows % 8 == columns % 8, acc[...], 0.0)
    by_row = jnp.sum(kept.reshape(64, 8, 256), axis=1)
    gather = (
        lax.broadcasted_iota(jnp.int32, (256, 32), 0) // 8
        == lax.broadcasted_iota(jnp.int32, (256, 32), 1)
    ).astype(f32)
    return jnp.dot(by_row, gather, precision=HIGH, preferred_element_type=f32)


def interior_kernel(
    modes, mean, ve, vn, fe, fn, mask, lower, upper, west, east,
    high_out, low_out, edge_out, weights_out, mean_out, sums_out,
    X, VE, FE, W, VN, FN, T, Z, acc, sems,
):
    zero_tile = jnp.zeros((8, LANES), f32)

    def clear(f, carry):
        for half in range(2):
            for z in range(NZ):
                X[half, f, z, 0:8, :] = zero_tile
                X[half, f, z, 24:32, :] = zero_tile
        return carry

    lax.fori_loop(0, F, clear, 0)
    for half in range(2):
        for z in range(NZ):
            lanes = slice(LANES * half, LANES * half + LANES)
            spread = lambda row: jnp.broadcast_to(row, (8, LANES))
            VE[half, z, 0:8, :] = spread(lower[0, z : z + 1, lanes])
            FE[half, z, 0:8, :] = spread(lower[1, z : z + 1, lanes])
            W[half, z, 0:8, :] = spread(lower[2, z : z + 1, lanes]).astype(jnp.int32)
            W[half, z, 24:32, :] = spread(upper[z : z + 1, lanes]).astype(jnp.int32)
    acc[...] = jnp.zeros((512, 256), f32)

    copies = []
    body = pl.ds(8, BX)
    for half in range(2):
        for source, target in (
            (modes, X.at[half, pl.ds(0, M), :, body]),
            (mean, X.at[half, M, :, body]),
            (ve, VE.at[half, :, body]),
            (mask, W.at[half, :, body]),
            (vn, VN.at[half]),
            (fn, FN.at[0, half]),
            (fe, FN.at[1, half]),
        ):
            copies.append(
                pltpu.make_async_copy(lane_half(source, half), target, sems.at[len(copies)])
            )
    for copy in copies:
        copy.start()
    for copy in copies:
        copy.wait()

    lanes = lane_ids()
    rows = row_ids()

    def level(z, carry):
        gain_up = jnp.where(z < NZ - 1, vert_diff, 0.0).astype(f32)
        gain_down = jnp.where(z > 0, vert_diff, 0.0).astype(f32)
        z_up = jnp.minimum(z + 1, NZ - 1)
        z_down = jnp.maximum(z - 1, 0)
        for half in range(2):
            for xt in range(2):
                FE[half, z, 8 + 8 * xt : 16 + 8 * xt, :] = FN[
                    1, half, z, 8 * xt : 8 * xt + 8, :
                ].astype(f32)
        for xt in range(2):
            start = 8 + 8 * xt
            slot = 2 * z + xt
            after_shift = lax.rem(LANES - 4 * slot, LANES)
            before_shift = LANES - 3 - 4 * slot

            def outer(index):
                return jnp.where(
                    lanes < 64,
                    pltpu.roll(east[index], after_shift, 1),
                    pltpu.roll(west[index], before_shift, 1),
                )

            def at(ref, half, offset):
                return ref[half, z, start + offset : start + offset + 8, :]

            wet = [at(W, half, 0).astype(f32) for half in range(2)]
            wx = []
            for half in range(2):
                before = wet[half] * at(W, half, -1).astype(f32)
                after = wet[half] * at(W, half, 1).astype(f32)
                wx.append(
                    cell_weights(
                        *face_parts(before, at(VE, half, -1), at(FE, half, -1)),
                        *face_parts(after, at(VE, half, 0), at(FE, half, 0)),
                    )
                )
            wet_out = outer(F + 2)
            following = along_lanes(wet[0], wet[1], wet_out, 1)
            own = [
                face_parts(
                    wet[half] * following[half],
                    VN[half, z, 8 * xt : 8 * xt + 8, :],
                    FN[0, half, z, 8 * xt : 8 * xt + 8, :].astype(f32),
                )
                for half in range(2)
            ]
            beyond = face_parts(wet_out * rolled(wet[0], -1, 1), outer(F), outer(F + 1))
            before = [along_lanes(own[0][i], own[1][i], beyond[i], -1) for i in range(3)]
            wy = [
                cell_weights(*(before[i][half] for i in range(3)), *own[half]) for half in range(2)
            ]
            centre = [
                wx[half][3] + wy[half][3] - (gain_up + gain_down) * wet[half] for half in range(2)
            ]
            w_up = [gain_up * wet[half] for half in range(2)]
            w_down = [gain_down * wet[half] for half in range(2)]
            for half in range(2):
                for d in range(1, 4):
                    if xt == 0:
                        weights_out[half, z, d - 1] = jnp.where(rows < d, wx[half][3 - d], 0.0)
                    else:
                        weights_out[half, z, d - 1] += jnp.where(
                            rows >= 8 - d, wx[half][3 + d], 0.0
                        )
            for f in range(F):
                own_cells = [X[half, f, z, start : start + 8, :] for half in range(2)]
                total = [
                    centre[half] * own_cells[half]
                    + w_up[half] * X[half, f, z_up, start : start + 8, :]
                    + w_down[half] * X[half, f, z_down, start : start + 8, :]
                    for half in range(2)
                ]
                edge = outer(f)
                for offset in (-3, -2, -1, 1, 2, 3):
                    moved = along_lanes(own_cells[0], own_cells[1], edge, offset)
                    for half in range(2):
                        total[half] += wx[half][3 + offset] * X[
                            half, f, z, start + offset : start + offset + 8, :
                        ]
                        total[half] += wy[half][3 + offset] * moved[half]
                for half in range(2):
                    columns = slice(LANES * half, LANES * half + LANES)
                    if f == M:
                        mean_out[z, 8 * xt : 8 * xt + 8, columns] = (
                            own_cells[half] + time_step * total[half]
                        )
                    elif xt == 0:
                        T[half, f] = total[half]
                    else:
                        near = T[half, f]
                        cells = X[half, f, z, 8:16, :]
                        low_rows = rows < 4
                        Z[8 * f : 8 * f + 8, columns] = jnp.where(
                            low_rows, own_cells[half], cells
                        )
                        Z[128 + 8 * f : 136 + 8 * f, columns] = jnp.where(
                            low_rows, total[half], near
                        )
                        edge_out[z, 8 * f : 8 * f + 8, columns] = jnp.where(
                            low_rows, cells, own_cells[half]
                        )
                        edge_out[z, 128 + 8 * f : 136 + 8 * f, columns] = jnp.where(
                            low_rows, near, total[half]
                        )
        high, low = split(Z[...])
        high_out[z] = high
        low_out[z] = low
        add_products(acc, high, low)
        return carry

    lax.fori_loop(0, NZ, level, 0)
    sums_out[...] = field_sums(acc)


def interior(modes, mean, ve, vn, fe, fn, mask, lower, upper, west, east):
    parts = jax.ShapeDtypeStruct((NZ, 256, 256), bf16)
    return pl.pallas_call(
        interior_kernel,
        out_shape=(
            parts,
            parts,
            jax.ShapeDtypeStruct((NZ, 256, 256), f32),
            jax.ShapeDtypeStruct((2, NZ, 3, 8, LANES), f32),
            jax.ShapeDtypeStruct(mean.shape, f32),
            jax.ShapeDtypeStruct((64, 32), f32),
        ),
        in_specs=[ANY] * 7 + [VMEM] * 4,
        out_specs=(VMEM,) * 6,
        scratch_shapes=[
            pltpu.VMEM((2, F, NZ, 32, LANES), f32),
            pltpu.VMEM((2, NZ, 32, LANES), f32),
            pltpu.VMEM((2, NZ, 32, LANES), f32),
            pltpu.VMEM((2, NZ, 32, LANES), jnp.int32),
            pltpu.VMEM((2, NZ, BX, LANES), f32),
            pltpu.VMEM((2, 2, NZ, BX, LANES), jnp.int32),
            pltpu.VMEM((2, M, 8, LANES), f32),
            pltpu.VMEM((256, 256), f32),
            pltpu.VMEM((512, 256), f32),
            pltpu.SemaphoreType.DMA((14,)),
        ],
        compiler_params=params(),
        cost_estimate=cost(10**10, 4 * 10**7),
        name="interior",
    )(modes, mean, ve, vn, fe, fn, mask, lower, upper, west, east)


def edge_kernel(
    below, above, edge_in, weights, mean_in, sums_in,
    high_out, low_out, mean_out, sums_out, HL, HU, E, acc, sems,
):
    copies = [
        pltpu.make_async_copy(below, HL.at[:, :, pl.ds(0, ROWS)], sems.at[0]),
        pltpu.make_async_copy(above, HU.at[:, :, pl.ds(8, ROWS)], sems.at[1]),
        pltpu.make_async_copy(edge_in, E, sems.at[2]),
    ]
    for half in range(2):
        for f in range(F):
            HL[half, f, ROWS : ROWS + 8, :] = jnp.zeros((8, LANES), f32)
            HU[half, f, 0:8, :] = jnp.zeros((8, LANES), f32)
    for copy in copies:
        copy.start()
    acc[...] = jnp.zeros((512, 256), f32)
    for copy in copies:
        copy.wait()
    low_rows = row_ids() < 4

    def change(f, half, z):
        total = None
        for d in range(1, 4):
            first = 3 * z + 3 - d
            second = 3 * z + d
            cells = jnp.where(
                low_rows, HL[half, f, first : first + 8, :], HU[half, f, second : second + 8, :]
            )
            term = weights[half, z, d - 1] * cells
            total = term if total is None else total + term
        return total

    def mode(f, carry):
        place = pl.ds(pl.multiple_of(128 + 8 * f, 8), 8)
        for half in range(2):
            columns = slice(LANES * half, LANES * half + LANES)
            for z in range(NZ):
                E[z, place, columns] += change(f, half, z)
        return carry

    lax.fori_loop(0, M, mode, 0)
    for half in range(2):
        columns = slice(LANES * half, LANES * half + LANES)
        for z in range(NZ):
            step = time_step * change(M, half, z)
            mean_out[z, 0:8, columns] = mean_in[z, 0:8, columns] + jnp.where(low_rows, step, 0.0)
            mean_out[z, 8:16, columns] = mean_in[z, 8:16, columns] + jnp.where(low_rows, 0.0, step)

    def level(z, carry):
        high, low = split(E[z])
        high_out[z] = high
        low_out[z] = low
        add_products(acc, high, low)
        return carry

    lax.fori_loop(0, NZ, level, 0)
    sums = sums_in[...] + field_sums(acc)
    identity = (
        lax.broadcasted_iota(jnp.int32, (32, 32), 0) == lax.broadcasted_iota(jnp.int32, (32, 32), 1)
    ).astype(f32)
    turned = lax.dot_general(
        identity, sums[32:64], (((1,), (1,)), ((), ())), precision=HIGH, preferred_element_type=f32
    )
    sums_out[...] = sums[0:32] + sums[32:64] + turned


def edges(below, above, edge_in, weights, mean_in, sums_in):
    parts = jax.ShapeDtypeStruct((NZ, 256, 256), bf16)
    return pl.pallas_call(
        edge_kernel,
        out_shape=(
            parts,
            parts,
            jax.ShapeDtypeStruct(mean_in.shape, f32),
            jax.ShapeDtypeStruct((32, 32), f32),
        ),
        in_specs=[ANY] * 3 + [VMEM] * 3,
        out_specs=(VMEM,) * 4,
        scratch_shapes=[
            pltpu.VMEM((2, F, ROWS + 8, LANES), f32),
            pltpu.VMEM((2, F, ROWS + 8, LANES), f32),
            pltpu.VMEM((NZ, 256, 256), f32),
            pltpu.VMEM((512, 256), f32),
            pltpu.SemaphoreType.DMA((3,)),
        ],
        compiler_params=params(),
        cost_estimate=cost(10**9, 10**7),
        name="edges",
    )(below, above, edge_in, weights, mean_in, sums_in)


def factor_and_map(sums, cell_count):
    inner = sums * (1.0 / cell_count)
    row = lax.broadcasted_iota(jnp.int32, (M, 2 * M), 0)
    column = lax.broadcasted_iota(jnp.int32, (M, 2 * M), 1)
    update = jnp.where(
        column < M,
        jnp.where(column == row, 1.0, 0.0) - time_step * inner[M : 2 * M, :],
        jnp.where(column == row + M, time_step, 0.0),
    )
    half_way = jnp.dot(update, inner, precision=HIGH, preferred_element_type=f32)
    gram = lax.dot_general(
        half_way, update, (((1,), (1,)), ((), ())), precision=HIGH, preferred_element_type=f32
    )
    row_g = lax.broadcasted_iota(jnp.int32, (M, M), 0)
    column_g = lax.broadcasted_iota(jnp.int32, (M, M), 1)
    left, right = gram, update
    for j in range(M):
        pivot = jnp.sum(jnp.where(column_g == j, left, 0.0), axis=1, keepdims=True)
        scale = 1.0 / jnp.sqrt(pivot[j : j + 1, :])
        left_row = left[j : j + 1, :] * scale
        right_row = right[j : j + 1, :] * scale
        share = jnp.where(row_g[:, 0:1] > j, pivot * scale, 0.0)
        left = jnp.where(row_g == j, left_row, left - share * left_row)
        right = jnp.where(row == j, right_row, right - share * right_row)
    return jnp.where(column_g >= row_g, left, 0.0), right


def spread_map(part):
    tall = (
        lax.broadcasted_iota(jnp.int32, (8 * M, M), 0) // 8
        == lax.broadcasted_iota(jnp.int32, (8 * M, M), 1)
    ).astype(bf16)
    wide = (
        lax.broadcasted_iota(jnp.int32, (2 * M, 256), 1) // 8
        == lax.broadcasted_iota(jnp.int32, (2 * M, 256), 0)
    ).astype(bf16)
    rows = jnp.dot(tall, part, preferred_element_type=f32).astype(bf16)
    full = jnp.dot(rows, wide, preferred_element_type=f32)
    row = lax.broadcasted_iota(jnp.int32, (8 * M, 256), 0)
    column = lax.broadcasted_iota(jnp.int32, (8 * M, 256), 1)
    return jnp.where(row % 8 == column % 8, full, 0.0).astype(bf16)


def make_apply_kernel(cell_count):
    def apply_kernel(sums, high_i, low_i, high_e, low_e, out, factor_out, maps):
        @pl.when(pl.program_id(0) == 0)
        def _():
            factor, mapping = factor_and_map(sums[...], cell_count)
            factor_out[...] = factor
            high, low = split(mapping)
            maps[0:128, :] = spread_map(high)
            maps[128:256, :] = spread_map(low)

        low_rows = lax.broadcasted_iota(jnp.int32, (M, 8, 256), 1) < 4
        for z in range(ZG):
            results = []
            for high, low in ((high_i, low_i), (high_e, low_e)):
                first = jnp.dot(maps[...], high[z], preferred_element_type=f32)
                second = jnp.dot(maps[0:128, :], low[z], preferred_element_type=f32)
                results.append((first[0:128] + first[128:256] + second).reshape(M, 8, 256))
            inner, edge = results
            out[:, z, 0:8, :] = jnp.where(low_rows, edge, inner)
            out[:, z, 8:16, :] = jnp.where(low_rows, inner, edge)

    return apply_kernel


def apply_map(sums, high_i, low_i, high_e, low_e, cell_count):
    block = pl.BlockSpec((ZG, 256, 256), lambda i: (i, 0, 0))
    return pl.pallas_call(
        make_apply_kernel(cell_count),
        grid=(NZ // ZG,),
        out_shape=(
            jax.ShapeDtypeStruct((M, NZ, BX, 256), f32),
            jax.ShapeDtypeStruct((M, M), f32),
        ),
        in_specs=[pl.BlockSpec((32, 32), lambda i: (0, 0)), block, block, block, block],
        out_specs=(
            pl.BlockSpec((M, ZG, BX, 256), lambda i: (0, i, 0, 0)),
            pl.BlockSpec((M, M), lambda i: (0, 0)),
        ),
        scratch_shapes=[pltpu.VMEM((256, 256), bf16)],
        compiler_params=params(),
        cost_estimate=cost(10**9, 13 * 10**6),
        name="apply",
    )(sums, high_i, low_i, high_e, low_e)


def onward(value, axis):
    size = lax.axis_size(axis)
    return lax.ppermute(value, axis, [(i, i + 1) for i in range(size - 1)])


def backward(value, axis):
    size = lax.axis_size(axis)
    return lax.ppermute(value, axis, [(i + 1, i) for i in range(size - 1)])


def exchanged(value, axes, distance):
    size = lax.axis_size(axes)
    return lax.ppermute(value, axes, [(i, i ^ distance) for i in range(size)])


def shards(
    mean_field, mode_fields, velocity_east, velocity_north, flag_east, flag_north, ocean_mask
):
    axes = ("gx", "gy")
    last = BX - 1
    lower_send = jnp.stack(
        [
            velocity_east[:, last],
            flag_east[:, last].astype(f32),
            ocean_mask[:, last].astype(f32),
        ]
    )
    lower = onward(lower_send, "gx")
    upper = backward(ocean_mask[:, 0].astype(f32), "gx")
    up, down, east_send, west_send = pack(
        mode_fields, mean_field, velocity_north, flag_north, ocean_mask
    )
    below = onward(up, "gx")
    above = backward(down, "gx")
    west = onward(east_send, "gy")
    east = backward(west_send, "gy")
    high_i, low_i, edge, weights, mean_part, sums_i = interior(
        mode_fields, mean_field, velocity_east, velocity_north, flag_east, flag_north,
        ocean_mask, lower, upper, west, east,
    )
    high_e, low_e, mean_next, sums = edges(below, above, edge, weights, mean_part, sums_i)
    for distance in (1, 2, 6, 8, 24, 32, 96):
        sums = sums + exchanged(sums, axes, distance)
    cell_count = float(NZ * BX * 256 * lax.axis_size("gx") * lax.axis_size("gy"))
    modes_next, factor = apply_map(sums, high_i, low_i, high_e, low_e, cell_count)
    return (mean_next, modes_next, factor)


def solution(mesh):
    plane = P(None, "gx", "gy")
    return jax.shard_map(
        shards,
        mesh=mesh,
        in_specs=(plane, P(None, None, "gx", "gy"), plane, plane, plane, plane, plane),
        out_specs=(plane, P(None, None, "gx", "gy"), P()),
        check_vma=False,
    )
```

time: 436 us -> 131 us (0.30); the launches traced: 429 us -> 129 us
  other arithmetic: 168 us -> 1.36 us
  blocking collectives: 130 us -> 0 us
  Pallas kernels: 0 us -> 73.4 us
  local copies, waits for them, and re-layouts: 67.6 us -> 5.3 us
  matrix products: 28.3 us -> 0 us
  starting transfers between devices: 17.8 us -> 37.1 us
  waiting for transfers between devices: 15.9 us -> 11.4 us
    psum x2 -> x0, blocking collectives: 130 us -> none  [the longest x1 66.4 us: shards(): lax.psum(jnp.dot(flat_modes, flat_tend.T, precision=highest), ('gx', 'gy'))]
    div x3 -> x0, other arithmetic: 85.3 us -> none  [the longest x1 85.3 us: lower_inverse(): rows_out.append(partial_value / lower_factor[row_index, row_index])]
    pallas_call x0 -> x4, Pallas kernels: none -> 73.4 us  [the longest x1 45.9 us: interior(): pl.pallas_call(interior_kernel, out_shape=(parts, parts, jax.ShapeDtypeSt...]
    mul x9 -> x0, other arithmetic: 56.1 us -> none  [the longest x2 30.7 us: face_fluxes(): openness * (pos_speed * left_side + neg_speed * right_side - horiz_diff *...]
    dot_general x4 -> x0, matrix products: 28.3 us -> none  [the longest x1 8.91 us: shards(): growth = flat_tend - jnp.dot(projection.T, flat_modes, precision=highest)]
    slice x16 -> x3, local copies, waits for them, and re-layouts: 27.6 us -> 2.84 us  [the longest x1 0.99 us: shards(): upper = backward(ocean_mask[:, 0].astype(f32), 'gx')]
    unnamed x38 -> x13, local copies, waits for them, and re-layouts: 25.5 us -> 2.46 us
    concatenate x4 -> x0, other arithmetic: 20.5 us -> none  [extended(): value = jnp.concatenate([before, value, after], axis=dim)]
  transfers between devices with their start and end apart: 6 -> 13, of which waited for: 2 -> 7; matrix products, arithmetic and copies ran while one was open for 18% -> 0% of each run, Pallas kernels for 0% -> 39%
where the time goes in v1:
time: 131 us; the launch traced here: 129 us
  Pallas kernels  73.4 us (56%)
  starting transfers between devices  37.1 us (28%)
  waiting for transfers between devices  11.4 us (9%)
  local copies, waits for them, and re-layouts  5.3 us (4%)
  other arithmetic  1.36 us (1%)
    pallas_call x1, Pallas kernels, interior(): pl.pallas_call(interior_kernel, out_shape=(parts, parts, jax.ShapeDtypeSt...  45.9 us
    ppermute x7, starting transfers between devices, exchanged(): return lax.ppermute(value, axes, [(i, i ^ distance) for i in range(size)])  23.2 us
    pallas_call x1, Pallas kernels, edges(): pl.pallas_call(edge_kernel, out_shape=(parts, parts, jax.ShapeDtypeStruct...  11.6 us
    ppermute x7, waiting for transfers between devices, exchanged(): return lax.ppermute(value, axes, [(i, i ^ distance) for i in range(size)])  11.3 us
    pallas_call x1, Pallas kernels, apply_map(): pl.pallas_call(make_apply_kernel(cell_count), grid=(NZ // ZG,), out_shape...  10.8 us
    ppermute x3, starting transfers between devices, onward(): return lax.ppermute(value, axis, [(i, i + 1) for i in range(size - 1)])  9.97 us
    pallas_call x1, Pallas kernels, pack(): pl.pallas_call(pack_kernel, out_shape=(rows, rows, columns, columns), in_...  5.11 us
    ppermute x3, starting transfers between devices, backward(): return lax.ppermute(value, axis, [(i + 1, i) for i in range(size - 1)])  3.88 us
  transfers between devices with their start and end apart: 13, of which 7 were waited for; matrix products, arithmetic and copies ran while one was open for 0% of the time, Pallas kernels for 39%

profile of v1, /device:TPU:0, one launch (start us, length us, event | category | flops | bytes accessed | tf_op | source)
XLA Modules:
  0.0 129.3 jit_solution(6102406281582188670)
XLA Ops:
  0.6 0.9 slice.12
  1.6 0.9 slice.13
  2.5 1.0 fusion.3
  3.5 3.9 %collective-permute-start.2 = (f32[3,16,256]{2,1,0:T(8,128)S(1)}, f32[3,16,256]{2,1,0:T(8,128)S(1)}, u32[]{:S(2)}, u32[]{:S(2)}) collective-permute-start(f32[3,16,256]{2,1,0:T(8,128)S(1)} %pad_maximum_fusion), channel_id=1, source_target_pairs={{0,8},{8,16},{16,24},{24,32},{32,40},{40,48},{48,56},{56,64},{64,7... | collective-permute-start | bytes 147464 | tf_op jit(solution)/shard_map/ppermute | solution.py:583
  7.4 5.1 %pack.1 = (f32[2,17,48,128]{3,2,1,0:T(8,128)}, f32[2,17,48,128]{3,2,1,0:T(8,128)}, f32[20,8,128]{2,1,0:T(8,128)}, f32[20,8,128]{2,1,0:T(8,128)}) custom-call(f32[16,16,16,256]{3,2,1,0:T(8,128)} %modes.3, f32[16,16,256]{2,1,0:T(8,128)} %mean.3, f32[16,16,256]{2,1,0:T(8,128)} %vn.3, s32[16,16,256]{2,1,0:T(8,128)} %fn.3, s32[16,16,256]{2,1,0:T(8,128)} %mask.3), custom_call_target="tpu_custom_call" | custom-call | flops 10000000 | bytes 7000000 | tf_op jit(solution)/shard_map/pack/pallas_call | solution.py:140
  12.6 1.5 %collective-permute-start.4 = (f32[20,8,128]{2,1,0:T(8,128)}, f32[20,8,128]{2,1,0:T(8,128)S(1)}, u32[]{:S(2)}, u32[]{:S(2)}) collective-permute-start(f32[20,8,128]{2,1,0:T(8,128)} %get-tuple-element.21), channel_id=1, source_target_pairs={{0,1},{1,2},{2,3},{3,4},{4,5},{5,6},{6,7},{8,9},{9,10},{10,11},{11... | collective-permute-start | bytes 245768 | tf_op jit(solution)/shard_map/ppermute | solution.py:583
  14.0 1.3 collective-permute-start.5
  15.3 1.3 collective-permute-start.3
  16.6 4.6 %collective-permute-start = (f32[2,17,48,128]{3,2,1,0:T(8,128)}, f32[2,17,48,128]{3,2,1,0:T(8,128)S(1)}, u32[]{:S(2)}, u32[]{:S(2)}) collective-permute-start(f32[2,17,48,128]{3,2,1,0:T(8,128)} %get-tuple-element.19), channel_id=1, source_target_pairs={{0,8},{8,16},{16,24},{24,32},{32,40},{40,48},{48,56},{56,64},{64,7... | collective-permute-start | bytes 2506760 | tf_op jit(solution)/shard_map/ppermute | solution.py:583
  21.3 0.0 collective-permute-done.3.upper
  21.3 0.0 copy-start.5
  21.3 1.3 collective-permute-start.1
  22.6 0.0 collective-permute-done.2.lower
  22.6 0.0 copy-start.4
  22.6 0.0 collective-permute-done.4.west
  22.6 0.0 copy-start.2
  22.6 0.0 collective-permute-done.5.east
  22.6 0.0 copy-done.5
  22.6 0.6 copy-done.4
  23.2 0.1 copy-done.2
  23.2 0.0 copy-start.3
  23.2 0.6 copy-done.3
  23.9 45.9 %interior.1 = (bf16[16,256,256]{2,1,0:T(8,128)(2,1)}, bf16[16,256,256]{2,1,0:T(8,128)(2,1)}, f32[16,256,256]{2,1,0:T(8,128)}, f32[2,16,3,8,128]{4,3,2,1,0:T(8,12...) custom-call(f32[16,16,16,256]{3,2,1,0:T(8,128)} %modes.3, f32[16,16,256]{2,1,0:T(8,128)} %mean.3, f32[16,16,256]{2,1,0:T(8,128)} %ve.1, ...), custom_call_target="tpu_custom_call" | custom-call | flops 10000000000 | bytes 40000000 | tf_op jit(solution)/shard_map/interior/pallas_call | solution.py:372
  69.8 0.0 collective-permute-done.below
  69.8 0.0 copy-start
  69.8 0.0 collective-permute-done.1.above
  69.8 0.0 copy-start.1
  69.8 1.0 copy-done
  70.8 0.2 copy-done.1
  71.0 11.6 %edges.1 = (bf16[16,256,256]{2,1,0:T(8,128)(2,1)}, bf16[16,256,256]{2,1,0:T(8,128)(2,1)}, f32[16,16,256]{2,1,0:T(8,128)}, f32[32,32]{1,0:T(8,128)}) custom-call(f32[2,17,48,128]{3,2,1,0:T(8,128)} %copy-done, f32[2,17,48,128]{3,2,1,0:T(8,128)} %copy-done.1, f32[16,256,256]{2,1,0:T(8,128)} %get-tuple-element.23.edge_in, ...), custom_call_target="tpu_custom_call" | custom-call | flops 1000000000 | bytes 10000000 | tf_op jit(solution)/shard_map/edges/pallas_call | solution.py:470
  82.6 2.5 %collective-permute-start.6 = (f32[32,32]{1,0:T(8,128)}, f32[32,32]{1,0:T(8,128)S(1)}, u32[]{:S(2)}, u32[]{:S(2)}) collective-permute-start(f32[32,32]{1,0:T(8,128)} %get-tuple-element.28), channel_id=1, source_target_pairs={{0,1},{1,0},{2,3},{3,2},{4,5},{5,4},{6,7},{7,6},{8,9},{9,8},{10,11... | collective-permute-start | bytes 12296 | tf_op jit(solution)/shard_map/ppermute | solution.py:593
  85.1 1.0 collective-permute-done.6
  86.2 0.7 add.21
  86.9 2.3 %collective-permute-start.7 = (f32[32,32]{1,0:T(8,128)S(1)}, f32[32,32]{1,0:T(8,128)S(1)}, u32[]{:S(2)}, u32[]{:S(2)}) collective-permute-start(f32[32,32]{1,0:T(8,128)S(1)} %add.21), channel_id=1, source_target_pairs={{0,2},{1,3},{2,0},{3,1},{4,6},{5,7},{6,4},{7,5},{8,10},{9,11},{10,... | collective-permute-start | bytes 12296 | tf_op jit(solution)/shard_map/ppermute | solution.py:593
  89.2 1.7 %collective-permute-done.7 = f32[32,32]{1,0:T(8,128)S(1)} collective-permute-done((f32[32,32]{1,0:T(8,128)S(1)}, f32[32,32]{1,0:T(8,128)S(1)}, u32[]{:S(2)}, u32[]{:S(2)}) %collective-permute-start.7) | collective-permute-done | bytes 4128 | tf_op jit(solution)/shard_map/ppermute | solution.py:593
  90.9 3.5 %collective-permute-start.8 = (f32[32,32]{1,0:T(8,128)S(1)}, f32[32,32]{1,0:T(8,128)S(1)}, u32[]{:S(2)}, u32[]{:S(2)}) collective-permute-start(f32[32,32]{1,0:T(8,128)S(1)} %add.22), channel_id=1, source_target_pairs={{0,6},{1,7},{2,4},{3,5},{4,2},{5,3},{6,0},{7,1},{8,14},{9,15},{10,... | collective-permute-start | bytes 12296 | tf_op jit(solution)/shard_map/ppermute | solution.py:593
  94.4 1.7 %collective-permute-done.8 = f32[32,32]{1,0:T(8,128)S(1)} collective-permute-done((f32[32,32]{1,0:T(8,128)S(1)}, f32[32,32]{1,0:T(8,128)S(1)}, u32[]{:S(2)}, u32[]{:S(2)}) %collective-permute-start.8) | collective-permute-done | bytes 4128 | tf_op jit(solution)/shard_map/ppermute | solution.py:593
  96.1 2.6 %collective-permute-start.9 = (f32[32,32]{1,0:T(8,128)S(1)}, f32[32,32]{1,0:T(8,128)S(1)}, u32[]{:S(2)}, u32[]{:S(2)}) collective-permute-start(f32[32,32]{1,0:T(8,128)S(1)} %add.23), channel_id=1, source_target_pairs={{0,8},{1,9},{2,10},{3,11},{4,12},{5,13},{6,14},{7,15},{8,0},{9,1},... | collective-permute-start | bytes 12296 | tf_op jit(solution)/shard_map/ppermute | solution.py:593
  98.8 1.7 %collective-permute-done.9 = f32[32,32]{1,0:T(8,128)S(1)} collective-permute-done((f32[32,32]{1,0:T(8,128)S(1)}, f32[32,32]{1,0:T(8,128)S(1)}, u32[]{:S(2)}, u32[]{:S(2)}) %collective-permute-start.9) | collective-permute-done | bytes 4128 | tf_op jit(solution)/shard_map/ppermute | solution.py:593
  100.5 4.3 %collective-permute-start.10 = (f32[32,32]{1,0:T(8,128)S(1)}, f32[32,32]{1,0:T(8,128)S(1)}, u32[]{:S(2)}, u32[]{:S(2)}) collective-permute-start(f32[32,32]{1,0:T(8,128)S(1)} %add.24), channel_id=1, source_target_pairs={{0,24},{1,25},{2,26},{3,27},{4,28},{5,29},{6,30},{7,31},{8,16},{9,... | collective-permute-start | bytes 12296 | tf_op jit(solution)/shard_map/ppermute | solution.py:593
  104.8 1.7 %collective-permute-done.10 = f32[32,32]{1,0:T(8,128)S(1)} collective-permute-done((f32[32,32]{1,0:T(8,128)S(1)}, f32[32,32]{1,0:T(8,128)S(1)}, u32[]{:S(2)}, u32[]{:S(2)}) %collective-permute-start.10) | collective-permute-done | bytes 4128 | tf_op jit(solution)/shard_map/ppermute | solution.py:593
  106.5 4.5 %collective-permute-start.11 = (f32[32,32]{1,0:T(8,128)S(1)}, f32[32,32]{1,0:T(8,128)S(1)}, u32[]{:S(2)}, u32[]{:S(2)}) collective-permute-start(f32[32,32]{1,0:T(8,128)S(1)} %add.25), channel_id=1, source_target_pairs={{0,32},{1,33},{2,34},{3,35},{4,36},{5,37},{6,38},{7,39},{8,40},{9,... | collective-permute-start | bytes 12296 | tf_op jit(solution)/shard_map/ppermute | solution.py:593
  111.0 1.7 %collective-permute-done.11 = f32[32,32]{1,0:T(8,128)S(1)} collective-permute-done((f32[32,32]{1,0:T(8,128)S(1)}, f32[32,32]{1,0:T(8,128)S(1)}, u32[]{:S(2)}, u32[]{:S(2)}) %collective-permute-start.11) | collective-permute-done | bytes 4128 | tf_op jit(solution)/shard_map/ppermute | solution.py:593
  112.8 3.5 %collective-permute-start.12 = (f32[32,32]{1,0:T(8,128)S(1)}, f32[32,32]{1,0:T(8,128)S(1)}, u32[]{:S(2)}, u32[]{:S(2)}) collective-permute-start(f32[32,32]{1,0:T(8,128)S(1)} %add.26), channel_id=1, source_target_pairs={{0,96},{1,97},{2,98},{3,99},{4,100},{5,101},{6,102},{7,103},{8,104... | collective-permute-start | bytes 12296 | tf_op jit(solution)/shard_map/ppermute | solution.py:593
  116.2 1.7 %collective-permute-done.12 = f32[32,32]{1,0:T(8,128)S(1)} collective-permute-done((f32[32,32]{1,0:T(8,128)S(1)}, f32[32,32]{1,0:T(8,128)S(1)}, u32[]{:S(2)}, u32[]{:S(2)}) %collective-permute-start.12) | collective-permute-done | bytes 4128 | tf_op jit(solution)/shard_map/ppermute | solution.py:593
  118.0 0.6 add.27.sums
  118.6 10.8 %apply.1 = (f32[16,16,16,256]{3,2,1,0:T(8,128)}, f32[16,16]{1,0:T(8,128)}) custom-call(f32[32,32]{1,0:T(8,128)} %add.27.sums, bf16[16,256,256]{2,1,0:T(8,128)(2,1)} %get-tuple-element.29.high_i, bf16[16,256,256]{2,1,0:T(8,128)(2,1)} %get-tuple-element.30.low_i, bf16[16,256,256]{2,1,0:T(8,128)(2,1)} %get-tuple-element.31.high_e, ...), custom_call_target="tpu_custom_call" | custom-call | flops 1000000000 | bytes 13000000 | tf_op jit(solution)/shard_map/apply/pallas_call | solution.py:562
  (10 shorter events, 0.0 us)
Async XLA Ops:
  3.5 19.0 %collective-permute-start.2 = (f32[3,16,256]{2,1,0:T(8,128)S(1)}, f32[3,16,256]{2,1,0:T(8,128)S(1)}, u32[]{:S(2)}, u32[]{:S(2)}) collective-permute-start(f32[3,16,256]{2,1,0:T(8,128)S(1)} %pad_maximum_fusion), channel_id=1, source_target_pairs={{0,8},{8,16},{16,24},{24,32},{32,40},{40,48},{48,56},{56,64},{64,7... | collective-permute-start | bytes 147464 | tf_op jit(solution)/shard_map/ppermute | solution.py:583
  12.6 10.0 %collective-permute-start.4 = (f32[20,8,128]{2,1,0:T(8,128)}, f32[20,8,128]{2,1,0:T(8,128)S(1)}, u32[]{:S(2)}, u32[]{:S(2)}) collective-permute-start(f32[20,8,128]{2,1,0:T(8,128)} %get-tuple-element.21), channel_id=1, source_target_pairs={{0,1},{1,2},{2,3},{3,4},{4,5},{5,6},{6,7},{8,9},{9,10},{10,11},{11... | collective-permute-start | bytes 245768 | tf_op jit(solution)/shard_map/ppermute | solution.py:583
  14.0 8.6 %collective-permute-start.5 = (f32[20,8,128]{2,1,0:T(8,128)}, f32[20,8,128]{2,1,0:T(8,128)S(1)}, u32[]{:S(2)}, u32[]{:S(2)}) collective-permute-start(f32[20,8,128]{2,1,0:T(8,128)} %get-tuple-element.22), channel_id=1, source_target_pairs={{1,0},{2,1},{3,2},{4,3},{5,4},{6,5},{7,6},{9,8},{10,9},{11,10},{12... | collective-permute-start | bytes 245768 | tf_op jit(solution)/shard_map/ppermute | solution.py:588
  15.3 5.9 %collective-permute-start.3 = (f32[16,256]{1,0:T(8,128)S(1)}, f32[16,256]{1,0:T(8,128)S(1)}, u32[]{:S(2)}, u32[]{:S(2)}) collective-permute-start(f32[16,256]{1,0:T(8,128)S(1)} %fusion), channel_id=1, source_target_pairs={{8,0},{16,8},{24,16},{32,24},{40,32},{48,40},{56,48},{64,56},{72,6... | collective-permute-start | bytes 49160 | tf_op jit(solution)/shard_map/ppermute | solution.py:588
  16.6 53.1 %collective-permute-start = (f32[2,17,48,128]{3,2,1,0:T(8,128)}, f32[2,17,48,128]{3,2,1,0:T(8,128)S(1)}, u32[]{:S(2)}, u32[]{:S(2)}) collective-permute-start(f32[2,17,48,128]{3,2,1,0:T(8,128)} %get-tuple-element.19), channel_id=1, source_target_pairs={{0,8},{8,16},{16,24},{24,32},{32,40},{40,48},{48,56},{56,64},{64,7... | collective-permute-start | bytes 2506760 | tf_op jit(solution)/shard_map/ppermute | solution.py:583
  21.3 1.4 %copy-start.5 = (f32[16,256]{1,0:T(8,128)}, f32[16,256]{1,0:T(8,128)S(1)}, u32[]{:S(2)}) copy-start(f32[16,256]{1,0:T(8,128)S(1)} %collective-permute-done.3.upper) | copy-start | bytes 49156
  21.3 48.5 %collective-permute-start.1 = (f32[2,17,48,128]{3,2,1,0:T(8,128)}, f32[2,17,48,128]{3,2,1,0:T(8,128)S(1)}, u32[]{:S(2)}, u32[]{:S(2)}) collective-permute-start(f32[2,17,48,128]{3,2,1,0:T(8,128)} %get-tuple-element.20), channel_id=1, source_target_pairs={{8,0},{16,8},{24,16},{32,24},{40,32},{48,40},{56,48},{64,56},{72,6... | collective-permute-start | bytes 2506760 | tf_op jit(solution)/shard_map/ppermute | solution.py:588
  22.6 0.6 copy-start.4
  22.6 0.6 copy-start.2
  23.2 0.6 copy-start.3
  69.8 1.0 copy-start
  69.8 1.2 copy-start.1
  82.6 3.5 %collective-permute-start.6 = (f32[32,32]{1,0:T(8,128)}, f32[32,32]{1,0:T(8,128)S(1)}, u32[]{:S(2)}, u32[]{:S(2)}) collective-permute-start(f32[32,32]{1,0:T(8,128)} %get-tuple-element.28), channel_id=1, source_target_pairs={{0,1},{1,0},{2,3},{3,2},{4,5},{5,4},{6,7},{7,6},{8,9},{9,8},{10,11... | collective-permute-start | bytes 12296 | tf_op jit(solution)/shard_map/ppermute | solution.py:593
  86.9 4.0 %collective-permute-start.7 = (f32[32,32]{1,0:T(8,128)S(1)}, f32[32,32]{1,0:T(8,128)S(1)}, u32[]{:S(2)}, u32[]{:S(2)}) collective-permute-start(f32[32,32]{1,0:T(8,128)S(1)} %add.21), channel_id=1, source_target_pairs={{0,2},{1,3},{2,0},{3,1},{4,6},{5,7},{6,4},{7,5},{8,10},{9,11},{10,... | collective-permute-start | bytes 12296 | tf_op jit(solution)/shard_map/ppermute | solution.py:593
  90.9 5.2 %collective-permute-start.8 = (f32[32,32]{1,0:T(8,128)S(1)}, f32[32,32]{1,0:T(8,128)S(1)}, u32[]{:S(2)}, u32[]{:S(2)}) collective-permute-start(f32[32,32]{1,0:T(8,128)S(1)} %add.22), channel_id=1, source_target_pairs={{0,6},{1,7},{2,4},{3,5},{4,2},{5,3},{6,0},{7,1},{8,14},{9,15},{10,... | collective-permute-start | bytes 12296 | tf_op jit(solution)/shard_map/ppermute | solution.py:593
  96.1 4.4 %collective-permute-start.9 = (f32[32,32]{1,0:T(8,128)S(1)}, f32[32,32]{1,0:T(8,128)S(1)}, u32[]{:S(2)}, u32[]{:S(2)}) collective-permute-start(f32[32,32]{1,0:T(8,128)S(1)} %add.23), channel_id=1, source_target_pairs={{0,8},{1,9},{2,10},{3,11},{4,12},{5,13},{6,14},{7,15},{8,0},{9,1},... | collective-permute-start | bytes 12296 | tf_op jit(solution)/shard_map/ppermute | solution.py:593
  100.5 6.0 %collective-permute-start.10 = (f32[32,32]{1,0:T(8,128)S(1)}, f32[32,32]{1,0:T(8,128)S(1)}, u32[]{:S(2)}, u32[]{:S(2)}) collective-permute-start(f32[32,32]{1,0:T(8,128)S(1)} %add.24), channel_id=1, source_target_pairs={{0,24},{1,25},{2,26},{3,27},{4,28},{5,29},{6,30},{7,31},{8,16},{9,... | collective-permute-start | bytes 12296 | tf_op jit(solution)/shard_map/ppermute | solution.py:593
  106.5 6.2 %collective-permute-start.11 = (f32[32,32]{1,0:T(8,128)S(1)}, f32[32,32]{1,0:T(8,128)S(1)}, u32[]{:S(2)}, u32[]{:S(2)}) collective-permute-start(f32[32,32]{1,0:T(8,128)S(1)} %add.25), channel_id=1, source_target_pairs={{0,32},{1,33},{2,34},{3,35},{4,36},{5,37},{6,38},{7,39},{8,40},{9,... | collective-permute-start | bytes 12296 | tf_op jit(solution)/shard_map/ppermute | solution.py:593
  112.8 5.2 %collective-permute-start.12 = (f32[32,32]{1,0:T(8,128)S(1)}, f32[32,32]{1,0:T(8,128)S(1)}, u32[]{:S(2)}, u32[]{:S(2)}) collective-permute-start(f32[32,32]{1,0:T(8,128)S(1)} %add.26), channel_id=1, source_target_pairs={{0,96},{1,97},{2,98},{3,99},{4,100},{5,101},{6,102},{7,103},{8,104... | collective-permute-start | bytes 12296 | tf_op jit(solution)/shard_map/ppermute | solution.py:593

commit v2 on v1

--- a/solution.py
+++ b/solution.py
@@ -15,7 +15,7 @@
 BX = 16
 LANES = 128
 ROWS = 3 * NZ
-ZG = 2
+SLOTS = 4
 HIGH = lax.Precision.HIGHEST
 f32 = jnp.float32
 bf16 = jnp.bfloat16
@@ -24,8 +24,8 @@
 VMEM = pl.BlockSpec(memory_space=pltpu.VMEM)
 
 
-def params():
-    return pltpu.CompilerParams(vmem_limit_bytes=56 * 1024 * 1024)
+def params(mib):
+    return pltpu.CompilerParams(vmem_limit_bytes=mib * 1024 * 1024)
 
 
 def cost(flops, nbytes):
@@ -77,7 +77,9 @@
     return out
 
 
-def pack_kernel(modes, mean, vn, fn, mask, up, down, east, west, X, V, I, sems):
+def pack_kernel(
+    modes, mean, ve, vn, fe, fn, mask, up, down, east, west, lower, upper, X, V, I, sems
+):
     copies = []
     for chunk in range(4):
         for half in range(2):
@@ -90,9 +92,11 @@
             )
     for source, target in (
         (mean, lambda half: X.at[half, M]),
-        (vn, lambda half: V.at[half]),
+        (vn, lambda half: V.at[0, half]),
+        (ve, lambda half: V.at[1, half]),
         (fn, lambda half: I.at[0, half]),
         (mask, lambda half: I.at[1, half]),
+        (fe, lambda half: I.at[2, half]),
     ):
         for half in range(2):
             copies.append(
@@ -109,7 +113,7 @@
                         lambda z: X[half, f, 8 * zh + z, 8 * tile : 8 * tile + 8, :], first
                     )
                     for t in range(3):
-                        target[half, f, 24 * zh + 8 * t : 24 * zh + 8 * t + 8, :] = tiles[t]
+                        target[half, f, zh, 8 * t : 8 * t + 8, :] = tiles[t]
         def tile_of(half):
             return lambda k: X[half, f, k // 2, 8 * (k % 2) : 8 * (k % 2) + 8, :]
         east[f] = pack_columns(tile_of(1), lambda k: 4 * k - 125)
@@ -125,33 +129,57 @@
     lax.fori_loop(M, F, field, 0)
     for index, plane in enumerate(
         (
-            lambda half, k: V[half, k // 2, 8 * (k % 2) : 8 * (k % 2) + 8, :],
+            lambda half, k: V[0, half, k // 2, 8 * (k % 2) : 8 * (k % 2) + 8, :],
             lambda half, k: I[0, half, k // 2, 8 * (k % 2) : 8 * (k % 2) + 8, :].astype(f32),
             lambda half, k: I[1, half, k // 2, 8 * (k % 2) : 8 * (k % 2) + 8, :].astype(f32),
         )
     ):
         east[F + index] = pack_columns(lambda k: plane(1, k), lambda k: 4 * k - 125)
         west[F + index] = pack_columns(lambda k: plane(0, k), lambda k: 4 * k)
-
-
-def pack(modes, mean, vn, fn, mask):
-    rows = jax.ShapeDtypeStruct((2, F, ROWS, LANES), f32)
+    rows = row_ids()
+    for half in range(2):
+        for zh in range(2):
+            tiles = [jnp.zeros((8, LANES), f32) for _ in range(4)]
+            for z in range(8):
+                level = 8 * zh + z
+                sources = (
+                    rolled(V[1, half, level, 8:16, :], z - 7, 0),
+                    rolled(I[2, half, level, 8:16, :].astype(f32), z - 7, 0),
+                    rolled(I[1, half, level, 8:16, :].astype(f32), z - 7, 0),
+                    rolled(I[1, half, level, 0:8, :].astype(f32), z, 0),
+                )
+                tiles = [jnp.where(rows == z, new, old) for new, old in zip(sources, tiles)]
+            place = slice(8 * zh, 8 * zh + 8), slice(LANES * half, LANES * half + LANES)
+            for index in range(3):
+                lower[index, place[0], place[1]] = tiles[index]
+            upper[place[0], place[1]] = tiles[3]
+
+
+def pack(modes, mean, ve, vn, fe, fn, mask):
+    rows = jax.ShapeDtypeStruct((2, F, 2, ROWS // 2, LANES), f32)
     columns = jax.ShapeDtypeStruct((F + 3, 8, LANES), f32)
     return pl.pallas_call(
         pack_kernel,
-        out_shape=(rows, rows, columns, columns),
-        in_specs=[ANY] * 5,
-        out_specs=(VMEM,) * 4,
+        out_shape=(
+            rows,
+            rows,
+            columns,
+            columns,
+            jax.ShapeDtypeStruct((3, NZ, 2 * LANES), f32),
+            jax.ShapeDtypeStruct((NZ, 2 * LANES), f32),
+        ),
+        in_specs=[ANY] * 7,
+        out_specs=(VMEM,) * 6,
         scratch_shapes=[
             pltpu.VMEM((2, F, NZ, BX, LANES), f32),
-            pltpu.VMEM((2, NZ, BX, LANES), f32),
-            pltpu.VMEM((2, 2, NZ, BX, LANES), jnp.int32),
-            pltpu.SemaphoreType.DMA((16,)),
+            pltpu.VMEM((2, 2, NZ, BX, LANES), f32),
+            pltpu.VMEM((3, 2, NZ, BX, LANES), jnp.int32),
+            pltpu.SemaphoreType.DMA((20,)),
         ],
-        compiler_params=params(),
+        compiler_params=params(12),
         cost_estimate=cost(10**7, 7 * 10**6),
         name="pack",
-    )(modes, mean, vn, fn, mask)
+    )(modes, mean, ve, vn, fe, fn, mask)
 
 
 def along_lanes(first, second, outer, offset):
@@ -207,7 +235,7 @@
 def interior_kernel(
     modes, mean, ve, vn, fe, fn, mask, lower, upper, west, east,
     high_out, low_out, edge_out, weights_out, mean_out, sums_out,
-    X, VE, FE, W, VN, FN, T, Z, acc, sems,
+    X, VE, FE, W, VN, FN, H, T, Z, acc, sems,
 ):
     zero_tile = jnp.zeros((8, LANES), f32)
 
@@ -228,6 +256,8 @@
             W[half, z, 0:8, :] = spread(lower[2, z : z + 1, lanes]).astype(jnp.int32)
             W[half, z, 24:32, :] = spread(upper[z : z + 1, lanes]).astype(jnp.int32)
     acc[...] = jnp.zeros((512, 256), f32)
+    lanes = lane_ids()
+    rows = row_ids()
 
     copies = []
     body = pl.ds(8, BX)
@@ -246,11 +276,18 @@
             )
     for copy in copies:
         copy.start()
+
+    def beside(f, carry):
+        after, before = east[f], west[f]
+        for k in range(2 * NZ):
+            H[f, k] = jnp.where(
+                lanes < 64, rolled(after, -4 * k, 1), rolled(before, LANES - 3 - 4 * k, 1)
+            )
+        return carry
+
+    lax.fori_loop(0, F + 3, beside, 0)
     for copy in copies:
         copy.wait()
-
-    lanes = lane_ids()
-    rows = row_ids()
 
     def level(z, carry):
         gain_up = jnp.where(z < NZ - 1, vert_diff, 0.0).astype(f32)
@@ -264,16 +301,9 @@
                 ].astype(f32)
         for xt in range(2):
             start = 8 + 8 * xt
-            slot = 2 * z + xt
-            after_shift = lax.rem(LANES - 4 * slot, LANES)
-            before_shift = LANES - 3 - 4 * slot
 
             def outer(index):
-                return jnp.where(
-                    lanes < 64,
-                    pltpu.roll(east[index], after_shift, 1),
-                    pltpu.roll(west[index], before_shift, 1),
-                )
+                return H[index, 2 * z + xt]
 
             def at(ref, half, offset):
                 return ref[half, z, start + offset : start + offset + 8, :]
@@ -388,73 +418,63 @@
             pltpu.VMEM((2, NZ, 32, LANES), jnp.int32),
             pltpu.VMEM((2, NZ, BX, LANES), f32),
             pltpu.VMEM((2, 2, NZ, BX, LANES), jnp.int32),
+            pltpu.VMEM((F + 3, 2 * NZ, 8, LANES), f32),
             pltpu.VMEM((2, M, 8, LANES), f32),
             pltpu.VMEM((256, 256), f32),
             pltpu.VMEM((512, 256), f32),
             pltpu.SemaphoreType.DMA((14,)),
         ],
-        compiler_params=params(),
-        cost_estimate=cost(10**10, 4 * 10**7),
+        compiler_params=params(28),
+        cost_estimate=cost(10**6, 10**6),
         name="interior",
     )(modes, mean, ve, vn, fe, fn, mask, lower, upper, west, east)
 
 
 def edge_kernel(
     below, above, edge_in, weights, mean_in, sums_in,
-    high_out, low_out, mean_out, sums_out, HL, HU, E, acc, sems,
+    high_out, low_out, mean_out, sums_out, Z, acc,
 ):
-    copies = [
-        pltpu.make_async_copy(below, HL.at[:, :, pl.ds(0, ROWS)], sems.at[0]),
-        pltpu.make_async_copy(above, HU.at[:, :, pl.ds(8, ROWS)], sems.at[1]),
-        pltpu.make_async_copy(edge_in, E, sems.at[2]),
-    ]
-    for half in range(2):
-        for f in range(F):
-            HL[half, f, ROWS : ROWS + 8, :] = jnp.zeros((8, LANES), f32)
-            HU[half, f, 0:8, :] = jnp.zeros((8, LANES), f32)
-    for copy in copies:
-        copy.start()
     acc[...] = jnp.zeros((512, 256), f32)
-    for copy in copies:
-        copy.wait()
     low_rows = row_ids() < 4
 
-    def change(f, half, z):
-        total = None
-        for d in range(1, 4):
-            first = 3 * z + 3 - d
-            second = 3 * z + d
-            cells = jnp.where(
-                low_rows, HL[half, f, first : first + 8, :], HU[half, f, second : second + 8, :]
-            )
-            term = weights[half, z, d - 1] * cells
-            total = term if total is None else total + term
-        return total
-
-    def mode(f, carry):
-        place = pl.ds(pl.multiple_of(128 + 8 * f, 8), 8)
-        for half in range(2):
-            columns = slice(LANES * half, LANES * half + LANES)
-            for z in range(NZ):
-                E[z, place, columns] += change(f, half, z)
+    def rows_from(ref, half, f, zh, first):
+        start = min(max(first, 0), 16)
+        return rolled(ref[half, f, zh, start : start + 8, :], start - first, 0)
+
+    def group(zh, carry):
+        for zi in range(8):
+            z = 8 * zh + zi
+            for half in range(2):
+                columns = slice(LANES * half, LANES * half + LANES)
+                gains = [weights[half, z, d - 1] for d in range(1, 4)]
+                for f in range(F):
+                    change = None
+                    for d in range(1, 4):
+                        cells = jnp.where(
+                            low_rows,
+                            rows_from(below, half, f, zh, 3 * zi + 3 - d),
+                            rows_from(above, half, f, zh, 3 * zi + d - 8),
+                        )
+                        term = gains[d - 1] * cells
+                        change = term if change is None else change + term
+                    if f < M:
+                        place = slice(8 * f, 8 * f + 8)
+                        Z[place, columns] = edge_in[z, 128 + 8 * f : 136 + 8 * f, columns] + change
+                    else:
+                        step = time_step * change
+                        mean_out[z, 0:8, columns] = mean_in[z, 0:8, columns] + jnp.where(
+                            low_rows, step, 0.0
+                        )
+                        mean_out[z, 8:16, columns] = mean_in[z, 8:16, columns] + jnp.where(
+                            low_rows, 0.0, step
+                        )
+            high, low = split(jnp.concatenate([edge_in[z, 0:128, :], Z[...]], axis=0))
+            high_out[z] = high
+            low_out[z] = low
+            add_products(acc, high, low)
         return carry
 
-    lax.fori_loop(0, M, mode, 0)
-    for half in range(2):
-        columns = slice(LANES * half, LANES * half + LANES)
-        for z in range(NZ):
-            step = time_step * change(M, half, z)
-            mean_out[z, 0:8, columns] = mean_in[z, 0:8, columns] + jnp.where(low_rows, step, 0.0)
-            mean_out[z, 8:16, columns] = mean_in[z, 8:16, columns] + jnp.where(low_rows, 0.0, step)
-
-    def level(z, carry):
-        high, low = split(E[z])
-        high_out[z] = high
-        low_out[z] = low
-        add_products(acc, high, low)
-        return carry
-
-    lax.fori_loop(0, NZ, level, 0)
+    lax.fori_loop(0, 2, group, 0)
     sums = sums_in[...] + field_sums(acc)
     identity = (
         lax.broadcasted_iota(jnp.int32, (32, 32), 0) == lax.broadcasted_iota(jnp.int32, (32, 32), 1)
@@ -475,16 +495,13 @@
             jax.ShapeDtypeStruct(mean_in.shape, f32),
             jax.ShapeDtypeStruct((32, 32), f32),
         ),
-        in_specs=[ANY] * 3 + [VMEM] * 3,
+        in_specs=[VMEM] * 6,
         out_specs=(VMEM,) * 4,
         scratch_shapes=[
-            pltpu.VMEM((2, F, ROWS + 8, LANES), f32),
-            pltpu.VMEM((2, F, ROWS + 8, LANES), f32),
-            pltpu.VMEM((NZ, 256, 256), f32),
+            pltpu.VMEM((128, 256), f32),
             pltpu.VMEM((512, 256), f32),
-            pltpu.SemaphoreType.DMA((3,)),
         ],
-        compiler_params=params(),
+        compiler_params=params(16),
         cost_estimate=cost(10**9, 10**7),
         name="edges",
     )(below, above, edge_in, weights, mean_in, sums_in)
@@ -534,45 +551,57 @@
 
 
 def make_apply_kernel(cell_count):
-    def apply_kernel(sums, high_i, low_i, high_e, low_e, out, factor_out, maps):
-        @pl.when(pl.program_id(0) == 0)
-        def _():
-            factor, mapping = factor_and_map(sums[...], cell_count)
-            factor_out[...] = factor
-            high, low = split(mapping)
-            maps[0:128, :] = spread_map(high)
-            maps[128:256, :] = spread_map(low)
-
+    def apply_kernel(sums, high_i, low_i, high_e, low_e, out, factor_out, maps, new, sems):
+        factor, mapping = factor_and_map(sums[...], cell_count)
+        factor_out[...] = factor
+        high, low = split(mapping)
+        maps[0:128, :] = spread_map(high)
+        maps[128:256, :] = spread_map(low)
         low_rows = lax.broadcasted_iota(jnp.int32, (M, 8, 256), 1) < 4
-        for z in range(ZG):
+
+        def put(z, slot):
+            return pltpu.make_async_copy(new.at[slot], out.at[:, z], sems.at[slot])
+
+        def level(z, carry):
+            slot = lax.rem(z, SLOTS)
+
+            @pl.when(z >= SLOTS)
+            def _():
+                put(z - SLOTS, slot).wait()
+
             results = []
             for high, low in ((high_i, low_i), (high_e, low_e)):
                 first = jnp.dot(maps[...], high[z], preferred_element_type=f32)
                 second = jnp.dot(maps[0:128, :], low[z], preferred_element_type=f32)
                 results.append((first[0:128] + first[128:256] + second).reshape(M, 8, 256))
             inner, edge = results
-            out[:, z, 0:8, :] = jnp.where(low_rows, edge, inner)
-            out[:, z, 8:16, :] = jnp.where(low_rows, inner, edge)
+            new[slot, :, 0:8, :] = jnp.where(low_rows, edge, inner)
+            new[slot, :, 8:16, :] = jnp.where(low_rows, inner, edge)
+            put(z, slot).start()
+            return carry
+
+        lax.fori_loop(0, NZ, level, 0)
+        for z in range(NZ - SLOTS, NZ):
+            put(z, z % SLOTS).wait()
 
     return apply_kernel
 
 
 def apply_map(sums, high_i, low_i, high_e, low_e, cell_count):
-    block = pl.BlockSpec((ZG, 256, 256), lambda i: (i, 0, 0))
     return pl.pallas_call(
         make_apply_kernel(cell_count),
-        grid=(NZ // ZG,),
         out_shape=(
             jax.ShapeDtypeStruct((M, NZ, BX, 256), f32),
             jax.ShapeDtypeStruct((M, M), f32),
         ),
-        in_specs=[pl.BlockSpec((32, 32), lambda i: (0, 0)), block, block, block, block],
-        out_specs=(
-            pl.BlockSpec((M, ZG, BX, 256), lambda i: (0, i, 0, 0)),
-            pl.BlockSpec((M, M), lambda i: (0, 0)),
-        ),
-        scratch_shapes=[pltpu.VMEM((256, 256), bf16)],
-        compiler_params=params(),
+        in_specs=[VMEM] * 5,
+        out_specs=(ANY, VMEM),
+        scratch_shapes=[
+            pltpu.VMEM((256, 256), bf16),
+            pltpu.VMEM((SLOTS, M, BX, 256), f32),
+            pltpu.SemaphoreType.DMA((SLOTS,)),
+        ],
+        compiler_params=params(12),
         cost_estimate=cost(10**9, 13 * 10**6),
         name="apply",
     )(sums, high_i, low_i, high_e, low_e)
@@ -597,21 +626,13 @@
     mean_field, mode_fields, velocity_east, velocity_north, flag_east, flag_north, ocean_mask
 ):
     axes = ("gx", "gy")
-    last = BX - 1
-    lower_send = jnp.stack(
-        [
-            velocity_east[:, last],
-            flag_east[:, last].astype(f32),
-            ocean_mask[:, last].astype(f32),
-        ]
-    )
-    lower = onward(lower_send, "gx")
-    upper = backward(ocean_mask[:, 0].astype(f32), "gx")
-    up, down, east_send, west_send = pack(
-        mode_fields, mean_field, velocity_north, flag_north, ocean_mask
+    up, down, east_send, west_send, lower_send, upper_send = pack(
+        mode_fields, mean_field, velocity_east, velocity_north, flag_east, flag_north, ocean_mask
     )
     below = onward(up, "gx")
     above = backward(down, "gx")
+    lower = onward(lower_send, "gx")
+    upper = backward(upper_send, "gx")
     west = onward(east_send, "gy")
     east = backward(west_send, "gy")
     high_i, low_i, edge, weights, mean_part, sums_i = interior(

time: 131 us -> 108 us (0.82)
  Pallas kernels: 73.4 us -> 36.6 us
  waiting for transfers between devices: 11.4 us -> 30.9 us
  starting transfers between devices: 37.1 us -> 30.8 us
  local copies, waits for them, and re-layouts: 5.3 us -> 7.91 us
  other arithmetic: 1.36 us -> 0.03 us
    pallas_call x1, Pallas kernels: 45.9 us -> 22.3 us  [interior(): pl.pallas_call(interior_kernel, out_shape=(parts, parts, jax.ShapeDtypeSt...]
    ppermute x3, waiting for transfers between devices: 0.01 us -> 17.1 us  [backward(): return lax.ppermute(value, axis, [(i + 1, i) for i in range(size - 1)])]
    pallas_call x1, Pallas kernels: 11.6 us -> 3.21 us  [edges(): pl.pallas_call(edge_kernel, out_shape=(parts, parts, jax.ShapeDtypeStruct...]
    unnamed x13 -> x28, local copies, waits for them, and re-layouts: 2.46 us -> 7.91 us
    ppermute x7, starting transfers between devices: 23.2 us -> 17.8 us  [exchanged(): return lax.ppermute(value, axes, [(i, i ^ distance) for i in range(size)])]
    pallas_call x2, Pallas kernels: 15.9 us -> 11.1 us  [the longest x1 7.85 us: apply_map(): pl.pallas_call(make_apply_kernel(cell_count), out_shape=(jax.ShapeDtypeSt...]
    slice x3 -> x0, local copies, waits for them, and re-layouts: 2.84 us -> none  [the longest x1 0.99 us: shards(): upper = backward(ocean_mask[:, 0].astype(f32), 'gx')]
    ppermute x3, waiting for transfers between devices: 0.01 us -> 1.74 us  [onward(): return lax.ppermute(value, axis, [(i, i + 1) for i in range(size - 1)])]
  transfers between devices with their start and end apart: 13 -> 13, of which waited for: 7 -> 9; matrix products, arithmetic and copies ran while one was open for 0% -> 0% of each run, Pallas kernels for 39% -> 21%
where the time goes in v2:
time: 108 us; the launch traced here: 107 us
  Pallas kernels  36.6 us (34%)
  waiting for transfers between devices  30.9 us (29%)
  starting transfers between devices  30.8 us (29%)
  local copies, waits for them, and re-layouts  7.91 us (7%)
    pallas_call x1, Pallas kernels, interior(): pl.pallas_call(interior_kernel, out_shape=(parts, parts, jax.ShapeDtypeSt...  22.3 us
    ppermute x7, starting transfers between devices, exchanged(): return lax.ppermute(value, axes, [(i, i ^ distance) for i in range(size)])  17.8 us
    ppermute x3, waiting for transfers between devices, backward(): return lax.ppermute(value, axis, [(i + 1, i) for i in range(size - 1)])  17.1 us
    ppermute x7, waiting for transfers between devices, exchanged(): return lax.ppermute(value, axes, [(i, i ^ distance) for i in range(size)])  12.1 us
    ppermute x3, starting transfers between devices, onward(): return lax.ppermute(value, axis, [(i, i + 1) for i in range(size - 1)])  9.05 us
    unnamed x28, local copies, waits for them, and re-layouts  7.91 us
    pallas_call x1, Pallas kernels, apply_map(): pl.pallas_call(make_apply_kernel(cell_count), out_shape=(jax.ShapeDtypeSt...  7.85 us
    ppermute x3, starting transfers between devices, backward(): return lax.ppermute(value, axis, [(i + 1, i) for i in range(size - 1)])  3.88 us
  transfers between devices with their start and end apart: 13, of which 9 were waited for; matrix products, arithmetic and copies ran while one was open for 0% of the time, Pallas kernels for 21%

profile of v2, /device:TPU:0, one launch (start us, length us, event | category | flops | bytes accessed | tf_op | source)
XLA Modules:
  0.0 107.0 jit_solution(10150721566774431788)
XLA Ops:
  0.6 0.0 copy-start
  0.6 2.2 %copy-done = f32[16,16,16,256]{3,2,1,0:T(8,128)S(1)} copy-done((f32[16,16,16,256]{3,2,1,0:T(8,128)S(1)}, f32[16,16,16,256]{3,2,1,0:T(8,128)}, u32[]{:S(2)}) %copy-start) | copy-done | bytes 4194328
  2.8 0.0 copy-start.2
  2.8 0.9 copy-done.2
  3.8 0.0 copy-start.4
  3.8 0.9 copy-done.4
  4.7 0.0 copy-start.6
  4.7 0.9 copy-done.6
  5.7 0.0 copy-start.8
  5.7 0.9 copy-done.8
  6.6 0.0 copy-start.10
  6.6 0.9 copy-done.10
  7.6 0.0 copy-start.12
  7.6 0.9 copy-done.12
  8.5 0.0 copy-start.1
  8.5 0.0 copy-start.3
  8.5 0.0 copy-start.5
  8.5 0.0 copy-start.7
  8.5 0.0 copy-start.9
  8.5 0.0 copy-start.11
  8.6 0.0 copy-start.13
  8.6 3.2 %pack.1 = (f32[2,17,2,24,128]{4,3,2,1,0:T(8,128)S(1)}, f32[2,17,2,24,128]{4,3,2,1,0:T(8,128)S(1)}, f32[20,8,128]{2,1,0:T(8,128)S(1)}, f32[20,8,128]{2,1,0:T(8,12...) custom-call(f32[16,16,16,256]{3,2,1,0:T(8,128)S(1)} %copy-done, f32[16,16,256]{2,1,0:T(8,128)S(1)} %copy-done.2, ...), custom_call_target="tpu_custom_call" | custom-call | flops 10000000 | bytes 7000000 | tf_op jit(solution)/shard_map/pack/pallas_call | solution.py:161
  11.8 4.0 %collective-permute-start = (f32[2,17,2,24,128]{4,3,2,1,0:T(8,128)S(1)}, f32[2,17,2,24,128]{4,3,2,1,0:T(8,128)S(1)}, u32[]{:S(2)}, u32[]{:S(2)}) collective-permute-start(f32[2,17,2,24,128]{4,3,2,1,0:T(8,128)S(1)} %get-tuple-element.21), channel_id=1, source_target_pairs={{0,8},{8,16},{16,24},{24,32},{32,40},{40,48},{48,56},{56,64},{64,7... | collective-permute-start | bytes 2506760 | tf_op jit(solution)/shard_map/ppermute | solution.py:612
  15.8 1.3 %collective-permute-start.1 = (f32[2,17,2,24,128]{4,3,2,1,0:T(8,128)S(1)}, f32[2,17,2,24,128]{4,3,2,1,0:T(8,128)S(1)}, u32[]{:S(2)}, u32[]{:S(2)}) collective-permute-start(f32[2,17,2,24,128]{4,3,2,1,0:T(8,128)S(1)} %get-tuple-element.22), channel_id=1, source_target_pairs={{8,0},{16,8},{24,16},{32,24},{40,32},{48,40},{56,48},{64,56},{72,6... | collective-permute-start | bytes 2506760 | tf_op jit(solution)/shard_map/ppermute | solution.py:617
  17.1 1.5 %collective-permute-start.4 = (f32[20,8,128]{2,1,0:T(8,128)S(1)}, f32[20,8,128]{2,1,0:T(8,128)S(1)}, u32[]{:S(2)}, u32[]{:S(2)}) collective-permute-start(f32[20,8,128]{2,1,0:T(8,128)S(1)} %get-tuple-element.25), channel_id=1, source_target_pairs={{0,1},{1,2},{2,3},{3,4},{4,5},{5,6},{6,7},{8,9},{9,10},{10,11},{11... | collective-permute-start | bytes 245768 | tf_op jit(solution)/shard_map/ppermute | solution.py:612
  18.6 1.3 %collective-permute-start.5 = (f32[20,8,128]{2,1,0:T(8,128)S(1)}, f32[20,8,128]{2,1,0:T(8,128)S(1)}, u32[]{:S(2)}, u32[]{:S(2)}) collective-permute-start(f32[20,8,128]{2,1,0:T(8,128)S(1)} %get-tuple-element.26), channel_id=1, source_target_pairs={{1,0},{2,1},{3,2},{4,3},{5,4},{6,5},{7,6},{9,8},{10,9},{11,10},{12... | collective-permute-start | bytes 245768 | tf_op jit(solution)/shard_map/ppermute | solution.py:617
  19.9 1.3 %collective-permute-start.3 = (f32[16,256]{1,0:T(8,128)S(1)}, f32[16,256]{1,0:T(8,128)S(1)}, u32[]{:S(2)}, u32[]{:S(2)}) collective-permute-start(f32[16,256]{1,0:T(8,128)S(1)} %get-tuple-element.24), channel_id=1, source_target_pairs={{8,0},{16,8},{24,16},{32,24},{40,32},{48,40},{56,48},{64,56},{72,6... | collective-permute-start | bytes 49160 | tf_op jit(solution)/shard_map/ppermute | solution.py:617
  21.2 17.1 %collective-permute-done.3.upper = f32[16,256]{1,0:T(8,128)S(1)} collective-permute-done((f32[16,256]{1,0:T(8,128)S(1)}, f32[16,256]{1,0:T(8,128)S(1)}, u32[]{:S(2)}, u32[]{:S(2)}) %collective-permute-start.3) | collective-permute-done | bytes 16416 | tf_op jit(solution)/shard_map/ppermute | solution.py:617
  38.2 3.6 %collective-permute-start.2 = (f32[3,16,256]{2,1,0:T(8,128)S(1)}, f32[3,16,256]{2,1,0:T(8,128)S(1)}, u32[]{:S(2)}, u32[]{:S(2)}) collective-permute-start(f32[3,16,256]{2,1,0:T(8,128)S(1)} %get-tuple-element.23), channel_id=1, source_target_pairs={{0,8},{8,16},{16,24},{24,32},{32,40},{40,48},{48,56},{56,64},{64,7... | collective-permute-start | bytes 147464 | tf_op jit(solution)/shard_map/ppermute | solution.py:612
  41.9 1.7 %collective-permute-done.2.lower = f32[3,16,256]{2,1,0:T(8,128)S(1)} collective-permute-done((f32[3,16,256]{2,1,0:T(8,128)S(1)}, f32[3,16,256]{2,1,0:T(8,128)S(1)}, u32[]{:S(2)}, u32[]{:S(2)}) %collective-permute-start.2) | collective-permute-done | bytes 49184 | tf_op jit(solution)/shard_map/ppermute | solution.py:612
  43.6 0.0 collective-permute-done.4.west
  43.6 0.0 collective-permute-done.5.east
  43.6 0.0 copy-done.1
  43.6 0.0 copy-done.3
  43.6 0.0 copy-done.5
  43.6 0.0 copy-done.7
  43.6 0.0 copy-done.9
  43.6 0.0 copy-done.11
  43.6 0.0 copy-done.13
  43.7 22.3 %interior.1 = (bf16[16,256,256]{2,1,0:T(8,128)(2,1)S(1)}, bf16[16,256,256]{2,1,0:T(8,128)(2,1)S(1)}, f32[16,256,256]{2,1,0:T(8,128)S(1)}, f32[2,16,3,8,128]{4,3,...) custom-call(f32[16,16,16,256]{3,2,1,0:T(8,128)S(1)} %copy-done.1, f32[16,16,256]{2,1,0:T(8,128)S(1)} %copy-done.3, ...), custom_call_target="tpu_custom_call" | custom-call | flops 1000000 | bytes 1000000 | tf_op jit(solution)/shard_map/interior/pallas_call | solution.py:402
  66.0 0.0 collective-permute-done.below
  66.0 0.0 collective-permute-done.1.above
  66.0 3.2 %edges.1 = (bf16[16,256,256]{2,1,0:T(8,128)(2,1)S(1)}, bf16[16,256,256]{2,1,0:T(8,128)(2,1)S(1)}, f32[16,16,256]{2,1,0:T(8,128)}, f32[32,32]{1,0:T(8,128)S(1)}) custom-call(f32[2,17,2,24,128]{4,3,2,1,0:T(8,128)S(1)} %collective-permute-done.below, f32[2,17,2,24,128]{4,3,2,1,0:T(8,128)S(1)} %collective-permute-done.1.above, ...), custom_call_target="tpu_custom_call" | custom-call | flops 1000000000 | bytes 10000000 | tf_op jit(solution)/shard_map/edges/pallas_call | solution.py:490
  69.2 0.0 collective-permute-start.6
  69.2 1.2 %collective-permute-done.6 = f32[32,32]{1,0:T(8,128)S(1)} collective-permute-done((f32[32,32]{1,0:T(8,128)S(1)}, f32[32,32]{1,0:T(8,128)S(1)}, u32[]{:S(2)}, u32[]{:S(2)}) %collective-permute-start.6) | collective-permute-done | bytes 4128 | tf_op jit(solution)/shard_map/ppermute | solution.py:622
  70.4 1.6 %collective-permute-start.7 = (f32[32,32]{1,0:T(8,128)S(1)}, f32[32,32]{1,0:T(8,128)S(1)}, u32[]{:S(2)}, u32[]{:S(2)}) collective-permute-start(f32[32,32]{1,0:T(8,128)S(1)} %add.21), channel_id=1, source_target_pairs={{0,2},{1,3},{2,0},{3,1},{4,6},{5,7},{6,4},{7,5},{8,10},{9,11},{10,... | collective-permute-start | bytes 12296 | tf_op jit(solution)/shard_map/ppermute | solution.py:622
  72.0 2.2 %collective-permute-done.7 = f32[32,32]{1,0:T(8,128)S(1)} collective-permute-done((f32[32,32]{1,0:T(8,128)S(1)}, f32[32,32]{1,0:T(8,128)S(1)}, u32[]{:S(2)}, u32[]{:S(2)}) %collective-permute-start.7) | collective-permute-done | bytes 4128 | tf_op jit(solution)/shard_map/ppermute | solution.py:622
  74.1 3.0 %collective-permute-start.8 = (f32[32,32]{1,0:T(8,128)S(1)}, f32[32,32]{1,0:T(8,128)S(1)}, u32[]{:S(2)}, u32[]{:S(2)}) collective-permute-start(f32[32,32]{1,0:T(8,128)S(1)} %add.22), channel_id=1, source_target_pairs={{0,6},{1,7},{2,4},{3,5},{4,2},{5,3},{6,0},{7,1},{8,14},{9,15},{10,... | collective-permute-start | bytes 12296 | tf_op jit(solution)/shard_map/ppermute | solution.py:622
  77.1 1.9 %collective-permute-done.8 = f32[32,32]{1,0:T(8,128)S(1)} collective-permute-done((f32[32,32]{1,0:T(8,128)S(1)}, f32[32,32]{1,0:T(8,128)S(1)}, u32[]{:S(2)}, u32[]{:S(2)}) %collective-permute-start.8) | collective-permute-done | bytes 4128 | tf_op jit(solution)/shard_map/ppermute | solution.py:622
  79.1 2.3 %collective-permute-start.9 = (f32[32,32]{1,0:T(8,128)S(1)}, f32[32,32]{1,0:T(8,128)S(1)}, u32[]{:S(2)}, u32[]{:S(2)}) collective-permute-start(f32[32,32]{1,0:T(8,128)S(1)} %add.23), channel_id=1, source_target_pairs={{0,8},{1,9},{2,10},{3,11},{4,12},{5,13},{6,14},{7,15},{8,0},{9,1},... | collective-permute-start | bytes 12296 | tf_op jit(solution)/shard_map/ppermute | solution.py:622
  81.4 1.7 %collective-permute-done.9 = f32[32,32]{1,0:T(8,128)S(1)} collective-permute-done((f32[32,32]{1,0:T(8,128)S(1)}, f32[32,32]{1,0:T(8,128)S(1)}, u32[]{:S(2)}, u32[]{:S(2)}) %collective-permute-start.9) | collective-permute-done | bytes 4128 | tf_op jit(solution)/shard_map/ppermute | solution.py:622
  83.1 4.6 %collective-permute-start.10 = (f32[32,32]{1,0:T(8,128)S(1)}, f32[32,32]{1,0:T(8,128)S(1)}, u32[]{:S(2)}, u32[]{:S(2)}) collective-permute-start(f32[32,32]{1,0:T(8,128)S(1)} %add.24), channel_id=1, source_target_pairs={{0,24},{1,25},{2,26},{3,27},{4,28},{5,29},{6,30},{7,31},{8,16},{9,... | collective-permute-start | bytes 12296 | tf_op jit(solution)/shard_map/ppermute | solution.py:622
  87.8 1.7 %collective-permute-done.10 = f32[32,32]{1,0:T(8,128)S(1)} collective-permute-done((f32[32,32]{1,0:T(8,128)S(1)}, f32[32,32]{1,0:T(8,128)S(1)}, u32[]{:S(2)}, u32[]{:S(2)}) %collective-permute-start.10) | collective-permute-done | bytes 4128 | tf_op jit(solution)/shard_map/ppermute | solution.py:622
  89.5 2.7 %collective-permute-start.11 = (f32[32,32]{1,0:T(8,128)S(1)}, f32[32,32]{1,0:T(8,128)S(1)}, u32[]{:S(2)}, u32[]{:S(2)}) collective-permute-start(f32[32,32]{1,0:T(8,128)S(1)} %add.25), channel_id=1, source_target_pairs={{0,32},{1,33},{2,34},{3,35},{4,36},{5,37},{6,38},{7,39},{8,40},{9,... | collective-permute-start | bytes 12296 | tf_op jit(solution)/shard_map/ppermute | solution.py:622
  92.2 1.7 %collective-permute-done.11 = f32[32,32]{1,0:T(8,128)S(1)} collective-permute-done((f32[32,32]{1,0:T(8,128)S(1)}, f32[32,32]{1,0:T(8,128)S(1)}, u32[]{:S(2)}, u32[]{:S(2)}) %collective-permute-start.11) | collective-permute-done | bytes 4128 | tf_op jit(solution)/shard_map/ppermute | solution.py:622
  93.9 3.6 %collective-permute-start.12 = (f32[32,32]{1,0:T(8,128)S(1)}, f32[32,32]{1,0:T(8,128)S(1)}, u32[]{:S(2)}, u32[]{:S(2)}) collective-permute-start(f32[32,32]{1,0:T(8,128)S(1)} %add.26), channel_id=1, source_target_pairs={{0,96},{1,97},{2,98},{3,99},{4,100},{5,101},{6,102},{7,103},{8,104... | collective-permute-start | bytes 12296 | tf_op jit(solution)/shard_map/ppermute | solution.py:622
  97.5 1.7 %collective-permute-done.12 = f32[32,32]{1,0:T(8,128)S(1)} collective-permute-done((f32[32,32]{1,0:T(8,128)S(1)}, f32[32,32]{1,0:T(8,128)S(1)}, u32[]{:S(2)}, u32[]{:S(2)}) %collective-permute-start.12) | collective-permute-done | bytes 4128 | tf_op jit(solution)/shard_map/ppermute | solution.py:622
  99.2 7.8 %apply.1 = (f32[16,16,16,256]{3,2,1,0:T(8,128)}, f32[16,16]{1,0:T(8,128)}) custom-call(f32[32,32]{1,0:T(8,128)S(1)} %add.27.sums, bf16[16,256,256]{2,1,0:T(8,128)(2,1)S(1)} %get-tuple-element.33.high_i, bf16[16,256,256]{2,1,0:T(8,128)(2,1)S(1)} %get-tuple-element.34.low_i, bf16[16,256,256]{2,1,0:T(8,128)(2,1)S(1)} %get-tuple-element.35.high_e, ...), custom_call_target="tpu_custom_call" | custom-call | flops 1000000000 | bytes 13000000 | tf_op jit(solution)/shard_map/apply/pallas_call | solution.py:591
  (7 shorter events, 0.0 us)
Async XLA Ops:
  0.6 2.2 %copy-start = (f32[16,16,16,256]{3,2,1,0:T(8,128)S(1)}, f32[16,16,16,256]{3,2,1,0:T(8,128)}, u32[]{:S(2)}) copy-start(f32[16,16,16,256]{3,2,1,0:T(8,128)} %modes.3) | copy-start | bytes 12582916
  2.8 0.9 copy-start.2
  3.8 0.9 copy-start.4
  4.7 0.9 copy-start.6
  5.7 0.9 copy-start.8
  6.6 0.9 copy-start.10
  7.6 0.9 copy-start.12
  8.5 35.1 %copy-start.1 = (f32[16,16,16,256]{3,2,1,0:T(8,128)S(1)}, f32[16,16,16,256]{3,2,1,0:T(8,128)}, u32[]{:S(2)}) copy-start(f32[16,16,16,256]{3,2,1,0:T(8,128)} %modes.3) | copy-start | bytes 12582916
  8.5 35.1 %copy-start.3 = (f32[16,16,256]{2,1,0:T(8,128)S(1)}, f32[16,16,256]{2,1,0:T(8,128)}, u32[]{:S(2)}) copy-start(f32[16,16,256]{2,1,0:T(8,128)} %mean.3) | copy-start | bytes 786436
  8.5 35.1 %copy-start.5 = (f32[16,16,256]{2,1,0:T(8,128)S(1)}, f32[16,16,256]{2,1,0:T(8,128)}, u32[]{:S(2)}) copy-start(f32[16,16,256]{2,1,0:T(8,128)} %ve.3) | copy-start | bytes 786436
  8.5 35.1 %copy-start.7 = (f32[16,16,256]{2,1,0:T(8,128)S(1)}, f32[16,16,256]{2,1,0:T(8,128)}, u32[]{:S(2)}) copy-start(f32[16,16,256]{2,1,0:T(8,128)} %vn.3) | copy-start | bytes 786436
  8.5 35.1 %copy-start.9 = (s32[16,16,256]{2,1,0:T(8,128)S(1)}, s32[16,16,256]{2,1,0:T(8,128)}, u32[]{:S(2)}) copy-start(s32[16,16,256]{2,1,0:T(8,128)} %fe.3) | copy-start | bytes 786436
  8.5 35.1 %copy-start.11 = (s32[16,16,256]{2,1,0:T(8,128)S(1)}, s32[16,16,256]{2,1,0:T(8,128)}, u32[]{:S(2)}) copy-start(s32[16,16,256]{2,1,0:T(8,128)} %fn.3) | copy-start | bytes 786436
  8.6 35.1 %copy-start.13 = (s32[16,16,256]{2,1,0:T(8,128)S(1)}, s32[16,16,256]{2,1,0:T(8,128)}, u32[]{:S(2)}) copy-start(s32[16,16,256]{2,1,0:T(8,128)} %mask.3) | copy-start | bytes 786436
  11.8 54.1 %collective-permute-start = (f32[2,17,2,24,128]{4,3,2,1,0:T(8,128)S(1)}, f32[2,17,2,24,128]{4,3,2,1,0:T(8,128)S(1)}, u32[]{:S(2)}, u32[]{:S(2)}) collective-permute-start(f32[2,17,2,24,128]{4,3,2,1,0:T(8,128)S(1)} %get-tuple-element.21), channel_id=1, source_target_pairs={{0,8},{8,16},{16,24},{24,32},{32,40},{40,48},{48,56},{56,64},{64,7... | collective-permute-start | bytes 2506760 | tf_op jit(solution)/shard_map/ppermute | solution.py:612
  15.8 50.2 %collective-permute-start.1 = (f32[2,17,2,24,128]{4,3,2,1,0:T(8,128)S(1)}, f32[2,17,2,24,128]{4,3,2,1,0:T(8,128)S(1)}, u32[]{:S(2)}, u32[]{:S(2)}) collective-permute-start(f32[2,17,2,24,128]{4,3,2,1,0:T(8,128)S(1)} %get-tuple-element.22), channel_id=1, source_target_pairs={{8,0},{16,8},{24,16},{32,24},{40,32},{48,40},{56,48},{64,56},{72,6... | collective-permute-start | bytes 2506760 | tf_op jit(solution)/shard_map/ppermute | solution.py:617
  17.1 26.5 %collective-permute-start.4 = (f32[20,8,128]{2,1,0:T(8,128)S(1)}, f32[20,8,128]{2,1,0:T(8,128)S(1)}, u32[]{:S(2)}, u32[]{:S(2)}) collective-permute-start(f32[20,8,128]{2,1,0:T(8,128)S(1)} %get-tuple-element.25), channel_id=1, source_target_pairs={{0,1},{1,2},{2,3},{3,4},{4,5},{5,6},{6,7},{8,9},{9,10},{10,11},{11... | collective-permute-start | bytes 245768 | tf_op jit(solution)/shard_map/ppermute | solution.py:612
  18.6 25.0 %collective-permute-start.5 = (f32[20,8,128]{2,1,0:T(8,128)S(1)}, f32[20,8,128]{2,1,0:T(8,128)S(1)}, u32[]{:S(2)}, u32[]{:S(2)}) collective-permute-start(f32[20,8,128]{2,1,0:T(8,128)S(1)} %get-tuple-element.26), channel_id=1, source_target_pairs={{1,0},{2,1},{3,2},{4,3},{5,4},{6,5},{7,6},{9,8},{10,9},{11,10},{12... | collective-permute-start | bytes 245768 | tf_op jit(solution)/shard_map/ppermute | solution.py:617
  19.9 18.4 %collective-permute-start.3 = (f32[16,256]{1,0:T(8,128)S(1)}, f32[16,256]{1,0:T(8,128)S(1)}, u32[]{:S(2)}, u32[]{:S(2)}) collective-permute-start(f32[16,256]{1,0:T(8,128)S(1)} %get-tuple-element.24), channel_id=1, source_target_pairs={{8,0},{16,8},{24,16},{32,24},{40,32},{48,40},{56,48},{64,56},{72,6... | collective-permute-start | bytes 49160 | tf_op jit(solution)/shard_map/ppermute | solution.py:617
  38.2 5.4 %collective-permute-start.2 = (f32[3,16,256]{2,1,0:T(8,128)S(1)}, f32[3,16,256]{2,1,0:T(8,128)S(1)}, u32[]{:S(2)}, u32[]{:S(2)}) collective-permute-start(f32[3,16,256]{2,1,0:T(8,128)S(1)} %get-tuple-element.23), channel_id=1, source_target_pairs={{0,8},{8,16},{16,24},{24,32},{32,40},{40,48},{48,56},{56,64},{64,7... | collective-permute-start | bytes 147464 | tf_op jit(solution)/shard_map/ppermute | solution.py:612
  69.2 1.2 %collective-permute-start.6 = (f32[32,32]{1,0:T(8,128)S(1)}, f32[32,32]{1,0:T(8,128)S(1)}, u32[]{:S(2)}, u32[]{:S(2)}) collective-permute-start(f32[32,32]{1,0:T(8,128)S(1)} %get-tuple-element.32), channel_id=1, source_target_pairs={{0,1},{1,0},{2,3},{3,2},{4,5},{5,4},{6,7},{7,6},{8,9},{9,8},{10,11... | collective-permute-start | bytes 12296 | tf_op jit(solution)/shard_map/ppermute | solution.py:622
  70.4 3.7 %collective-permute-start.7 = (f32[32,32]{1,0:T(8,128)S(1)}, f32[32,32]{1,0:T(8,128)S(1)}, u32[]{:S(2)}, u32[]{:S(2)}) collective-permute-start(f32[32,32]{1,0:T(8,128)S(1)} %add.21), channel_id=1, source_target_pairs={{0,2},{1,3},{2,0},{3,1},{4,6},{5,7},{6,4},{7,5},{8,10},{9,11},{10,... | collective-permute-start | bytes 12296 | tf_op jit(solution)/shard_map/ppermute | solution.py:622
  74.1 4.9 %collective-permute-start.8 = (f32[32,32]{1,0:T(8,128)S(1)}, f32[32,32]{1,0:T(8,128)S(1)}, u32[]{:S(2)}, u32[]{:S(2)}) collective-permute-start(f32[32,32]{1,0:T(8,128)S(1)} %add.22), channel_id=1, source_target_pairs={{0,6},{1,7},{2,4},{3,5},{4,2},{5,3},{6,0},{7,1},{8,14},{9,15},{10,... | collective-permute-start | bytes 12296 | tf_op jit(solution)/shard_map/ppermute | solution.py:622
  79.1 4.1 %collective-permute-start.9 = (f32[32,32]{1,0:T(8,128)S(1)}, f32[32,32]{1,0:T(8,128)S(1)}, u32[]{:S(2)}, u32[]{:S(2)}) collective-permute-start(f32[32,32]{1,0:T(8,128)S(1)} %add.23), channel_id=1, source_target_pairs={{0,8},{1,9},{2,10},{3,11},{4,12},{5,13},{6,14},{7,15},{8,0},{9,1},... | collective-permute-start | bytes 12296 | tf_op jit(solution)/shard_map/ppermute | solution.py:622
  83.1 6.3 %collective-permute-start.10 = (f32[32,32]{1,0:T(8,128)S(1)}, f32[32,32]{1,0:T(8,128)S(1)}, u32[]{:S(2)}, u32[]{:S(2)}) collective-permute-start(f32[32,32]{1,0:T(8,128)S(1)} %add.24), channel_id=1, source_target_pairs={{0,24},{1,25},{2,26},{3,27},{4,28},{5,29},{6,30},{7,31},{8,16},{9,... | collective-permute-start | bytes 12296 | tf_op jit(solution)/shard_map/ppermute | solution.py:622
  89.5 4.4 %collective-permute-start.11 = (f32[32,32]{1,0:T(8,128)S(1)}, f32[32,32]{1,0:T(8,128)S(1)}, u32[]{:S(2)}, u32[]{:S(2)}) collective-permute-start(f32[32,32]{1,0:T(8,128)S(1)} %add.25), channel_id=1, source_target_pairs={{0,32},{1,33},{2,34},{3,35},{4,36},{5,37},{6,38},{7,39},{8,40},{9,... | collective-permute-start | bytes 12296 | tf_op jit(solution)/shard_map/ppermute | solution.py:622
  93.9 5.3 %collective-permute-start.12 = (f32[32,32]{1,0:T(8,128)S(1)}, f32[32,32]{1,0:T(8,128)S(1)}, u32[]{:S(2)}, u32[]{:S(2)}) collective-permute-start(f32[32,32]{1,0:T(8,128)S(1)} %add.26), channel_id=1, source_target_pairs={{0,96},{1,97},{2,98},{3,99},{4,100},{5,101},{6,102},{7,103},{8,104... | collective-permute-start | bytes 12296 | tf_op jit(solution)/shard_map/ppermute | solution.py:622

commit v3 on v2

--- a/solution.py
+++ b/solution.py
@@ -16,6 +16,7 @@
 LANES = 128
 ROWS = 3 * NZ
 SLOTS = 4
+TAIL = 8 + 8 * F
 HIGH = lax.Precision.HIGHEST
 f32 = jnp.float32
 bf16 = jnp.bfloat16
@@ -78,7 +79,7 @@
 
 
 def pack_kernel(
-    modes, mean, ve, vn, fe, fn, mask, up, down, east, west, lower, upper, X, V, I, sems
+    modes, mean, ve, vn, fe, fn, mask, up, down, east, west, X, V, I, sems
 ):
     copies = []
     for chunk in range(4):
@@ -139,24 +140,25 @@
     rows = row_ids()
     for half in range(2):
         for zh in range(2):
-            tiles = [jnp.zeros((8, LANES), f32) for _ in range(4)]
-            for z in range(8):
+
+            def last_row(z):
                 level = 8 * zh + z
-                sources = (
-                    rolled(V[1, half, level, 8:16, :], z - 7, 0),
-                    rolled(I[2, half, level, 8:16, :].astype(f32), z - 7, 0),
-                    rolled(I[1, half, level, 8:16, :].astype(f32), z - 7, 0),
-                    rolled(I[1, half, level, 0:8, :].astype(f32), z, 0),
-                )
-                tiles = [jnp.where(rows == z, new, old) for new, old in zip(sources, tiles)]
-            place = slice(8 * zh, 8 * zh + 8), slice(LANES * half, LANES * half + LANES)
-            for index in range(3):
-                lower[index, place[0], place[1]] = tiles[index]
-            upper[place[0], place[1]] = tiles[3]
+                speed = rolled(V[1, half, level, 8:16, :], -2, 0)
+                flag = rolled(I[2, half, level, 8:16, :].astype(f32), -1, 0)
+                wet = I[1, half, level, 8:16, :].astype(f32)
+                return jnp.where(rows == 5, speed, jnp.where(rows == 6, flag, wet))
+
+            for target, get, first in (
+                (up, last_row, 5),
+                (down, lambda z: I[1, half, 8 * zh + z, 0:8, :].astype(f32), 0),
+            ):
+                tiles = pack_rows(get, first)
+                for t in range(3):
+                    target[half, F, zh, 8 * t : 8 * t + 8, :] = tiles[t]
 
 
 def pack(modes, mean, ve, vn, fe, fn, mask):
-    rows = jax.ShapeDtypeStruct((2, F, 2, ROWS // 2, LANES), f32)
+    rows = jax.ShapeDtypeStruct((2, F + 1, 2, ROWS // 2, LANES), f32)
     columns = jax.ShapeDtypeStruct((F + 3, 8, LANES), f32)
     return pl.pallas_call(
         pack_kernel,
@@ -165,18 +167,16 @@
             rows,
             columns,
             columns,
-            jax.ShapeDtypeStruct((3, NZ, 2 * LANES), f32),
-            jax.ShapeDtypeStruct((NZ, 2 * LANES), f32),
         ),
         in_specs=[ANY] * 7,
-        out_specs=(VMEM,) * 6,
+        out_specs=(VMEM,) * 4,
         scratch_shapes=[
             pltpu.VMEM((2, F, NZ, BX, LANES), f32),
             pltpu.VMEM((2, 2, NZ, BX, LANES), f32),
             pltpu.VMEM((3, 2, NZ, BX, LANES), jnp.int32),
             pltpu.SemaphoreType.DMA((20,)),
         ],
-        compiler_params=params(12),
+        compiler_params=params(62),
         cost_estimate=cost(10**7, 7 * 10**6),
         name="pack",
     )(modes, mean, ve, vn, fe, fn, mask)
@@ -233,7 +233,7 @@
 
 
 def interior_kernel(
-    modes, mean, ve, vn, fe, fn, mask, lower, upper, west, east,
+    modes, mean, ve, vn, fe, fn, mask, west, east,
     high_out, low_out, edge_out, weights_out, mean_out, sums_out,
     X, VE, FE, W, VN, FN, H, T, Z, acc, sems,
 ):
@@ -249,12 +249,13 @@
     lax.fori_loop(0, F, clear, 0)
     for half in range(2):
         for z in range(NZ):
-            lanes = slice(LANES * half, LANES * half + LANES)
-            spread = lambda row: jnp.broadcast_to(row, (8, LANES))
-            VE[half, z, 0:8, :] = spread(lower[0, z : z + 1, lanes])
-            FE[half, z, 0:8, :] = spread(lower[1, z : z + 1, lanes])
-            W[half, z, 0:8, :] = spread(lower[2, z : z + 1, lanes]).astype(jnp.int32)
-            W[half, z, 24:32, :] = spread(upper[z : z + 1, lanes]).astype(jnp.int32)
+            edge_out[z, half, 0:8, :] = zero_tile
+    for half in range(2):
+        for z in range(NZ):
+            VE[half, z, 0:8, :] = zero_tile
+            FE[half, z, 0:8, :] = zero_tile
+            W[half, z, 0:8, :] = zero_tile.astype(jnp.int32)
+            W[half, z, 24:32, :] = zero_tile.astype(jnp.int32)
     acc[...] = jnp.zeros((512, 256), f32)
     lanes = lane_ids()
     rows = row_ids()
@@ -340,6 +341,13 @@
             w_up = [gain_up * wet[half] for half in range(2)]
             w_down = [gain_down * wet[half] for half in range(2)]
             for half in range(2):
+                for index, plane in enumerate((at(VE, half, 0), at(FE, half, 0), wet[half])):
+                    if xt == 0:
+                        weights_out[half, z, 3 + index] = plane
+                    else:
+                        weights_out[half, z, 3 + index] = jnp.where(
+                            rows < 4, weights_out[half, z, 3 + index], plane
+                        )
                 for d in range(1, 4):
                     if xt == 0:
                         weights_out[half, z, d - 1] = jnp.where(rows < d, wx[half][3 - d], 0.0)
@@ -365,6 +373,12 @@
                         total[half] += wy[half][3 + offset] * moved[half]
                 for half in range(2):
                     columns = slice(LANES * half, LANES * half + LANES)
+                    low_rows = rows < 4
+                    if xt == 1:
+                        cells = X[half, f, z, 8:16, :]
+                        edge_out[z, half, 8 + 8 * f : 16 + 8 * f, :] = jnp.where(
+                            low_rows, cells, own_cells[half]
+                        )
                     if f == M:
                         mean_out[z, 8 * xt : 8 * xt + 8, columns] = (
                             own_cells[half] + time_step * total[half]
@@ -373,20 +387,14 @@
                         T[half, f] = total[half]
                     else:
                         near = T[half, f]
-                        cells = X[half, f, z, 8:16, :]
-                        low_rows = rows < 4
                         Z[8 * f : 8 * f + 8, columns] = jnp.where(
                             low_rows, own_cells[half], cells
                         )
                         Z[128 + 8 * f : 136 + 8 * f, columns] = jnp.where(
                             low_rows, total[half], near
                         )
-                        edge_out[z, 8 * f : 8 * f + 8, columns] = jnp.where(
-                            low_rows, cells, own_cells[half]
-                        )
-                        edge_out[z, 128 + 8 * f : 136 + 8 * f, columns] = jnp.where(
-                            low_rows, near, total[half]
-                        )
+                        place = slice(TAIL + 8 * f, TAIL + 8 * f + 8)
+                        edge_out[z, half, place, :] = jnp.where(low_rows, near, total[half])
         high, low = split(Z[...])
         high_out[z] = high
         low_out[z] = low
@@ -397,19 +405,19 @@
     sums_out[...] = field_sums(acc)
 
 
-def interior(modes, mean, ve, vn, fe, fn, mask, lower, upper, west, east):
+def interior(modes, mean, ve, vn, fe, fn, mask, west, east):
     parts = jax.ShapeDtypeStruct((NZ, 256, 256), bf16)
     return pl.pallas_call(
         interior_kernel,
         out_shape=(
             parts,
             parts,
-            jax.ShapeDtypeStruct((NZ, 256, 256), f32),
-            jax.ShapeDtypeStruct((2, NZ, 3, 8, LANES), f32),
+            jax.ShapeDtypeStruct((NZ, 2, TAIL + 8 * M, LANES), f32),
+            jax.ShapeDtypeStruct((2, NZ, 6, 8, LANES), f32),
             jax.ShapeDtypeStruct(mean.shape, f32),
             jax.ShapeDtypeStruct((64, 32), f32),
         ),
-        in_specs=[ANY] * 7 + [VMEM] * 4,
+        in_specs=[ANY] * 7 + [VMEM] * 2,
         out_specs=(VMEM,) * 6,
         scratch_shapes=[
             pltpu.VMEM((2, F, NZ, 32, LANES), f32),
@@ -427,7 +435,7 @@
         compiler_params=params(28),
         cost_estimate=cost(10**6, 10**6),
         name="interior",
-    )(modes, mean, ve, vn, fe, fn, mask, lower, upper, west, east)
+    )(modes, mean, ve, vn, fe, fn, mask, west, east)
 
 
 def edge_kernel(
@@ -435,32 +443,64 @@
     high_out, low_out, mean_out, sums_out, Z, acc,
 ):
     acc[...] = jnp.zeros((512, 256), f32)
-    low_rows = row_ids() < 4
+    rows = row_ids()
+    low_rows = rows < 4
+    first_row = rows == 0
+    last_row = rows == 7
 
     def rows_from(ref, half, f, zh, first):
         start = min(max(first, 0), 16)
         return rolled(ref[half, f, zh, start : start + 8, :], start - first, 0)
+
+    def gains_of(half, z, zh, zi):
+        speed, flag, wet = (weights[half, z, 3 + i] for i in range(3))
+        speed = jnp.where(first_row, rows_from(below, half, F, zh, 3 * zi), speed)
+        flag = jnp.where(first_row, rows_from(below, half, F, zh, 3 * zi + 1), flag)
+        beyond = jnp.where(first_row, rows_from(below, half, F, zh, 3 * zi + 2), 0.0)
+        beyond = jnp.where(last_row, rows_from(above, half, F, zh, 3 * zi - 7), beyond)
+        a, b, d = face_parts(beyond * wet, speed, flag)
+        near, far = 47.0 * a + 27.0 * b + d, 27.0 * a + 47.0 * b - d
+        left, right = -13.0 * a - 3.0 * b, -3.0 * a - 13.0 * b
+        outside = (
+            weights[half, z, 0] + jnp.where(first_row, near, -far),
+            weights[half, z, 1] + jnp.where(first_row, left, -right),
+            weights[half, z, 2] + jnp.where(first_row, 2.0 * a, -2.0 * b),
+        )
+        inside = (
+            jnp.where(first_row, far, -near),
+            jnp.where(first_row, right, -left),
+            jnp.where(first_row, 2.0 * b, -2.0 * a),
+        )
+        return outside, inside
 
     def group(zh, carry):
         for zi in range(8):
             z = 8 * zh + zi
             for half in range(2):
-                columns = slice(LANES * half, LANES * half + LANES)
-                gains = [weights[half, z, d - 1] for d in range(1, 4)]
+                outside, inside = gains_of(half, z, zh, zi)
                 for f in range(F):
-                    change = None
+                    base = 8 + 8 * f
+                    change = inside[0] * edge_in[z, half, base : base + 8, :]
                     for d in range(1, 4):
                         cells = jnp.where(
                             low_rows,
                             rows_from(below, half, f, zh, 3 * zi + 3 - d),
                             rows_from(above, half, f, zh, 3 * zi + d - 8),
                         )
-                        term = gains[d - 1] * cells
-                        change = term if change is None else change + term
+                        change = change + outside[d - 1] * cells
+                    for d in range(1, 3):
+                        cells = jnp.where(
+                            low_rows,
+                            edge_in[z, half, base + d : base + d + 8, :],
+                            edge_in[z, half, base - d : base - d + 8, :],
+                        )
+                        change = change + inside[d] * cells
                     if f < M:
-                        place = slice(8 * f, 8 * f + 8)
-                        Z[place, columns] = edge_in[z, 128 + 8 * f : 136 + 8 * f, columns] + change
+                        Z[half, 8 * f : 8 * f + 8, :] = (
+                            edge_in[z, half, TAIL + 8 * f : TAIL + 8 * f + 8, :] + change
+                        )
                     else:
+                        columns = slice(LANES * half, LANES * half + LANES)
                         step = time_step * change
                         mean_out[z, 0:8, columns] = mean_in[z, 0:8, columns] + jnp.where(
                             low_rows, step, 0.0
@@ -468,7 +508,11 @@
                         mean_out[z, 8:16, columns] = mean_in[z, 8:16, columns] + jnp.where(
                             low_rows, 0.0, step
                         )
-            high, low = split(jnp.concatenate([edge_in[z, 0:128, :], Z[...]], axis=0))
+            halves = [
+                jnp.concatenate([edge_in[z, half, 8 : 8 + 8 * M, :], Z[half]], axis=0)
+                for half in range(2)
+            ]
+            high, low = split(jnp.concatenate(halves, axis=1))
             high_out[z] = high
             low_out[z] = low
             add_products(acc, high, low)
@@ -498,7 +542,7 @@
         in_specs=[VMEM] * 6,
         out_specs=(VMEM,) * 4,
         scratch_shapes=[
-            pltpu.VMEM((128, 256), f32),
+            pltpu.VMEM((2, 8 * M, LANES), f32),
             pltpu.VMEM((512, 256), f32),
         ],
         compiler_params=params(16),
@@ -626,18 +670,16 @@
     mean_field, mode_fields, velocity_east, velocity_north, flag_east, flag_north, ocean_mask
 ):
     axes = ("gx", "gy")
-    up, down, east_send, west_send, lower_send, upper_send = pack(
+    up, down, east_send, west_send = pack(
         mode_fields, mean_field, velocity_east, velocity_north, flag_east, flag_north, ocean_mask
     )
     below = onward(up, "gx")
     above = backward(down, "gx")
-    lower = onward(lower_send, "gx")
-    upper = backward(upper_send, "gx")
     west = onward(east_send, "gy")
     east = backward(west_send, "gy")
     high_i, low_i, edge, weights, mean_part, sums_i = interior(
         mode_fields, mean_field, velocity_east, velocity_north, flag_east, flag_north,
-        ocean_mask, lower, upper, west, east,
+        ocean_mask, west, east,
     )
     high_e, low_e, mean_next, sums = edges(below, above, edge, weights, mean_part, sums_i)
     for distance in (1, 2, 6, 8, 24, 32, 96):

time: 108 us -> 87.8 us (0.81)
  waiting for transfers between devices: 30.9 us -> 17.1 us
  local copies, waits for them, and re-layouts: 7.91 us -> 2.21 us
  starting transfers between devices: 30.8 us -> 27.4 us
  Pallas kernels: 36.6 us -> 39.7 us
    ppermute x3 -> x2, waiting for transfers between devices: 17.1 us -> 3.71 us  [backward(): return lax.ppermute(value, axis, [(i + 1, i) for i in range(size - 1)])]
    unnamed x28 -> x14, local copies, waits for them, and re-layouts: 7.91 us -> 2.21 us
    ppermute x3 -> x2, starting transfers between devices: 9.05 us -> 5.42 us  [onward(): return lax.ppermute(value, axis, [(i, i + 1) for i in range(size - 1)])]
    pallas_call x1, Pallas kernels: 3.24 us -> 5.31 us  [pack(): pl.pallas_call(pack_kernel, out_shape=(rows, rows, columns, columns), in_...]
    ppermute x3 -> x2, waiting for transfers between devices: 1.74 us -> 0.01 us  [onward(): return lax.ppermute(value, axis, [(i, i + 1) for i in range(size - 1)])]
    ppermute x7, starting transfers between devices: 17.8 us -> 19.4 us  [exchanged(): return lax.ppermute(value, axes, [(i, i ^ distance) for i in range(size)])]
    ppermute x3 -> x2, starting transfers between devices: 3.88 us -> 2.58 us  [backward(): return lax.ppermute(value, axis, [(i + 1, i) for i in range(size - 1)])]
    ppermute x7, waiting for transfers between devices: 12.1 us -> 13.3 us  [exchanged(): return lax.ppermute(value, axes, [(i, i ^ distance) for i in range(size)])]
  transfers between devices with their start and end apart: 13 -> 11, of which waited for: 9 -> 8; matrix products, arithmetic and copies ran while one was open for 0% -> 0% of each run, Pallas kernels for 21% -> 26%
where the time goes in v3:
time: 87.8 us; the launch traced here: 87.2 us
  Pallas kernels  39.7 us (45%)
  starting transfers between devices  27.4 us (31%)
  waiting for transfers between devices  17.1 us (19%)
  local copies, waits for them, and re-layouts  2.21 us (3%)
    pallas_call x1, Pallas kernels, interior(): pl.pallas_call(interior_kernel, out_shape=(parts, parts, jax.ShapeDtypeSt...  22.3 us
    ppermute x7, starting transfers between devices, exchanged(): return lax.ppermute(value, axes, [(i, i ^ distance) for i in range(size)])  19.4 us
    ppermute x7, waiting for transfers between devices, exchanged(): return lax.ppermute(value, axes, [(i, i ^ distance) for i in range(size)])  13.3 us
    pallas_call x1, Pallas kernels, apply_map(): pl.pallas_call(make_apply_kernel(cell_count), out_shape=(jax.ShapeDtypeSt...  7.85 us
    ppermute x2, starting transfers between devices, onward(): return lax.ppermute(value, axis, [(i, i + 1) for i in range(size - 1)])  5.42 us
    pallas_call x1, Pallas kernels, pack(): pl.pallas_call(pack_kernel, out_shape=(rows, rows, columns, columns), in_...  5.31 us
    pallas_call x1, Pallas kernels, edges(): pl.pallas_call(edge_kernel, out_shape=(parts, parts, jax.ShapeDtypeStruct...  4.21 us
    ppermute x2, waiting for transfers between devices, backward(): return lax.ppermute(value, axis, [(i + 1, i) for i in range(size - 1)])  3.71 us
  transfers between devices with their start and end apart: 11, of which 8 were waited for; matrix products, arithmetic and copies ran while one was open for 0% of the time, Pallas kernels for 26%

profile of v3, /device:TPU:0, one launch (start us, length us, event | category | flops | bytes accessed | tf_op | source)
XLA Modules:
  0.0 87.2 jit_solution(13873863242309533086)
XLA Ops:
  0.6 0.0 copy-start.6
  0.6 0.0 copy-start.5
  0.7 0.0 copy-start.4
  0.7 0.0 copy-start.3
  0.7 0.0 copy-start.2
  0.7 0.0 copy-start.1
  0.7 5.3 %pack.1 = (f32[2,18,2,24,128]{4,3,2,1,0:T(8,128)}, f32[2,18,2,24,128]{4,3,2,1,0:T(8,128)}, f32[20,8,128]{2,1,0:T(8,128)}, f32[20,8,128]{2,1,0:T(8,128)}) custom-call(f32[16,16,16,256]{3,2,1,0:T(8,128)} %modes.3, f32[16,16,256]{2,1,0:T(8,128)} %mean.3, f32[16,16,256]{2,1,0:T(8,128)} %ve.3, f32[16,16,256]{2,1,0:T(8,128)} %vn.3, s32[16,16,256]{2,1,0:T(8,128)} %fe.3, ...), custom_call_target="tpu_custom_call" | custom-call | flops 10000000 | bytes 7000000 | tf_op jit(solution)/shard_map/pack/pallas_call | solution.py:163
  6.0 4.0 %collective-permute-start = (f32[2,18,2,24,128]{4,3,2,1,0:T(8,128)}, f32[2,18,2,24,128]{4,3,2,1,0:T(8,128)S(1)}, u32[]{:S(2)}, u32[]{:S(2)}) collective-permute-start(f32[2,18,2,24,128]{4,3,2,1,0:T(8,128)} %get-tuple-element.19), channel_id=1, source_target_pairs={{0,8},{8,16},{16,24},{24,32},{32,40},{40,48},{48,56},{56,64},{64,7... | collective-permute-start | bytes 2654216 | tf_op jit(solution)/shard_map/ppermute | solution.py:656
  10.0 1.3 %collective-permute-start.1 = (f32[2,18,2,24,128]{4,3,2,1,0:T(8,128)}, f32[2,18,2,24,128]{4,3,2,1,0:T(8,128)S(1)}, u32[]{:S(2)}, u32[]{:S(2)}) collective-permute-start(f32[2,18,2,24,128]{4,3,2,1,0:T(8,128)} %get-tuple-element.20), channel_id=1, source_target_pairs={{8,0},{16,8},{24,16},{32,24},{40,32},{48,40},{56,48},{64,56},{72,6... | collective-permute-start | bytes 2654216 | tf_op jit(solution)/shard_map/ppermute | solution.py:661
  11.3 1.5 %collective-permute-start.2 = (f32[20,8,128]{2,1,0:T(8,128)}, f32[20,8,128]{2,1,0:T(8,128)S(1)}, u32[]{:S(2)}, u32[]{:S(2)}) collective-permute-start(f32[20,8,128]{2,1,0:T(8,128)} %get-tuple-element.21), channel_id=1, source_target_pairs={{0,1},{1,2},{2,3},{3,4},{4,5},{5,6},{6,7},{8,9},{9,10},{10,11},{11... | collective-permute-start | bytes 245768 | tf_op jit(solution)/shard_map/ppermute | solution.py:656
  12.7 1.3 %collective-permute-start.3 = (f32[20,8,128]{2,1,0:T(8,128)}, f32[20,8,128]{2,1,0:T(8,128)S(1)}, u32[]{:S(2)}, u32[]{:S(2)}) collective-permute-start(f32[20,8,128]{2,1,0:T(8,128)} %get-tuple-element.22), channel_id=1, source_target_pairs={{1,0},{2,1},{3,2},{4,3},{5,4},{6,5},{7,6},{9,8},{10,9},{11,10},{12... | collective-permute-start | bytes 245768 | tf_op jit(solution)/shard_map/ppermute | solution.py:661
  14.0 0.0 collective-permute-done.2.west
  14.1 3.7 %collective-permute-done.3.east = f32[20,8,128]{2,1,0:T(8,128)S(1)} collective-permute-done((f32[20,8,128]{2,1,0:T(8,128)}, f32[20,8,128]{2,1,0:T(8,128)S(1)}, u32[]{:S(2)}, u32[]{:S(2)}) %collective-permute-start.3) | collective-permute-done | bytes 81952 | tf_op jit(solution)/shard_map/ppermute | solution.py:661
  17.8 0.0 copy-done.6
  17.8 0.0 copy-done.5
  17.8 0.0 copy-done.4
  17.8 0.0 copy-done.3
  17.8 0.0 copy-done.2
  17.8 0.0 copy-done.1
  17.8 0.0 copy-start
  17.8 2.2 %copy-done = f32[16,16,16,256]{3,2,1,0:T(8,128)S(1)} copy-done((f32[16,16,16,256]{3,2,1,0:T(8,128)S(1)}, f32[16,16,16,256]{3,2,1,0:T(8,128)}, u32[]{:S(2)}) %copy-start) | copy-done | bytes 4194328
  20.0 22.3 %interior.1 = (bf16[16,256,256]{2,1,0:T(8,128)(2,1)S(1)}, bf16[16,256,256]{2,1,0:T(8,128)(2,1)S(1)}, f32[16,2,272,128]{3,2,1,0:T(8,128)S(1)}, f32[2,16,6,8,128]{...) custom-call(f32[16,16,16,256]{3,2,1,0:T(8,128)S(1)} %copy-done, f32[16,16,256]{2,1,0:T(8,128)S(1)} %copy-done.1, ...), custom_call_target="tpu_custom_call" | custom-call | flops 1000000 | bytes 1000000 | tf_op jit(solution)/shard_map/interior/pallas_call | solution.py:410
  42.3 0.0 collective-permute-done.below
  42.3 0.0 collective-permute-done.1.above
  42.3 4.2 %edges.1 = (bf16[16,256,256]{2,1,0:T(8,128)(2,1)S(1)}, bf16[16,256,256]{2,1,0:T(8,128)(2,1)S(1)}, f32[16,16,256]{2,1,0:T(8,128)}, f32[32,32]{1,0:T(8,128)S(1)}) custom-call(f32[2,18,2,24,128]{4,3,2,1,0:T(8,128)S(1)} %collective-permute-done.below, f32[2,18,2,24,128]{4,3,2,1,0:T(8,128)S(1)} %collective-permute-done.1.above, ...), custom_call_target="tpu_custom_call" | custom-call | flops 1000000000 | bytes 10000000 | tf_op jit(solution)/shard_map/edges/pallas_call | solution.py:534
  46.6 3.4 %collective-permute-start.4 = (f32[32,32]{1,0:T(8,128)S(1)}, f32[32,32]{1,0:T(8,128)S(1)}, u32[]{:S(2)}, u32[]{:S(2)}) collective-permute-start(f32[32,32]{1,0:T(8,128)S(1)} %get-tuple-element.28), channel_id=1, source_target_pairs={{0,1},{1,0},{2,3},{3,2},{4,5},{5,4},{6,7},{7,6},{8,9},{9,8},{10,11... | collective-permute-start | bytes 12296 | tf_op jit(solution)/shard_map/ppermute | solution.py:666
  49.9 0.8 collective-permute-done.4
  50.8 1.6 %collective-permute-start.5 = (f32[32,32]{1,0:T(8,128)S(1)}, f32[32,32]{1,0:T(8,128)S(1)}, u32[]{:S(2)}, u32[]{:S(2)}) collective-permute-start(f32[32,32]{1,0:T(8,128)S(1)} %add.21), channel_id=1, source_target_pairs={{0,2},{1,3},{2,0},{3,1},{4,6},{5,7},{6,4},{7,5},{8,10},{9,11},{10,... | collective-permute-start | bytes 12296 | tf_op jit(solution)/shard_map/ppermute | solution.py:666
  52.4 2.1 %collective-permute-done.5 = f32[32,32]{1,0:T(8,128)S(1)} collective-permute-done((f32[32,32]{1,0:T(8,128)S(1)}, f32[32,32]{1,0:T(8,128)S(1)}, u32[]{:S(2)}, u32[]{:S(2)}) %collective-permute-start.5) | collective-permute-done | bytes 4128 | tf_op jit(solution)/shard_map/ppermute | solution.py:666
  54.5 1.5 %collective-permute-start.6 = (f32[32,32]{1,0:T(8,128)S(1)}, f32[32,32]{1,0:T(8,128)S(1)}, u32[]{:S(2)}, u32[]{:S(2)}) collective-permute-start(f32[32,32]{1,0:T(8,128)S(1)} %add.22), channel_id=1, source_target_pairs={{0,6},{1,7},{2,4},{3,5},{4,2},{5,3},{6,0},{7,1},{8,14},{9,15},{10,... | collective-permute-start | bytes 12296 | tf_op jit(solution)/shard_map/ppermute | solution.py:666
  56.0 3.5 %collective-permute-done.6 = f32[32,32]{1,0:T(8,128)S(1)} collective-permute-done((f32[32,32]{1,0:T(8,128)S(1)}, f32[32,32]{1,0:T(8,128)S(1)}, u32[]{:S(2)}, u32[]{:S(2)}) %collective-permute-start.6) | collective-permute-done | bytes 4128 | tf_op jit(solution)/shard_map/ppermute | solution.py:666
  59.5 2.6 %collective-permute-start.7 = (f32[32,32]{1,0:T(8,128)S(1)}, f32[32,32]{1,0:T(8,128)S(1)}, u32[]{:S(2)}, u32[]{:S(2)}) collective-permute-start(f32[32,32]{1,0:T(8,128)S(1)} %add.23), channel_id=1, source_target_pairs={{0,8},{1,9},{2,10},{3,11},{4,12},{5,13},{6,14},{7,15},{8,0},{9,1},... | collective-permute-start | bytes 12296 | tf_op jit(solution)/shard_map/ppermute | solution.py:666
  62.1 1.7 %collective-permute-done.7 = f32[32,32]{1,0:T(8,128)S(1)} collective-permute-done((f32[32,32]{1,0:T(8,128)S(1)}, f32[32,32]{1,0:T(8,128)S(1)}, u32[]{:S(2)}, u32[]{:S(2)}) %collective-permute-start.7) | collective-permute-done | bytes 4128 | tf_op jit(solution)/shard_map/ppermute | solution.py:666
  63.8 4.1 %collective-permute-start.8 = (f32[32,32]{1,0:T(8,128)S(1)}, f32[32,32]{1,0:T(8,128)S(1)}, u32[]{:S(2)}, u32[]{:S(2)}) collective-permute-start(f32[32,32]{1,0:T(8,128)S(1)} %add.24), channel_id=1, source_target_pairs={{0,24},{1,25},{2,26},{3,27},{4,28},{5,29},{6,30},{7,31},{8,16},{9,... | collective-permute-start | bytes 12296 | tf_op jit(solution)/shard_map/ppermute | solution.py:666
  67.9 1.7 %collective-permute-done.8 = f32[32,32]{1,0:T(8,128)S(1)} collective-permute-done((f32[32,32]{1,0:T(8,128)S(1)}, f32[32,32]{1,0:T(8,128)S(1)}, u32[]{:S(2)}, u32[]{:S(2)}) %collective-permute-start.8) | collective-permute-done | bytes 4128 | tf_op jit(solution)/shard_map/ppermute | solution.py:666
  69.7 2.8 %collective-permute-start.9 = (f32[32,32]{1,0:T(8,128)S(1)}, f32[32,32]{1,0:T(8,128)S(1)}, u32[]{:S(2)}, u32[]{:S(2)}) collective-permute-start(f32[32,32]{1,0:T(8,128)S(1)} %add.25), channel_id=1, source_target_pairs={{0,32},{1,33},{2,34},{3,35},{4,36},{5,37},{6,38},{7,39},{8,40},{9,... | collective-permute-start | bytes 12296 | tf_op jit(solution)/shard_map/ppermute | solution.py:666
  72.5 1.7 %collective-permute-done.9 = f32[32,32]{1,0:T(8,128)S(1)} collective-permute-done((f32[32,32]{1,0:T(8,128)S(1)}, f32[32,32]{1,0:T(8,128)S(1)}, u32[]{:S(2)}, u32[]{:S(2)}) %collective-permute-start.9) | collective-permute-done | bytes 4128 | tf_op jit(solution)/shard_map/ppermute | solution.py:666
  74.2 3.5 %collective-permute-start.10 = (f32[32,32]{1,0:T(8,128)S(1)}, f32[32,32]{1,0:T(8,128)S(1)}, u32[]{:S(2)}, u32[]{:S(2)}) collective-permute-start(f32[32,32]{1,0:T(8,128)S(1)} %add.26), channel_id=1, source_target_pairs={{0,96},{1,97},{2,98},{3,99},{4,100},{5,101},{6,102},{7,103},{8,104... | collective-permute-start | bytes 12296 | tf_op jit(solution)/shard_map/ppermute | solution.py:666
  77.6 1.7 %collective-permute-done.10 = f32[32,32]{1,0:T(8,128)S(1)} collective-permute-done((f32[32,32]{1,0:T(8,128)S(1)}, f32[32,32]{1,0:T(8,128)S(1)}, u32[]{:S(2)}, u32[]{:S(2)}) %collective-permute-start.10) | collective-permute-done | bytes 4128 | tf_op jit(solution)/shard_map/ppermute | solution.py:666
  79.4 7.8 %apply.1 = (f32[16,16,16,256]{3,2,1,0:T(8,128)}, f32[16,16]{1,0:T(8,128)}) custom-call(f32[32,32]{1,0:T(8,128)S(1)} %add.27.sums, bf16[16,256,256]{2,1,0:T(8,128)(2,1)S(1)} %get-tuple-element.29.high_i, bf16[16,256,256]{2,1,0:T(8,128)(2,1)S(1)} %get-tuple-element.30.low_i, bf16[16,256,256]{2,1,0:T(8,128)(2,1)S(1)} %get-tuple-element.31.high_e, ...), custom_call_target="tpu_custom_call" | custom-call | flops 1000000000 | bytes 13000000 | tf_op jit(solution)/shard_map/apply/pallas_call | solution.py:635
  (7 shorter events, 0.0 us)
Async XLA Ops:
  0.6 17.1 %copy-start.6 = (s32[16,16,256]{2,1,0:T(8,128)S(1)}, s32[16,16,256]{2,1,0:T(8,128)}, u32[]{:S(2)}) copy-start(s32[16,16,256]{2,1,0:T(8,128)} %mask.3) | copy-start | bytes 786436
  0.6 17.1 %copy-start.5 = (s32[16,16,256]{2,1,0:T(8,128)S(1)}, s32[16,16,256]{2,1,0:T(8,128)}, u32[]{:S(2)}) copy-start(s32[16,16,256]{2,1,0:T(8,128)} %fn.3) | copy-start | bytes 786436
  0.7 17.1 %copy-start.4 = (s32[16,16,256]{2,1,0:T(8,128)S(1)}, s32[16,16,256]{2,1,0:T(8,128)}, u32[]{:S(2)}) copy-start(s32[16,16,256]{2,1,0:T(8,128)} %fe.3) | copy-start | bytes 786436
  0.7 17.1 %copy-start.3 = (f32[16,16,256]{2,1,0:T(8,128)S(1)}, f32[16,16,256]{2,1,0:T(8,128)}, u32[]{:S(2)}) copy-start(f32[16,16,256]{2,1,0:T(8,128)} %vn.3) | copy-start | bytes 786436
  0.7 17.1 %copy-start.2 = (f32[16,16,256]{2,1,0:T(8,128)S(1)}, f32[16,16,256]{2,1,0:T(8,128)}, u32[]{:S(2)}) copy-start(f32[16,16,256]{2,1,0:T(8,128)} %ve.3) | copy-start | bytes 786436
  0.7 17.1 %copy-start.1 = (f32[16,16,256]{2,1,0:T(8,128)S(1)}, f32[16,16,256]{2,1,0:T(8,128)}, u32[]{:S(2)}) copy-start(f32[16,16,256]{2,1,0:T(8,128)} %mean.3) | copy-start | bytes 786436
  6.0 36.3 %collective-permute-start = (f32[2,18,2,24,128]{4,3,2,1,0:T(8,128)}, f32[2,18,2,24,128]{4,3,2,1,0:T(8,128)S(1)}, u32[]{:S(2)}, u32[]{:S(2)}) collective-permute-start(f32[2,18,2,24,128]{4,3,2,1,0:T(8,128)} %get-tuple-element.19), channel_id=1, source_target_pairs={{0,8},{8,16},{16,24},{24,32},{32,40},{40,48},{48,56},{56,64},{64,7... | collective-permute-start | bytes 2654216 | tf_op jit(solution)/shard_map/ppermute | solution.py:656
  10.0 32.4 %collective-permute-start.1 = (f32[2,18,2,24,128]{4,3,2,1,0:T(8,128)}, f32[2,18,2,24,128]{4,3,2,1,0:T(8,128)S(1)}, u32[]{:S(2)}, u32[]{:S(2)}) collective-permute-start(f32[2,18,2,24,128]{4,3,2,1,0:T(8,128)} %get-tuple-element.20), channel_id=1, source_target_pairs={{8,0},{16,8},{24,16},{32,24},{40,32},{48,40},{56,48},{64,56},{72,6... | collective-permute-start | bytes 2654216 | tf_op jit(solution)/shard_map/ppermute | solution.py:661
  11.3 2.8 %collective-permute-start.2 = (f32[20,8,128]{2,1,0:T(8,128)}, f32[20,8,128]{2,1,0:T(8,128)S(1)}, u32[]{:S(2)}, u32[]{:S(2)}) collective-permute-start(f32[20,8,128]{2,1,0:T(8,128)} %get-tuple-element.21), channel_id=1, source_target_pairs={{0,1},{1,2},{2,3},{3,4},{4,5},{5,6},{6,7},{8,9},{9,10},{10,11},{11... | collective-permute-start | bytes 245768 | tf_op jit(solution)/shard_map/ppermute | solution.py:656
  12.7 5.0 %collective-permute-start.3 = (f32[20,8,128]{2,1,0:T(8,128)}, f32[20,8,128]{2,1,0:T(8,128)S(1)}, u32[]{:S(2)}, u32[]{:S(2)}) collective-permute-start(f32[20,8,128]{2,1,0:T(8,128)} %get-tuple-element.22), channel_id=1, source_target_pairs={{1,0},{2,1},{3,2},{4,3},{5,4},{6,5},{7,6},{9,8},{10,9},{11,10},{12... | collective-permute-start | bytes 245768 | tf_op jit(solution)/shard_map/ppermute | solution.py:661
  17.8 2.2 %copy-start = (f32[16,16,16,256]{3,2,1,0:T(8,128)S(1)}, f32[16,16,16,256]{3,2,1,0:T(8,128)}, u32[]{:S(2)}) copy-start(f32[16,16,16,256]{3,2,1,0:T(8,128)} %modes.3) | copy-start | bytes 12582916
  46.6 4.2 %collective-permute-start.4 = (f32[32,32]{1,0:T(8,128)S(1)}, f32[32,32]{1,0:T(8,128)S(1)}, u32[]{:S(2)}, u32[]{:S(2)}) collective-permute-start(f32[32,32]{1,0:T(8,128)S(1)} %get-tuple-element.28), channel_id=1, source_target_pairs={{0,1},{1,0},{2,3},{3,2},{4,5},{5,4},{6,7},{7,6},{8,9},{9,8},{10,11... | collective-permute-start | bytes 12296 | tf_op jit(solution)/shard_map/ppermute | solution.py:666
  50.8 3.7 %collective-permute-start.5 = (f32[32,32]{1,0:T(8,128)S(1)}, f32[32,32]{1,0:T(8,128)S(1)}, u32[]{:S(2)}, u32[]{:S(2)}) collective-permute-start(f32[32,32]{1,0:T(8,128)S(1)} %add.21), channel_id=1, source_target_pairs={{0,2},{1,3},{2,0},{3,1},{4,6},{5,7},{6,4},{7,5},{8,10},{9,11},{10,... | collective-permute-start | bytes 12296 | tf_op jit(solution)/shard_map/ppermute | solution.py:666
  54.5 4.9 %collective-permute-start.6 = (f32[32,32]{1,0:T(8,128)S(1)}, f32[32,32]{1,0:T(8,128)S(1)}, u32[]{:S(2)}, u32[]{:S(2)}) collective-permute-start(f32[32,32]{1,0:T(8,128)S(1)} %add.22), channel_id=1, source_target_pairs={{0,6},{1,7},{2,4},{3,5},{4,2},{5,3},{6,0},{7,1},{8,14},{9,15},{10,... | collective-permute-start | bytes 12296 | tf_op jit(solution)/shard_map/ppermute | solution.py:666
  59.5 4.4 %collective-permute-start.7 = (f32[32,32]{1,0:T(8,128)S(1)}, f32[32,32]{1,0:T(8,128)S(1)}, u32[]{:S(2)}, u32[]{:S(2)}) collective-permute-start(f32[32,32]{1,0:T(8,128)S(1)} %add.23), channel_id=1, source_target_pairs={{0,8},{1,9},{2,10},{3,11},{4,12},{5,13},{6,14},{7,15},{8,0},{9,1},... | collective-permute-start | bytes 12296 | tf_op jit(solution)/shard_map/ppermute | solution.py:666
  63.8 5.8 %collective-permute-start.8 = (f32[32,32]{1,0:T(8,128)S(1)}, f32[32,32]{1,0:T(8,128)S(1)}, u32[]{:S(2)}, u32[]{:S(2)}) collective-permute-start(f32[32,32]{1,0:T(8,128)S(1)} %add.24), channel_id=1, source_target_pairs={{0,24},{1,25},{2,26},{3,27},{4,28},{5,29},{6,30},{7,31},{8,16},{9,... | collective-permute-start | bytes 12296 | tf_op jit(solution)/shard_map/ppermute | solution.py:666
  69.7 4.5 %collective-permute-start.9 = (f32[32,32]{1,0:T(8,128)S(1)}, f32[32,32]{1,0:T(8,128)S(1)}, u32[]{:S(2)}, u32[]{:S(2)}) collective-permute-start(f32[32,32]{1,0:T(8,128)S(1)} %add.25), channel_id=1, source_target_pairs={{0,32},{1,33},{2,34},{3,35},{4,36},{5,37},{6,38},{7,39},{8,40},{9,... | collective-permute-start | bytes 12296 | tf_op jit(solution)/shard_map/ppermute | solution.py:666
  74.2 5.2 %collective-permute-start.10 = (f32[32,32]{1,0:T(8,128)S(1)}, f32[32,32]{1,0:T(8,128)S(1)}, u32[]{:S(2)}, u32[]{:S(2)}) collective-permute-start(f32[32,32]{1,0:T(8,128)S(1)} %add.26), channel_id=1, source_target_pairs={{0,96},{1,97},{2,98},{3,99},{4,100},{5,101},{6,102},{7,103},{8,104... | collective-permute-start | bytes 12296 | tf_op jit(solution)/shard_map/ppermute | solution.py:666

commit v4 on v3

--- a/solution.py
+++ b/solution.py
@@ -22,6 +22,7 @@
 bf16 = jnp.bfloat16
 
 ANY = pl.BlockSpec(memory_space=pl.ANY)
+HBM = pl.BlockSpec(memory_space=pltpu.HBM)
 VMEM = pl.BlockSpec(memory_space=pltpu.VMEM)
 
 
@@ -87,12 +88,12 @@
             copies.append(
                 pltpu.make_async_copy(
                     lane_half(modes, half).at[pl.ds(4 * chunk, 4)],
-                    X.at[half, pl.ds(4 * chunk, 4)],
+                    X.at[half, pl.ds(4 * chunk, 4), :, pl.ds(8, BX)],
                     sems.at[len(copies)],
                 )
             )
     for source, target in (
-        (mean, lambda half: X.at[half, M]),
+        (mean, lambda half: X.at[half, M, :, pl.ds(8, BX)]),
         (vn, lambda half: V.at[0, half]),
         (ve, lambda half: V.at[1, half]),
         (fn, lambda half: I.at[0, half]),
@@ -105,18 +106,28 @@
             )
     for copy in copies:
         copy.start()
+    zero_tile = jnp.zeros((8, LANES), f32)
+
+    def clear(f, carry):
+        for half in range(2):
+            for z in range(NZ):
+                X[half, f, z, 0:8, :] = zero_tile
+                X[half, f, z, 24:32, :] = zero_tile
+        return carry
+
+    lax.fori_loop(0, F, clear, 0)
 
     def field(f, carry):
         for half in range(2):
             for zh in range(2):
                 for target, tile, first in ((up, 1, 5), (down, 0, 0)):
                     tiles = pack_rows(
-                        lambda z: X[half, f, 8 * zh + z, 8 * tile : 8 * tile + 8, :], first
+                        lambda z: X[half, f, 8 * zh + z, 8 + 8 * tile : 16 + 8 * tile, :], first
                     )
                     for t in range(3):
                         target[half, f, zh, 8 * t : 8 * t + 8, :] = tiles[t]
         def tile_of(half):
-            return lambda k: X[half, f, k // 2, 8 * (k % 2) : 8 * (k % 2) + 8, :]
+            return lambda k: X[half, f, k // 2, 8 + 8 * (k % 2) : 16 + 8 * (k % 2), :]
         east[f] = pack_columns(tile_of(1), lambda k: 4 * k - 125)
         west[f] = pack_columns(tile_of(0), lambda k: 4 * k)
         return carry
@@ -167,16 +178,16 @@
             rows,
             columns,
             columns,
+            jax.ShapeDtypeStruct((2, F, NZ, 32, LANES), f32),
         ),
-        in_specs=[ANY] * 7,
-        out_specs=(VMEM,) * 4,
+        in_specs=[HBM] * 7,
+        out_specs=(VMEM,) * 5,
         scratch_shapes=[
-            pltpu.VMEM((2, F, NZ, BX, LANES), f32),
             pltpu.VMEM((2, 2, NZ, BX, LANES), f32),
             pltpu.VMEM((3, 2, NZ, BX, LANES), jnp.int32),
             pltpu.SemaphoreType.DMA((20,)),
         ],
-        compiler_params=params(62),
+        compiler_params=params(24),
         cost_estimate=cost(10**7, 7 * 10**6),
         name="pack",
     )(modes, mean, ve, vn, fe, fn, mask)
@@ -190,6 +201,13 @@
         return jnp.where(inside, a, b), jnp.where(inside, b, c)
     outside = lanes < -offset
     return jnp.where(outside, c, a), jnp.where(outside, a, b)
+
+
+def around_lanes(first, second, offset):
+    lanes = lane_ids()
+    a, b = (rolled(v, -offset, 1) for v in (first, second))
+    kept = lanes < LANES - offset if offset > 0 else lanes >= -offset
+    return jnp.where(kept, a, b), jnp.where(kept, b, a)
 
 
 def cell_weights(a_low, b_low, d_low, a_high, b_high, d_high):
@@ -218,6 +236,10 @@
     dims = (((1,), (1,)), ((), ()))
     acc[0:256, :] += lax.dot_general(high, high, dims, preferred_element_type=f32)
     acc[256:512, :] += lax.dot_general(low, high, dims, preferred_element_type=f32)
+
+
+def joined(parts):
+    return jnp.concatenate([parts[z] for z in range(NZ)], axis=1)
 
 
 def field_sums(acc):
@@ -233,20 +255,11 @@
 
 
 def interior_kernel(
-    modes, mean, ve, vn, fe, fn, mask, west, east,
+    X, ve, vn, fe, fn, mask, west, east, own_last, own_first,
     high_out, low_out, edge_out, weights_out, mean_out, sums_out,
-    X, VE, FE, W, VN, FN, H, T, Z, acc, sems,
+    VE, FE, W, VN, FN, H, G, T, Z, acc, sems,
 ):
     zero_tile = jnp.zeros((8, LANES), f32)
-
-    def clear(f, carry):
-        for half in range(2):
-            for z in range(NZ):
-                X[half, f, z, 0:8, :] = zero_tile
-                X[half, f, z, 24:32, :] = zero_tile
-        return carry
-
-    lax.fori_loop(0, F, clear, 0)
     for half in range(2):
         for z in range(NZ):
             edge_out[z, half, 0:8, :] = zero_tile
@@ -264,8 +277,6 @@
     body = pl.ds(8, BX)
     for half in range(2):
         for source, target in (
-            (modes, X.at[half, pl.ds(0, M), :, body]),
-            (mean, X.at[half, M, :, body]),
             (ve, VE.at[half, :, body]),
             (mask, W.at[half, :, body]),
             (vn, VN.at[half]),
@@ -278,15 +289,53 @@
     for copy in copies:
         copy.start()
 
+    def spread(index, before, after):
+        for k in range(2 * NZ):
+            moved_after = rolled(after, -4 * k, 1)
+            moved_before = rolled(before, LANES - 3 - 4 * k, 1)
+            yield index, k, moved_before, moved_after
+
+    for f in range(F, F + 3):
+        for index, k, moved_before, moved_after in spread(f, west[f], east[f]):
+            H[index, k] = jnp.where(lanes < 64, moved_after, moved_before)
+
+    place = lanes % 4
+
+    (v_in, f_in, w_in) = (west[F + i] for i in range(3))
+    (v_own, f_own, w_own) = (own_first[F + i] for i in range(3))
+    lower_of = lambda outer_plane, own: jnp.where(
+        place == 0, rolled(outer_plane, -2, 1), rolled(own, 1, 1)
+    )
+    low_face = face_parts(
+        lower_of(w_in, w_own) * w_own, lower_of(v_in, v_own), lower_of(f_in, f_own)
+    )
+    high_face = face_parts(w_own * rolled(w_own, -1, 1), v_own, f_own)
+    first_gains = cell_weights(*low_face, *high_face)
+    for d in range(1, 4):
+        G[d - 1] = jnp.where(place < d, first_gains[3 - d], 0.0)
+    w_next = east[F + 2]
+    (v_own, f_own, w_own) = (own_last[F + i] for i in range(3))
+    high_face = face_parts(
+        w_own * jnp.where(place == 2, rolled(w_next, 2, 1), rolled(w_own, -1, 1)), v_own, f_own
+    )
+    low_face = tuple(rolled(part, 1, 1) for part in high_face)
+    last_gains = cell_weights(*low_face, *high_face)
+    for d in range(1, 4):
+        G[2 + d] = jnp.where((place >= 3 - d) & (place < 3), last_gains[3 + d], 0.0)
+
     def beside(f, carry):
-        after, before = east[f], west[f]
-        for k in range(2 * NZ):
-            H[f, k] = jnp.where(
-                lanes < 64, rolled(after, -4 * k, 1), rolled(before, LANES - 3 - 4 * k, 1)
+        before, after = west[f], east[f]
+        first = (
+            G[0] * rolled(before, -2, 1) + G[1] * rolled(before, -1, 1) + G[2] * before
+        )
+        last = G[3] * rolled(after, 2, 1) + G[4] * rolled(after, 1, 1) + G[5] * after
+        for index, k, moved_last, moved_first in spread(f, last, first):
+            H[index, k] = jnp.where(
+                lanes < 3, moved_first, jnp.where(lanes >= LANES - 3, moved_last, 0.0)
             )
         return carry
 
-    lax.fori_loop(0, F + 3, beside, 0)
+    lax.fori_loop(0, F, beside, 0)
     for copy in copies:
         copy.wait()
 
@@ -335,6 +384,17 @@
             wy = [
                 cell_weights(*(before[i][half] for i in range(3)), *own[half]) for half in range(2)
             ]
+            wy = [
+                [
+                    jnp.where(
+                        (lanes < 3 - j) if half == 0 else (lanes >= LANES + 3 - j), 0.0, wy[half][j]
+                    )
+                    if (half == 0) == (j < 3) and j != 3
+                    else wy[half][j]
+                    for j in range(7)
+                ]
+                for half in range(2)
+            ]
             centre = [
                 wx[half][3] + wy[half][3] - (gain_up + gain_down) * wet[half] for half in range(2)
             ]
@@ -363,9 +423,11 @@
                     + w_down[half] * X[half, f, z_down, start : start + 8, :]
                     for half in range(2)
                 ]
-                edge = outer(f)
+                beyond_block = outer(f)
+                total[0] += jnp.where(lanes < 64, beyond_block, 0.0)
+                total[1] += jnp.where(lanes < 64, 0.0, beyond_block)
                 for offset in (-3, -2, -1, 1, 2, 3):
-                    moved = along_lanes(own_cells[0], own_cells[1], edge, offset)
+                    moved = around_lanes(own_cells[0], own_cells[1], offset)
                     for half in range(2):
                         total[half] += wx[half][3 + offset] * X[
                             half, f, z, start + offset : start + offset + 8, :
@@ -398,14 +460,14 @@
         high, low = split(Z[...])
         high_out[z] = high
         low_out[z] = low
-        add_products(acc, high, low)
         return carry
 
     lax.fori_loop(0, NZ, level, 0)
+    add_products(acc, joined(high_out), joined(low_out))
     sums_out[...] = field_sums(acc)
 
 
-def interior(modes, mean, ve, vn, fe, fn, mask, west, east):
+def interior(cells, ve, vn, fe, fn, mask, west, east, own_last, own_first):
     parts = jax.ShapeDtypeStruct((NZ, 256, 256), bf16)
     return pl.pallas_call(
         interior_kernel,
@@ -414,28 +476,28 @@
             parts,
             jax.ShapeDtypeStruct((NZ, 2, TAIL + 8 * M, LANES), f32),
             jax.ShapeDtypeStruct((2, NZ, 6, 8, LANES), f32),
-            jax.ShapeDtypeStruct(mean.shape, f32),
+            jax.ShapeDtypeStruct(ve.shape, f32),
             jax.ShapeDtypeStruct((64, 32), f32),
         ),
-        in_specs=[ANY] * 7 + [VMEM] * 2,
+        in_specs=[VMEM] + [HBM] * 5 + [VMEM] * 4,
         out_specs=(VMEM,) * 6,
         scratch_shapes=[
-            pltpu.VMEM((2, F, NZ, 32, LANES), f32),
             pltpu.VMEM((2, NZ, 32, LANES), f32),
             pltpu.VMEM((2, NZ, 32, LANES), f32),
             pltpu.VMEM((2, NZ, 32, LANES), jnp.int32),
             pltpu.VMEM((2, NZ, BX, LANES), f32),
             pltpu.VMEM((2, 2, NZ, BX, LANES), jnp.int32),
             pltpu.VMEM((F + 3, 2 * NZ, 8, LANES), f32),
+            pltpu.VMEM((6, 8, LANES), f32),
             pltpu.VMEM((2, M, 8, LANES), f32),
             pltpu.VMEM((256, 256), f32),
             pltpu.VMEM((512, 256), f32),
-            pltpu.SemaphoreType.DMA((14,)),
+            pltpu.SemaphoreType.DMA((10,)),
         ],
         compiler_params=params(28),
-        cost_estimate=cost(10**6, 10**6),
+        cost_estimate=cost(10**10, 4 * 10**7),
         name="interior",
-    )(modes, mean, ve, vn, fe, fn, mask, west, east)
+    )(cells, ve, vn, fe, fn, mask, west, east, own_last, own_first)
 
 
 def edge_kernel(
@@ -670,16 +732,25 @@
     mean_field, mode_fields, velocity_east, velocity_north, flag_east, flag_north, ocean_mask
 ):
     axes = ("gx", "gy")
-    up, down, east_send, west_send = pack(
+    (
+        mean_field, mode_fields, velocity_east, velocity_north, flag_east, flag_north, ocean_mask
+    ) = (
+        pltpu.with_memory_space_constraint(value, pltpu.HBM)
+        for value in (
+            mean_field, mode_fields, velocity_east, velocity_north, flag_east, flag_north,
+            ocean_mask,
+        )
+    )
+    up, down, east_send, west_send, cells = pack(
         mode_fields, mean_field, velocity_east, velocity_north, flag_east, flag_north, ocean_mask
     )
+    west = onward(east_send, "gy")
+    east = backward(west_send, "gy")
     below = onward(up, "gx")
     above = backward(down, "gx")
-    west = onward(east_send, "gy")
-    east = backward(west_send, "gy")
     high_i, low_i, edge, weights, mean_part, sums_i = interior(
-        mode_fields, mean_field, velocity_east, velocity_north, flag_east, flag_north,
-        ocean_mask, west, east,
+        cells, velocity_east, velocity_north, flag_east, flag_north, ocean_mask,
+        west, east, east_send, west_send,
     )
     high_e, low_e, mean_next, sums = edges(below, above, edge, weights, mean_part, sums_i)
     for distance in (1, 2, 6, 8, 24, 32, 96):

time: 87.8 us -> 77.8 us (0.89)
  Pallas kernels: 39.7 us -> 33.6 us
  starting transfers between devices: 27.4 us -> 24.5 us
  local copies, waits for them, and re-layouts: 2.21 us -> 0 us
  waiting for transfers between devices: 17.1 us -> 18.7 us
    pallas_call x1, Pallas kernels: 22.3 us -> 17.5 us  [interior(): pl.pallas_call(interior_kernel, out_shape=(parts, parts, jax.ShapeDtypeSt...]
    ppermute x7, starting transfers between devices: 19.4 us -> 16.2 us  [exchanged(): return lax.ppermute(value, axes, [(i, i ^ distance) for i in range(size)])]
    unnamed x14 -> x0, local copies, waits for them, and re-layouts: 2.21 us -> none
    pallas_call x1, Pallas kernels: 5.31 us -> 4.1 us  [pack(): pl.pallas_call(pack_kernel, out_shape=(rows, rows, columns, columns, jax....]
    ppermute x7, waiting for transfers between devices: 13.3 us -> 14.5 us  [exchanged(): return lax.ppermute(value, axes, [(i, i ^ distance) for i in range(size)])]
  transfers between devices with their start and end apart: 11 -> 11, of which waited for: 8 -> 8; matrix products, arithmetic and copies ran while one was open for 0% -> 0% of each run, Pallas kernels for 26% -> 23%
where the time goes in v4:
time: 77.8 us; the launch traced here: 77.6 us
  Pallas kernels  33.6 us (43%)
  starting transfers between devices  24.5 us (31%)
  waiting for transfers between devices  18.7 us (24%)
    pallas_call x1, Pallas kernels, interior(): pl.pallas_call(interior_kernel, out_shape=(parts, parts, jax.ShapeDtypeSt...  17.5 us
    ppermute x7, starting transfers between devices, exchanged(): return lax.ppermute(value, axes, [(i, i ^ distance) for i in range(size)])  16.2 us
    ppermute x7, waiting for transfers between devices, exchanged(): return lax.ppermute(value, axes, [(i, i ^ distance) for i in range(size)])  14.5 us
    pallas_call x1, Pallas kernels, apply_map(): pl.pallas_call(make_apply_kernel(cell_count), out_shape=(jax.ShapeDtypeSt...  7.85 us
    ppermute x2, starting transfers between devices, onward(): return lax.ppermute(value, axis, [(i, i + 1) for i in range(size - 1)])  5.7 us
    pallas_call x1, Pallas kernels, edges(): pl.pallas_call(edge_kernel, out_shape=(parts, parts, jax.ShapeDtypeStruct...  4.22 us
    ppermute x2, waiting for transfers between devices, backward(): return lax.ppermute(value, axis, [(i + 1, i) for i in range(size - 1)])  4.19 us
    pallas_call x1, Pallas kernels, pack(): pl.pallas_call(pack_kernel, out_shape=(rows, rows, columns, columns, jax....  4.1 us
  transfers between devices with their start and end apart: 11, of which 8 were waited for; matrix products, arithmetic and copies ran while one was open for 0% of the time, Pallas kernels for 23%

profile of v4, /device:TPU:0, one launch (start us, length us, event | category | flops | bytes accessed | tf_op | source)
XLA Modules:
  0.0 77.6 jit_solution(2694294363826260777)
XLA Ops:
  0.6 4.1 %pack.1 = (f32[2,18,2,24,128]{4,3,2,1,0:T(8,128)S(1)}, f32[2,18,2,24,128]{4,3,2,1,0:T(8,128)S(1)}, f32[20,8,128]{2,1,0:T(8,128)S(1)}, f32[20,8,128]{2,1,0:T(8,128)S(1)}, f32[2,17,16,32,128]{4,3,2,1,0:T(8,128)S(1)}) custom-call(f32[16,16,16,256]{3,2,1,0:T(8,128)} %modes.1, f32[16,16,256]{2,1,0:T(8,128)} %mean.1, f32[16,16,256]{2,1,0:T(8,128)} %ve.3, ...), custom_call_target="tpu_custom_call" | custom-call | flops 10000000 | bytes 7000000 | tf_op jit(solution)/shard_map/pack/pallas_call | solution.py:174
  4.7 1.3 %collective-permute-start.2 = (f32[20,8,128]{2,1,0:T(8,128)S(1)}, f32[20,8,128]{2,1,0:T(8,128)S(1)}, u32[]{:S(2)}, u32[]{:S(2)}) collective-permute-start(f32[20,8,128]{2,1,0:T(8,128)S(1)} %get-tuple-element.23.own_last), channel_id=1, source_target_pairs={{0,1},{1,2},{2,3},{3,4},{4,5},{5,6},{6,7},{8,9},{9,10},{10,11},{11... | collective-permute-start | bytes 245768 | tf_op jit(solution)/shard_map/ppermute | solution.py:718
  6.0 1.3 %collective-permute-start.3 = (f32[20,8,128]{2,1,0:T(8,128)S(1)}, f32[20,8,128]{2,1,0:T(8,128)S(1)}, u32[]{:S(2)}, u32[]{:S(2)}) collective-permute-start(f32[20,8,128]{2,1,0:T(8,128)S(1)} %get-tuple-element.24.own_first), channel_id=1, source_target_pairs={{1,0},{2,1},{3,2},{4,3},{5,4},{6,5},{7,6},{9,8},{10,9},{11,10},{12... | collective-permute-start | bytes 245768 | tf_op jit(solution)/shard_map/ppermute | solution.py:723
  7.3 4.4 %collective-permute-start = (f32[2,18,2,24,128]{4,3,2,1,0:T(8,128)S(1)}, f32[2,18,2,24,128]{4,3,2,1,0:T(8,128)S(1)}, u32[]{:S(2)}, u32[]{:S(2)}) collective-permute-start(f32[2,18,2,24,128]{4,3,2,1,0:T(8,128)S(1)} %get-tuple-element.20), channel_id=1, source_target_pairs={{0,8},{8,16},{16,24},{24,32},{32,40},{40,48},{48,56},{56,64},{64,7... | collective-permute-start | bytes 2654216 | tf_op jit(solution)/shard_map/ppermute | solution.py:718
  11.8 1.3 %collective-permute-start.1 = (f32[2,18,2,24,128]{4,3,2,1,0:T(8,128)S(1)}, f32[2,18,2,24,128]{4,3,2,1,0:T(8,128)S(1)}, u32[]{:S(2)}, u32[]{:S(2)}) collective-permute-start(f32[2,18,2,24,128]{4,3,2,1,0:T(8,128)S(1)} %get-tuple-element.21), channel_id=1, source_target_pairs={{8,0},{16,8},{24,16},{32,24},{40,32},{48,40},{56,48},{64,56},{72,6... | collective-permute-start | bytes 2654216 | tf_op jit(solution)/shard_map/ppermute | solution.py:723
  13.1 0.0 collective-permute-done.2.west
  13.1 0.0 collective-permute-done.3.east
  13.1 17.5 %interior.1 = (bf16[16,256,256]{2,1,0:T(8,128)(2,1)S(1)}, bf16[16,256,256]{2,1,0:T(8,128)(2,1)S(1)}, f32[16,2,272,128]{3,2,1,0:T(8,128)S(1)}, f32[2,16,6,8,128]{...) custom-call(f32[2,17,16,32,128]{4,3,2,1,0:T(8,128)S(1)} %get-tuple-element.22.X, ...), custom_call_target="tpu_custom_call" | custom-call | flops 10000000000 | bytes 40000000 | tf_op jit(solution)/shard_map/interior/pallas_call | solution.py:472
  30.6 0.0 collective-permute-done.below
  30.6 4.2 %collective-permute-done.1.above = f32[2,18,2,24,128]{4,3,2,1,0:T(8,128)S(1)} collective-permute-done((f32[2,18,2,24,128]{4,3,2,1,0:T(8,128)S(1)}, f32[2,18,2,24,128]{4,3,2,1,0:T(8,128)S(1)}, u32[]{:S(2)}, u32[]{:S(2)}) %collective-permute-start.1) | collective-permute-done | bytes 884768 | tf_op jit(solution)/shard_map/ppermute | solution.py:723
  34.8 4.2 %edges.1 = (bf16[16,256,256]{2,1,0:T(8,128)(2,1)S(1)}, bf16[16,256,256]{2,1,0:T(8,128)(2,1)S(1)}, f32[16,16,256]{2,1,0:T(8,128)}, f32[32,32]{1,0:T(8,128)S(1)}) custom-call(f32[2,18,2,24,128]{4,3,2,1,0:T(8,128)S(1)} %collective-permute-done.below, f32[2,18,2,24,128]{4,3,2,1,0:T(8,128)S(1)} %collective-permute-done.1.above, ...), custom_call_target="tpu_custom_call" | custom-call | flops 1000000000 | bytes 10000000 | tf_op jit(solution)/shard_map/edges/pallas_call | solution.py:596
  39.0 1.2 %collective-permute-start.4 = (f32[32,32]{1,0:T(8,128)S(1)}, f32[32,32]{1,0:T(8,128)S(1)}, u32[]{:S(2)}, u32[]{:S(2)}) collective-permute-start(f32[32,32]{1,0:T(8,128)S(1)} %get-tuple-element.30), channel_id=1, source_target_pairs={{0,1},{1,0},{2,3},{3,2},{4,5},{5,4},{6,7},{7,6},{8,9},{9,8},{10,11... | collective-permute-start | bytes 12296 | tf_op jit(solution)/shard_map/ppermute | solution.py:728
  40.2 0.8 %collective-permute-done.4 = f32[32,32]{1,0:T(8,128)S(1)} collective-permute-done((f32[32,32]{1,0:T(8,128)S(1)}, f32[32,32]{1,0:T(8,128)S(1)}, u32[]{:S(2)}, u32[]{:S(2)}) %collective-permute-start.4) | collective-permute-done | bytes 4128 | tf_op jit(solution)/shard_map/ppermute | solution.py:728
  41.0 3.5 %collective-permute-start.5 = (f32[32,32]{1,0:T(8,128)S(1)}, f32[32,32]{1,0:T(8,128)S(1)}, u32[]{:S(2)}, u32[]{:S(2)}) collective-permute-start(f32[32,32]{1,0:T(8,128)S(1)} %add.21), channel_id=1, source_target_pairs={{0,2},{1,3},{2,0},{3,1},{4,6},{5,7},{6,4},{7,5},{8,10},{9,11},{10,... | collective-permute-start | bytes 12296 | tf_op jit(solution)/shard_map/ppermute | solution.py:728
  44.5 1.7 %collective-permute-done.5 = f32[32,32]{1,0:T(8,128)S(1)} collective-permute-done((f32[32,32]{1,0:T(8,128)S(1)}, f32[32,32]{1,0:T(8,128)S(1)}, u32[]{:S(2)}, u32[]{:S(2)}) %collective-permute-start.5) | collective-permute-done | bytes 4128 | tf_op jit(solution)/shard_map/ppermute | solution.py:728
  46.2 2.3 %collective-permute-start.6 = (f32[32,32]{1,0:T(8,128)S(1)}, f32[32,32]{1,0:T(8,128)S(1)}, u32[]{:S(2)}, u32[]{:S(2)}) collective-permute-start(f32[32,32]{1,0:T(8,128)S(1)} %add.22), channel_id=1, source_target_pairs={{0,6},{1,7},{2,4},{3,5},{4,2},{5,3},{6,0},{7,1},{8,14},{9,15},{10,... | collective-permute-start | bytes 12296 | tf_op jit(solution)/shard_map/ppermute | solution.py:728
  48.5 2.7 %collective-permute-done.6 = f32[32,32]{1,0:T(8,128)S(1)} collective-permute-done((f32[32,32]{1,0:T(8,128)S(1)}, f32[32,32]{1,0:T(8,128)S(1)}, u32[]{:S(2)}, u32[]{:S(2)}) %collective-permute-start.6) | collective-permute-done | bytes 4128 | tf_op jit(solution)/shard_map/ppermute | solution.py:728
  51.2 1.7 %collective-permute-start.7 = (f32[32,32]{1,0:T(8,128)S(1)}, f32[32,32]{1,0:T(8,128)S(1)}, u32[]{:S(2)}, u32[]{:S(2)}) collective-permute-start(f32[32,32]{1,0:T(8,128)S(1)} %add.23), channel_id=1, source_target_pairs={{0,8},{1,9},{2,10},{3,11},{4,12},{5,13},{6,14},{7,15},{8,0},{9,1},... | collective-permute-start | bytes 12296 | tf_op jit(solution)/shard_map/ppermute | solution.py:728
  52.9 2.0 %collective-permute-done.7 = f32[32,32]{1,0:T(8,128)S(1)} collective-permute-done((f32[32,32]{1,0:T(8,128)S(1)}, f32[32,32]{1,0:T(8,128)S(1)}, u32[]{:S(2)}, u32[]{:S(2)}) %collective-permute-start.7) | collective-permute-done | bytes 4128 | tf_op jit(solution)/shard_map/ppermute | solution.py:728
  54.9 4.3 %collective-permute-start.8 = (f32[32,32]{1,0:T(8,128)S(1)}, f32[32,32]{1,0:T(8,128)S(1)}, u32[]{:S(2)}, u32[]{:S(2)}) collective-permute-start(f32[32,32]{1,0:T(8,128)S(1)} %add.24), channel_id=1, source_target_pairs={{0,24},{1,25},{2,26},{3,27},{4,28},{5,29},{6,30},{7,31},{8,16},{9,... | collective-permute-start | bytes 12296 | tf_op jit(solution)/shard_map/ppermute | solution.py:728
  59.3 1.7 %collective-permute-done.8 = f32[32,32]{1,0:T(8,128)S(1)} collective-permute-done((f32[32,32]{1,0:T(8,128)S(1)}, f32[32,32]{1,0:T(8,128)S(1)}, u32[]{:S(2)}, u32[]{:S(2)}) %collective-permute-start.8) | collective-permute-done | bytes 4128 | tf_op jit(solution)/shard_map/ppermute | solution.py:728
  61.0 1.5 %collective-permute-start.9 = (f32[32,32]{1,0:T(8,128)S(1)}, f32[32,32]{1,0:T(8,128)S(1)}, u32[]{:S(2)}, u32[]{:S(2)}) collective-permute-start(f32[32,32]{1,0:T(8,128)S(1)} %add.25), channel_id=1, source_target_pairs={{0,32},{1,33},{2,34},{3,35},{4,36},{5,37},{6,38},{7,39},{8,40},{9,... | collective-permute-start | bytes 12296 | tf_op jit(solution)/shard_map/ppermute | solution.py:728
  62.5 2.3 %collective-permute-done.9 = f32[32,32]{1,0:T(8,128)S(1)} collective-permute-done((f32[32,32]{1,0:T(8,128)S(1)}, f32[32,32]{1,0:T(8,128)S(1)}, u32[]{:S(2)}, u32[]{:S(2)}) %collective-permute-start.9) | collective-permute-done | bytes 4128 | tf_op jit(solution)/shard_map/ppermute | solution.py:728
  64.7 1.7 %collective-permute-start.10 = (f32[32,32]{1,0:T(8,128)S(1)}, f32[32,32]{1,0:T(8,128)S(1)}, u32[]{:S(2)}, u32[]{:S(2)}) collective-permute-start(f32[32,32]{1,0:T(8,128)S(1)} %add.26), channel_id=1, source_target_pairs={{0,96},{1,97},{2,98},{3,99},{4,100},{5,101},{6,102},{7,103},{8,104... | collective-permute-start | bytes 12296 | tf_op jit(solution)/shard_map/ppermute | solution.py:728
  66.4 3.3 %collective-permute-done.10 = f32[32,32]{1,0:T(8,128)S(1)} collective-permute-done((f32[32,32]{1,0:T(8,128)S(1)}, f32[32,32]{1,0:T(8,128)S(1)}, u32[]{:S(2)}, u32[]{:S(2)}) %collective-permute-start.10) | collective-permute-done | bytes 4128 | tf_op jit(solution)/shard_map/ppermute | solution.py:728
  69.7 7.8 %apply.1 = (f32[16,16,16,256]{3,2,1,0:T(8,128)}, f32[16,16]{1,0:T(8,128)}) custom-call(f32[32,32]{1,0:T(8,128)S(1)} %add.27.sums, bf16[16,256,256]{2,1,0:T(8,128)(2,1)S(1)} %get-tuple-element.31.high_i, bf16[16,256,256]{2,1,0:T(8,128)(2,1)S(1)} %get-tuple-element.32.low_i, bf16[16,256,256]{2,1,0:T(8,128)(2,1)S(1)} %get-tuple-element.33.high_e, ...), custom_call_target="tpu_custom_call" | custom-call | flops 1000000000 | bytes 13000000 | tf_op jit(solution)/shard_map/apply/pallas_call | solution.py:697
  (7 shorter events, 0.0 us)
Async XLA Ops:
  4.7 8.3 %collective-permute-start.2 = (f32[20,8,128]{2,1,0:T(8,128)S(1)}, f32[20,8,128]{2,1,0:T(8,128)S(1)}, u32[]{:S(2)}, u32[]{:S(2)}) collective-permute-start(f32[20,8,128]{2,1,0:T(8,128)S(1)} %get-tuple-element.23.own_last), channel_id=1, source_target_pairs={{0,1},{1,2},{2,3},{3,4},{4,5},{5,6},{6,7},{8,9},{9,10},{10,11},{11... | collective-permute-start | bytes 245768 | tf_op jit(solution)/shard_map/ppermute | solution.py:718
  6.0 7.0 %collective-permute-start.3 = (f32[20,8,128]{2,1,0:T(8,128)S(1)}, f32[20,8,128]{2,1,0:T(8,128)S(1)}, u32[]{:S(2)}, u32[]{:S(2)}) collective-permute-start(f32[20,8,128]{2,1,0:T(8,128)S(1)} %get-tuple-element.24.own_first), channel_id=1, source_target_pairs={{1,0},{2,1},{3,2},{4,3},{5,4},{6,5},{7,6},{9,8},{10,9},{11,10},{12... | collective-permute-start | bytes 245768 | tf_op jit(solution)/shard_map/ppermute | solution.py:723
  7.3 23.2 %collective-permute-start = (f32[2,18,2,24,128]{4,3,2,1,0:T(8,128)S(1)}, f32[2,18,2,24,128]{4,3,2,1,0:T(8,128)S(1)}, u32[]{:S(2)}, u32[]{:S(2)}) collective-permute-start(f32[2,18,2,24,128]{4,3,2,1,0:T(8,128)S(1)} %get-tuple-element.20), channel_id=1, source_target_pairs={{0,8},{8,16},{16,24},{24,32},{32,40},{40,48},{48,56},{56,64},{64,7... | collective-permute-start | bytes 2654216 | tf_op jit(solution)/shard_map/ppermute | solution.py:718
  11.8 23.0 %collective-permute-start.1 = (f32[2,18,2,24,128]{4,3,2,1,0:T(8,128)S(1)}, f32[2,18,2,24,128]{4,3,2,1,0:T(8,128)S(1)}, u32[]{:S(2)}, u32[]{:S(2)}) collective-permute-start(f32[2,18,2,24,128]{4,3,2,1,0:T(8,128)S(1)} %get-tuple-element.21), channel_id=1, source_target_pairs={{8,0},{16,8},{24,16},{32,24},{40,32},{48,40},{56,48},{64,56},{72,6... | collective-permute-start | bytes 2654216 | tf_op jit(solution)/shard_map/ppermute | solution.py:723
  39.0 2.1 %collective-permute-start.4 = (f32[32,32]{1,0:T(8,128)S(1)}, f32[32,32]{1,0:T(8,128)S(1)}, u32[]{:S(2)}, u32[]{:S(2)}) collective-permute-start(f32[32,32]{1,0:T(8,128)S(1)} %get-tuple-element.30), channel_id=1, source_target_pairs={{0,1},{1,0},{2,3},{3,2},{4,5},{5,4},{6,7},{7,6},{8,9},{9,8},{10,11... | collective-permute-start | bytes 12296 | tf_op jit(solution)/shard_map/ppermute | solution.py:728
  41.0 5.2 %collective-permute-start.5 = (f32[32,32]{1,0:T(8,128)S(1)}, f32[32,32]{1,0:T(8,128)S(1)}, u32[]{:S(2)}, u32[]{:S(2)}) collective-permute-start(f32[32,32]{1,0:T(8,128)S(1)} %add.21), channel_id=1, source_target_pairs={{0,2},{1,3},{2,0},{3,1},{4,6},{5,7},{6,4},{7,5},{8,10},{9,11},{10,... | collective-permute-start | bytes 12296 | tf_op jit(solution)/shard_map/ppermute | solution.py:728
  46.2 4.9 %collective-permute-start.6 = (f32[32,32]{1,0:T(8,128)S(1)}, f32[32,32]{1,0:T(8,128)S(1)}, u32[]{:S(2)}, u32[]{:S(2)}) collective-permute-start(f32[32,32]{1,0:T(8,128)S(1)} %add.22), channel_id=1, source_target_pairs={{0,6},{1,7},{2,4},{3,5},{4,2},{5,3},{6,0},{7,1},{8,14},{9,15},{10,... | collective-permute-start | bytes 12296 | tf_op jit(solution)/shard_map/ppermute | solution.py:728
  51.2 3.7 %collective-permute-start.7 = (f32[32,32]{1,0:T(8,128)S(1)}, f32[32,32]{1,0:T(8,128)S(1)}, u32[]{:S(2)}, u32[]{:S(2)}) collective-permute-start(f32[32,32]{1,0:T(8,128)S(1)} %add.23), channel_id=1, source_target_pairs={{0,8},{1,9},{2,10},{3,11},{4,12},{5,13},{6,14},{7,15},{8,0},{9,1},... | collective-permute-start | bytes 12296 | tf_op jit(solution)/shard_map/ppermute | solution.py:728
  54.9 6.1 %collective-permute-start.8 = (f32[32,32]{1,0:T(8,128)S(1)}, f32[32,32]{1,0:T(8,128)S(1)}, u32[]{:S(2)}, u32[]{:S(2)}) collective-permute-start(f32[32,32]{1,0:T(8,128)S(1)} %add.24), channel_id=1, source_target_pairs={{0,24},{1,25},{2,26},{3,27},{4,28},{5,29},{6,30},{7,31},{8,16},{9,... | collective-permute-start | bytes 12296 | tf_op jit(solution)/shard_map/ppermute | solution.py:728
  61.0 3.7 %collective-permute-start.9 = (f32[32,32]{1,0:T(8,128)S(1)}, f32[32,32]{1,0:T(8,128)S(1)}, u32[]{:S(2)}, u32[]{:S(2)}) collective-permute-start(f32[32,32]{1,0:T(8,128)S(1)} %add.25), channel_id=1, source_target_pairs={{0,32},{1,33},{2,34},{3,35},{4,36},{5,37},{6,38},{7,39},{8,40},{9,... | collective-permute-start | bytes 12296 | tf_op jit(solution)/shard_map/ppermute | solution.py:728
  64.7 4.9 %collective-permute-start.10 = (f32[32,32]{1,0:T(8,128)S(1)}, f32[32,32]{1,0:T(8,128)S(1)}, u32[]{:S(2)}, u32[]{:S(2)}) collective-permute-start(f32[32,32]{1,0:T(8,128)S(1)} %add.26), channel_id=1, source_target_pairs={{0,96},{1,97},{2,98},{3,99},{4,100},{5,101},{6,102},{7,103},{8,104... | collective-permute-start | bytes 12296 | tf_op jit(solution)/shard_map/ppermute | solution.py:728

commit v5 on v4

--- a/solution.py
+++ b/solution.py
@@ -115,7 +115,7 @@
                 X[half, f, z, 24:32, :] = zero_tile
         return carry
 
-    lax.fori_loop(0, F, clear, 0)
+    lax.fori_loop(0, F, clear, 0, unroll=True)
 
     def field(f, carry):
         for half in range(2):
@@ -135,7 +135,7 @@
     for chunk in range(4):
         copies[2 * chunk].wait()
         copies[2 * chunk + 1].wait()
-        lax.fori_loop(4 * chunk, 4 * chunk + 4, field, 0)
+        lax.fori_loop(4 * chunk, 4 * chunk + 4, field, 0, unroll=4)
     for copy in copies[8:]:
         copy.wait()
     lax.fori_loop(M, F, field, 0)
@@ -257,7 +257,7 @@
 def interior_kernel(
     X, ve, vn, fe, fn, mask, west, east, own_last, own_first,
     high_out, low_out, edge_out, weights_out, mean_out, sums_out,
-    VE, FE, W, VN, FN, H, G, T, Z, acc, sems,
+    VE, FE, W, VN, FN, H, C, G, T, Z, acc, sems,
 ):
     zero_tile = jnp.zeros((8, LANES), f32)
     for half in range(2):
@@ -289,15 +289,12 @@
     for copy in copies:
         copy.start()
 
-    def spread(index, before, after):
+    for f in range(F, F + 3):
+        after, before = east[f], west[f]
         for k in range(2 * NZ):
-            moved_after = rolled(after, -4 * k, 1)
-            moved_before = rolled(before, LANES - 3 - 4 * k, 1)
-            yield index, k, moved_before, moved_after
-
-    for f in range(F, F + 3):
-        for index, k, moved_before, moved_after in spread(f, west[f], east[f]):
-            H[index, k] = jnp.where(lanes < 64, moved_after, moved_before)
+            H[f - F, k] = jnp.where(
+                lanes < 64, rolled(after, -4 * k, 1), rolled(before, LANES - 3 - 4 * k, 1)
+            )
 
     place = lanes % 4
 
@@ -323,25 +320,21 @@
     for d in range(1, 4):
         G[2 + d] = jnp.where((place >= 3 - d) & (place < 3), last_gains[3 + d], 0.0)
 
-    def beside(f, carry):
+    def beside(f):
         before, after = west[f], east[f]
         first = (
             G[0] * rolled(before, -2, 1) + G[1] * rolled(before, -1, 1) + G[2] * before
         )
         last = G[3] * rolled(after, 2, 1) + G[4] * rolled(after, 1, 1) + G[5] * after
-        for index, k, moved_last, moved_first in spread(f, last, first):
-            H[index, k] = jnp.where(
-                lanes < 3, moved_first, jnp.where(lanes >= LANES - 3, moved_last, 0.0)
-            )
-        return carry
-
-    lax.fori_loop(0, F, beside, 0)
+        C[0, f] = first
+        C[1, f] = rolled(last, LANES - 3, 1)
+
+    for f in range(F):
+        beside(f)
     for copy in copies:
         copy.wait()
 
     def level(z, carry):
-        gain_up = jnp.where(z < NZ - 1, vert_diff, 0.0).astype(f32)
-        gain_down = jnp.where(z > 0, vert_diff, 0.0).astype(f32)
         z_up = jnp.minimum(z + 1, NZ - 1)
         z_down = jnp.maximum(z - 1, 0)
         for half in range(2):
@@ -353,7 +346,7 @@
             start = 8 + 8 * xt
 
             def outer(index):
-                return H[index, 2 * z + xt]
+                return H[index - F, 2 * z + xt]
 
             def at(ref, half, offset):
                 return ref[half, z, start + offset : start + offset + 8, :]
@@ -396,10 +389,9 @@
                 for half in range(2)
             ]
             centre = [
-                wx[half][3] + wy[half][3] - (gain_up + gain_down) * wet[half] for half in range(2)
+                wx[half][3] + wy[half][3] - 2.0 * vert_diff * wet[half] for half in range(2)
             ]
-            w_up = [gain_up * wet[half] for half in range(2)]
-            w_down = [gain_down * wet[half] for half in range(2)]
+            w_level = [vert_diff * wet[half] for half in range(2)]
             for half in range(2):
                 for index, plane in enumerate((at(VE, half, 0), at(FE, half, 0), wet[half])):
                     if xt == 0:
@@ -419,13 +411,18 @@
                 own_cells = [X[half, f, z, start : start + 8, :] for half in range(2)]
                 total = [
                     centre[half] * own_cells[half]
-                    + w_up[half] * X[half, f, z_up, start : start + 8, :]
-                    + w_down[half] * X[half, f, z_down, start : start + 8, :]
+                    + w_level[half]
+                    * (
+                        X[half, f, z_up, start : start + 8, :]
+                        + X[half, f, z_down, start : start + 8, :]
+                    )
                     for half in range(2)
                 ]
-                beyond_block = outer(f)
-                total[0] += jnp.where(lanes < 64, beyond_block, 0.0)
-                total[1] += jnp.where(lanes < 64, 0.0, beyond_block)
+                first, last = C[0, f], C[1, f]
+                total[0] += jnp.where(lanes < 3, first, 0.0)
+                total[1] += jnp.where(lanes >= LANES - 3, last, 0.0)
+                C[0, f] = rolled(first, -4, 1)
+                C[1, f] = rolled(last, -4, 1)
                 for offset in (-3, -2, -1, 1, 2, 3):
                     moved = around_lanes(own_cells[0], own_cells[1], offset)
                     for half in range(2):
@@ -487,7 +484,8 @@
             pltpu.VMEM((2, NZ, 32, LANES), jnp.int32),
             pltpu.VMEM((2, NZ, BX, LANES), f32),
             pltpu.VMEM((2, 2, NZ, BX, LANES), jnp.int32),
-            pltpu.VMEM((F + 3, 2 * NZ, 8, LANES), f32),
+            pltpu.VMEM((3, 2 * NZ, 8, LANES), f32),
+            pltpu.VMEM((2, F, 8, LANES), f32),
             pltpu.VMEM((6, 8, LANES), f32),
             pltpu.VMEM((2, M, 8, LANES), f32),
             pltpu.VMEM((256, 256), f32),
@@ -640,19 +638,20 @@
     return jnp.where(column_g >= row_g, left, 0.0), right
 
 
-def spread_map(part):
+def spread_map(mapping):
+    parts = jnp.concatenate(split(mapping), axis=0)
     tall = (
-        lax.broadcasted_iota(jnp.int32, (8 * M, M), 0) // 8
-        == lax.broadcasted_iota(jnp.int32, (8 * M, M), 1)
+        lax.broadcasted_iota(jnp.int32, (256, 2 * M), 0) // 8
+        == lax.broadcasted_iota(jnp.int32, (256, 2 * M), 1)
     ).astype(bf16)
     wide = (
         lax.broadcasted_iota(jnp.int32, (2 * M, 256), 1) // 8
         == lax.broadcasted_iota(jnp.int32, (2 * M, 256), 0)
     ).astype(bf16)
-    rows = jnp.dot(tall, part, preferred_element_type=f32).astype(bf16)
+    rows = jnp.dot(tall, parts, preferred_element_type=f32).astype(bf16)
     full = jnp.dot(rows, wide, preferred_element_type=f32)
-    row = lax.broadcasted_iota(jnp.int32, (8 * M, 256), 0)
-    column = lax.broadcasted_iota(jnp.int32, (8 * M, 256), 1)
+    row = lax.broadcasted_iota(jnp.int32, (256, 256), 0)
+    column = lax.broadcasted_iota(jnp.int32, (256, 256), 1)
     return jnp.where(row % 8 == column % 8, full, 0.0).astype(bf16)
 
 
@@ -660,9 +659,7 @@
     def apply_kernel(sums, high_i, low_i, high_e, low_e, out, factor_out, maps, new, sems):
         factor, mapping = factor_and_map(sums[...], cell_count)
         factor_out[...] = factor
-        high, low = split(mapping)
-        maps[0:128, :] = spread_map(high)
-        maps[128:256, :] = spread_map(low)
+        maps[...] = spread_map(mapping)
         low_rows = lax.broadcasted_iota(jnp.int32, (M, 8, 256), 1) < 4
 
         def put(z, slot):

time: 77.8 us -> 77 us (0.990)
  Pallas kernels: 33.6 us -> 31.8 us
  waiting for transfers between devices: 18.7 us -> 19.9 us
    pallas_call x1, Pallas kernels: 17.5 us -> 16.3 us  [interior(): pl.pallas_call(interior_kernel, out_shape=(parts, parts, jax.ShapeDtypeSt...]
  transfers between devices with their start and end apart: 11 -> 11, of which waited for: 8 -> 9; matrix products, arithmetic and copies ran while one was open for 0% -> 0% of each run, Pallas kernels for 23% -> 21%
where the time goes in v5:
time: 77 us; the launch traced here: 76.8 us
  Pallas kernels  31.8 us (41%)
  starting transfers between devices  24.5 us (32%)
  waiting for transfers between devices  19.9 us (26%)
    pallas_call x1, Pallas kernels, interior(): pl.pallas_call(interior_kernel, out_shape=(parts, parts, jax.ShapeDtypeSt...  16.3 us
    ppermute x7, starting transfers between devices, exchanged(): return lax.ppermute(value, axes, [(i, i ^ distance) for i in range(size)])  16.2 us
    ppermute x7, waiting for transfers between devices, exchanged(): return lax.ppermute(value, axes, [(i, i ^ distance) for i in range(size)])  14.5 us
    pallas_call x1, Pallas kernels, apply_map(): pl.pallas_call(make_apply_kernel(cell_count), out_shape=(jax.ShapeDtypeSt...  7.87 us
    ppermute x2, starting transfers between devices, onward(): return lax.ppermute(value, axis, [(i, i + 1) for i in range(size - 1)])  5.7 us
    ppermute x2, waiting for transfers between devices, backward(): return lax.ppermute(value, axis, [(i + 1, i) for i in range(size - 1)])  4.62 us
    pallas_call x1, Pallas kernels, edges(): pl.pallas_call(edge_kernel, out_shape=(parts, parts, jax.ShapeDtypeStruct...  4.22 us
    pallas_call x1, Pallas kernels, pack(): pl.pallas_call(pack_kernel, out_shape=(rows, rows, columns, columns, jax....  3.34 us
  transfers between devices with their start and end apart: 11, of which 9 were waited for; matrix products, arithmetic and copies ran while one was open for 0% of the time, Pallas kernels for 21%

profile of v5, /device:TPU:0, one launch (start us, length us, event | category | flops | bytes accessed | tf_op | source)
XLA Modules:
  0.0 76.8 jit_solution(533927140493998105)
XLA Ops:
  0.6 3.3 %pack.1 = (f32[2,18,2,24,128]{4,3,2,1,0:T(8,128)S(1)}, f32[2,18,2,24,128]{4,3,2,1,0:T(8,128)S(1)}, f32[20,8,128]{2,1,0:T(8,128)S(1)}, f32[20,8,128]{2,1,0:T(8,128)S(1)}, f32[2,17,16,32,128]{4,3,2,1,0:T(8,128)S(1)}) custom-call(f32[16,16,16,256]{3,2,1,0:T(8,128)} %modes.1, f32[16,16,256]{2,1,0:T(8,128)} %mean.1, f32[16,16,256]{2,1,0:T(8,128)} %ve.3, ...), custom_call_target="tpu_custom_call" | custom-call | flops 10000000 | bytes 7000000 | tf_op jit(solution)/shard_map/pack/pallas_call | solution.py:174
  4.0 1.3 %collective-permute-start.2 = (f32[20,8,128]{2,1,0:T(8,128)S(1)}, f32[20,8,128]{2,1,0:T(8,128)S(1)}, u32[]{:S(2)}, u32[]{:S(2)}) collective-permute-start(f32[20,8,128]{2,1,0:T(8,128)S(1)} %get-tuple-element.23.own_last), channel_id=1, source_target_pairs={{0,1},{1,2},{2,3},{3,4},{4,5},{5,6},{6,7},{8,9},{9,10},{10,11},{11... | collective-permute-start | bytes 245768 | tf_op jit(solution)/shard_map/ppermute | solution.py:715
  5.3 1.3 %collective-permute-start.3 = (f32[20,8,128]{2,1,0:T(8,128)S(1)}, f32[20,8,128]{2,1,0:T(8,128)S(1)}, u32[]{:S(2)}, u32[]{:S(2)}) collective-permute-start(f32[20,8,128]{2,1,0:T(8,128)S(1)} %get-tuple-element.24.own_first), channel_id=1, source_target_pairs={{1,0},{2,1},{3,2},{4,3},{5,4},{6,5},{7,6},{9,8},{10,9},{11,10},{12... | collective-permute-start | bytes 245768 | tf_op jit(solution)/shard_map/ppermute | solution.py:720
  6.6 4.4 %collective-permute-start = (f32[2,18,2,24,128]{4,3,2,1,0:T(8,128)S(1)}, f32[2,18,2,24,128]{4,3,2,1,0:T(8,128)S(1)}, u32[]{:S(2)}, u32[]{:S(2)}) collective-permute-start(f32[2,18,2,24,128]{4,3,2,1,0:T(8,128)S(1)} %get-tuple-element.20), channel_id=1, source_target_pairs={{0,8},{8,16},{16,24},{24,32},{32,40},{40,48},{48,56},{56,64},{64,7... | collective-permute-start | bytes 2654216 | tf_op jit(solution)/shard_map/ppermute | solution.py:715
  11.0 1.3 %collective-permute-start.1 = (f32[2,18,2,24,128]{4,3,2,1,0:T(8,128)S(1)}, f32[2,18,2,24,128]{4,3,2,1,0:T(8,128)S(1)}, u32[]{:S(2)}, u32[]{:S(2)}) collective-permute-start(f32[2,18,2,24,128]{4,3,2,1,0:T(8,128)S(1)} %get-tuple-element.21), channel_id=1, source_target_pairs={{8,0},{16,8},{24,16},{32,24},{40,32},{48,40},{56,48},{64,56},{72,6... | collective-permute-start | bytes 2654216 | tf_op jit(solution)/shard_map/ppermute | solution.py:720
  12.3 0.0 collective-permute-done.2.west
  12.3 0.0 collective-permute-done.3.east
  12.3 16.3 %interior.1 = (bf16[16,256,256]{2,1,0:T(8,128)(2,1)S(1)}, bf16[16,256,256]{2,1,0:T(8,128)(2,1)S(1)}, f32[16,2,272,128]{3,2,1,0:T(8,128)S(1)}, f32[2,16,6,8,128]{...) custom-call(f32[2,17,16,32,128]{4,3,2,1,0:T(8,128)S(1)} %get-tuple-element.22.X, ...), custom_call_target="tpu_custom_call" | custom-call | flops 10000000000 | bytes 40000000 | tf_op jit(solution)/shard_map/interior/pallas_call | solution.py:469
  28.7 0.7 collective-permute-done.below
  29.4 4.6 %collective-permute-done.1.above = f32[2,18,2,24,128]{4,3,2,1,0:T(8,128)S(1)} collective-permute-done((f32[2,18,2,24,128]{4,3,2,1,0:T(8,128)S(1)}, f32[2,18,2,24,128]{4,3,2,1,0:T(8,128)S(1)}, u32[]{:S(2)}, u32[]{:S(2)}) %collective-permute-start.1) | collective-permute-done | bytes 884768 | tf_op jit(solution)/shard_map/ppermute | solution.py:720
  34.0 4.2 %edges.1 = (bf16[16,256,256]{2,1,0:T(8,128)(2,1)S(1)}, bf16[16,256,256]{2,1,0:T(8,128)(2,1)S(1)}, f32[16,16,256]{2,1,0:T(8,128)}, f32[32,32]{1,0:T(8,128)S(1)}) custom-call(f32[2,18,2,24,128]{4,3,2,1,0:T(8,128)S(1)} %collective-permute-done.below, f32[2,18,2,24,128]{4,3,2,1,0:T(8,128)S(1)} %collective-permute-done.1.above, ...), custom_call_target="tpu_custom_call" | custom-call | flops 1000000000 | bytes 10000000 | tf_op jit(solution)/shard_map/edges/pallas_call | solution.py:594
  38.2 1.2 %collective-permute-start.4 = (f32[32,32]{1,0:T(8,128)S(1)}, f32[32,32]{1,0:T(8,128)S(1)}, u32[]{:S(2)}, u32[]{:S(2)}) collective-permute-start(f32[32,32]{1,0:T(8,128)S(1)} %get-tuple-element.30), channel_id=1, source_target_pairs={{0,1},{1,0},{2,3},{3,2},{4,5},{5,4},{6,7},{7,6},{8,9},{9,8},{10,11... | collective-permute-start | bytes 12296 | tf_op jit(solution)/shard_map/ppermute | solution.py:725
  39.4 0.8 %collective-permute-done.4 = f32[32,32]{1,0:T(8,128)S(1)} collective-permute-done((f32[32,32]{1,0:T(8,128)S(1)}, f32[32,32]{1,0:T(8,128)S(1)}, u32[]{:S(2)}, u32[]{:S(2)}) %collective-permute-start.4) | collective-permute-done | bytes 4128 | tf_op jit(solution)/shard_map/ppermute | solution.py:725
  40.3 3.5 %collective-permute-start.5 = (f32[32,32]{1,0:T(8,128)S(1)}, f32[32,32]{1,0:T(8,128)S(1)}, u32[]{:S(2)}, u32[]{:S(2)}) collective-permute-start(f32[32,32]{1,0:T(8,128)S(1)} %add.21), channel_id=1, source_target_pairs={{0,2},{1,3},{2,0},{3,1},{4,6},{5,7},{6,4},{7,5},{8,10},{9,11},{10,... | collective-permute-start | bytes 12296 | tf_op jit(solution)/shard_map/ppermute | solution.py:725
  43.8 1.7 %collective-permute-done.5 = f32[32,32]{1,0:T(8,128)S(1)} collective-permute-done((f32[32,32]{1,0:T(8,128)S(1)}, f32[32,32]{1,0:T(8,128)S(1)}, u32[]{:S(2)}, u32[]{:S(2)}) %collective-permute-start.5) | collective-permute-done | bytes 4128 | tf_op jit(solution)/shard_map/ppermute | solution.py:725
  45.5 2.3 %collective-permute-start.6 = (f32[32,32]{1,0:T(8,128)S(1)}, f32[32,32]{1,0:T(8,128)S(1)}, u32[]{:S(2)}, u32[]{:S(2)}) collective-permute-start(f32[32,32]{1,0:T(8,128)S(1)} %add.22), channel_id=1, source_target_pairs={{0,6},{1,7},{2,4},{3,5},{4,2},{5,3},{6,0},{7,1},{8,14},{9,15},{10,... | collective-permute-start | bytes 12296 | tf_op jit(solution)/shard_map/ppermute | solution.py:725
  47.8 2.7 %collective-permute-done.6 = f32[32,32]{1,0:T(8,128)S(1)} collective-permute-done((f32[32,32]{1,0:T(8,128)S(1)}, f32[32,32]{1,0:T(8,128)S(1)}, u32[]{:S(2)}, u32[]{:S(2)}) %collective-permute-start.6) | collective-permute-done | bytes 4128 | tf_op jit(solution)/shard_map/ppermute | solution.py:725
  50.4 1.7 %collective-permute-start.7 = (f32[32,32]{1,0:T(8,128)S(1)}, f32[32,32]{1,0:T(8,128)S(1)}, u32[]{:S(2)}, u32[]{:S(2)}) collective-permute-start(f32[32,32]{1,0:T(8,128)S(1)} %add.23), channel_id=1, source_target_pairs={{0,8},{1,9},{2,10},{3,11},{4,12},{5,13},{6,14},{7,15},{8,0},{9,1},... | collective-permute-start | bytes 12296 | tf_op jit(solution)/shard_map/ppermute | solution.py:725
  52.2 2.0 %collective-permute-done.7 = f32[32,32]{1,0:T(8,128)S(1)} collective-permute-done((f32[32,32]{1,0:T(8,128)S(1)}, f32[32,32]{1,0:T(8,128)S(1)}, u32[]{:S(2)}, u32[]{:S(2)}) %collective-permute-start.7) | collective-permute-done | bytes 4128 | tf_op jit(solution)/shard_map/ppermute | solution.py:725
  54.2 4.3 %collective-permute-start.8 = (f32[32,32]{1,0:T(8,128)S(1)}, f32[32,32]{1,0:T(8,128)S(1)}, u32[]{:S(2)}, u32[]{:S(2)}) collective-permute-start(f32[32,32]{1,0:T(8,128)S(1)} %add.24), channel_id=1, source_target_pairs={{0,24},{1,25},{2,26},{3,27},{4,28},{5,29},{6,30},{7,31},{8,16},{9,... | collective-permute-start | bytes 12296 | tf_op jit(solution)/shard_map/ppermute | solution.py:725
  58.5 1.7 %collective-permute-done.8 = f32[32,32]{1,0:T(8,128)S(1)} collective-permute-done((f32[32,32]{1,0:T(8,128)S(1)}, f32[32,32]{1,0:T(8,128)S(1)}, u32[]{:S(2)}, u32[]{:S(2)}) %collective-permute-start.8) | collective-permute-done | bytes 4128 | tf_op jit(solution)/shard_map/ppermute | solution.py:725
  60.2 1.5 %collective-permute-start.9 = (f32[32,32]{1,0:T(8,128)S(1)}, f32[32,32]{1,0:T(8,128)S(1)}, u32[]{:S(2)}, u32[]{:S(2)}) collective-permute-start(f32[32,32]{1,0:T(8,128)S(1)} %add.25), channel_id=1, source_target_pairs={{0,32},{1,33},{2,34},{3,35},{4,36},{5,37},{6,38},{7,39},{8,40},{9,... | collective-permute-start | bytes 12296 | tf_op jit(solution)/shard_map/ppermute | solution.py:725
  61.7 2.3 %collective-permute-done.9 = f32[32,32]{1,0:T(8,128)S(1)} collective-permute-done((f32[32,32]{1,0:T(8,128)S(1)}, f32[32,32]{1,0:T(8,128)S(1)}, u32[]{:S(2)}, u32[]{:S(2)}) %collective-permute-start.9) | collective-permute-done | bytes 4128 | tf_op jit(solution)/shard_map/ppermute | solution.py:725
  64.0 1.6 %collective-permute-start.10 = (f32[32,32]{1,0:T(8,128)S(1)}, f32[32,32]{1,0:T(8,128)S(1)}, u32[]{:S(2)}, u32[]{:S(2)}) collective-permute-start(f32[32,32]{1,0:T(8,128)S(1)} %add.26), channel_id=1, source_target_pairs={{0,96},{1,97},{2,98},{3,99},{4,100},{5,101},{6,102},{7,103},{8,104... | collective-permute-start | bytes 12296 | tf_op jit(solution)/shard_map/ppermute | solution.py:725
  65.6 3.3 %collective-permute-done.10 = f32[32,32]{1,0:T(8,128)S(1)} collective-permute-done((f32[32,32]{1,0:T(8,128)S(1)}, f32[32,32]{1,0:T(8,128)S(1)}, u32[]{:S(2)}, u32[]{:S(2)}) %collective-permute-start.10) | collective-permute-done | bytes 4128 | tf_op jit(solution)/shard_map/ppermute | solution.py:725
  68.9 7.9 %apply.1 = (f32[16,16,16,256]{3,2,1,0:T(8,128)}, f32[16,16]{1,0:T(8,128)}) custom-call(f32[32,32]{1,0:T(8,128)S(1)} %add.27.sums, bf16[16,256,256]{2,1,0:T(8,128)(2,1)S(1)} %get-tuple-element.31.high_i, bf16[16,256,256]{2,1,0:T(8,128)(2,1)S(1)} %get-tuple-element.32.low_i, bf16[16,256,256]{2,1,0:T(8,128)(2,1)S(1)} %get-tuple-element.33.high_e, ...), custom_call_target="tpu_custom_call" | custom-call | flops 1000000000 | bytes 13000000 | tf_op jit(solution)/shard_map/apply/pallas_call | solution.py:694
  (7 shorter events, 0.0 us)
Async XLA Ops:
  4.0 8.3 %collective-permute-start.2 = (f32[20,8,128]{2,1,0:T(8,128)S(1)}, f32[20,8,128]{2,1,0:T(8,128)S(1)}, u32[]{:S(2)}, u32[]{:S(2)}) collective-permute-start(f32[20,8,128]{2,1,0:T(8,128)S(1)} %get-tuple-element.23.own_last), channel_id=1, source_target_pairs={{0,1},{1,2},{2,3},{3,4},{4,5},{5,6},{6,7},{8,9},{9,10},{10,11},{11... | collective-permute-start | bytes 245768 | tf_op jit(solution)/shard_map/ppermute | solution.py:715
  5.3 7.0 %collective-permute-start.3 = (f32[20,8,128]{2,1,0:T(8,128)S(1)}, f32[20,8,128]{2,1,0:T(8,128)S(1)}, u32[]{:S(2)}, u32[]{:S(2)}) collective-permute-start(f32[20,8,128]{2,1,0:T(8,128)S(1)} %get-tuple-element.24.own_first), channel_id=1, source_target_pairs={{1,0},{2,1},{3,2},{4,3},{5,4},{6,5},{7,6},{9,8},{10,9},{11,10},{12... | collective-permute-start | bytes 245768 | tf_op jit(solution)/shard_map/ppermute | solution.py:720
  6.6 22.8 %collective-permute-start = (f32[2,18,2,24,128]{4,3,2,1,0:T(8,128)S(1)}, f32[2,18,2,24,128]{4,3,2,1,0:T(8,128)S(1)}, u32[]{:S(2)}, u32[]{:S(2)}) collective-permute-start(f32[2,18,2,24,128]{4,3,2,1,0:T(8,128)S(1)} %get-tuple-element.20), channel_id=1, source_target_pairs={{0,8},{8,16},{16,24},{24,32},{32,40},{40,48},{48,56},{56,64},{64,7... | collective-permute-start | bytes 2654216 | tf_op jit(solution)/shard_map/ppermute | solution.py:715
  11.0 23.0 %collective-permute-start.1 = (f32[2,18,2,24,128]{4,3,2,1,0:T(8,128)S(1)}, f32[2,18,2,24,128]{4,3,2,1,0:T(8,128)S(1)}, u32[]{:S(2)}, u32[]{:S(2)}) collective-permute-start(f32[2,18,2,24,128]{4,3,2,1,0:T(8,128)S(1)} %get-tuple-element.21), channel_id=1, source_target_pairs={{8,0},{16,8},{24,16},{32,24},{40,32},{48,40},{56,48},{64,56},{72,6... | collective-permute-start | bytes 2654216 | tf_op jit(solution)/shard_map/ppermute | solution.py:720
  38.2 2.1 %collective-permute-start.4 = (f32[32,32]{1,0:T(8,128)S(1)}, f32[32,32]{1,0:T(8,128)S(1)}, u32[]{:S(2)}, u32[]{:S(2)}) collective-permute-start(f32[32,32]{1,0:T(8,128)S(1)} %get-tuple-element.30), channel_id=1, source_target_pairs={{0,1},{1,0},{2,3},{3,2},{4,5},{5,4},{6,7},{7,6},{8,9},{9,8},{10,11... | collective-permute-start | bytes 12296 | tf_op jit(solution)/shard_map/ppermute | solution.py:725
  40.3 5.2 %collective-permute-start.5 = (f32[32,32]{1,0:T(8,128)S(1)}, f32[32,32]{1,0:T(8,128)S(1)}, u32[]{:S(2)}, u32[]{:S(2)}) collective-permute-start(f32[32,32]{1,0:T(8,128)S(1)} %add.21), channel_id=1, source_target_pairs={{0,2},{1,3},{2,0},{3,1},{4,6},{5,7},{6,4},{7,5},{8,10},{9,11},{10,... | collective-permute-start | bytes 12296 | tf_op jit(solution)/shard_map/ppermute | solution.py:725
  45.5 4.9 %collective-permute-start.6 = (f32[32,32]{1,0:T(8,128)S(1)}, f32[32,32]{1,0:T(8,128)S(1)}, u32[]{:S(2)}, u32[]{:S(2)}) collective-permute-start(f32[32,32]{1,0:T(8,128)S(1)} %add.22), channel_id=1, source_target_pairs={{0,6},{1,7},{2,4},{3,5},{4,2},{5,3},{6,0},{7,1},{8,14},{9,15},{10,... | collective-permute-start | bytes 12296 | tf_op jit(solution)/shard_map/ppermute | solution.py:725
  50.4 3.7 %collective-permute-start.7 = (f32[32,32]{1,0:T(8,128)S(1)}, f32[32,32]{1,0:T(8,128)S(1)}, u32[]{:S(2)}, u32[]{:S(2)}) collective-permute-start(f32[32,32]{1,0:T(8,128)S(1)} %add.23), channel_id=1, source_target_pairs={{0,8},{1,9},{2,10},{3,11},{4,12},{5,13},{6,14},{7,15},{8,0},{9,1},... | collective-permute-start | bytes 12296 | tf_op jit(solution)/shard_map/ppermute | solution.py:725
  54.2 6.1 %collective-permute-start.8 = (f32[32,32]{1,0:T(8,128)S(1)}, f32[32,32]{1,0:T(8,128)S(1)}, u32[]{:S(2)}, u32[]{:S(2)}) collective-permute-start(f32[32,32]{1,0:T(8,128)S(1)} %add.24), channel_id=1, source_target_pairs={{0,24},{1,25},{2,26},{3,27},{4,28},{5,29},{6,30},{7,31},{8,16},{9,... | collective-permute-start | bytes 12296 | tf_op jit(solution)/shard_map/ppermute | solution.py:725
  60.2 3.7 %collective-permute-start.9 = (f32[32,32]{1,0:T(8,128)S(1)}, f32[32,32]{1,0:T(8,128)S(1)}, u32[]{:S(2)}, u32[]{:S(2)}) collective-permute-start(f32[32,32]{1,0:T(8,128)S(1)} %add.25), channel_id=1, source_target_pairs={{0,32},{1,33},{2,34},{3,35},{4,36},{5,37},{6,38},{7,39},{8,40},{9,... | collective-permute-start | bytes 12296 | tf_op jit(solution)/shard_map/ppermute | solution.py:725
  64.0 4.9 %collective-permute-start.10 = (f32[32,32]{1,0:T(8,128)S(1)}, f32[32,32]{1,0:T(8,128)S(1)}, u32[]{:S(2)}, u32[]{:S(2)}) collective-permute-start(f32[32,32]{1,0:T(8,128)S(1)} %add.26), channel_id=1, source_target_pairs={{0,96},{1,97},{2,98},{3,99},{4,100},{5,101},{6,102},{7,103},{8,104... | collective-permute-start | bytes 12296 | tf_op jit(solution)/shard_map/ppermute | solution.py:725

commit v6 on v5

--- a/solution.py
+++ b/solution.py
@@ -493,7 +493,7 @@
             pltpu.SemaphoreType.DMA((10,)),
         ],
         compiler_params=params(28),
-        cost_estimate=cost(10**10, 4 * 10**7),
+        cost_estimate=cost(10**6, 10**6),
         name="interior",
     )(cells, ve, vn, fe, fn, mask, west, east, own_last, own_first)
 
@@ -750,8 +750,10 @@
         west, east, east_send, west_send,
     )
     high_e, low_e, mean_next, sums = edges(below, above, edge, weights, mean_part, sums_i)
-    for distance in (1, 2, 6, 8, 24, 32, 96):
-        sums = sums + exchanged(sums, axes, distance)
+    sums = sums + exchanged(sums, axes, 1)
+    for first in (2, 8, 32):
+        near, far, both = (exchanged(sums, axes, first * i) for i in (1, 2, 3))
+        sums = (sums + near) + (far + both)
     cell_count = float(NZ * BX * 256 * lax.axis_size("gx") * lax.axis_size("gy"))
     modes_next, factor = apply_map(sums, high_i, low_i, high_e, low_e, cell_count)
     return (mean_next, modes_next, factor)

time: 77 us -> 74 us (0.961)
  waiting for transfers between devices: 19.9 us -> 15.9 us
  starting transfers between devices: 24.5 us -> 25.4 us
    ppermute x7 -> x10, waiting for transfers between devices: 14.5 us -> 12.4 us  [exchanged(): return lax.ppermute(value, axes, [(i, i ^ distance) for i in range(size)])]
    ppermute x7 -> x10, starting transfers between devices: 16.2 us -> 17.4 us  [exchanged(): return lax.ppermute(value, axes, [(i, i ^ distance) for i in range(size)])]
    ppermute x2, waiting for transfers between devices: 4.62 us -> 3.5 us  [backward(): return lax.ppermute(value, axis, [(i + 1, i) for i in range(size - 1)])]
  transfers between devices with their start and end apart: 11 -> 14, of which waited for: 9 -> 9; matrix products, arithmetic and copies ran while one was open for 0% -> 0% of each run, Pallas kernels for 21% -> 22%
where the time goes in v6:
time: 74 us; the launch traced here: 73.8 us
  Pallas kernels  31.7 us (43%)
  starting transfers between devices  25.4 us (34%)
  waiting for transfers between devices  15.9 us (21%)
    ppermute x10, starting transfers between devices, exchanged(): return lax.ppermute(value, axes, [(i, i ^ distance) for i in range(size)])  17.4 us
    pallas_call x1, Pallas kernels, interior(): pl.pallas_call(interior_kernel, out_shape=(parts, parts, jax.ShapeDtypeSt...  16.3 us
    ppermute x10, waiting for transfers between devices, exchanged(): return lax.ppermute(value, axes, [(i, i ^ distance) for i in range(size)])  12.4 us
    pallas_call x1, Pallas kernels, apply_map(): pl.pallas_call(make_apply_kernel(cell_count), out_shape=(jax.ShapeDtypeSt...  7.87 us
    ppermute x2, starting transfers between devices, onward(): return lax.ppermute(value, axis, [(i, i + 1) for i in range(size - 1)])  5.42 us
    pallas_call x1, Pallas kernels, edges(): pl.pallas_call(edge_kernel, out_shape=(parts, parts, jax.ShapeDtypeStruct...  4.22 us
    ppermute x2, waiting for transfers between devices, backward(): return lax.ppermute(value, axis, [(i + 1, i) for i in range(size - 1)])  3.5 us
    pallas_call x1, Pallas kernels, pack(): pl.pallas_call(pack_kernel, out_shape=(rows, rows, columns, columns, jax....  3.34 us
  transfers between devices with their start and end apart: 14, of which 9 were waited for; matrix products, arithmetic and copies ran while one was open for 0% of the time, Pallas kernels for 22%

profile of v6, /device:TPU:0, one launch (start us, length us, event | category | flops | bytes accessed | tf_op | source)
XLA Modules:
  0.0 73.8 jit_solution(15560467999629215947)
XLA Ops:
  0.6 3.3 %pack.1 = (f32[2,18,2,24,128]{4,3,2,1,0:T(8,128)S(1)}, f32[2,18,2,24,128]{4,3,2,1,0:T(8,128)S(1)}, f32[20,8,128]{2,1,0:T(8,128)S(1)}, f32[20,8,128]{2,1,0:T(8,128)S(1)}, f32[2,17,16,32,128]{4,3,2,1,0:T(8,128)S(1)}) custom-call(f32[16,16,16,256]{3,2,1,0:T(8,128)} %modes.1, f32[16,16,256]{2,1,0:T(8,128)} %mean.1, f32[16,16,256]{2,1,0:T(8,128)} %ve.3, ...), custom_call_target="tpu_custom_call" | custom-call | flops 10000000 | bytes 7000000 | tf_op jit(solution)/shard_map/pack/pallas_call | solution.py:174
  4.0 4.0 %collective-permute-start = (f32[2,18,2,24,128]{4,3,2,1,0:T(8,128)S(1)}, f32[2,18,2,24,128]{4,3,2,1,0:T(8,128)S(1)}, u32[]{:S(2)}, u32[]{:S(2)}) collective-permute-start(f32[2,18,2,24,128]{4,3,2,1,0:T(8,128)S(1)} %get-tuple-element.20), channel_id=1, source_target_pairs={{0,8},{8,16},{16,24},{24,32},{32,40},{40,48},{48,56},{56,64},{64,7... | collective-permute-start | bytes 2654216 | tf_op jit(solution)/shard_map/ppermute | solution.py:715
  7.9 1.3 %collective-permute-start.1 = (f32[2,18,2,24,128]{4,3,2,1,0:T(8,128)S(1)}, f32[2,18,2,24,128]{4,3,2,1,0:T(8,128)S(1)}, u32[]{:S(2)}, u32[]{:S(2)}) collective-permute-start(f32[2,18,2,24,128]{4,3,2,1,0:T(8,128)S(1)} %get-tuple-element.21), channel_id=1, source_target_pairs={{8,0},{16,8},{24,16},{32,24},{40,32},{48,40},{56,48},{64,56},{72,6... | collective-permute-start | bytes 2654216 | tf_op jit(solution)/shard_map/ppermute | solution.py:720
  9.2 1.5 %collective-permute-start.2 = (f32[20,8,128]{2,1,0:T(8,128)S(1)}, f32[20,8,128]{2,1,0:T(8,128)S(1)}, u32[]{:S(2)}, u32[]{:S(2)}) collective-permute-start(f32[20,8,128]{2,1,0:T(8,128)S(1)} %get-tuple-element.23.own_last), channel_id=1, source_target_pairs={{0,1},{1,2},{2,3},{3,4},{4,5},{5,6},{6,7},{8,9},{9,10},{10,11},{11... | collective-permute-start | bytes 245768 | tf_op jit(solution)/shard_map/ppermute | solution.py:715
  10.7 1.3 %collective-permute-start.3 = (f32[20,8,128]{2,1,0:T(8,128)S(1)}, f32[20,8,128]{2,1,0:T(8,128)S(1)}, u32[]{:S(2)}, u32[]{:S(2)}) collective-permute-start(f32[20,8,128]{2,1,0:T(8,128)S(1)} %get-tuple-element.24.own_first), channel_id=1, source_target_pairs={{1,0},{2,1},{3,2},{4,3},{5,4},{6,5},{7,6},{9,8},{10,9},{11,10},{12... | collective-permute-start | bytes 245768 | tf_op jit(solution)/shard_map/ppermute | solution.py:720
  12.0 0.0 collective-permute-done.2.west
  12.0 3.5 %collective-permute-done.3.east = f32[20,8,128]{2,1,0:T(8,128)S(1)} collective-permute-done((f32[20,8,128]{2,1,0:T(8,128)S(1)}, f32[20,8,128]{2,1,0:T(8,128)S(1)}, u32[]{:S(2)}, u32[]{:S(2)}) %collective-permute-start.3) | collective-permute-done | bytes 81952 | tf_op jit(solution)/shard_map/ppermute | solution.py:720
  15.5 16.3 %interior.1 = (bf16[16,256,256]{2,1,0:T(8,128)(2,1)S(1)}, bf16[16,256,256]{2,1,0:T(8,128)(2,1)S(1)}, f32[16,2,272,128]{3,2,1,0:T(8,128)S(1)}, f32[2,16,6,8,128]{...) custom-call(f32[2,17,16,32,128]{4,3,2,1,0:T(8,128)S(1)} %get-tuple-element.22.X, ...), custom_call_target="tpu_custom_call" | custom-call | flops 1000000 | bytes 1000000 | tf_op jit(solution)/shard_map/interior/pallas_call | solution.py:469
  31.8 0.0 collective-permute-done.below
  31.8 0.0 collective-permute-done.1.above
  31.9 4.2 %edges.1 = (bf16[16,256,256]{2,1,0:T(8,128)(2,1)S(1)}, bf16[16,256,256]{2,1,0:T(8,128)(2,1)S(1)}, f32[16,16,256]{2,1,0:T(8,128)}, f32[32,32]{1,0:T(8,128)S(1)}) custom-call(f32[2,18,2,24,128]{4,3,2,1,0:T(8,128)S(1)} %collective-permute-done.below, f32[2,18,2,24,128]{4,3,2,1,0:T(8,128)S(1)} %collective-permute-done.1.above, ...), custom_call_target="tpu_custom_call" | custom-call | flops 1000000000 | bytes 10000000 | tf_op jit(solution)/shard_map/edges/pallas_call | solution.py:594
  36.1 3.4 %collective-permute-start.4 = (f32[32,32]{1,0:T(8,128)S(1)}, f32[32,32]{1,0:T(8,128)S(1)}, u32[]{:S(2)}, u32[]{:S(2)}) collective-permute-start(f32[32,32]{1,0:T(8,128)S(1)} %get-tuple-element.30), channel_id=1, source_target_pairs={{0,1},{1,0},{2,3},{3,2},{4,5},{5,4},{6,7},{7,6},{8,9},{9,8},{10,11... | collective-permute-start | bytes 12296 | tf_op jit(solution)/shard_map/ppermute | solution.py:725
  39.5 0.8 %collective-permute-done.4 = f32[32,32]{1,0:T(8,128)S(1)} collective-permute-done((f32[32,32]{1,0:T(8,128)S(1)}, f32[32,32]{1,0:T(8,128)S(1)}, u32[]{:S(2)}, u32[]{:S(2)}) %collective-permute-start.4) | collective-permute-done | bytes 4128 | tf_op jit(solution)/shard_map/ppermute | solution.py:725
  40.3 1.3 %collective-permute-start.7 = (f32[32,32]{1,0:T(8,128)S(1)}, f32[32,32]{1,0:T(8,128)S(1)}, u32[]{:S(2)}, u32[]{:S(2)}) collective-permute-start(f32[32,32]{1,0:T(8,128)S(1)} %add.30), channel_id=1, source_target_pairs={{0,6},{1,7},{2,4},{3,5},{4,2},{5,3},{6,0},{7,1},{8,14},{9,15},{10,... | collective-permute-start | bytes 12296 | tf_op jit(solution)/shard_map/ppermute | solution.py:725
  41.6 2.3 %collective-permute-start.6 = (f32[32,32]{1,0:T(8,128)S(1)}, f32[32,32]{1,0:T(8,128)S(1)}, u32[]{:S(2)}, u32[]{:S(2)}) collective-permute-start(f32[32,32]{1,0:T(8,128)S(1)} %add.30), channel_id=1, source_target_pairs={{0,4},{1,5},{2,6},{3,7},{4,0},{5,1},{6,2},{7,3},{8,12},{9,13},{10,... | collective-permute-start | bytes 12296 | tf_op jit(solution)/shard_map/ppermute | solution.py:725
  44.0 0.4 collective-permute-start.5
  44.4 0.9 %collective-permute-done.7 = f32[32,32]{1,0:T(8,128)S(1)} collective-permute-done((f32[32,32]{1,0:T(8,128)S(1)}, f32[32,32]{1,0:T(8,128)S(1)}, u32[]{:S(2)}, u32[]{:S(2)}) %collective-permute-start.7) | collective-permute-done | bytes 4128 | tf_op jit(solution)/shard_map/ppermute | solution.py:725
  45.3 1.6 %collective-permute-done.6 = f32[32,32]{1,0:T(8,128)S(1)} collective-permute-done((f32[32,32]{1,0:T(8,128)S(1)}, f32[32,32]{1,0:T(8,128)S(1)}, u32[]{:S(2)}, u32[]{:S(2)}) %collective-permute-start.6) | collective-permute-done | bytes 4128 | tf_op jit(solution)/shard_map/ppermute | solution.py:725
  46.9 0.8 %collective-permute-done.5 = f32[32,32]{1,0:T(8,128)S(1)} collective-permute-done((f32[32,32]{1,0:T(8,128)S(1)}, f32[32,32]{1,0:T(8,128)S(1)}, u32[]{:S(2)}, u32[]{:S(2)}) %collective-permute-start.5) | collective-permute-done | bytes 4128 | tf_op jit(solution)/shard_map/ppermute | solution.py:725
  47.7 4.8 %collective-permute-start.10 = (f32[32,32]{1,0:T(8,128)S(1)}, f32[32,32]{1,0:T(8,128)S(1)}, u32[]{:S(2)}, u32[]{:S(2)}) collective-permute-start(f32[32,32]{1,0:T(8,128)S(1)} %add_add_fusion.2), channel_id=1, source_target_pairs={{0,24},{1,25},{2,26},{3,27},{4,28},{5,29},{6,30},{7,31},{8,16},{9,... | collective-permute-start | bytes 12296 | tf_op jit(solution)/shard_map/ppermute | solution.py:725
  52.5 0.0 collective-permute-start.9
  52.5 0.9 %collective-permute-start.8 = (f32[32,32]{1,0:T(8,128)S(1)}, f32[32,32]{1,0:T(8,128)S(1)}, u32[]{:S(2)}, u32[]{:S(2)}) collective-permute-start(f32[32,32]{1,0:T(8,128)S(1)} %add_add_fusion.2), channel_id=1, source_target_pairs={{0,8},{1,9},{2,10},{3,11},{4,12},{5,13},{6,14},{7,15},{8,0},{9,1},... | collective-permute-start | bytes 12296 | tf_op jit(solution)/shard_map/ppermute | solution.py:725
  53.4 0.8 %collective-permute-done.10 = f32[32,32]{1,0:T(8,128)S(1)} collective-permute-done((f32[32,32]{1,0:T(8,128)S(1)}, f32[32,32]{1,0:T(8,128)S(1)}, u32[]{:S(2)}, u32[]{:S(2)}) %collective-permute-start.10) | collective-permute-done | bytes 4128 | tf_op jit(solution)/shard_map/ppermute | solution.py:725
  54.2 3.5 %collective-permute-done.9 = f32[32,32]{1,0:T(8,128)S(1)} collective-permute-done((f32[32,32]{1,0:T(8,128)S(1)}, f32[32,32]{1,0:T(8,128)S(1)}, u32[]{:S(2)}, u32[]{:S(2)}) %collective-permute-start.9) | collective-permute-done | bytes 4128 | tf_op jit(solution)/shard_map/ppermute | solution.py:725
  57.7 0.0 collective-permute-done.8
  57.7 2.9 %collective-permute-start.13 = (f32[32,32]{1,0:T(8,128)S(1)}, f32[32,32]{1,0:T(8,128)S(1)}, u32[]{:S(2)}, u32[]{:S(2)}) collective-permute-start(f32[32,32]{1,0:T(8,128)S(1)} %add_add_fusion.1), channel_id=1, source_target_pairs={{0,96},{1,97},{2,98},{3,99},{4,100},{5,101},{6,102},{7,103},{8,104... | collective-permute-start | bytes 12296 | tf_op jit(solution)/shard_map/ppermute | solution.py:725
  60.6 0.7 %collective-permute-start.12 = (f32[32,32]{1,0:T(8,128)S(1)}, f32[32,32]{1,0:T(8,128)S(1)}, u32[]{:S(2)}, u32[]{:S(2)}) collective-permute-start(f32[32,32]{1,0:T(8,128)S(1)} %add_add_fusion.1), channel_id=1, source_target_pairs={{0,64},{1,65},{2,66},{3,67},{4,68},{5,69},{6,70},{7,71},{8,72},{9,... | collective-permute-start | bytes 12296 | tf_op jit(solution)/shard_map/ppermute | solution.py:725
  61.4 0.5 collective-permute-start.11
  61.9 0.9 %collective-permute-done.13 = f32[32,32]{1,0:T(8,128)S(1)} collective-permute-done((f32[32,32]{1,0:T(8,128)S(1)}, f32[32,32]{1,0:T(8,128)S(1)}, u32[]{:S(2)}, u32[]{:S(2)}) %collective-permute-start.13) | collective-permute-done | bytes 4128 | tf_op jit(solution)/shard_map/ppermute | solution.py:725
  62.8 3.1 %collective-permute-done.12 = f32[32,32]{1,0:T(8,128)S(1)} collective-permute-done((f32[32,32]{1,0:T(8,128)S(1)}, f32[32,32]{1,0:T(8,128)S(1)}, u32[]{:S(2)}, u32[]{:S(2)}) %collective-permute-start.12) | collective-permute-done | bytes 4128 | tf_op jit(solution)/shard_map/ppermute | solution.py:725
  65.9 0.0 collective-permute-done.11
  65.9 7.9 %apply.1 = (f32[16,16,16,256]{3,2,1,0:T(8,128)}, f32[16,16]{1,0:T(8,128)}) custom-call(f32[32,32]{1,0:T(8,128)S(1)} %add_add_fusion.sums, bf16[16,256,256]{2,1,0:T(8,128)(2,1)S(1)} %get-tuple-element.31.high_i, bf16[16,256,256]{2,1,0:T(8,128)(2,1)S(1)} %get-tuple-element.32.low_i, bf16[16,256,256]{2,1,0:T(8,128)(2,1)S(1)} %get-tuple-element.33.high_e, ...), custom_call_target="tpu_custom_call" | custom-call | flops 1000000000 | bytes 13000000 | tf_op jit(solution)/shard_map/apply/pallas_call | solution.py:694
  (4 shorter events, 0.0 us)
Async XLA Ops:
  4.0 27.9 %collective-permute-start = (f32[2,18,2,24,128]{4,3,2,1,0:T(8,128)S(1)}, f32[2,18,2,24,128]{4,3,2,1,0:T(8,128)S(1)}, u32[]{:S(2)}, u32[]{:S(2)}) collective-permute-start(f32[2,18,2,24,128]{4,3,2,1,0:T(8,128)S(1)} %get-tuple-element.20), channel_id=1, source_target_pairs={{0,8},{8,16},{16,24},{24,32},{32,40},{40,48},{48,56},{56,64},{64,7... | collective-permute-start | bytes 2654216 | tf_op jit(solution)/shard_map/ppermute | solution.py:715
  7.9 23.9 %collective-permute-start.1 = (f32[2,18,2,24,128]{4,3,2,1,0:T(8,128)S(1)}, f32[2,18,2,24,128]{4,3,2,1,0:T(8,128)S(1)}, u32[]{:S(2)}, u32[]{:S(2)}) collective-permute-start(f32[2,18,2,24,128]{4,3,2,1,0:T(8,128)S(1)} %get-tuple-element.21), channel_id=1, source_target_pairs={{8,0},{16,8},{24,16},{32,24},{40,32},{48,40},{56,48},{64,56},{72,6... | collective-permute-start | bytes 2654216 | tf_op jit(solution)/shard_map/ppermute | solution.py:720
  9.2 2.8 %collective-permute-start.2 = (f32[20,8,128]{2,1,0:T(8,128)S(1)}, f32[20,8,128]{2,1,0:T(8,128)S(1)}, u32[]{:S(2)}, u32[]{:S(2)}) collective-permute-start(f32[20,8,128]{2,1,0:T(8,128)S(1)} %get-tuple-element.23.own_last), channel_id=1, source_target_pairs={{0,1},{1,2},{2,3},{3,4},{4,5},{5,6},{6,7},{8,9},{9,10},{10,11},{11... | collective-permute-start | bytes 245768 | tf_op jit(solution)/shard_map/ppermute | solution.py:715
  10.7 4.8 %collective-permute-start.3 = (f32[20,8,128]{2,1,0:T(8,128)S(1)}, f32[20,8,128]{2,1,0:T(8,128)S(1)}, u32[]{:S(2)}, u32[]{:S(2)}) collective-permute-start(f32[20,8,128]{2,1,0:T(8,128)S(1)} %get-tuple-element.24.own_first), channel_id=1, source_target_pairs={{1,0},{2,1},{3,2},{4,3},{5,4},{6,5},{7,6},{9,8},{10,9},{11,10},{12... | collective-permute-start | bytes 245768 | tf_op jit(solution)/shard_map/ppermute | solution.py:720
  36.1 4.2 %collective-permute-start.4 = (f32[32,32]{1,0:T(8,128)S(1)}, f32[32,32]{1,0:T(8,128)S(1)}, u32[]{:S(2)}, u32[]{:S(2)}) collective-permute-start(f32[32,32]{1,0:T(8,128)S(1)} %get-tuple-element.30), channel_id=1, source_target_pairs={{0,1},{1,0},{2,3},{3,2},{4,5},{5,4},{6,7},{7,6},{8,9},{9,8},{10,11... | collective-permute-start | bytes 12296 | tf_op jit(solution)/shard_map/ppermute | solution.py:725
  40.3 4.9 %collective-permute-start.7 = (f32[32,32]{1,0:T(8,128)S(1)}, f32[32,32]{1,0:T(8,128)S(1)}, u32[]{:S(2)}, u32[]{:S(2)}) collective-permute-start(f32[32,32]{1,0:T(8,128)S(1)} %add.30), channel_id=1, source_target_pairs={{0,6},{1,7},{2,4},{3,5},{4,2},{5,3},{6,0},{7,1},{8,14},{9,15},{10,... | collective-permute-start | bytes 12296 | tf_op jit(solution)/shard_map/ppermute | solution.py:725
  41.6 5.2 %collective-permute-start.6 = (f32[32,32]{1,0:T(8,128)S(1)}, f32[32,32]{1,0:T(8,128)S(1)}, u32[]{:S(2)}, u32[]{:S(2)}) collective-permute-start(f32[32,32]{1,0:T(8,128)S(1)} %add.30), channel_id=1, source_target_pairs={{0,4},{1,5},{2,6},{3,7},{4,0},{5,1},{6,2},{7,3},{8,12},{9,13},{10,... | collective-permute-start | bytes 12296 | tf_op jit(solution)/shard_map/ppermute | solution.py:725
  44.0 3.7 %collective-permute-start.5 = (f32[32,32]{1,0:T(8,128)S(1)}, f32[32,32]{1,0:T(8,128)S(1)}, u32[]{:S(2)}, u32[]{:S(2)}) collective-permute-start(f32[32,32]{1,0:T(8,128)S(1)} %add.30), channel_id=1, source_target_pairs={{0,2},{1,3},{2,0},{3,1},{4,6},{5,7},{6,4},{7,5},{8,10},{9,11},{10,... | collective-permute-start | bytes 12296 | tf_op jit(solution)/shard_map/ppermute | solution.py:725
  47.7 6.5 %collective-permute-start.10 = (f32[32,32]{1,0:T(8,128)S(1)}, f32[32,32]{1,0:T(8,128)S(1)}, u32[]{:S(2)}, u32[]{:S(2)}) collective-permute-start(f32[32,32]{1,0:T(8,128)S(1)} %add_add_fusion.2), channel_id=1, source_target_pairs={{0,24},{1,25},{2,26},{3,27},{4,28},{5,29},{6,30},{7,31},{8,16},{9,... | collective-permute-start | bytes 12296 | tf_op jit(solution)/shard_map/ppermute | solution.py:725
  52.5 5.2 %collective-permute-start.9 = (f32[32,32]{1,0:T(8,128)S(1)}, f32[32,32]{1,0:T(8,128)S(1)}, u32[]{:S(2)}, u32[]{:S(2)}) collective-permute-start(f32[32,32]{1,0:T(8,128)S(1)} %add_add_fusion.2), channel_id=1, source_target_pairs={{0,16},{1,17},{2,18},{3,19},{4,20},{5,21},{6,22},{7,23},{8,24},{9,... | collective-permute-start | bytes 12296 | tf_op jit(solution)/shard_map/ppermute | solution.py:725
  52.5 5.2 %collective-permute-start.8 = (f32[32,32]{1,0:T(8,128)S(1)}, f32[32,32]{1,0:T(8,128)S(1)}, u32[]{:S(2)}, u32[]{:S(2)}) collective-permute-start(f32[32,32]{1,0:T(8,128)S(1)} %add_add_fusion.2), channel_id=1, source_target_pairs={{0,8},{1,9},{2,10},{3,11},{4,12},{5,13},{6,14},{7,15},{8,0},{9,1},... | collective-permute-start | bytes 12296 | tf_op jit(solution)/shard_map/ppermute | solution.py:725
  57.7 5.0 %collective-permute-start.13 = (f32[32,32]{1,0:T(8,128)S(1)}, f32[32,32]{1,0:T(8,128)S(1)}, u32[]{:S(2)}, u32[]{:S(2)}) collective-permute-start(f32[32,32]{1,0:T(8,128)S(1)} %add_add_fusion.1), channel_id=1, source_target_pairs={{0,96},{1,97},{2,98},{3,99},{4,100},{5,101},{6,102},{7,103},{8,104... | collective-permute-start | bytes 12296 | tf_op jit(solution)/shard_map/ppermute | solution.py:725
  60.6 5.2 %collective-permute-start.12 = (f32[32,32]{1,0:T(8,128)S(1)}, f32[32,32]{1,0:T(8,128)S(1)}, u32[]{:S(2)}, u32[]{:S(2)}) collective-permute-start(f32[32,32]{1,0:T(8,128)S(1)} %add_add_fusion.1), channel_id=1, source_target_pairs={{0,64},{1,65},{2,66},{3,67},{4,68},{5,69},{6,70},{7,71},{8,72},{9,... | collective-permute-start | bytes 12296 | tf_op jit(solution)/shard_map/ppermute | solution.py:725
  61.4 4.5 %collective-permute-start.11 = (f32[32,32]{1,0:T(8,128)S(1)}, f32[32,32]{1,0:T(8,128)S(1)}, u32[]{:S(2)}, u32[]{:S(2)}) collective-permute-start(f32[32,32]{1,0:T(8,128)S(1)} %add_add_fusion.1), channel_id=1, source_target_pairs={{0,32},{1,33},{2,34},{3,35},{4,36},{5,37},{6,38},{7,39},{8,40},{9,... | collective-permute-start | bytes 12296 | tf_op jit(solution)/shard_map/ppermute | solution.py:725

commit v7 on v6

--- a/solution.py
+++ b/solution.py
@@ -238,8 +238,12 @@
     acc[256:512, :] += lax.dot_general(low, high, dims, preferred_element_type=f32)
 
 
-def joined(parts):
-    return jnp.concatenate([parts[z] for z in range(NZ)], axis=1)
+def joined(upper, lower):
+    return jnp.concatenate([both(upper, lower, z) for z in range(NZ)], axis=1)
+
+
+def both(upper, lower, z):
+    return jnp.concatenate([upper[z], lower[z]], axis=0)
 
 
 def field_sums(acc):
@@ -254,40 +258,101 @@
     return jnp.dot(by_row, gather, precision=HIGH, preferred_element_type=f32)
 
 
-def interior_kernel(
-    X, ve, vn, fe, fn, mask, west, east, own_last, own_first,
-    high_out, low_out, edge_out, weights_out, mean_out, sums_out,
-    VE, FE, W, VN, FN, H, C, G, T, Z, acc, sems,
+def prepare_kernel(
+    X, ve, vn, fe, fn, mask,
+    high_in, low_in, high_edge, low_edge, edge_out, VE, FE, W, VN, FN, ints, Z, sems,
 ):
     zero_tile = jnp.zeros((8, LANES), f32)
-    for half in range(2):
-        for z in range(NZ):
-            edge_out[z, half, 0:8, :] = zero_tile
-    for half in range(2):
-        for z in range(NZ):
-            VE[half, z, 0:8, :] = zero_tile
-            FE[half, z, 0:8, :] = zero_tile
-            W[half, z, 0:8, :] = zero_tile.astype(jnp.int32)
-            W[half, z, 24:32, :] = zero_tile.astype(jnp.int32)
-    acc[...] = jnp.zeros((512, 256), f32)
-    lanes = lane_ids()
-    rows = row_ids()
-
     copies = []
-    body = pl.ds(8, BX)
     for half in range(2):
         for source, target in (
-            (ve, VE.at[half, :, body]),
-            (mask, W.at[half, :, body]),
+            (ve, VE.at[half, :, pl.ds(8, BX)]),
             (vn, VN.at[half]),
-            (fn, FN.at[0, half]),
-            (fe, FN.at[1, half]),
+            (mask, ints.at[0, half]),
+            (fn, ints.at[1, half]),
+            (fe, ints.at[2, half]),
         ):
             copies.append(
                 pltpu.make_async_copy(lane_half(source, half), target, sems.at[len(copies)])
             )
     for copy in copies:
         copy.start()
+    low_rows = row_ids() < 4
+    for half in range(2):
+        for z in range(NZ):
+            edge_out[z, half, 0:8, :] = zero_tile
+            edge_out[z, half, TAIL : TAIL + 8, :] = zero_tile
+
+    def level(z, carry):
+        for half in range(2):
+            columns = slice(LANES * half, LANES * half + LANES)
+            for f in range(F):
+                first, second = X[half, f, z, 8:16, :], X[half, f, z, 16:24, :]
+                edge = jnp.where(low_rows, first, second)
+                edge_out[z, half, 8 + 8 * f : 16 + 8 * f, :] = edge
+                if f < M:
+                    Z[0, 8 * f : 8 * f + 8, columns] = jnp.where(low_rows, second, first)
+                    Z[1, 8 * f : 8 * f + 8, columns] = edge
+        high_in[z], low_in[z] = split(Z[0])
+        high_edge[z], low_edge[z] = split(Z[1])
+        return carry
+
+    lax.fori_loop(0, NZ, level, 0, unroll=2)
+    for copy in copies:
+        copy.wait()
+    for half in range(2):
+        for z in range(NZ):
+            VE[half, z, 0:8, :] = zero_tile
+            FE[half, z, 0:8, :] = zero_tile
+            W[half, z, 0:8, :] = zero_tile
+            W[half, z, 24:32, :] = zero_tile
+            for xt in range(2):
+                rows = slice(8 * xt, 8 * xt + 8)
+                padded = slice(8 * xt + 8, 8 * xt + 16)
+                W[half, z, padded, :] = ints[0, half, z, rows, :].astype(f32)
+                FN[half, z, rows, :] = ints[1, half, z, rows, :].astype(f32)
+                FE[half, z, padded, :] = ints[2, half, z, rows, :].astype(f32)
+
+
+def prepare(cells, ve, vn, fe, fn, mask):
+    parts = jax.ShapeDtypeStruct((NZ, 8 * M, 256), bf16)
+    padded = jax.ShapeDtypeStruct((2, NZ, 32, LANES), f32)
+    plain = jax.ShapeDtypeStruct((2, NZ, BX, LANES), f32)
+    return pl.pallas_call(
+        prepare_kernel,
+        out_shape=(
+            parts,
+            parts,
+            parts,
+            parts,
+            jax.ShapeDtypeStruct((NZ, 2, TAIL + 8, LANES), f32),
+            padded,
+            padded,
+            padded,
+            plain,
+            plain,
+        ),
+        in_specs=[VMEM] + [HBM] * 5,
+        out_specs=(VMEM,) * 10,
+        scratch_shapes=[
+            pltpu.VMEM((3, 2, NZ, BX, LANES), jnp.int32),
+            pltpu.VMEM((2, 8 * M, 256), f32),
+            pltpu.SemaphoreType.DMA((10,)),
+        ],
+        compiler_params=params(16),
+        cost_estimate=cost(10**6, 10**6),
+        name="prepare",
+    )(cells, ve, vn, fe, fn, mask)
+
+
+def interior_kernel(
+    X, VE, FE, W, VN, FN, high_in, low_in, west, east, own_last, own_first,
+    high_out, low_out, edge_out, weights_out, mean_out, sums_out,
+    H, C, G, T, Z, acc,
+):
+    acc[...] = jnp.zeros((512, 256), f32)
+    lanes = lane_ids()
+    rows = row_ids()
 
     for f in range(F, F + 3):
         after, before = east[f], west[f]
@@ -331,17 +396,10 @@
 
     for f in range(F):
         beside(f)
-    for copy in copies:
-        copy.wait()
 
     def level(z, carry):
         z_up = jnp.minimum(z + 1, NZ - 1)
         z_down = jnp.maximum(z - 1, 0)
-        for half in range(2):
-            for xt in range(2):
-                FE[half, z, 8 + 8 * xt : 16 + 8 * xt, :] = FN[
-                    1, half, z, 8 * xt : 8 * xt + 8, :
-                ].astype(f32)
         for xt in range(2):
             start = 8 + 8 * xt
 
@@ -351,11 +409,11 @@
             def at(ref, half, offset):
                 return ref[half, z, start + offset : start + offset + 8, :]
 
-            wet = [at(W, half, 0).astype(f32) for half in range(2)]
+            wet = [at(W, half, 0) for half in range(2)]
             wx = []
             for half in range(2):
-                before = wet[half] * at(W, half, -1).astype(f32)
-                after = wet[half] * at(W, half, 1).astype(f32)
+                before = wet[half] * at(W, half, -1)
+                after = wet[half] * at(W, half, 1)
                 wx.append(
                     cell_weights(
                         *face_parts(before, at(VE, half, -1), at(FE, half, -1)),
@@ -368,7 +426,7 @@
                 face_parts(
                     wet[half] * following[half],
                     VN[half, z, 8 * xt : 8 * xt + 8, :],
-                    FN[0, half, z, 8 * xt : 8 * xt + 8, :].astype(f32),
+                    FN[half, z, 8 * xt : 8 * xt + 8, :],
                 )
                 for half in range(2)
             ]
@@ -433,11 +491,6 @@
                 for half in range(2):
                     columns = slice(LANES * half, LANES * half + LANES)
                     low_rows = rows < 4
-                    if xt == 1:
-                        cells = X[half, f, z, 8:16, :]
-                        edge_out[z, half, 8 + 8 * f : 16 + 8 * f, :] = jnp.where(
-                            low_rows, cells, own_cells[half]
-                        )
                     if f == M:
                         mean_out[z, 8 * xt : 8 * xt + 8, columns] = (
                             own_cells[half] + time_step * total[half]
@@ -446,13 +499,8 @@
                         T[half, f] = total[half]
                     else:
                         near = T[half, f]
-                        Z[8 * f : 8 * f + 8, columns] = jnp.where(
-                            low_rows, own_cells[half], cells
-                        )
-                        Z[128 + 8 * f : 136 + 8 * f, columns] = jnp.where(
-                            low_rows, total[half], near
-                        )
-                        place = slice(TAIL + 8 * f, TAIL + 8 * f + 8)
+                        place = slice(8 * f, 8 * f + 8)
+                        Z[place, columns] = jnp.where(low_rows, total[half], near)
                         edge_out[z, half, place, :] = jnp.where(low_rows, near, total[half])
         high, low = split(Z[...])
         high_out[z] = high
@@ -460,46 +508,40 @@
         return carry
 
     lax.fori_loop(0, NZ, level, 0)
-    add_products(acc, joined(high_out), joined(low_out))
+    add_products(acc, joined(high_in, high_out), joined(low_in, low_out))
     sums_out[...] = field_sums(acc)
 
 
-def interior(cells, ve, vn, fe, fn, mask, west, east, own_last, own_first):
-    parts = jax.ShapeDtypeStruct((NZ, 256, 256), bf16)
+def interior(cells, planes, high_in, low_in, west, east, own_last, own_first):
+    parts = jax.ShapeDtypeStruct((NZ, 8 * M, 256), bf16)
     return pl.pallas_call(
         interior_kernel,
         out_shape=(
             parts,
             parts,
-            jax.ShapeDtypeStruct((NZ, 2, TAIL + 8 * M, LANES), f32),
+            jax.ShapeDtypeStruct((NZ, 2, 8 * M, LANES), f32),
             jax.ShapeDtypeStruct((2, NZ, 6, 8, LANES), f32),
-            jax.ShapeDtypeStruct(ve.shape, f32),
+            jax.ShapeDtypeStruct((NZ, BX, 2 * LANES), f32),
             jax.ShapeDtypeStruct((64, 32), f32),
         ),
-        in_specs=[VMEM] + [HBM] * 5 + [VMEM] * 4,
+        in_specs=[VMEM] * 12,
         out_specs=(VMEM,) * 6,
         scratch_shapes=[
-            pltpu.VMEM((2, NZ, 32, LANES), f32),
-            pltpu.VMEM((2, NZ, 32, LANES), f32),
-            pltpu.VMEM((2, NZ, 32, LANES), jnp.int32),
-            pltpu.VMEM((2, NZ, BX, LANES), f32),
-            pltpu.VMEM((2, 2, NZ, BX, LANES), jnp.int32),
             pltpu.VMEM((3, 2 * NZ, 8, LANES), f32),
             pltpu.VMEM((2, F, 8, LANES), f32),
             pltpu.VMEM((6, 8, LANES), f32),
             pltpu.VMEM((2, M, 8, LANES), f32),
-            pltpu.VMEM((256, 256), f32),
+            pltpu.VMEM((8 * M, 256), f32),
             pltpu.VMEM((512, 256), f32),
-            pltpu.SemaphoreType.DMA((10,)),
         ],
-        compiler_params=params(28),
+        compiler_params=params(20),
         cost_estimate=cost(10**6, 10**6),
         name="interior",
-    )(cells, ve, vn, fe, fn, mask, west, east, own_last, own_first)
+    )(cells, *planes, high_in, low_in, west, east, own_last, own_first)
 
 
 def edge_kernel(
-    below, above, edge_in, weights, mean_in, sums_in,
+    below, above, edge_in, edge_tail, high_in, low_in, weights, mean_in, sums_in,
     high_out, low_out, mean_out, sums_out, Z, acc,
 ):
     acc[...] = jnp.zeros((512, 256), f32)
@@ -557,7 +599,7 @@
                         change = change + inside[d] * cells
                     if f < M:
                         Z[half, 8 * f : 8 * f + 8, :] = (
-                            edge_in[z, half, TAIL + 8 * f : TAIL + 8 * f + 8, :] + change
+                            edge_tail[z, half, 8 * f : 8 * f + 8, :] + change
                         )
                     else:
                         columns = slice(LANES * half, LANES * half + LANES)
@@ -568,14 +610,14 @@
                         mean_out[z, 8:16, columns] = mean_in[z, 8:16, columns] + jnp.where(
                             low_rows, 0.0, step
                         )
-            halves = [
-                jnp.concatenate([edge_in[z, half, 8 : 8 + 8 * M, :], Z[half]], axis=0)
-                for half in range(2)
-            ]
-            high, low = split(jnp.concatenate(halves, axis=1))
+            high, low = split(jnp.concatenate([Z[0], Z[1]], axis=1))
             high_out[z] = high
             low_out[z] = low
-            add_products(acc, high, low)
+            add_products(
+                acc,
+                jnp.concatenate([high_in[z], high], axis=0),
+                jnp.concatenate([low_in[z], low], axis=0),
+            )
         return carry
 
     lax.fori_loop(0, 2, group, 0)
@@ -589,8 +631,8 @@
     sums_out[...] = sums[0:32] + sums[32:64] + turned
 
 
-def edges(below, above, edge_in, weights, mean_in, sums_in):
-    parts = jax.ShapeDtypeStruct((NZ, 256, 256), bf16)
+def edges(below, above, edge_in, edge_tail, high_in, low_in, weights, mean_in, sums_in):
+    parts = jax.ShapeDtypeStruct((NZ, 8 * M, 256), bf16)
     return pl.pallas_call(
         edge_kernel,
         out_shape=(
@@ -599,7 +641,7 @@
             jax.ShapeDtypeStruct(mean_in.shape, f32),
             jax.ShapeDtypeStruct((32, 32), f32),
         ),
-        in_specs=[VMEM] * 6,
+        in_specs=[VMEM] * 9,
         out_specs=(VMEM,) * 4,
         scratch_shapes=[
             pltpu.VMEM((2, 8 * M, LANES), f32),
@@ -608,7 +650,7 @@
         compiler_params=params(16),
         cost_estimate=cost(10**9, 10**7),
         name="edges",
-    )(below, above, edge_in, weights, mean_in, sums_in)
+    )(below, above, edge_in, edge_tail, high_in, low_in, weights, mean_in, sums_in)
 
 
 def factor_and_map(sums, cell_count):
@@ -656,7 +698,8 @@
 
 
 def make_apply_kernel(cell_count):
-    def apply_kernel(sums, high_i, low_i, high_e, low_e, out, factor_out, maps, new, sems):
+    def apply_kernel(sums, *refs):
+        parts, (out, factor_out, maps, new, sems) = refs[:8], refs[8:]
         factor, mapping = factor_and_map(sums[...], cell_count)
         factor_out[...] = factor
         maps[...] = spread_map(mapping)
@@ -673,9 +716,10 @@
                 put(z - SLOTS, slot).wait()
 
             results = []
-            for high, low in ((high_i, low_i), (high_e, low_e)):
-                first = jnp.dot(maps[...], high[z], preferred_element_type=f32)
-                second = jnp.dot(maps[0:128, :], low[z], preferred_element_type=f32)
+            for i in (0, 4):
+                high, low = both(parts[i], parts[i + 2], z), both(parts[i + 1], parts[i + 3], z)
+                first = jnp.dot(maps[...], high, preferred_element_type=f32)
+                second = jnp.dot(maps[0:128, :], low, preferred_element_type=f32)
                 results.append((first[0:128] + first[128:256] + second).reshape(M, 8, 256))
             inner, edge = results
             new[slot, :, 0:8, :] = jnp.where(low_rows, edge, inner)
@@ -690,14 +734,14 @@
     return apply_kernel
 
 
-def apply_map(sums, high_i, low_i, high_e, low_e, cell_count):
+def apply_map(sums, parts, cell_count):
     return pl.pallas_call(
         make_apply_kernel(cell_count),
         out_shape=(
             jax.ShapeDtypeStruct((M, NZ, BX, 256), f32),
             jax.ShapeDtypeStruct((M, M), f32),
         ),
-        in_specs=[VMEM] * 5,
+        in_specs=[VMEM] * 9,
         out_specs=(ANY, VMEM),
         scratch_shapes=[
             pltpu.VMEM((256, 256), bf16),
@@ -707,7 +751,7 @@
         compiler_params=params(12),
         cost_estimate=cost(10**9, 13 * 10**6),
         name="apply",
-    )(sums, high_i, low_i, high_e, low_e)
+    )(sums, *parts)
 
 
 def onward(value, axis):
@@ -745,17 +789,22 @@
     east = backward(west_send, "gy")
     below = onward(up, "gx")
     above = backward(down, "gx")
-    high_i, low_i, edge, weights, mean_part, sums_i = interior(
-        cells, velocity_east, velocity_north, flag_east, flag_north, ocean_mask,
-        west, east, east_send, west_send,
-    )
-    high_e, low_e, mean_next, sums = edges(below, above, edge, weights, mean_part, sums_i)
+    high_x, low_x, high_xe, low_xe, edge, *planes = prepare(
+        cells, velocity_east, velocity_north, flag_east, flag_north, ocean_mask
+    )
+    high_t, low_t, edge_tail, weights, mean_part, sums_i = interior(
+        cells, planes, high_x, low_x, west, east, east_send, west_send
+    )
+    high_te, low_te, mean_next, sums = edges(
+        below, above, edge, edge_tail, high_xe, low_xe, weights, mean_part, sums_i
+    )
     sums = sums + exchanged(sums, axes, 1)
     for first in (2, 8, 32):
         near, far, both = (exchanged(sums, axes, first * i) for i in (1, 2, 3))
         sums = (sums + near) + (far + both)
     cell_count = float(NZ * BX * 256 * lax.axis_size("gx") * lax.axis_size("gy"))
-    modes_next, factor = apply_map(sums, high_i, low_i, high_e, low_e, cell_count)
+    parts = high_x, low_x, high_t, low_t, high_xe, low_xe, high_te, low_te
+    modes_next, factor = apply_map(sums, parts, cell_count)
     return (mean_next, modes_next, factor)
 
 

time: 74 us -> 72.4 us (0.978)
  waiting for transfers between devices: 15.9 us -> 14.9 us
    pallas_call x0 -> x1, Pallas kernels: none -> 1.58 us  [prepare(): pl.pallas_call(prepare_kernel, out_shape=(parts, parts, parts, parts, jax...]
    pallas_call x1, Pallas kernels: 16.3 us -> 15 us  [interior(): pl.pallas_call(interior_kernel, out_shape=(parts, parts, jax.ShapeDtypeSt...]
    ppermute x2, waiting for transfers between devices: 3.5 us -> 2.49 us  [backward(): return lax.ppermute(value, axis, [(i + 1, i) for i in range(size - 1)])]
  transfers between devices with their start and end apart: 14 -> 14, of which waited for: 9 -> 10; matrix products, arithmetic and copies ran while one was open for 0% -> 0% of each run, Pallas kernels for 22% -> 23%
where the time goes in v7:
time: 72.4 us; the launch traced here: 72.2 us
  Pallas kernels  31.7 us (44%)
  starting transfers between devices  24.8 us (34%)
  waiting for transfers between devices  14.9 us (21%)
    ppermute x10, starting transfers between devices, exchanged(): return lax.ppermute(value, axes, [(i, i ^ distance) for i in range(size)])  16.8 us
    pallas_call x1, Pallas kernels, interior(): pl.pallas_call(interior_kernel, out_shape=(parts, parts, jax.ShapeDtypeSt...  15 us
    ppermute x10, waiting for transfers between devices, exchanged(): return lax.ppermute(value, axes, [(i, i ^ distance) for i in range(size)])  12.4 us
    pallas_call x1, Pallas kernels, apply_map(): pl.pallas_call(make_apply_kernel(cell_count), out_shape=(jax.ShapeDtypeSt...  7.87 us
    ppermute x2, starting transfers between devices, onward(): return lax.ppermute(value, axis, [(i, i + 1) for i in range(size - 1)])  5.42 us
    pallas_call x1, Pallas kernels, edges(): pl.pallas_call(edge_kernel, out_shape=(parts, parts, jax.ShapeDtypeStruct...  3.97 us
    pallas_call x1, Pallas kernels, pack(): pl.pallas_call(pack_kernel, out_shape=(rows, rows, columns, columns, jax....  3.34 us
    ppermute x2, starting transfers between devices, backward(): return lax.ppermute(value, axis, [(i + 1, i) for i in range(size - 1)])  2.58 us
  transfers between devices with their start and end apart: 14, of which 10 were waited for; matrix products, arithmetic and copies ran while one was open for 0% of the time, Pallas kernels for 23%

profile of v7, /device:TPU:0, one launch (start us, length us, event | category | flops | bytes accessed | tf_op | source)
XLA Modules:
  0.0 72.2 jit_solution(10668898161963445996)
XLA Ops:
  0.6 3.3 %pack.1 = (f32[2,18,2,24,128]{4,3,2,1,0:T(8,128)S(1)}, f32[2,18,2,24,128]{4,3,2,1,0:T(8,128)S(1)}, f32[20,8,128]{2,1,0:T(8,128)S(1)}, f32[20,8,128]{2,1,0:T(8,128)S(1)}, f32[2,17,16,32,128]{4,3,2,1,0:T(8,128)S(1)}) custom-call(f32[16,16,16,256]{3,2,1,0:T(8,128)} %modes.1, f32[16,16,256]{2,1,0:T(8,128)} %mean.1, f32[16,16,256]{2,1,0:T(8,128)} %ve.3, ...), custom_call_target="tpu_custom_call" | custom-call | flops 10000000 | bytes 7000000 | tf_op jit(solution)/shard_map/pack/pallas_call | solution.py:174
  4.0 4.0 %collective-permute-start = (f32[2,18,2,24,128]{4,3,2,1,0:T(8,128)S(1)}, f32[2,18,2,24,128]{4,3,2,1,0:T(8,128)S(1)}, u32[]{:S(2)}, u32[]{:S(2)}) collective-permute-start(f32[2,18,2,24,128]{4,3,2,1,0:T(8,128)S(1)} %get-tuple-element.30), channel_id=1, source_target_pairs={{0,8},{8,16},{16,24},{24,32},{32,40},{40,48},{48,56},{56,64},{64,7... | collective-permute-start | bytes 2654216 | tf_op jit(solution)/shard_map/ppermute | solution.py:759
  7.9 1.3 %collective-permute-start.1 = (f32[2,18,2,24,128]{4,3,2,1,0:T(8,128)S(1)}, f32[2,18,2,24,128]{4,3,2,1,0:T(8,128)S(1)}, u32[]{:S(2)}, u32[]{:S(2)}) collective-permute-start(f32[2,18,2,24,128]{4,3,2,1,0:T(8,128)S(1)} %get-tuple-element.31), channel_id=1, source_target_pairs={{8,0},{16,8},{24,16},{32,24},{40,32},{48,40},{56,48},{64,56},{72,6... | collective-permute-start | bytes 2654216 | tf_op jit(solution)/shard_map/ppermute | solution.py:764
  9.2 1.5 %collective-permute-start.2 = (f32[20,8,128]{2,1,0:T(8,128)S(1)}, f32[20,8,128]{2,1,0:T(8,128)S(1)}, u32[]{:S(2)}, u32[]{:S(2)}) collective-permute-start(f32[20,8,128]{2,1,0:T(8,128)S(1)} %get-tuple-element.41.own_last), channel_id=1, source_target_pairs={{0,1},{1,2},{2,3},{3,4},{4,5},{5,6},{6,7},{8,9},{9,10},{10,11},{11... | collective-permute-start | bytes 245768 | tf_op jit(solution)/shard_map/ppermute | solution.py:759
  10.7 1.3 %collective-permute-start.3 = (f32[20,8,128]{2,1,0:T(8,128)S(1)}, f32[20,8,128]{2,1,0:T(8,128)S(1)}, u32[]{:S(2)}, u32[]{:S(2)}) collective-permute-start(f32[20,8,128]{2,1,0:T(8,128)S(1)} %get-tuple-element.42.own_first), channel_id=1, source_target_pairs={{1,0},{2,1},{3,2},{4,3},{5,4},{6,5},{7,6},{9,8},{10,9},{11,10},{12... | collective-permute-start | bytes 245768 | tf_op jit(solution)/shard_map/ppermute | solution.py:764
  12.0 1.6 %prepare.1 = (bf16[16,128,256]{2,1,0:T(8,128)(2,1)S(1)}, bf16[16,128,256]{2,1,0:T(8,128)(2,1)S(1)}, bf16[16,128,256]{2,1,0:T(8,128)(2,1)S(1)}, bf16[16,128,256]{...) custom-call(f32[2,17,16,32,128]{4,3,2,1,0:T(8,128)S(1)} %get-tuple-e, ...), custom_call_target="tpu_custom_call" | custom-call | flops 1000000 | bytes 1000000 | tf_op jit(solution)/shard_map/prepare/pallas_call | solution.py:321
  13.6 0.0 collective-permute-done.2.west
  13.6 1.9 %collective-permute-done.3.east = f32[20,8,128]{2,1,0:T(8,128)S(1)} collective-permute-done((f32[20,8,128]{2,1,0:T(8,128)S(1)}, f32[20,8,128]{2,1,0:T(8,128)S(1)}, u32[]{:S(2)}, u32[]{:S(2)}) %collective-permute-start.3) | collective-permute-done | bytes 81952 | tf_op jit(solution)/shard_map/ppermute | solution.py:764
  15.5 15.0 %interior.1 = (bf16[16,128,256]{2,1,0:T(8,128)(2,1)S(1)}, bf16[16,128,256]{2,1,0:T(8,128)(2,1)S(1)}, f32[16,2,128,128]{3,2,1,0:T(8,128)S(1)}, f32[2,16,6,8,128]{...) custom-call(f32[2,17,16,32,128]{4,3,2,1,0:T(8,128)S(1)} %get-tuple-element.32.X, ...), custom_call_target="tpu_custom_call" | custom-call | flops 1000000 | bytes 1000000 | tf_op jit(solution)/shard_map/interior/pallas_call | solution.py:517
  30.5 0.0 collective-permute-done.below
  30.5 0.6 collective-permute-done.1.above
  31.1 4.0 %edges.1 = (bf16[16,128,256]{2,1,0:T(8,128)(2,1)S(1)}, bf16[16,128,256]{2,1,0:T(8,128)(2,1)S(1)}, f32[16,16,256]{2,1,0:T(8,128)}, f32[32,32]{1,0:T(8,128)S(1)}) custom-call(f32[2,18,2,24,128]{4,3,2,1,0:T(8,128)S(1)} %collective-permute-done.below, f32[2,18,2,24,128]{4,3,2,1,0:T(8,128)S(1)} %collective-permute-done.1.above, ...), custom_call_target="tpu_custom_call" | custom-call | flops 1000000000 | bytes 10000000 | tf_op jit(solution)/shard_map/edges/pallas_call | solution.py:636
  35.0 2.8 %collective-permute-start.4 = (f32[32,32]{1,0:T(8,128)S(1)}, f32[32,32]{1,0:T(8,128)S(1)}, u32[]{:S(2)}, u32[]{:S(2)}) collective-permute-start(f32[32,32]{1,0:T(8,128)S(1)} %get-tuple-element.50), channel_id=1, source_target_pairs={{0,1},{1,0},{2,3},{3,2},{4,5},{5,4},{6,7},{7,6},{8,9},{9,8},{10,11... | collective-permute-start | bytes 12296 | tf_op jit(solution)/shard_map/ppermute | solution.py:769
  37.9 0.8 %collective-permute-done.4 = f32[32,32]{1,0:T(8,128)S(1)} collective-permute-done((f32[32,32]{1,0:T(8,128)S(1)}, f32[32,32]{1,0:T(8,128)S(1)}, u32[]{:S(2)}, u32[]{:S(2)}) %collective-permute-start.4) | collective-permute-done | bytes 4128 | tf_op jit(solution)/shard_map/ppermute | solution.py:769
  38.7 1.3 %collective-permute-start.7 = (f32[32,32]{1,0:T(8,128)S(1)}, f32[32,32]{1,0:T(8,128)S(1)}, u32[]{:S(2)}, u32[]{:S(2)}) collective-permute-start(f32[32,32]{1,0:T(8,128)S(1)} %add.30), channel_id=1, source_target_pairs={{0,6},{1,7},{2,4},{3,5},{4,2},{5,3},{6,0},{7,1},{8,14},{9,15},{10,... | collective-permute-start | bytes 12296 | tf_op jit(solution)/shard_map/ppermute | solution.py:769
  40.0 2.3 %collective-permute-start.6 = (f32[32,32]{1,0:T(8,128)S(1)}, f32[32,32]{1,0:T(8,128)S(1)}, u32[]{:S(2)}, u32[]{:S(2)}) collective-permute-start(f32[32,32]{1,0:T(8,128)S(1)} %add.30), channel_id=1, source_target_pairs={{0,4},{1,5},{2,6},{3,7},{4,0},{5,1},{6,2},{7,3},{8,12},{9,13},{10,... | collective-permute-start | bytes 12296 | tf_op jit(solution)/shard_map/ppermute | solution.py:769
  42.4 0.4 collective-permute-start.5
  42.8 0.9 %collective-permute-done.7 = f32[32,32]{1,0:T(8,128)S(1)} collective-permute-done((f32[32,32]{1,0:T(8,128)S(1)}, f32[32,32]{1,0:T(8,128)S(1)}, u32[]{:S(2)}, u32[]{:S(2)}) %collective-permute-start.7) | collective-permute-done | bytes 4128 | tf_op jit(solution)/shard_map/ppermute | solution.py:769
  43.7 1.6 %collective-permute-done.6 = f32[32,32]{1,0:T(8,128)S(1)} collective-permute-done((f32[32,32]{1,0:T(8,128)S(1)}, f32[32,32]{1,0:T(8,128)S(1)}, u32[]{:S(2)}, u32[]{:S(2)}) %collective-permute-start.6) | collective-permute-done | bytes 4128 | tf_op jit(solution)/shard_map/ppermute | solution.py:769
  45.3 0.8 %collective-permute-done.5 = f32[32,32]{1,0:T(8,128)S(1)} collective-permute-done((f32[32,32]{1,0:T(8,128)S(1)}, f32[32,32]{1,0:T(8,128)S(1)}, u32[]{:S(2)}, u32[]{:S(2)}) %collective-permute-start.5) | collective-permute-done | bytes 4128 | tf_op jit(solution)/shard_map/ppermute | solution.py:769
  46.1 4.8 %collective-permute-start.10 = (f32[32,32]{1,0:T(8,128)S(1)}, f32[32,32]{1,0:T(8,128)S(1)}, u32[]{:S(2)}, u32[]{:S(2)}) collective-permute-start(f32[32,32]{1,0:T(8,128)S(1)} %add_add_fusion.2), channel_id=1, source_target_pairs={{0,24},{1,25},{2,26},{3,27},{4,28},{5,29},{6,30},{7,31},{8,16},{9,... | collective-permute-start | bytes 12296 | tf_op jit(solution)/shard_map/ppermute | solution.py:769
  50.9 0.0 collective-permute-start.9
  50.9 0.9 %collective-permute-start.8 = (f32[32,32]{1,0:T(8,128)S(1)}, f32[32,32]{1,0:T(8,128)S(1)}, u32[]{:S(2)}, u32[]{:S(2)}) collective-permute-start(f32[32,32]{1,0:T(8,128)S(1)} %add_add_fusion.2), channel_id=1, source_target_pairs={{0,8},{1,9},{2,10},{3,11},{4,12},{5,13},{6,14},{7,15},{8,0},{9,1},... | collective-permute-start | bytes 12296 | tf_op jit(solution)/shard_map/ppermute | solution.py:769
  51.8 0.8 %collective-permute-done.10 = f32[32,32]{1,0:T(8,128)S(1)} collective-permute-done((f32[32,32]{1,0:T(8,128)S(1)}, f32[32,32]{1,0:T(8,128)S(1)}, u32[]{:S(2)}, u32[]{:S(2)}) %collective-permute-start.10) | collective-permute-done | bytes 4128 | tf_op jit(solution)/shard_map/ppermute | solution.py:769
  52.6 3.5 %collective-permute-done.9 = f32[32,32]{1,0:T(8,128)S(1)} collective-permute-done((f32[32,32]{1,0:T(8,128)S(1)}, f32[32,32]{1,0:T(8,128)S(1)}, u32[]{:S(2)}, u32[]{:S(2)}) %collective-permute-start.9) | collective-permute-done | bytes 4128 | tf_op jit(solution)/shard_map/ppermute | solution.py:769
  56.1 0.0 collective-permute-done.8
  56.1 2.9 %collective-permute-start.13 = (f32[32,32]{1,0:T(8,128)S(1)}, f32[32,32]{1,0:T(8,128)S(1)}, u32[]{:S(2)}, u32[]{:S(2)}) collective-permute-start(f32[32,32]{1,0:T(8,128)S(1)} %add_add_fusion.1), channel_id=1, source_target_pairs={{0,96},{1,97},{2,98},{3,99},{4,100},{5,101},{6,102},{7,103},{8,104... | collective-permute-start | bytes 12296 | tf_op jit(solution)/shard_map/ppermute | solution.py:769
  59.0 0.7 %collective-permute-start.12 = (f32[32,32]{1,0:T(8,128)S(1)}, f32[32,32]{1,0:T(8,128)S(1)}, u32[]{:S(2)}, u32[]{:S(2)}) collective-permute-start(f32[32,32]{1,0:T(8,128)S(1)} %add_add_fusion.1), channel_id=1, source_target_pairs={{0,64},{1,65},{2,66},{3,67},{4,68},{5,69},{6,70},{7,71},{8,72},{9,... | collective-permute-start | bytes 12296 | tf_op jit(solution)/shard_map/ppermute | solution.py:769
  59.8 0.5 collective-permute-start.11
  60.3 0.9 %collective-permute-done.13 = f32[32,32]{1,0:T(8,128)S(1)} collective-permute-done((f32[32,32]{1,0:T(8,128)S(1)}, f32[32,32]{1,0:T(8,128)S(1)}, u32[]{:S(2)}, u32[]{:S(2)}) %collective-permute-start.13) | collective-permute-done | bytes 4128 | tf_op jit(solution)/shard_map/ppermute | solution.py:769
  61.2 3.1 %collective-permute-done.12 = f32[32,32]{1,0:T(8,128)S(1)} collective-permute-done((f32[32,32]{1,0:T(8,128)S(1)}, f32[32,32]{1,0:T(8,128)S(1)}, u32[]{:S(2)}, u32[]{:S(2)}) %collective-permute-start.12) | collective-permute-done | bytes 4128 | tf_op jit(solution)/shard_map/ppermute | solution.py:769
  64.3 0.0 collective-permute-done.11
  64.3 7.9 %apply.1 = (f32[16,16,16,256]{3,2,1,0:T(8,128)}, f32[16,16]{1,0:T(8,128)}) custom-call(f32[32,32]{1,0:T(8,128)S(1)} %add_add_fusion.sums, bf16[16,128,256]{2,1,0:T(8,128)(2,1)S(1)} %get-tuple-element.39.high_in.refs_0_, bf16[16,128,256]{2,1,0:T(8,128)(2,1)S(1)} %get-tuple-element.40.low_in.refs_1_, bf16[16,128,256]{2,1,0:T(8,128)(2,1)S(1)} %get-tuple-element.51.refs_2_, ...), custom_call_target="tpu_custom_call" | custom-call | flops 1000000000 | bytes 13000000 | tf_op jit(solution)/shard_map/apply/pallas_call | solution.py:738
  (4 shorter events, 0.0 us)
Async XLA Ops:
  4.0 26.5 %collective-permute-start = (f32[2,18,2,24,128]{4,3,2,1,0:T(8,128)S(1)}, f32[2,18,2,24,128]{4,3,2,1,0:T(8,128)S(1)}, u32[]{:S(2)}, u32[]{:S(2)}) collective-permute-start(f32[2,18,2,24,128]{4,3,2,1,0:T(8,128)S(1)} %get-tuple-element.30), channel_id=1, source_target_pairs={{0,8},{8,16},{16,24},{24,32},{32,40},{40,48},{48,56},{56,64},{64,7... | collective-permute-start | bytes 2654216 | tf_op jit(solution)/shard_map/ppermute | solution.py:759
  7.9 23.1 %collective-permute-start.1 = (f32[2,18,2,24,128]{4,3,2,1,0:T(8,128)S(1)}, f32[2,18,2,24,128]{4,3,2,1,0:T(8,128)S(1)}, u32[]{:S(2)}, u32[]{:S(2)}) collective-permute-start(f32[2,18,2,24,128]{4,3,2,1,0:T(8,128)S(1)} %get-tuple-element.31), channel_id=1, source_target_pairs={{8,0},{16,8},{24,16},{32,24},{40,32},{48,40},{56,48},{64,56},{72,6... | collective-permute-start | bytes 2654216 | tf_op jit(solution)/shard_map/ppermute | solution.py:764
  9.2 4.4 %collective-permute-start.2 = (f32[20,8,128]{2,1,0:T(8,128)S(1)}, f32[20,8,128]{2,1,0:T(8,128)S(1)}, u32[]{:S(2)}, u32[]{:S(2)}) collective-permute-start(f32[20,8,128]{2,1,0:T(8,128)S(1)} %get-tuple-element.41.own_last), channel_id=1, source_target_pairs={{0,1},{1,2},{2,3},{3,4},{4,5},{5,6},{6,7},{8,9},{9,10},{10,11},{11... | collective-permute-start | bytes 245768 | tf_op jit(solution)/shard_map/ppermute | solution.py:759
  10.7 4.8 %collective-permute-start.3 = (f32[20,8,128]{2,1,0:T(8,128)S(1)}, f32[20,8,128]{2,1,0:T(8,128)S(1)}, u32[]{:S(2)}, u32[]{:S(2)}) collective-permute-start(f32[20,8,128]{2,1,0:T(8,128)S(1)} %get-tuple-element.42.own_first), channel_id=1, source_target_pairs={{1,0},{2,1},{3,2},{4,3},{5,4},{6,5},{7,6},{9,8},{10,9},{11,10},{12... | collective-permute-start | bytes 245768 | tf_op jit(solution)/shard_map/ppermute | solution.py:764
  35.0 3.7 %collective-permute-start.4 = (f32[32,32]{1,0:T(8,128)S(1)}, f32[32,32]{1,0:T(8,128)S(1)}, u32[]{:S(2)}, u32[]{:S(2)}) collective-permute-start(f32[32,32]{1,0:T(8,128)S(1)} %get-tuple-element.50), channel_id=1, source_target_pairs={{0,1},{1,0},{2,3},{3,2},{4,5},{5,4},{6,7},{7,6},{8,9},{9,8},{10,11... | collective-permute-start | bytes 12296 | tf_op jit(solution)/shard_map/ppermute | solution.py:769
  38.7 4.9 %collective-permute-start.7 = (f32[32,32]{1,0:T(8,128)S(1)}, f32[32,32]{1,0:T(8,128)S(1)}, u32[]{:S(2)}, u32[]{:S(2)}) collective-permute-start(f32[32,32]{1,0:T(8,128)S(1)} %add.30), channel_id=1, source_target_pairs={{0,6},{1,7},{2,4},{3,5},{4,2},{5,3},{6,0},{7,1},{8,14},{9,15},{10,... | collective-permute-start | bytes 12296 | tf_op jit(solution)/shard_map/ppermute | solution.py:769
  40.0 5.2 %collective-permute-start.6 = (f32[32,32]{1,0:T(8,128)S(1)}, f32[32,32]{1,0:T(8,128)S(1)}, u32[]{:S(2)}, u32[]{:S(2)}) collective-permute-start(f32[32,32]{1,0:T(8,128)S(1)} %add.30), channel_id=1, source_target_pairs={{0,4},{1,5},{2,6},{3,7},{4,0},{5,1},{6,2},{7,3},{8,12},{9,13},{10,... | collective-permute-start | bytes 12296 | tf_op jit(solution)/shard_map/ppermute | solution.py:769
  42.4 3.7 %collective-permute-start.5 = (f32[32,32]{1,0:T(8,128)S(1)}, f32[32,32]{1,0:T(8,128)S(1)}, u32[]{:S(2)}, u32[]{:S(2)}) collective-permute-start(f32[32,32]{1,0:T(8,128)S(1)} %add.30), channel_id=1, source_target_pairs={{0,2},{1,3},{2,0},{3,1},{4,6},{5,7},{6,4},{7,5},{8,10},{9,11},{10,... | collective-permute-start | bytes 12296 | tf_op jit(solution)/shard_map/ppermute | solution.py:769
  46.1 6.5 %collective-permute-start.10 = (f32[32,32]{1,0:T(8,128)S(1)}, f32[32,32]{1,0:T(8,128)S(1)}, u32[]{:S(2)}, u32[]{:S(2)}) collective-permute-start(f32[32,32]{1,0:T(8,128)S(1)} %add_add_fusion.2), channel_id=1, source_target_pairs={{0,24},{1,25},{2,26},{3,27},{4,28},{5,29},{6,30},{7,31},{8,16},{9,... | collective-permute-start | bytes 12296 | tf_op jit(solution)/shard_map/ppermute | solution.py:769
  50.9 5.2 %collective-permute-start.9 = (f32[32,32]{1,0:T(8,128)S(1)}, f32[32,32]{1,0:T(8,128)S(1)}, u32[]{:S(2)}, u32[]{:S(2)}) collective-permute-start(f32[32,32]{1,0:T(8,128)S(1)} %add_add_fusion.2), channel_id=1, source_target_pairs={{0,16},{1,17},{2,18},{3,19},{4,20},{5,21},{6,22},{7,23},{8,24},{9,... | collective-permute-start | bytes 12296 | tf_op jit(solution)/shard_map/ppermute | solution.py:769
  50.9 5.2 %collective-permute-start.8 = (f32[32,32]{1,0:T(8,128)S(1)}, f32[32,32]{1,0:T(8,128)S(1)}, u32[]{:S(2)}, u32[]{:S(2)}) collective-permute-start(f32[32,32]{1,0:T(8,128)S(1)} %add_add_fusion.2), channel_id=1, source_target_pairs={{0,8},{1,9},{2,10},{3,11},{4,12},{5,13},{6,14},{7,15},{8,0},{9,1},... | collective-permute-start | bytes 12296 | tf_op jit(solution)/shard_map/ppermute | solution.py:769
  56.1 5.0 %collective-permute-start.13 = (f32[32,32]{1,0:T(8,128)S(1)}, f32[32,32]{1,0:T(8,128)S(1)}, u32[]{:S(2)}, u32[]{:S(2)}) collective-permute-start(f32[32,32]{1,0:T(8,128)S(1)} %add_add_fusion.1), channel_id=1, source_target_pairs={{0,96},{1,97},{2,98},{3,99},{4,100},{5,101},{6,102},{7,103},{8,104... | collective-permute-start | bytes 12296 | tf_op jit(solution)/shard_map/ppermute | solution.py:769
  59.0 5.2 %collective-permute-start.12 = (f32[32,32]{1,0:T(8,128)S(1)}, f32[32,32]{1,0:T(8,128)S(1)}, u32[]{:S(2)}, u32[]{:S(2)}) collective-permute-start(f32[32,32]{1,0:T(8,128)S(1)} %add_add_fusion.1), channel_id=1, source_target_pairs={{0,64},{1,65},{2,66},{3,67},{4,68},{5,69},{6,70},{7,71},{8,72},{9,... | collective-permute-start | bytes 12296 | tf_op jit(solution)/shard_map/ppermute | solution.py:769
  59.8 4.5 %collective-permute-start.11 = (f32[32,32]{1,0:T(8,128)S(1)}, f32[32,32]{1,0:T(8,128)S(1)}, u32[]{:S(2)}, u32[]{:S(2)}) collective-permute-start(f32[32,32]{1,0:T(8,128)S(1)} %add_add_fusion.1), channel_id=1, source_target_pairs={{0,32},{1,33},{2,34},{3,35},{4,36},{5,37},{6,38},{7,39},{8,40},{9,... | collective-permute-start | bytes 12296 | tf_op jit(solution)/shard_map/ppermute | solution.py:769

commit v8 on v7

--- a/solution.py
+++ b/solution.py
@@ -16,6 +16,7 @@
 LANES = 128
 ROWS = 3 * NZ
 SLOTS = 4
+GROUP = 4
 TAIL = 8 + 8 * F
 HIGH = lax.Precision.HIGHEST
 f32 = jnp.float32
@@ -628,7 +629,8 @@
     turned = lax.dot_general(
         identity, sums[32:64], (((1,), (1,)), ((), ())), precision=HIGH, preferred_element_type=f32
     )
-    sums_out[...] = sums[0:32] + sums[32:64] + turned
+    whole = sums[0:32] + sums[32:64] + turned
+    sums_out[...] = jnp.concatenate([whole[8 * i : 8 * i + 8] for i in range(4)], axis=1)
 
 
 def edges(below, above, edge_in, edge_tail, high_in, low_in, weights, mean_in, sums_in):
@@ -639,7 +641,7 @@
             parts,
             parts,
             jax.ShapeDtypeStruct(mean_in.shape, f32),
-            jax.ShapeDtypeStruct((32, 32), f32),
+            jax.ShapeDtypeStruct((8, LANES), f32),
         ),
         in_specs=[VMEM] * 9,
         out_specs=(VMEM,) * 4,
@@ -654,7 +656,8 @@
 
 
 def factor_and_map(sums, cell_count):
-    inner = sums * (1.0 / cell_count)
+    whole = jnp.concatenate([sums[:, 32 * i : 32 * i + 32] for i in range(4)], axis=0)
+    inner = whole * (1.0 / cell_count)
     row = lax.broadcasted_iota(jnp.int32, (M, 2 * M), 0)
     column = lax.broadcasted_iota(jnp.int32, (M, 2 * M), 1)
     update = jnp.where(
@@ -705,31 +708,30 @@
         maps[...] = spread_map(mapping)
         low_rows = lax.broadcasted_iota(jnp.int32, (M, 8, 256), 1) < 4
 
-        def put(z, slot):
-            return pltpu.make_async_copy(new.at[slot], out.at[:, z], sems.at[slot])
-
-        def level(z, carry):
-            slot = lax.rem(z, SLOTS)
-
-            @pl.when(z >= SLOTS)
-            def _():
-                put(z - SLOTS, slot).wait()
-
-            results = []
-            for i in (0, 4):
-                high, low = both(parts[i], parts[i + 2], z), both(parts[i + 1], parts[i + 3], z)
-                first = jnp.dot(maps[...], high, preferred_element_type=f32)
-                second = jnp.dot(maps[0:128, :], low, preferred_element_type=f32)
-                results.append((first[0:128] + first[128:256] + second).reshape(M, 8, 256))
-            inner, edge = results
-            new[slot, :, 0:8, :] = jnp.where(low_rows, edge, inner)
-            new[slot, :, 8:16, :] = jnp.where(low_rows, inner, edge)
-            put(z, slot).start()
-            return carry
-
-        lax.fori_loop(0, NZ, level, 0)
-        for z in range(NZ - SLOTS, NZ):
-            put(z, z % SLOTS).wait()
+        def put(group, slot):
+            return pltpu.make_async_copy(
+                new.at[slot], out.at[:, pl.ds(GROUP * group, GROUP)], sems.at[slot]
+            )
+
+        for group in range(NZ // GROUP):
+            slot = group % SLOTS
+            if group >= SLOTS:
+                put(group - SLOTS, slot).wait()
+            for k in range(GROUP):
+                z = GROUP * group + k
+                results = []
+                for i in (0, 4):
+                    high = both(parts[i], parts[i + 2], z)
+                    low = both(parts[i + 1], parts[i + 3], z)
+                    first = jnp.dot(maps[...], high, preferred_element_type=f32)
+                    second = jnp.dot(maps[0:128, :], low, preferred_element_type=f32)
+                    results.append((first[0:128] + first[128:256] + second).reshape(M, 8, 256))
+                inner, edge = results
+                new[slot, :, k, 0:8, :] = jnp.where(low_rows, edge, inner)
+                new[slot, :, k, 8:16, :] = jnp.where(low_rows, inner, edge)
+            put(group, slot).start()
+        for group in range(NZ // GROUP - SLOTS, NZ // GROUP):
+            put(group, group % SLOTS).wait()
 
     return apply_kernel
 
@@ -745,10 +747,10 @@
         out_specs=(ANY, VMEM),
         scratch_shapes=[
             pltpu.VMEM((256, 256), bf16),
-            pltpu.VMEM((SLOTS, M, BX, 256), f32),
+            pltpu.VMEM((SLOTS, M, GROUP, BX, 256), f32),
             pltpu.SemaphoreType.DMA((SLOTS,)),
         ],
-        compiler_params=params(12),
+        compiler_params=params(16),
         cost_estimate=cost(10**9, 13 * 10**6),
         name="apply",
     )(sums, *parts)

time: 72.4 us -> 69.5 us (0.960)
  Pallas kernels: 31.7 us -> 29.3 us
    pallas_call x1, Pallas kernels: 7.87 us -> 5.53 us  [apply_map(): pl.pallas_call(make_apply_kernel(cell_count), out_shape=(jax.ShapeDtypeSt...]
  transfers between devices with their start and end apart: 14 -> 14, of which waited for: 10 -> 10; matrix products, arithmetic and copies ran while one was open for 0% -> 0% of each run, Pallas kernels for 23% -> 24%
where the time goes in v8:
time: 69.5 us; the launch traced here: 69.3 us
  Pallas kernels  29.3 us (42%)
  starting transfers between devices  24.8 us (36%)
  waiting for transfers between devices  14.4 us (21%)
  between operations  0.72 us (1%)
    ppermute x10, starting transfers between devices, exchanged(): return lax.ppermute(value, axes, [(i, i ^ distance) for i in range(size)])  16.8 us
    pallas_call x1, Pallas kernels, interior(): pl.pallas_call(interior_kernel, out_shape=(parts, parts, jax.ShapeDtypeSt...  15 us
    ppermute x10, waiting for transfers between devices, exchanged(): return lax.ppermute(value, axes, [(i, i ^ distance) for i in range(size)])  12 us
    pallas_call x1, Pallas kernels, apply_map(): pl.pallas_call(make_apply_kernel(cell_count), out_shape=(jax.ShapeDtypeSt...  5.53 us
    ppermute x2, starting transfers between devices, onward(): return lax.ppermute(value, axis, [(i, i + 1) for i in range(size - 1)])  5.42 us
    pallas_call x1, Pallas kernels, edges(): pl.pallas_call(edge_kernel, out_shape=(parts, parts, jax.ShapeDtypeStruct...  3.85 us
    pallas_call x1, Pallas kernels, pack(): pl.pallas_call(pack_kernel, out_shape=(rows, rows, columns, columns, jax....  3.34 us
    ppermute x2, starting transfers between devices, backward(): return lax.ppermute(value, axis, [(i + 1, i) for i in range(size - 1)])  2.58 us
  transfers between devices with their start and end apart: 14, of which 10 were waited for; matrix products, arithmetic and copies ran while one was open for 0% of the time, Pallas kernels for 24%

profile of v8, /device:TPU:0, one launch (start us, length us, event | category | flops | bytes accessed | tf_op | source)
XLA Modules:
  0.0 69.3 jit_solution(17073020356380991475)
XLA Ops:
  0.6 3.3 %pack.1 = (f32[2,18,2,24,128]{4,3,2,1,0:T(8,128)S(1)}, f32[2,18,2,24,128]{4,3,2,1,0:T(8,128)S(1)}, f32[20,8,128]{2,1,0:T(8,128)S(1)}, f32[20,8,128]{2,1,0:T(8,128)S(1)}, f32[2,17,16,32,128]{4,3,2,1,0:T(8,128)S(1)}) custom-call(f32[16,16,16,256]{3,2,1,0:T(8,128)} %modes.1, f32[16,16,256]{2,1,0:T(8,128)} %mean.1, f32[16,16,256]{2,1,0:T(8,128)} %ve.3, ...), custom_call_target="tpu_custom_call" | custom-call | flops 10000000 | bytes 7000000 | tf_op jit(solution)/shard_map/pack/pallas_call | solution.py:175
  4.0 4.0 %collective-permute-start = (f32[2,18,2,24,128]{4,3,2,1,0:T(8,128)S(1)}, f32[2,18,2,24,128]{4,3,2,1,0:T(8,128)S(1)}, u32[]{:S(2)}, u32[]{:S(2)}) collective-permute-start(f32[2,18,2,24,128]{4,3,2,1,0:T(8,128)S(1)} %get-tuple-element.30), channel_id=1, source_target_pairs={{0,8},{8,16},{16,24},{24,32},{32,40},{40,48},{48,56},{56,64},{64,7... | collective-permute-start | bytes 2654216 | tf_op jit(solution)/shard_map/ppermute | solution.py:761
  7.9 1.3 %collective-permute-start.1 = (f32[2,18,2,24,128]{4,3,2,1,0:T(8,128)S(1)}, f32[2,18,2,24,128]{4,3,2,1,0:T(8,128)S(1)}, u32[]{:S(2)}, u32[]{:S(2)}) collective-permute-start(f32[2,18,2,24,128]{4,3,2,1,0:T(8,128)S(1)} %get-tuple-element.31), channel_id=1, source_target_pairs={{8,0},{16,8},{24,16},{32,24},{40,32},{48,40},{56,48},{64,56},{72,6... | collective-permute-start | bytes 2654216 | tf_op jit(solution)/shard_map/ppermute | solution.py:766
  9.2 1.5 %collective-permute-start.2 = (f32[20,8,128]{2,1,0:T(8,128)S(1)}, f32[20,8,128]{2,1,0:T(8,128)S(1)}, u32[]{:S(2)}, u32[]{:S(2)}) collective-permute-start(f32[20,8,128]{2,1,0:T(8,128)S(1)} %get-tuple-element.41.own_last), channel_id=1, source_target_pairs={{0,1},{1,2},{2,3},{3,4},{4,5},{5,6},{6,7},{8,9},{9,10},{10,11},{11... | collective-permute-start | bytes 245768 | tf_op jit(solution)/shard_map/ppermute | solution.py:761
  10.7 1.3 %collective-permute-start.3 = (f32[20,8,128]{2,1,0:T(8,128)S(1)}, f32[20,8,128]{2,1,0:T(8,128)S(1)}, u32[]{:S(2)}, u32[]{:S(2)}) collective-permute-start(f32[20,8,128]{2,1,0:T(8,128)S(1)} %get-tuple-element.42.own_first), channel_id=1, source_target_pairs={{1,0},{2,1},{3,2},{4,3},{5,4},{6,5},{7,6},{9,8},{10,9},{11,10},{12... | collective-permute-start | bytes 245768 | tf_op jit(solution)/shard_map/ppermute | solution.py:766
  12.0 1.6 %prepare.1 = (bf16[16,128,256]{2,1,0:T(8,128)(2,1)S(1)}, bf16[16,128,256]{2,1,0:T(8,128)(2,1)S(1)}, bf16[16,128,256]{2,1,0:T(8,128)(2,1)S(1)}, bf16[16,128,256]{...) custom-call(f32[2,17,16,32,128]{4,3,2,1,0:T(8,128)S(1)} %get-tuple-e, ...), custom_call_target="tpu_custom_call" | custom-call | flops 1000000 | bytes 1000000 | tf_op jit(solution)/shard_map/prepare/pallas_call | solution.py:322
  13.6 0.0 collective-permute-done.2.west
  13.6 1.9 %collective-permute-done.3.east = f32[20,8,128]{2,1,0:T(8,128)S(1)} collective-permute-done((f32[20,8,128]{2,1,0:T(8,128)S(1)}, f32[20,8,128]{2,1,0:T(8,128)S(1)}, u32[]{:S(2)}, u32[]{:S(2)}) %collective-permute-start.3) | collective-permute-done | bytes 81952 | tf_op jit(solution)/shard_map/ppermute | solution.py:766
  15.5 15.0 %interior.1 = (bf16[16,128,256]{2,1,0:T(8,128)(2,1)S(1)}, bf16[16,128,256]{2,1,0:T(8,128)(2,1)S(1)}, f32[16,2,128,128]{3,2,1,0:T(8,128)S(1)}, f32[2,16,6,8,128]{...) custom-call(f32[2,17,16,32,128]{4,3,2,1,0:T(8,128)S(1)} %get-tuple-element.32.X, ...), custom_call_target="tpu_custom_call" | custom-call | flops 1000000 | bytes 1000000 | tf_op jit(solution)/shard_map/interior/pallas_call | solution.py:518
  30.5 0.0 collective-permute-done.below
  30.5 0.5 collective-permute-done.1.above
  31.1 3.9 %edges.1 = (bf16[16,128,256]{2,1,0:T(8,128)(2,1)S(1)}, bf16[16,128,256]{2,1,0:T(8,128)(2,1)S(1)}, f32[16,16,256]{2,1,0:T(8,128)}, f32[8,128]{1,0:T(8,128)S(1)}) custom-call(f32[2,18,2,24,128]{4,3,2,1,0:T(8,128)S(1)} %collective-permute-done.below, f32[2,18,2,24,128]{4,3,2,1,0:T(8,128)S(1)} %collective-permute-done.1.above, ...), custom_call_target="tpu_custom_call" | custom-call | flops 1000000000 | bytes 10000000 | tf_op jit(solution)/shard_map/edges/pallas_call | solution.py:638
  34.9 2.9 %collective-permute-start.4 = (f32[8,128]{1,0:T(8,128)S(1)}, f32[8,128]{1,0:T(8,128)S(1)}, u32[]{:S(2)}, u32[]{:S(2)}) collective-permute-start(f32[8,128]{1,0:T(8,128)S(1)} %get-tuple-element.50), channel_id=1, source_target_pairs={{0,1},{1,0},{2,3},{3,2},{4,5},{5,4},{6,7},{7,6},{8,9},{9,8},{10,11... | collective-permute-start | bytes 12296 | tf_op jit(solution)/shard_map/ppermute | solution.py:771
  37.9 0.8 %collective-permute-done.4 = f32[8,128]{1,0:T(8,128)S(1)} collective-permute-done((f32[8,128]{1,0:T(8,128)S(1)}, f32[8,128]{1,0:T(8,128)S(1)}, u32[]{:S(2)}, u32[]{:S(2)}) %collective-permute-start.4) | collective-permute-done | bytes 4128 | tf_op jit(solution)/shard_map/ppermute | solution.py:771
  38.7 1.3 %collective-permute-start.7 = (f32[8,128]{1,0:T(8,128)S(1)}, f32[8,128]{1,0:T(8,128)S(1)}, u32[]{:S(2)}, u32[]{:S(2)}) collective-permute-start(f32[8,128]{1,0:T(8,128)S(1)} %add.30), channel_id=1, source_target_pairs={{0,6},{1,7},{2,4},{3,5},{4,2},{5,3},{6,0},{7,1},{8,14},{9,15},{10,... | collective-permute-start | bytes 12296 | tf_op jit(solution)/shard_map/ppermute | solution.py:771
  40.0 2.3 %collective-permute-start.6 = (f32[8,128]{1,0:T(8,128)S(1)}, f32[8,128]{1,0:T(8,128)S(1)}, u32[]{:S(2)}, u32[]{:S(2)}) collective-permute-start(f32[8,128]{1,0:T(8,128)S(1)} %add.30), channel_id=1, source_target_pairs={{0,4},{1,5},{2,6},{3,7},{4,0},{5,1},{6,2},{7,3},{8,12},{9,13},{10,... | collective-permute-start | bytes 12296 | tf_op jit(solution)/shard_map/ppermute | solution.py:771
  42.3 0.4 collective-permute-start.5
  42.8 0.7 %collective-permute-done.7 = f32[8,128]{1,0:T(8,128)S(1)} collective-permute-done((f32[8,128]{1,0:T(8,128)S(1)}, f32[8,128]{1,0:T(8,128)S(1)}, u32[]{:S(2)}, u32[]{:S(2)}) %collective-permute-start.7) | collective-permute-done | bytes 4128 | tf_op jit(solution)/shard_map/ppermute | solution.py:771
  43.5 1.6 %collective-permute-done.6 = f32[8,128]{1,0:T(8,128)S(1)} collective-permute-done((f32[8,128]{1,0:T(8,128)S(1)}, f32[8,128]{1,0:T(8,128)S(1)}, u32[]{:S(2)}, u32[]{:S(2)}) %collective-permute-start.6) | collective-permute-done | bytes 4128 | tf_op jit(solution)/shard_map/ppermute | solution.py:771
  45.1 0.8 %collective-permute-done.5 = f32[8,128]{1,0:T(8,128)S(1)} collective-permute-done((f32[8,128]{1,0:T(8,128)S(1)}, f32[8,128]{1,0:T(8,128)S(1)}, u32[]{:S(2)}, u32[]{:S(2)}) %collective-permute-start.5) | collective-permute-done | bytes 4128 | tf_op jit(solution)/shard_map/ppermute | solution.py:771
  45.9 4.7 %collective-permute-start.10 = (f32[8,128]{1,0:T(8,128)S(1)}, f32[8,128]{1,0:T(8,128)S(1)}, u32[]{:S(2)}, u32[]{:S(2)}) collective-permute-start(f32[8,128]{1,0:T(8,128)S(1)} %add_add_fusion.2), channel_id=1, source_target_pairs={{0,24},{1,25},{2,26},{3,27},{4,28},{5,29},{6,30},{7,31},{8,16},{9,... | collective-permute-start | bytes 12296 | tf_op jit(solution)/shard_map/ppermute | solution.py:771
  50.6 0.0 collective-permute-start.9
  50.7 0.9 %collective-permute-start.8 = (f32[8,128]{1,0:T(8,128)S(1)}, f32[8,128]{1,0:T(8,128)S(1)}, u32[]{:S(2)}, u32[]{:S(2)}) collective-permute-start(f32[8,128]{1,0:T(8,128)S(1)} %add_add_fusion.2), channel_id=1, source_target_pairs={{0,8},{1,9},{2,10},{3,11},{4,12},{5,13},{6,14},{7,15},{8,0},{9,1},... | collective-permute-start | bytes 12296 | tf_op jit(solution)/shard_map/ppermute | solution.py:771
  51.6 0.6 collective-permute-done.10
  52.2 3.5 %collective-permute-done.9 = f32[8,128]{1,0:T(8,128)S(1)} collective-permute-done((f32[8,128]{1,0:T(8,128)S(1)}, f32[8,128]{1,0:T(8,128)S(1)}, u32[]{:S(2)}, u32[]{:S(2)}) %collective-permute-start.9) | collective-permute-done | bytes 4128 | tf_op jit(solution)/shard_map/ppermute | solution.py:771
  55.8 0.0 collective-permute-done.8
  55.8 2.9 %collective-permute-start.13 = (f32[8,128]{1,0:T(8,128)S(1)}, f32[8,128]{1,0:T(8,128)S(1)}, u32[]{:S(2)}, u32[]{:S(2)}) collective-permute-start(f32[8,128]{1,0:T(8,128)S(1)} %add_add_fusion.1), channel_id=1, source_target_pairs={{0,96},{1,97},{2,98},{3,99},{4,100},{5,101},{6,102},{7,103},{8,104... | collective-permute-start | bytes 12296 | tf_op jit(solution)/shard_map/ppermute | solution.py:771
  58.7 0.8 %collective-permute-start.12 = (f32[8,128]{1,0:T(8,128)S(1)}, f32[8,128]{1,0:T(8,128)S(1)}, u32[]{:S(2)}, u32[]{:S(2)}) collective-permute-start(f32[8,128]{1,0:T(8,128)S(1)} %add_add_fusion.1), channel_id=1, source_target_pairs={{0,64},{1,65},{2,66},{3,67},{4,68},{5,69},{6,70},{7,71},{8,72},{9,... | collective-permute-start | bytes 12296 | tf_op jit(solution)/shard_map/ppermute | solution.py:771
  59.4 0.5 collective-permute-start.11
  59.9 0.7 %collective-permute-done.13 = f32[8,128]{1,0:T(8,128)S(1)} collective-permute-done((f32[8,128]{1,0:T(8,128)S(1)}, f32[8,128]{1,0:T(8,128)S(1)}, u32[]{:S(2)}, u32[]{:S(2)}) %collective-permute-start.13) | collective-permute-done | bytes 4128 | tf_op jit(solution)/shard_map/ppermute | solution.py:771
  60.7 3.1 %collective-permute-done.12 = f32[8,128]{1,0:T(8,128)S(1)} collective-permute-done((f32[8,128]{1,0:T(8,128)S(1)}, f32[8,128]{1,0:T(8,128)S(1)}, u32[]{:S(2)}, u32[]{:S(2)}) %collective-permute-start.12) | collective-permute-done | bytes 4128 | tf_op jit(solution)/shard_map/ppermute | solution.py:771
  63.8 0.0 collective-permute-done.11
  63.8 5.5 %apply.1 = (f32[16,16,16,256]{3,2,1,0:T(8,128)}, f32[16,16]{1,0:T(8,128)}) custom-call(f32[8,128]{1,0:T(8,128)S(1)} %add_add_fusion.sums, bf16[16,128,256]{2,1,0:T(8,128)(2,1)S(1)} %get-tuple-element.39.high_in.refs_0_, bf16[16,128,256]{2,1,0:T(8,128)(2,1)S(1)} %get-tuple-element.40.low_in.refs_1_, bf16[16,128,256]{2,1,0:T(8,128)(2,1)S(1)} %get-tuple-element.51.refs_2_, ...), custom_call_target="tpu_custom_call" | custom-call | flops 1000000000 | bytes 13000000 | tf_op jit(solution)/shard_map/apply/pallas_call | solution.py:740
  (4 shorter events, 0.0 us)
Async XLA Ops:
  4.0 26.5 %collective-permute-start = (f32[2,18,2,24,128]{4,3,2,1,0:T(8,128)S(1)}, f32[2,18,2,24,128]{4,3,2,1,0:T(8,128)S(1)}, u32[]{:S(2)}, u32[]{:S(2)}) collective-permute-start(f32[2,18,2,24,128]{4,3,2,1,0:T(8,128)S(1)} %get-tuple-element.30), channel_id=1, source_target_pairs={{0,8},{8,16},{16,24},{24,32},{32,40},{40,48},{48,56},{56,64},{64,7... | collective-permute-start | bytes 2654216 | tf_op jit(solution)/shard_map/ppermute | solution.py:761
  7.9 23.1 %collective-permute-start.1 = (f32[2,18,2,24,128]{4,3,2,1,0:T(8,128)S(1)}, f32[2,18,2,24,128]{4,3,2,1,0:T(8,128)S(1)}, u32[]{:S(2)}, u32[]{:S(2)}) collective-permute-start(f32[2,18,2,24,128]{4,3,2,1,0:T(8,128)S(1)} %get-tuple-element.31), channel_id=1, source_target_pairs={{8,0},{16,8},{24,16},{32,24},{40,32},{48,40},{56,48},{64,56},{72,6... | collective-permute-start | bytes 2654216 | tf_op jit(solution)/shard_map/ppermute | solution.py:766
  9.2 4.4 %collective-permute-start.2 = (f32[20,8,128]{2,1,0:T(8,128)S(1)}, f32[20,8,128]{2,1,0:T(8,128)S(1)}, u32[]{:S(2)}, u32[]{:S(2)}) collective-permute-start(f32[20,8,128]{2,1,0:T(8,128)S(1)} %get-tuple-element.41.own_last), channel_id=1, source_target_pairs={{0,1},{1,2},{2,3},{3,4},{4,5},{5,6},{6,7},{8,9},{9,10},{10,11},{11... | collective-permute-start | bytes 245768 | tf_op jit(solution)/shard_map/ppermute | solution.py:761
  10.7 4.8 %collective-permute-start.3 = (f32[20,8,128]{2,1,0:T(8,128)S(1)}, f32[20,8,128]{2,1,0:T(8,128)S(1)}, u32[]{:S(2)}, u32[]{:S(2)}) collective-permute-start(f32[20,8,128]{2,1,0:T(8,128)S(1)} %get-tuple-element.42.own_first), channel_id=1, source_target_pairs={{1,0},{2,1},{3,2},{4,3},{5,4},{6,5},{7,6},{9,8},{10,9},{11,10},{12... | collective-permute-start | bytes 245768 | tf_op jit(solution)/shard_map/ppermute | solution.py:766
  34.9 3.7 %collective-permute-start.4 = (f32[8,128]{1,0:T(8,128)S(1)}, f32[8,128]{1,0:T(8,128)S(1)}, u32[]{:S(2)}, u32[]{:S(2)}) collective-permute-start(f32[8,128]{1,0:T(8,128)S(1)} %get-tuple-element.50), channel_id=1, source_target_pairs={{0,1},{1,0},{2,3},{3,2},{4,5},{5,4},{6,7},{7,6},{8,9},{9,8},{10,11... | collective-permute-start | bytes 12296 | tf_op jit(solution)/shard_map/ppermute | solution.py:771
  38.7 4.8 %collective-permute-start.7 = (f32[8,128]{1,0:T(8,128)S(1)}, f32[8,128]{1,0:T(8,128)S(1)}, u32[]{:S(2)}, u32[]{:S(2)}) collective-permute-start(f32[8,128]{1,0:T(8,128)S(1)} %add.30), channel_id=1, source_target_pairs={{0,6},{1,7},{2,4},{3,5},{4,2},{5,3},{6,0},{7,1},{8,14},{9,15},{10,... | collective-permute-start | bytes 12296 | tf_op jit(solution)/shard_map/ppermute | solution.py:771
  40.0 5.1 %collective-permute-start.6 = (f32[8,128]{1,0:T(8,128)S(1)}, f32[8,128]{1,0:T(8,128)S(1)}, u32[]{:S(2)}, u32[]{:S(2)}) collective-permute-start(f32[8,128]{1,0:T(8,128)S(1)} %add.30), channel_id=1, source_target_pairs={{0,4},{1,5},{2,6},{3,7},{4,0},{5,1},{6,2},{7,3},{8,12},{9,13},{10,... | collective-permute-start | bytes 12296 | tf_op jit(solution)/shard_map/ppermute | solution.py:771
  42.3 3.6 %collective-permute-start.5 = (f32[8,128]{1,0:T(8,128)S(1)}, f32[8,128]{1,0:T(8,128)S(1)}, u32[]{:S(2)}, u32[]{:S(2)}) collective-permute-start(f32[8,128]{1,0:T(8,128)S(1)} %add.30), channel_id=1, source_target_pairs={{0,2},{1,3},{2,0},{3,1},{4,6},{5,7},{6,4},{7,5},{8,10},{9,11},{10,... | collective-permute-start | bytes 12296 | tf_op jit(solution)/shard_map/ppermute | solution.py:771
  45.9 6.3 %collective-permute-start.10 = (f32[8,128]{1,0:T(8,128)S(1)}, f32[8,128]{1,0:T(8,128)S(1)}, u32[]{:S(2)}, u32[]{:S(2)}) collective-permute-start(f32[8,128]{1,0:T(8,128)S(1)} %add_add_fusion.2), channel_id=1, source_target_pairs={{0,24},{1,25},{2,26},{3,27},{4,28},{5,29},{6,30},{7,31},{8,16},{9,... | collective-permute-start | bytes 12296 | tf_op jit(solution)/shard_map/ppermute | solution.py:771
  50.6 5.1 %collective-permute-start.9 = (f32[8,128]{1,0:T(8,128)S(1)}, f32[8,128]{1,0:T(8,128)S(1)}, u32[]{:S(2)}, u32[]{:S(2)}) collective-permute-start(f32[8,128]{1,0:T(8,128)S(1)} %add_add_fusion.2), channel_id=1, source_target_pairs={{0,16},{1,17},{2,18},{3,19},{4,20},{5,21},{6,22},{7,23},{8,24},{9,... | collective-permute-start | bytes 12296 | tf_op jit(solution)/shard_map/ppermute | solution.py:771
  50.7 5.1 %collective-permute-start.8 = (f32[8,128]{1,0:T(8,128)S(1)}, f32[8,128]{1,0:T(8,128)S(1)}, u32[]{:S(2)}, u32[]{:S(2)}) collective-permute-start(f32[8,128]{1,0:T(8,128)S(1)} %add_add_fusion.2), channel_id=1, source_target_pairs={{0,8},{1,9},{2,10},{3,11},{4,12},{5,13},{6,14},{7,15},{8,0},{9,1},... | collective-permute-start | bytes 12296 | tf_op jit(solution)/shard_map/ppermute | solution.py:771
  55.8 4.9 %collective-permute-start.13 = (f32[8,128]{1,0:T(8,128)S(1)}, f32[8,128]{1,0:T(8,128)S(1)}, u32[]{:S(2)}, u32[]{:S(2)}) collective-permute-start(f32[8,128]{1,0:T(8,128)S(1)} %add_add_fusion.1), channel_id=1, source_target_pairs={{0,96},{1,97},{2,98},{3,99},{4,100},{5,101},{6,102},{7,103},{8,104... | collective-permute-start | bytes 12296 | tf_op jit(solution)/shard_map/ppermute | solution.py:771
  58.7 5.1 %collective-permute-start.12 = (f32[8,128]{1,0:T(8,128)S(1)}, f32[8,128]{1,0:T(8,128)S(1)}, u32[]{:S(2)}, u32[]{:S(2)}) collective-permute-start(f32[8,128]{1,0:T(8,128)S(1)} %add_add_fusion.1), channel_id=1, source_target_pairs={{0,64},{1,65},{2,66},{3,67},{4,68},{5,69},{6,70},{7,71},{8,72},{9,... | collective-permute-start | bytes 12296 | tf_op jit(solution)/shard_map/ppermute | solution.py:771
  59.4 4.4 %collective-permute-start.11 = (f32[8,128]{1,0:T(8,128)S(1)}, f32[8,128]{1,0:T(8,128)S(1)}, u32[]{:S(2)}, u32[]{:S(2)}) collective-permute-start(f32[8,128]{1,0:T(8,128)S(1)} %add_add_fusion.1), channel_id=1, source_target_pairs={{0,32},{1,33},{2,34},{3,35},{4,36},{5,37},{6,38},{7,39},{8,40},{9,... | collective-permute-start | bytes 12296 | tf_op jit(solution)/shard_map/ppermute | solution.py:771

commit v9 on v8

--- a/solution.py
+++ b/solution.py
@@ -15,8 +15,8 @@
 BX = 16
 LANES = 128
 ROWS = 3 * NZ
-SLOTS = 4
-GROUP = 4
+SLOTS = 16
+GROUP = 1
 TAIL = 8 + 8 * F
 HIGH = lax.Precision.HIGHEST
 f32 = jnp.float32
@@ -508,7 +508,7 @@
         low_out[z] = low
         return carry
 
-    lax.fori_loop(0, NZ, level, 0)
+    lax.fori_loop(0, NZ, level, 0, unroll=2)
     add_products(acc, joined(high_in, high_out), joined(low_in, low_out))
     sums_out[...] = field_sums(acc)
 
@@ -673,14 +673,12 @@
     column_g = lax.broadcasted_iota(jnp.int32, (M, M), 1)
     left, right = gram, update
     for j in range(M):
-        pivot = jnp.sum(jnp.where(column_g == j, left, 0.0), axis=1, keepdims=True)
-        scale = 1.0 / jnp.sqrt(pivot[j : j + 1, :])
-        left_row = left[j : j + 1, :] * scale
-        right_row = right[j : j + 1, :] * scale
-        share = jnp.where(row_g[:, 0:1] > j, pivot * scale, 0.0)
-        left = jnp.where(row_g == j, left_row, left - share * left_row)
-        right = jnp.where(row == j, right_row, right - share * right_row)
-    return jnp.where(column_g >= row_g, left, 0.0), right
+        share = jnp.where(row_g[:, 0:1] > j, left[:, j : j + 1] / left[j : j + 1, j : j + 1], 0.0)
+        left = left - share * left[j : j + 1, :]
+        right = right - share * right[j : j + 1, :]
+    diagonal = jnp.sum(jnp.where(column_g == row_g, left, 0.0), axis=1, keepdims=True)
+    scale = 1.0 / jnp.sqrt(diagonal)
+    return jnp.where(column_g >= row_g, left * scale, 0.0), right * scale
 
 
 def spread_map(mapping):

time: 69.5 us -> 68.9 us (level)
  Pallas kernels: 29.3 us -> 28.6 us
where the time goes in v9:
time: 68.9 us; the launch traced here: 68.7 us
  Pallas kernels  28.6 us (42%)
  starting transfers between devices  24.6 us (36%)
  waiting for transfers between devices  14.7 us (21%)
  between operations  0.72 us (1%)
    ppermute x10, starting transfers between devices, exchanged(): return lax.ppermute(value, axes, [(i, i ^ distance) for i in range(size)])  16.6 us
    pallas_call x1, Pallas kernels, interior(): pl.pallas_call(interior_kernel, out_shape=(parts, parts, jax.ShapeDtypeSt...  14.8 us
    ppermute x10, waiting for transfers between devices, exchanged(): return lax.ppermute(value, axes, [(i, i ^ distance) for i in range(size)])  12 us
    ppermute x2, starting transfers between devices, onward(): return lax.ppermute(value, axis, [(i, i + 1) for i in range(size - 1)])  5.42 us
    pallas_call x1, Pallas kernels, apply_map(): pl.pallas_call(make_apply_kernel(cell_count), out_shape=(jax.ShapeDtypeSt...  5.12 us
    pallas_call x1, Pallas kernels, edges(): pl.pallas_call(edge_kernel, out_shape=(parts, parts, jax.ShapeDtypeStruct...  3.85 us
    pallas_call x1, Pallas kernels, pack(): pl.pallas_call(pack_kernel, out_shape=(rows, rows, columns, columns, jax....  3.34 us
    ppermute x2, waiting for transfers between devices, backward(): return lax.ppermute(value, axis, [(i + 1, i) for i in range(size - 1)])  2.7 us
  transfers between devices with their start and end apart: 14, of which 10 were waited for; matrix products, arithmetic and copies ran while one was open for 0% of the time, Pallas kernels for 24%

profile of v9, /device:TPU:0, one launch (start us, length us, event | category | flops | bytes accessed | tf_op | source)
XLA Modules:
  0.0 68.7 jit_solution(7332796395500840466)
XLA Ops:
  0.6 3.3 %pack.1 = (f32[2,18,2,24,128]{4,3,2,1,0:T(8,128)S(1)}, f32[2,18,2,24,128]{4,3,2,1,0:T(8,128)S(1)}, f32[20,8,128]{2,1,0:T(8,128)S(1)}, f32[20,8,128]{2,1,0:T(8,128)S(1)}, f32[2,17,16,32,128]{4,3,2,1,0:T(8,128)S(1)}) custom-call(f32[16,16,16,256]{3,2,1,0:T(8,128)} %modes.1, f32[16,16,256]{2,1,0:T(8,128)} %mean.1, f32[16,16,256]{2,1,0:T(8,128)} %ve.3, ...), custom_call_target="tpu_custom_call" | custom-call | flops 10000000 | bytes 7000000 | tf_op jit(solution)/shard_map/pack/pallas_call | solution.py:175
  4.0 4.0 %collective-permute-start = (f32[2,18,2,24,128]{4,3,2,1,0:T(8,128)S(1)}, f32[2,18,2,24,128]{4,3,2,1,0:T(8,128)S(1)}, u32[]{:S(2)}, u32[]{:S(2)}) collective-permute-start(f32[2,18,2,24,128]{4,3,2,1,0:T(8,128)S(1)} %get-tuple-element.30), channel_id=1, source_target_pairs={{0,8},{8,16},{16,24},{24,32},{32,40},{40,48},{48,56},{56,64},{64,7... | collective-permute-start | bytes 2654216 | tf_op jit(solution)/shard_map/ppermute | solution.py:759
  7.9 1.3 %collective-permute-start.1 = (f32[2,18,2,24,128]{4,3,2,1,0:T(8,128)S(1)}, f32[2,18,2,24,128]{4,3,2,1,0:T(8,128)S(1)}, u32[]{:S(2)}, u32[]{:S(2)}) collective-permute-start(f32[2,18,2,24,128]{4,3,2,1,0:T(8,128)S(1)} %get-tuple-element.31), channel_id=1, source_target_pairs={{8,0},{16,8},{24,16},{32,24},{40,32},{48,40},{56,48},{64,56},{72,6... | collective-permute-start | bytes 2654216 | tf_op jit(solution)/shard_map/ppermute | solution.py:764
  9.2 1.5 %collective-permute-start.2 = (f32[20,8,128]{2,1,0:T(8,128)S(1)}, f32[20,8,128]{2,1,0:T(8,128)S(1)}, u32[]{:S(2)}, u32[]{:S(2)}) collective-permute-start(f32[20,8,128]{2,1,0:T(8,128)S(1)} %get-tuple-element.41.own_last), channel_id=1, source_target_pairs={{0,1},{1,2},{2,3},{3,4},{4,5},{5,6},{6,7},{8,9},{9,10},{10,11},{11... | collective-permute-start | bytes 245768 | tf_op jit(solution)/shard_map/ppermute | solution.py:759
  10.7 1.3 %collective-permute-start.3 = (f32[20,8,128]{2,1,0:T(8,128)S(1)}, f32[20,8,128]{2,1,0:T(8,128)S(1)}, u32[]{:S(2)}, u32[]{:S(2)}) collective-permute-start(f32[20,8,128]{2,1,0:T(8,128)S(1)} %get-tuple-element.42.own_first), channel_id=1, source_target_pairs={{1,0},{2,1},{3,2},{4,3},{5,4},{6,5},{7,6},{9,8},{10,9},{11,10},{12... | collective-permute-start | bytes 245768 | tf_op jit(solution)/shard_map/ppermute | solution.py:764
  12.0 1.6 %prepare.1 = (bf16[16,128,256]{2,1,0:T(8,128)(2,1)S(1)}, bf16[16,128,256]{2,1,0:T(8,128)(2,1)S(1)}, bf16[16,128,256]{2,1,0:T(8,128)(2,1)S(1)}, bf16[16,128,256]{...) custom-call(f32[2,17,16,32,128]{4,3,2,1,0:T(8,128)S(1)} %get-tuple-e, ...), custom_call_target="tpu_custom_call" | custom-call | flops 1000000 | bytes 1000000 | tf_op jit(solution)/shard_map/prepare/pallas_call | solution.py:322
  13.6 0.0 collective-permute-done.2.west
  13.6 1.9 %collective-permute-done.3.east = f32[20,8,128]{2,1,0:T(8,128)S(1)} collective-permute-done((f32[20,8,128]{2,1,0:T(8,128)S(1)}, f32[20,8,128]{2,1,0:T(8,128)S(1)}, u32[]{:S(2)}, u32[]{:S(2)}) %collective-permute-start.3) | collective-permute-done | bytes 81952 | tf_op jit(solution)/shard_map/ppermute | solution.py:764
  15.5 14.8 %interior.1 = (bf16[16,128,256]{2,1,0:T(8,128)(2,1)S(1)}, bf16[16,128,256]{2,1,0:T(8,128)(2,1)S(1)}, f32[16,2,128,128]{3,2,1,0:T(8,128)S(1)}, f32[2,16,6,8,128]{...) custom-call(f32[2,17,16,32,128]{4,3,2,1,0:T(8,128)S(1)} %get-tuple-element.32.X, ...), custom_call_target="tpu_custom_call" | custom-call | flops 1000000 | bytes 1000000 | tf_op jit(solution)/shard_map/interior/pallas_call | solution.py:518
  30.3 0.0 collective-permute-done.below
  30.3 0.8 %collective-permute-done.1.above = f32[2,18,2,24,128]{4,3,2,1,0:T(8,128)S(1)} collective-permute-done((f32[2,18,2,24,128]{4,3,2,1,0:T(8,128)S(1)}, f32[2,18,2,24,128]{4,3,2,1,0:T(8,128)S(1)}, u32[]{:S(2)}, u32[]{:S(2)}) %collective-permute-start.1) | collective-permute-done | bytes 884768 | tf_op jit(solution)/shard_map/ppermute | solution.py:764
  31.1 3.9 %edges.1 = (bf16[16,128,256]{2,1,0:T(8,128)(2,1)S(1)}, bf16[16,128,256]{2,1,0:T(8,128)(2,1)S(1)}, f32[16,16,256]{2,1,0:T(8,128)}, f32[8,128]{1,0:T(8,128)S(1)}) custom-call(f32[2,18,2,24,128]{4,3,2,1,0:T(8,128)S(1)} %collective-permute-done.below, f32[2,18,2,24,128]{4,3,2,1,0:T(8,128)S(1)} %collective-permute-done.1.above, ...), custom_call_target="tpu_custom_call" | custom-call | flops 1000000000 | bytes 10000000 | tf_op jit(solution)/shard_map/edges/pallas_call | solution.py:638
  34.9 2.7 %collective-permute-start.4 = (f32[8,128]{1,0:T(8,128)S(1)}, f32[8,128]{1,0:T(8,128)S(1)}, u32[]{:S(2)}, u32[]{:S(2)}) collective-permute-start(f32[8,128]{1,0:T(8,128)S(1)} %get-tuple-element.50), channel_id=1, source_target_pairs={{0,1},{1,0},{2,3},{3,2},{4,5},{5,4},{6,7},{7,6},{8,9},{9,8},{10,11... | collective-permute-start | bytes 12296 | tf_op jit(solution)/shard_map/ppermute | solution.py:769
  37.6 0.8 %collective-permute-done.4 = f32[8,128]{1,0:T(8,128)S(1)} collective-permute-done((f32[8,128]{1,0:T(8,128)S(1)}, f32[8,128]{1,0:T(8,128)S(1)}, u32[]{:S(2)}, u32[]{:S(2)}) %collective-permute-start.4) | collective-permute-done | bytes 4128 | tf_op jit(solution)/shard_map/ppermute | solution.py:769
  38.4 1.3 %collective-permute-start.7 = (f32[8,128]{1,0:T(8,128)S(1)}, f32[8,128]{1,0:T(8,128)S(1)}, u32[]{:S(2)}, u32[]{:S(2)}) collective-permute-start(f32[8,128]{1,0:T(8,128)S(1)} %add.30), channel_id=1, source_target_pairs={{0,6},{1,7},{2,4},{3,5},{4,2},{5,3},{6,0},{7,1},{8,14},{9,15},{10,... | collective-permute-start | bytes 12296 | tf_op jit(solution)/shard_map/ppermute | solution.py:769
  39.8 2.3 %collective-permute-start.6 = (f32[8,128]{1,0:T(8,128)S(1)}, f32[8,128]{1,0:T(8,128)S(1)}, u32[]{:S(2)}, u32[]{:S(2)}) collective-permute-start(f32[8,128]{1,0:T(8,128)S(1)} %add.30), channel_id=1, source_target_pairs={{0,4},{1,5},{2,6},{3,7},{4,0},{5,1},{6,2},{7,3},{8,12},{9,13},{10,... | collective-permute-start | bytes 12296 | tf_op jit(solution)/shard_map/ppermute | solution.py:769
  42.1 0.4 collective-permute-start.5
  42.5 0.7 %collective-permute-done.7 = f32[8,128]{1,0:T(8,128)S(1)} collective-permute-done((f32[8,128]{1,0:T(8,128)S(1)}, f32[8,128]{1,0:T(8,128)S(1)}, u32[]{:S(2)}, u32[]{:S(2)}) %collective-permute-start.7) | collective-permute-done | bytes 4128 | tf_op jit(solution)/shard_map/ppermute | solution.py:769
  43.3 1.6 %collective-permute-done.6 = f32[8,128]{1,0:T(8,128)S(1)} collective-permute-done((f32[8,128]{1,0:T(8,128)S(1)}, f32[8,128]{1,0:T(8,128)S(1)}, u32[]{:S(2)}, u32[]{:S(2)}) %collective-permute-start.6) | collective-permute-done | bytes 4128 | tf_op jit(solution)/shard_map/ppermute | solution.py:769
  44.9 0.8 %collective-permute-done.5 = f32[8,128]{1,0:T(8,128)S(1)} collective-permute-done((f32[8,128]{1,0:T(8,128)S(1)}, f32[8,128]{1,0:T(8,128)S(1)}, u32[]{:S(2)}, u32[]{:S(2)}) %collective-permute-start.5) | collective-permute-done | bytes 4128 | tf_op jit(solution)/shard_map/ppermute | solution.py:769
  45.7 4.7 %collective-permute-start.10 = (f32[8,128]{1,0:T(8,128)S(1)}, f32[8,128]{1,0:T(8,128)S(1)}, u32[]{:S(2)}, u32[]{:S(2)}) collective-permute-start(f32[8,128]{1,0:T(8,128)S(1)} %add_add_fusion.2), channel_id=1, source_target_pairs={{0,24},{1,25},{2,26},{3,27},{4,28},{5,29},{6,30},{7,31},{8,16},{9,... | collective-permute-start | bytes 12296 | tf_op jit(solution)/shard_map/ppermute | solution.py:769
  50.4 0.0 collective-permute-start.9
  50.4 0.9 %collective-permute-start.8 = (f32[8,128]{1,0:T(8,128)S(1)}, f32[8,128]{1,0:T(8,128)S(1)}, u32[]{:S(2)}, u32[]{:S(2)}) collective-permute-start(f32[8,128]{1,0:T(8,128)S(1)} %add_add_fusion.2), channel_id=1, source_target_pairs={{0,8},{1,9},{2,10},{3,11},{4,12},{5,13},{6,14},{7,15},{8,0},{9,1},... | collective-permute-start | bytes 12296 | tf_op jit(solution)/shard_map/ppermute | solution.py:769
  51.4 0.6 collective-permute-done.10
  52.0 3.5 %collective-permute-done.9 = f32[8,128]{1,0:T(8,128)S(1)} collective-permute-done((f32[8,128]{1,0:T(8,128)S(1)}, f32[8,128]{1,0:T(8,128)S(1)}, u32[]{:S(2)}, u32[]{:S(2)}) %collective-permute-start.9) | collective-permute-done | bytes 4128 | tf_op jit(solution)/shard_map/ppermute | solution.py:769
  55.5 0.0 collective-permute-done.8
  55.5 2.9 %collective-permute-start.13 = (f32[8,128]{1,0:T(8,128)S(1)}, f32[8,128]{1,0:T(8,128)S(1)}, u32[]{:S(2)}, u32[]{:S(2)}) collective-permute-start(f32[8,128]{1,0:T(8,128)S(1)} %add_add_fusion.1), channel_id=1, source_target_pairs={{0,96},{1,97},{2,98},{3,99},{4,100},{5,101},{6,102},{7,103},{8,104... | collective-permute-start | bytes 12296 | tf_op jit(solution)/shard_map/ppermute | solution.py:769
  58.4 0.7 %collective-permute-start.12 = (f32[8,128]{1,0:T(8,128)S(1)}, f32[8,128]{1,0:T(8,128)S(1)}, u32[]{:S(2)}, u32[]{:S(2)}) collective-permute-start(f32[8,128]{1,0:T(8,128)S(1)} %add_add_fusion.1), channel_id=1, source_target_pairs={{0,64},{1,65},{2,66},{3,67},{4,68},{5,69},{6,70},{7,71},{8,72},{9,... | collective-permute-start | bytes 12296 | tf_op jit(solution)/shard_map/ppermute | solution.py:769
  59.2 0.5 collective-permute-start.11
  59.7 0.7 %collective-permute-done.13 = f32[8,128]{1,0:T(8,128)S(1)} collective-permute-done((f32[8,128]{1,0:T(8,128)S(1)}, f32[8,128]{1,0:T(8,128)S(1)}, u32[]{:S(2)}, u32[]{:S(2)}) %collective-permute-start.13) | collective-permute-done | bytes 4128 | tf_op jit(solution)/shard_map/ppermute | solution.py:769
  60.4 3.1 %collective-permute-done.12 = f32[8,128]{1,0:T(8,128)S(1)} collective-permute-done((f32[8,128]{1,0:T(8,128)S(1)}, f32[8,128]{1,0:T(8,128)S(1)}, u32[]{:S(2)}, u32[]{:S(2)}) %collective-permute-start.12) | collective-permute-done | bytes 4128 | tf_op jit(solution)/shard_map/ppermute | solution.py:769
  63.5 0.0 collective-permute-done.11
  63.5 5.1 %apply.1 = (f32[16,16,16,256]{3,2,1,0:T(8,128)}, f32[16,16]{1,0:T(8,128)}) custom-call(f32[8,128]{1,0:T(8,128)S(1)} %add_add_fusion.sums, bf16[16,128,256]{2,1,0:T(8,128)(2,1)S(1)} %get-tuple-element.39.high_in.refs_0_, bf16[16,128,256]{2,1,0:T(8,128)(2,1)S(1)} %get-tuple-element.40.low_in.refs_1_, bf16[16,128,256]{2,1,0:T(8,128)(2,1)S(1)} %get-tuple-element.51.refs_2_, ...), custom_call_target="tpu_custom_call" | custom-call | flops 1000000000 | bytes 13000000 | tf_op jit(solution)/shard_map/apply/pallas_call | solution.py:738
  (4 shorter events, 0.0 us)
Async XLA Ops:
  4.0 26.3 %collective-permute-start = (f32[2,18,2,24,128]{4,3,2,1,0:T(8,128)S(1)}, f32[2,18,2,24,128]{4,3,2,1,0:T(8,128)S(1)}, u32[]{:S(2)}, u32[]{:S(2)}) collective-permute-start(f32[2,18,2,24,128]{4,3,2,1,0:T(8,128)S(1)} %get-tuple-element.30), channel_id=1, source_target_pairs={{0,8},{8,16},{16,24},{24,32},{32,40},{40,48},{48,56},{56,64},{64,7... | collective-permute-start | bytes 2654216 | tf_op jit(solution)/shard_map/ppermute | solution.py:759
  7.9 23.1 %collective-permute-start.1 = (f32[2,18,2,24,128]{4,3,2,1,0:T(8,128)S(1)}, f32[2,18,2,24,128]{4,3,2,1,0:T(8,128)S(1)}, u32[]{:S(2)}, u32[]{:S(2)}) collective-permute-start(f32[2,18,2,24,128]{4,3,2,1,0:T(8,128)S(1)} %get-tuple-element.31), channel_id=1, source_target_pairs={{8,0},{16,8},{24,16},{32,24},{40,32},{48,40},{56,48},{64,56},{72,6... | collective-permute-start | bytes 2654216 | tf_op jit(solution)/shard_map/ppermute | solution.py:764
  9.2 4.4 %collective-permute-start.2 = (f32[20,8,128]{2,1,0:T(8,128)S(1)}, f32[20,8,128]{2,1,0:T(8,128)S(1)}, u32[]{:S(2)}, u32[]{:S(2)}) collective-permute-start(f32[20,8,128]{2,1,0:T(8,128)S(1)} %get-tuple-element.41.own_last), channel_id=1, source_target_pairs={{0,1},{1,2},{2,3},{3,4},{4,5},{5,6},{6,7},{8,9},{9,10},{10,11},{11... | collective-permute-start | bytes 245768 | tf_op jit(solution)/shard_map/ppermute | solution.py:759
  10.7 4.8 %collective-permute-start.3 = (f32[20,8,128]{2,1,0:T(8,128)S(1)}, f32[20,8,128]{2,1,0:T(8,128)S(1)}, u32[]{:S(2)}, u32[]{:S(2)}) collective-permute-start(f32[20,8,128]{2,1,0:T(8,128)S(1)} %get-tuple-element.42.own_first), channel_id=1, source_target_pairs={{1,0},{2,1},{3,2},{4,3},{5,4},{6,5},{7,6},{9,8},{10,9},{11,10},{12... | collective-permute-start | bytes 245768 | tf_op jit(solution)/shard_map/ppermute | solution.py:764
  34.9 3.5 %collective-permute-start.4 = (f32[8,128]{1,0:T(8,128)S(1)}, f32[8,128]{1,0:T(8,128)S(1)}, u32[]{:S(2)}, u32[]{:S(2)}) collective-permute-start(f32[8,128]{1,0:T(8,128)S(1)} %get-tuple-element.50), channel_id=1, source_target_pairs={{0,1},{1,0},{2,3},{3,2},{4,5},{5,4},{6,7},{7,6},{8,9},{9,8},{10,11... | collective-permute-start | bytes 12296 | tf_op jit(solution)/shard_map/ppermute | solution.py:769
  38.4 4.8 %collective-permute-start.7 = (f32[8,128]{1,0:T(8,128)S(1)}, f32[8,128]{1,0:T(8,128)S(1)}, u32[]{:S(2)}, u32[]{:S(2)}) collective-permute-start(f32[8,128]{1,0:T(8,128)S(1)} %add.30), channel_id=1, source_target_pairs={{0,6},{1,7},{2,4},{3,5},{4,2},{5,3},{6,0},{7,1},{8,14},{9,15},{10,... | collective-permute-start | bytes 12296 | tf_op jit(solution)/shard_map/ppermute | solution.py:769
  39.8 5.1 %collective-permute-start.6 = (f32[8,128]{1,0:T(8,128)S(1)}, f32[8,128]{1,0:T(8,128)S(1)}, u32[]{:S(2)}, u32[]{:S(2)}) collective-permute-start(f32[8,128]{1,0:T(8,128)S(1)} %add.30), channel_id=1, source_target_pairs={{0,4},{1,5},{2,6},{3,7},{4,0},{5,1},{6,2},{7,3},{8,12},{9,13},{10,... | collective-permute-start | bytes 12296 | tf_op jit(solution)/shard_map/ppermute | solution.py:769
  42.1 3.6 %collective-permute-start.5 = (f32[8,128]{1,0:T(8,128)S(1)}, f32[8,128]{1,0:T(8,128)S(1)}, u32[]{:S(2)}, u32[]{:S(2)}) collective-permute-start(f32[8,128]{1,0:T(8,128)S(1)} %add.30), channel_id=1, source_target_pairs={{0,2},{1,3},{2,0},{3,1},{4,6},{5,7},{6,4},{7,5},{8,10},{9,11},{10,... | collective-permute-start | bytes 12296 | tf_op jit(solution)/shard_map/ppermute | solution.py:769
  45.7 6.3 %collective-permute-start.10 = (f32[8,128]{1,0:T(8,128)S(1)}, f32[8,128]{1,0:T(8,128)S(1)}, u32[]{:S(2)}, u32[]{:S(2)}) collective-permute-start(f32[8,128]{1,0:T(8,128)S(1)} %add_add_fusion.2), channel_id=1, source_target_pairs={{0,24},{1,25},{2,26},{3,27},{4,28},{5,29},{6,30},{7,31},{8,16},{9,... | collective-permute-start | bytes 12296 | tf_op jit(solution)/shard_map/ppermute | solution.py:769
  50.4 5.1 %collective-permute-start.9 = (f32[8,128]{1,0:T(8,128)S(1)}, f32[8,128]{1,0:T(8,128)S(1)}, u32[]{:S(2)}, u32[]{:S(2)}) collective-permute-start(f32[8,128]{1,0:T(8,128)S(1)} %add_add_fusion.2), channel_id=1, source_target_pairs={{0,16},{1,17},{2,18},{3,19},{4,20},{5,21},{6,22},{7,23},{8,24},{9,... | collective-permute-start | bytes 12296 | tf_op jit(solution)/shard_map/ppermute | solution.py:769
  50.4 5.1 %collective-permute-start.8 = (f32[8,128]{1,0:T(8,128)S(1)}, f32[8,128]{1,0:T(8,128)S(1)}, u32[]{:S(2)}, u32[]{:S(2)}) collective-permute-start(f32[8,128]{1,0:T(8,128)S(1)} %add_add_fusion.2), channel_id=1, source_target_pairs={{0,8},{1,9},{2,10},{3,11},{4,12},{5,13},{6,14},{7,15},{8,0},{9,1},... | collective-permute-start | bytes 12296 | tf_op jit(solution)/shard_map/ppermute | solution.py:769
  55.5 4.9 %collective-permute-start.13 = (f32[8,128]{1,0:T(8,128)S(1)}, f32[8,128]{1,0:T(8,128)S(1)}, u32[]{:S(2)}, u32[]{:S(2)}) collective-permute-start(f32[8,128]{1,0:T(8,128)S(1)} %add_add_fusion.1), channel_id=1, source_target_pairs={{0,96},{1,97},{2,98},{3,99},{4,100},{5,101},{6,102},{7,103},{8,104... | collective-permute-start | bytes 12296 | tf_op jit(solution)/shard_map/ppermute | solution.py:769
  58.4 5.1 %collective-permute-start.12 = (f32[8,128]{1,0:T(8,128)S(1)}, f32[8,128]{1,0:T(8,128)S(1)}, u32[]{:S(2)}, u32[]{:S(2)}) collective-permute-start(f32[8,128]{1,0:T(8,128)S(1)} %add_add_fusion.1), channel_id=1, source_target_pairs={{0,64},{1,65},{2,66},{3,67},{4,68},{5,69},{6,70},{7,71},{8,72},{9,... | collective-permute-start | bytes 12296 | tf_op jit(solution)/shard_map/ppermute | solution.py:769
  59.2 4.4 %collective-permute-start.11 = (f32[8,128]{1,0:T(8,128)S(1)}, f32[8,128]{1,0:T(8,128)S(1)}, u32[]{:S(2)}, u32[]{:S(2)}) collective-permute-start(f32[8,128]{1,0:T(8,128)S(1)} %add_add_fusion.1), channel_id=1, source_target_pairs={{0,32},{1,33},{2,34},{3,35},{4,36},{5,37},{6,38},{7,39},{8,40},{9,... | collective-permute-start | bytes 12296 | tf_op jit(solution)/shard_map/ppermute | solution.py:769

commit v10 on v9

--- a/solution.py
+++ b/solution.py
@@ -621,7 +621,7 @@
             )
         return carry
 
-    lax.fori_loop(0, 2, group, 0)
+    lax.fori_loop(0, 2, group, 0, unroll=True)
     sums = sums_in[...] + field_sums(acc)
     identity = (
         lax.broadcasted_iota(jnp.int32, (32, 32), 0) == lax.broadcasted_iota(jnp.int32, (32, 32), 1)

time: 68.9 us -> 68.4 us (level)
  no operation moved by 1% of the time
where the time goes in v10:
time: 68.4 us; the launch traced here: 68.2 us
  Pallas kernels  28.2 us (41%)
  starting transfers between devices  24.6 us (36%)
  waiting for transfers between devices  14.7 us (21%)
  between operations  0.72 us (1%)
    ppermute x10, starting transfers between devices, exchanged(): return lax.ppermute(value, axes, [(i, i ^ distance) for i in range(size)])  16.5 us
    pallas_call x1, Pallas kernels, interior(): pl.pallas_call(interior_kernel, out_shape=(parts, parts, jax.ShapeDtypeSt...  14.8 us
    ppermute x10, waiting for transfers between devices, exchanged(): return lax.ppermute(value, axes, [(i, i ^ distance) for i in range(size)])  12 us
    ppermute x2, starting transfers between devices, onward(): return lax.ppermute(value, axis, [(i, i + 1) for i in range(size - 1)])  5.42 us
    pallas_call x1, Pallas kernels, apply_map(): pl.pallas_call(make_apply_kernel(cell_count), out_shape=(jax.ShapeDtypeSt...  5.12 us
    pallas_call x1, Pallas kernels, edges(): pl.pallas_call(edge_kernel, out_shape=(parts, parts, jax.ShapeDtypeStruct...  3.43 us
    pallas_call x1, Pallas kernels, pack(): pl.pallas_call(pack_kernel, out_shape=(rows, rows, columns, columns, jax....  3.34 us
    ppermute x2, waiting for transfers between devices, backward(): return lax.ppermute(value, axis, [(i + 1, i) for i in range(size - 1)])  2.7 us
  transfers between devices with their start and end apart: 14, of which 10 were waited for; matrix products, arithmetic and copies ran while one was open for 0% of the time, Pallas kernels for 24%

profile of v10, /device:TPU:0, one launch (start us, length us, event | category | flops | bytes accessed | tf_op | source)
XLA Modules:
  0.0 68.2 jit_solution(17416457902697391338)
XLA Ops:
  0.6 3.3 %pack.1 = (f32[2,18,2,24,128]{4,3,2,1,0:T(8,128)S(1)}, f32[2,18,2,24,128]{4,3,2,1,0:T(8,128)S(1)}, f32[20,8,128]{2,1,0:T(8,128)S(1)}, f32[20,8,128]{2,1,0:T(8,128)S(1)}, f32[2,17,16,32,128]{4,3,2,1,0:T(8,128)S(1)}) custom-call(f32[16,16,16,256]{3,2,1,0:T(8,128)} %modes.1, f32[16,16,256]{2,1,0:T(8,128)} %mean.1, f32[16,16,256]{2,1,0:T(8,128)} %ve.3, ...), custom_call_target="tpu_custom_call" | custom-call | flops 10000000 | bytes 7000000 | tf_op jit(solution)/shard_map/pack/pallas_call | solution.py:175
  4.0 4.0 %collective-permute-start = (f32[2,18,2,24,128]{4,3,2,1,0:T(8,128)S(1)}, f32[2,18,2,24,128]{4,3,2,1,0:T(8,128)S(1)}, u32[]{:S(2)}, u32[]{:S(2)}) collective-permute-start(f32[2,18,2,24,128]{4,3,2,1,0:T(8,128)S(1)} %get-tuple-element.30), channel_id=1, source_target_pairs={{0,8},{8,16},{16,24},{24,32},{32,40},{40,48},{48,56},{56,64},{64,7... | collective-permute-start | bytes 2654216 | tf_op jit(solution)/shard_map/ppermute | solution.py:759
  7.9 1.3 %collective-permute-start.1 = (f32[2,18,2,24,128]{4,3,2,1,0:T(8,128)S(1)}, f32[2,18,2,24,128]{4,3,2,1,0:T(8,128)S(1)}, u32[]{:S(2)}, u32[]{:S(2)}) collective-permute-start(f32[2,18,2,24,128]{4,3,2,1,0:T(8,128)S(1)} %get-tuple-element.31), channel_id=1, source_target_pairs={{8,0},{16,8},{24,16},{32,24},{40,32},{48,40},{56,48},{64,56},{72,6... | collective-permute-start | bytes 2654216 | tf_op jit(solution)/shard_map/ppermute | solution.py:764
  9.2 1.5 %collective-permute-start.2 = (f32[20,8,128]{2,1,0:T(8,128)S(1)}, f32[20,8,128]{2,1,0:T(8,128)S(1)}, u32[]{:S(2)}, u32[]{:S(2)}) collective-permute-start(f32[20,8,128]{2,1,0:T(8,128)S(1)} %get-tuple-element.41.own_last), channel_id=1, source_target_pairs={{0,1},{1,2},{2,3},{3,4},{4,5},{5,6},{6,7},{8,9},{9,10},{10,11},{11... | collective-permute-start | bytes 245768 | tf_op jit(solution)/shard_map/ppermute | solution.py:759
  10.7 1.3 %collective-permute-start.3 = (f32[20,8,128]{2,1,0:T(8,128)S(1)}, f32[20,8,128]{2,1,0:T(8,128)S(1)}, u32[]{:S(2)}, u32[]{:S(2)}) collective-permute-start(f32[20,8,128]{2,1,0:T(8,128)S(1)} %get-tuple-element.42.own_first), channel_id=1, source_target_pairs={{1,0},{2,1},{3,2},{4,3},{5,4},{6,5},{7,6},{9,8},{10,9},{11,10},{12... | collective-permute-start | bytes 245768 | tf_op jit(solution)/shard_map/ppermute | solution.py:764
  12.0 1.6 %prepare.1 = (bf16[16,128,256]{2,1,0:T(8,128)(2,1)S(1)}, bf16[16,128,256]{2,1,0:T(8,128)(2,1)S(1)}, bf16[16,128,256]{2,1,0:T(8,128)(2,1)S(1)}, bf16[16,128,256]{...) custom-call(f32[2,17,16,32,128]{4,3,2,1,0:T(8,128)S(1)} %get-tuple-e, ...), custom_call_target="tpu_custom_call" | custom-call | flops 1000000 | bytes 1000000 | tf_op jit(solution)/shard_map/prepare/pallas_call | solution.py:322
  13.6 0.0 collective-permute-done.2.west
  13.6 1.9 %collective-permute-done.3.east = f32[20,8,128]{2,1,0:T(8,128)S(1)} collective-permute-done((f32[20,8,128]{2,1,0:T(8,128)S(1)}, f32[20,8,128]{2,1,0:T(8,128)S(1)}, u32[]{:S(2)}, u32[]{:S(2)}) %collective-permute-start.3) | collective-permute-done | bytes 81952 | tf_op jit(solution)/shard_map/ppermute | solution.py:764
  15.5 14.8 %interior.1 = (bf16[16,128,256]{2,1,0:T(8,128)(2,1)S(1)}, bf16[16,128,256]{2,1,0:T(8,128)(2,1)S(1)}, f32[16,2,128,128]{3,2,1,0:T(8,128)S(1)}, f32[2,16,6,8,128]{...) custom-call(f32[2,17,16,32,128]{4,3,2,1,0:T(8,128)S(1)} %get-tuple-element.32.X, ...), custom_call_target="tpu_custom_call" | custom-call | flops 1000000 | bytes 1000000 | tf_op jit(solution)/shard_map/interior/pallas_call | solution.py:518
  30.3 0.0 collective-permute-done.below
  30.3 0.8 %collective-permute-done.1.above = f32[2,18,2,24,128]{4,3,2,1,0:T(8,128)S(1)} collective-permute-done((f32[2,18,2,24,128]{4,3,2,1,0:T(8,128)S(1)}, f32[2,18,2,24,128]{4,3,2,1,0:T(8,128)S(1)}, u32[]{:S(2)}, u32[]{:S(2)}) %collective-permute-start.1) | collective-permute-done | bytes 884768 | tf_op jit(solution)/shard_map/ppermute | solution.py:764
  31.1 3.4 %edges.1 = (bf16[16,128,256]{2,1,0:T(8,128)(2,1)S(1)}, bf16[16,128,256]{2,1,0:T(8,128)(2,1)S(1)}, f32[16,16,256]{2,1,0:T(8,128)}, f32[8,128]{1,0:T(8,128)S(1)}) custom-call(f32[2,18,2,24,128]{4,3,2,1,0:T(8,128)S(1)} %collective-permute-done.below, f32[2,18,2,24,128]{4,3,2,1,0:T(8,128)S(1)} %collective-permute-done.1.above, ...), custom_call_target="tpu_custom_call" | custom-call | flops 1000000000 | bytes 10000000 | tf_op jit(solution)/shard_map/edges/pallas_call | solution.py:638
  34.5 2.6 %collective-permute-start.4 = (f32[8,128]{1,0:T(8,128)S(1)}, f32[8,128]{1,0:T(8,128)S(1)}, u32[]{:S(2)}, u32[]{:S(2)}) collective-permute-start(f32[8,128]{1,0:T(8,128)S(1)} %get-tuple-element.50), channel_id=1, source_target_pairs={{0,1},{1,0},{2,3},{3,2},{4,5},{5,4},{6,7},{7,6},{8,9},{9,8},{10,11... | collective-permute-start | bytes 12296 | tf_op jit(solution)/shard_map/ppermute | solution.py:769
  37.1 0.8 %collective-permute-done.4 = f32[8,128]{1,0:T(8,128)S(1)} collective-permute-done((f32[8,128]{1,0:T(8,128)S(1)}, f32[8,128]{1,0:T(8,128)S(1)}, u32[]{:S(2)}, u32[]{:S(2)}) %collective-permute-start.4) | collective-permute-done | bytes 4128 | tf_op jit(solution)/shard_map/ppermute | solution.py:769
  38.0 1.3 %collective-permute-start.7 = (f32[8,128]{1,0:T(8,128)S(1)}, f32[8,128]{1,0:T(8,128)S(1)}, u32[]{:S(2)}, u32[]{:S(2)}) collective-permute-start(f32[8,128]{1,0:T(8,128)S(1)} %add.30), channel_id=1, source_target_pairs={{0,6},{1,7},{2,4},{3,5},{4,2},{5,3},{6,0},{7,1},{8,14},{9,15},{10,... | collective-permute-start | bytes 12296 | tf_op jit(solution)/shard_map/ppermute | solution.py:769
  39.3 2.3 %collective-permute-start.6 = (f32[8,128]{1,0:T(8,128)S(1)}, f32[8,128]{1,0:T(8,128)S(1)}, u32[]{:S(2)}, u32[]{:S(2)}) collective-permute-start(f32[8,128]{1,0:T(8,128)S(1)} %add.30), channel_id=1, source_target_pairs={{0,4},{1,5},{2,6},{3,7},{4,0},{5,1},{6,2},{7,3},{8,12},{9,13},{10,... | collective-permute-start | bytes 12296 | tf_op jit(solution)/shard_map/ppermute | solution.py:769
  41.6 0.4 collective-permute-start.5
  42.1 0.7 %collective-permute-done.7 = f32[8,128]{1,0:T(8,128)S(1)} collective-permute-done((f32[8,128]{1,0:T(8,128)S(1)}, f32[8,128]{1,0:T(8,128)S(1)}, u32[]{:S(2)}, u32[]{:S(2)}) %collective-permute-start.7) | collective-permute-done | bytes 4128 | tf_op jit(solution)/shard_map/ppermute | solution.py:769
  42.8 1.6 %collective-permute-done.6 = f32[8,128]{1,0:T(8,128)S(1)} collective-permute-done((f32[8,128]{1,0:T(8,128)S(1)}, f32[8,128]{1,0:T(8,128)S(1)}, u32[]{:S(2)}, u32[]{:S(2)}) %collective-permute-start.6) | collective-permute-done | bytes 4128 | tf_op jit(solution)/shard_map/ppermute | solution.py:769
  44.4 0.8 %collective-permute-done.5 = f32[8,128]{1,0:T(8,128)S(1)} collective-permute-done((f32[8,128]{1,0:T(8,128)S(1)}, f32[8,128]{1,0:T(8,128)S(1)}, u32[]{:S(2)}, u32[]{:S(2)}) %collective-permute-start.5) | collective-permute-done | bytes 4128 | tf_op jit(solution)/shard_map/ppermute | solution.py:769
  45.2 4.7 %collective-permute-start.10 = (f32[8,128]{1,0:T(8,128)S(1)}, f32[8,128]{1,0:T(8,128)S(1)}, u32[]{:S(2)}, u32[]{:S(2)}) collective-permute-start(f32[8,128]{1,0:T(8,128)S(1)} %add_add_fusion.2), channel_id=1, source_target_pairs={{0,24},{1,25},{2,26},{3,27},{4,28},{5,29},{6,30},{7,31},{8,16},{9,... | collective-permute-start | bytes 12296 | tf_op jit(solution)/shard_map/ppermute | solution.py:769
  49.9 0.0 collective-permute-start.9
  49.9 0.9 %collective-permute-start.8 = (f32[8,128]{1,0:T(8,128)S(1)}, f32[8,128]{1,0:T(8,128)S(1)}, u32[]{:S(2)}, u32[]{:S(2)}) collective-permute-start(f32[8,128]{1,0:T(8,128)S(1)} %add_add_fusion.2), channel_id=1, source_target_pairs={{0,8},{1,9},{2,10},{3,11},{4,12},{5,13},{6,14},{7,15},{8,0},{9,1},... | collective-permute-start | bytes 12296 | tf_op jit(solution)/shard_map/ppermute | solution.py:769
  50.9 0.6 collective-permute-done.10
  51.5 3.5 %collective-permute-done.9 = f32[8,128]{1,0:T(8,128)S(1)} collective-permute-done((f32[8,128]{1,0:T(8,128)S(1)}, f32[8,128]{1,0:T(8,128)S(1)}, u32[]{:S(2)}, u32[]{:S(2)}) %collective-permute-start.9) | collective-permute-done | bytes 4128 | tf_op jit(solution)/shard_map/ppermute | solution.py:769
  55.0 0.0 collective-permute-done.8
  55.1 2.9 %collective-permute-start.13 = (f32[8,128]{1,0:T(8,128)S(1)}, f32[8,128]{1,0:T(8,128)S(1)}, u32[]{:S(2)}, u32[]{:S(2)}) collective-permute-start(f32[8,128]{1,0:T(8,128)S(1)} %add_add_fusion.1), channel_id=1, source_target_pairs={{0,96},{1,97},{2,98},{3,99},{4,100},{5,101},{6,102},{7,103},{8,104... | collective-permute-start | bytes 12296 | tf_op jit(solution)/shard_map/ppermute | solution.py:769
  57.9 0.7 %collective-permute-start.12 = (f32[8,128]{1,0:T(8,128)S(1)}, f32[8,128]{1,0:T(8,128)S(1)}, u32[]{:S(2)}, u32[]{:S(2)}) collective-permute-start(f32[8,128]{1,0:T(8,128)S(1)} %add_add_fusion.1), channel_id=1, source_target_pairs={{0,64},{1,65},{2,66},{3,67},{4,68},{5,69},{6,70},{7,71},{8,72},{9,... | collective-permute-start | bytes 12296 | tf_op jit(solution)/shard_map/ppermute | solution.py:769
  58.7 0.5 collective-permute-start.11
  59.2 0.7 %collective-permute-done.13 = f32[8,128]{1,0:T(8,128)S(1)} collective-permute-done((f32[8,128]{1,0:T(8,128)S(1)}, f32[8,128]{1,0:T(8,128)S(1)}, u32[]{:S(2)}, u32[]{:S(2)}) %collective-permute-start.13) | collective-permute-done | bytes 4128 | tf_op jit(solution)/shard_map/ppermute | solution.py:769
  60.0 3.1 %collective-permute-done.12 = f32[8,128]{1,0:T(8,128)S(1)} collective-permute-done((f32[8,128]{1,0:T(8,128)S(1)}, f32[8,128]{1,0:T(8,128)S(1)}, u32[]{:S(2)}, u32[]{:S(2)}) %collective-permute-start.12) | collective-permute-done | bytes 4128 | tf_op jit(solution)/shard_map/ppermute | solution.py:769
  63.1 0.0 collective-permute-done.11
  63.1 5.1 %apply.1 = (f32[16,16,16,256]{3,2,1,0:T(8,128)}, f32[16,16]{1,0:T(8,128)}) custom-call(f32[8,128]{1,0:T(8,128)S(1)} %add_add_fusion.sums, bf16[16,128,256]{2,1,0:T(8,128)(2,1)S(1)} %get-tuple-element.39.high_in.refs_0_, bf16[16,128,256]{2,1,0:T(8,128)(2,1)S(1)} %get-tuple-element.40.low_in.refs_1_, bf16[16,128,256]{2,1,0:T(8,128)(2,1)S(1)} %get-tuple-element.51.refs_2_, ...), custom_call_target="tpu_custom_call" | custom-call | flops 1000000000 | bytes 13000000 | tf_op jit(solution)/shard_map/apply/pallas_call | solution.py:738
  (4 shorter events, 0.0 us)
Async XLA Ops:
  4.0 26.3 %collective-permute-start = (f32[2,18,2,24,128]{4,3,2,1,0:T(8,128)S(1)}, f32[2,18,2,24,128]{4,3,2,1,0:T(8,128)S(1)}, u32[]{:S(2)}, u32[]{:S(2)}) collective-permute-start(f32[2,18,2,24,128]{4,3,2,1,0:T(8,128)S(1)} %get-tuple-element.30), channel_id=1, source_target_pairs={{0,8},{8,16},{16,24},{24,32},{32,40},{40,48},{48,56},{56,64},{64,7... | collective-permute-start | bytes 2654216 | tf_op jit(solution)/shard_map/ppermute | solution.py:759
  7.9 23.1 %collective-permute-start.1 = (f32[2,18,2,24,128]{4,3,2,1,0:T(8,128)S(1)}, f32[2,18,2,24,128]{4,3,2,1,0:T(8,128)S(1)}, u32[]{:S(2)}, u32[]{:S(2)}) collective-permute-start(f32[2,18,2,24,128]{4,3,2,1,0:T(8,128)S(1)} %get-tuple-element.31), channel_id=1, source_target_pairs={{8,0},{16,8},{24,16},{32,24},{40,32},{48,40},{56,48},{64,56},{72,6... | collective-permute-start | bytes 2654216 | tf_op jit(solution)/shard_map/ppermute | solution.py:764
  9.2 4.4 %collective-permute-start.2 = (f32[20,8,128]{2,1,0:T(8,128)S(1)}, f32[20,8,128]{2,1,0:T(8,128)S(1)}, u32[]{:S(2)}, u32[]{:S(2)}) collective-permute-start(f32[20,8,128]{2,1,0:T(8,128)S(1)} %get-tuple-element.41.own_last), channel_id=1, source_target_pairs={{0,1},{1,2},{2,3},{3,4},{4,5},{5,6},{6,7},{8,9},{9,10},{10,11},{11... | collective-permute-start | bytes 245768 | tf_op jit(solution)/shard_map/ppermute | solution.py:759
  10.7 4.8 %collective-permute-start.3 = (f32[20,8,128]{2,1,0:T(8,128)S(1)}, f32[20,8,128]{2,1,0:T(8,128)S(1)}, u32[]{:S(2)}, u32[]{:S(2)}) collective-permute-start(f32[20,8,128]{2,1,0:T(8,128)S(1)} %get-tuple-element.42.own_first), channel_id=1, source_target_pairs={{1,0},{2,1},{3,2},{4,3},{5,4},{6,5},{7,6},{9,8},{10,9},{11,10},{12... | collective-permute-start | bytes 245768 | tf_op jit(solution)/shard_map/ppermute | solution.py:764
  34.5 3.5 %collective-permute-start.4 = (f32[8,128]{1,0:T(8,128)S(1)}, f32[8,128]{1,0:T(8,128)S(1)}, u32[]{:S(2)}, u32[]{:S(2)}) collective-permute-start(f32[8,128]{1,0:T(8,128)S(1)} %get-tuple-element.50), channel_id=1, source_target_pairs={{0,1},{1,0},{2,3},{3,2},{4,5},{5,4},{6,7},{7,6},{8,9},{9,8},{10,11... | collective-permute-start | bytes 12296 | tf_op jit(solution)/shard_map/ppermute | solution.py:769
  38.0 4.8 %collective-permute-start.7 = (f32[8,128]{1,0:T(8,128)S(1)}, f32[8,128]{1,0:T(8,128)S(1)}, u32[]{:S(2)}, u32[]{:S(2)}) collective-permute-start(f32[8,128]{1,0:T(8,128)S(1)} %add.30), channel_id=1, source_target_pairs={{0,6},{1,7},{2,4},{3,5},{4,2},{5,3},{6,0},{7,1},{8,14},{9,15},{10,... | collective-permute-start | bytes 12296 | tf_op jit(solution)/shard_map/ppermute | solution.py:769
  39.3 5.1 %collective-permute-start.6 = (f32[8,128]{1,0:T(8,128)S(1)}, f32[8,128]{1,0:T(8,128)S(1)}, u32[]{:S(2)}, u32[]{:S(2)}) collective-permute-start(f32[8,128]{1,0:T(8,128)S(1)} %add.30), channel_id=1, source_target_pairs={{0,4},{1,5},{2,6},{3,7},{4,0},{5,1},{6,2},{7,3},{8,12},{9,13},{10,... | collective-permute-start | bytes 12296 | tf_op jit(solution)/shard_map/ppermute | solution.py:769
  41.6 3.6 %collective-permute-start.5 = (f32[8,128]{1,0:T(8,128)S(1)}, f32[8,128]{1,0:T(8,128)S(1)}, u32[]{:S(2)}, u32[]{:S(2)}) collective-permute-start(f32[8,128]{1,0:T(8,128)S(1)} %add.30), channel_id=1, source_target_pairs={{0,2},{1,3},{2,0},{3,1},{4,6},{5,7},{6,4},{7,5},{8,10},{9,11},{10,... | collective-permute-start | bytes 12296 | tf_op jit(solution)/shard_map/ppermute | solution.py:769
  45.2 6.3 %collective-permute-start.10 = (f32[8,128]{1,0:T(8,128)S(1)}, f32[8,128]{1,0:T(8,128)S(1)}, u32[]{:S(2)}, u32[]{:S(2)}) collective-permute-start(f32[8,128]{1,0:T(8,128)S(1)} %add_add_fusion.2), channel_id=1, source_target_pairs={{0,24},{1,25},{2,26},{3,27},{4,28},{5,29},{6,30},{7,31},{8,16},{9,... | collective-permute-start | bytes 12296 | tf_op jit(solution)/shard_map/ppermute | solution.py:769
  49.9 5.1 %collective-permute-start.9 = (f32[8,128]{1,0:T(8,128)S(1)}, f32[8,128]{1,0:T(8,128)S(1)}, u32[]{:S(2)}, u32[]{:S(2)}) collective-permute-start(f32[8,128]{1,0:T(8,128)S(1)} %add_add_fusion.2), channel_id=1, source_target_pairs={{0,16},{1,17},{2,18},{3,19},{4,20},{5,21},{6,22},{7,23},{8,24},{9,... | collective-permute-start | bytes 12296 | tf_op jit(solution)/shard_map/ppermute | solution.py:769
  49.9 5.1 %collective-permute-start.8 = (f32[8,128]{1,0:T(8,128)S(1)}, f32[8,128]{1,0:T(8,128)S(1)}, u32[]{:S(2)}, u32[]{:S(2)}) collective-permute-start(f32[8,128]{1,0:T(8,128)S(1)} %add_add_fusion.2), channel_id=1, source_target_pairs={{0,8},{1,9},{2,10},{3,11},{4,12},{5,13},{6,14},{7,15},{8,0},{9,1},... | collective-permute-start | bytes 12296 | tf_op jit(solution)/shard_map/ppermute | solution.py:769
  55.1 4.9 %collective-permute-start.13 = (f32[8,128]{1,0:T(8,128)S(1)}, f32[8,128]{1,0:T(8,128)S(1)}, u32[]{:S(2)}, u32[]{:S(2)}) collective-permute-start(f32[8,128]{1,0:T(8,128)S(1)} %add_add_fusion.1), channel_id=1, source_target_pairs={{0,96},{1,97},{2,98},{3,99},{4,100},{5,101},{6,102},{7,103},{8,104... | collective-permute-start | bytes 12296 | tf_op jit(solution)/shard_map/ppermute | solution.py:769
  57.9 5.1 %collective-permute-start.12 = (f32[8,128]{1,0:T(8,128)S(1)}, f32[8,128]{1,0:T(8,128)S(1)}, u32[]{:S(2)}, u32[]{:S(2)}) collective-permute-start(f32[8,128]{1,0:T(8,128)S(1)} %add_add_fusion.1), channel_id=1, source_target_pairs={{0,64},{1,65},{2,66},{3,67},{4,68},{5,69},{6,70},{7,71},{8,72},{9,... | collective-permute-start | bytes 12296 | tf_op jit(solution)/shard_map/ppermute | solution.py:769
  58.7 4.4 %collective-permute-start.11 = (f32[8,128]{1,0:T(8,128)S(1)}, f32[8,128]{1,0:T(8,128)S(1)}, u32[]{:S(2)}, u32[]{:S(2)}) collective-permute-start(f32[8,128]{1,0:T(8,128)S(1)} %add_add_fusion.1), channel_id=1, source_target_pairs={{0,32},{1,33},{2,34},{3,35},{4,36},{5,37},{6,38},{7,39},{8,40},{9,... | collective-permute-start | bytes 12296 | tf_op jit(solution)/shard_map/ppermute | solution.py:769

commit v11 on v10

--- a/solution.py
+++ b/solution.py
@@ -298,7 +298,7 @@
         high_edge[z], low_edge[z] = split(Z[1])
         return carry
 
-    lax.fori_loop(0, NZ, level, 0, unroll=2)
+    lax.fori_loop(0, NZ, level, 0, unroll=4)
     for copy in copies:
         copy.wait()
     for half in range(2):
@@ -508,7 +508,7 @@
         low_out[z] = low
         return carry
 
-    lax.fori_loop(0, NZ, level, 0, unroll=2)
+    lax.fori_loop(0, NZ, level, 0, unroll=4)
     add_products(acc, joined(high_in, high_out), joined(low_in, low_out))
     sums_out[...] = field_sums(acc)
 
@@ -799,7 +799,7 @@
         below, above, edge, edge_tail, high_xe, low_xe, weights, mean_part, sums_i
     )
     sums = sums + exchanged(sums, axes, 1)
-    for first in (2, 8, 32):
+    for first in (8, 32, 2):
         near, far, both = (exchanged(sums, axes, first * i) for i in (1, 2, 3))
         sums = (sums + near) + (far + both)
     cell_count = float(NZ * BX * 256 * lax.axis_size("gx") * lax.axis_size("gy"))

time: 68.4 us -> 68.8 us (level)
  no operation moved by 1% of the time
where the time goes in v11:
time: 68.8 us; the launch traced here: 68.6 us
  Pallas kernels  28.2 us (41%)
  starting transfers between devices  24.7 us (36%)
  waiting for transfers between devices  14.8 us (22%)
  between operations  0.88 us (1%)
    ppermute x10, starting transfers between devices, exchanged(): return lax.ppermute(value, axes, [(i, i ^ distance) for i in range(size)])  16.7 us
    pallas_call x1, Pallas kernels, interior(): pl.pallas_call(interior_kernel, out_shape=(parts, parts, jax.ShapeDtypeSt...  14.7 us
    ppermute x10, waiting for transfers between devices, exchanged(): return lax.ppermute(value, axes, [(i, i ^ distance) for i in range(size)])  12.1 us
    ppermute x2, starting transfers between devices, onward(): return lax.ppermute(value, axis, [(i, i + 1) for i in range(size - 1)])  5.42 us
    pallas_call x1, Pallas kernels, apply_map(): pl.pallas_call(make_apply_kernel(cell_count), out_shape=(jax.ShapeDtypeSt...  5.12 us
    pallas_call x1, Pallas kernels, edges(): pl.pallas_call(edge_kernel, out_shape=(parts, parts, jax.ShapeDtypeStruct...  3.43 us
    pallas_call x1, Pallas kernels, pack(): pl.pallas_call(pack_kernel, out_shape=(rows, rows, columns, columns, jax....  3.34 us
    ppermute x2, waiting for transfers between devices, backward(): return lax.ppermute(value, axis, [(i + 1, i) for i in range(size - 1)])  2.75 us
  transfers between devices with their start and end apart: 14, of which 10 were waited for; matrix products, arithmetic and copies ran while one was open for 0% of the time, Pallas kernels for 24%

profile of v11, /device:TPU:0, one launch (start us, length us, event | category | flops | bytes accessed | tf_op | source)
XLA Modules:
  0.0 68.6 jit_solution(4008383135610392649)
XLA Ops:
  0.6 3.3 %pack.1 = (f32[2,18,2,24,128]{4,3,2,1,0:T(8,128)S(1)}, f32[2,18,2,24,128]{4,3,2,1,0:T(8,128)S(1)}, f32[20,8,128]{2,1,0:T(8,128)S(1)}, f32[20,8,128]{2,1,0:T(8,128)S(1)}, f32[2,17,16,32,128]{4,3,2,1,0:T(8,128)S(1)}) custom-call(f32[16,16,16,256]{3,2,1,0:T(8,128)} %modes.1, f32[16,16,256]{2,1,0:T(8,128)} %mean.1, f32[16,16,256]{2,1,0:T(8,128)} %ve.3, ...), custom_call_target="tpu_custom_call" | custom-call | flops 10000000 | bytes 7000000 | tf_op jit(solution)/shard_map/pack/pallas_call | solution.py:175
  4.0 4.0 %collective-permute-start = (f32[2,18,2,24,128]{4,3,2,1,0:T(8,128)S(1)}, f32[2,18,2,24,128]{4,3,2,1,0:T(8,128)S(1)}, u32[]{:S(2)}, u32[]{:S(2)}) collective-permute-start(f32[2,18,2,24,128]{4,3,2,1,0:T(8,128)S(1)} %get-tuple-element.30), channel_id=1, source_target_pairs={{0,8},{8,16},{16,24},{24,32},{32,40},{40,48},{48,56},{56,64},{64,7... | collective-permute-start | bytes 2654216 | tf_op jit(solution)/shard_map/ppermute | solution.py:759
  7.9 1.3 %collective-permute-start.1 = (f32[2,18,2,24,128]{4,3,2,1,0:T(8,128)S(1)}, f32[2,18,2,24,128]{4,3,2,1,0:T(8,128)S(1)}, u32[]{:S(2)}, u32[]{:S(2)}) collective-permute-start(f32[2,18,2,24,128]{4,3,2,1,0:T(8,128)S(1)} %get-tuple-element.31), channel_id=1, source_target_pairs={{8,0},{16,8},{24,16},{32,24},{40,32},{48,40},{56,48},{64,56},{72,6... | collective-permute-start | bytes 2654216 | tf_op jit(solution)/shard_map/ppermute | solution.py:764
  9.2 1.5 %collective-permute-start.2 = (f32[20,8,128]{2,1,0:T(8,128)S(1)}, f32[20,8,128]{2,1,0:T(8,128)S(1)}, u32[]{:S(2)}, u32[]{:S(2)}) collective-permute-start(f32[20,8,128]{2,1,0:T(8,128)S(1)} %get-tuple-element.41.own_last), channel_id=1, source_target_pairs={{0,1},{1,2},{2,3},{3,4},{4,5},{5,6},{6,7},{8,9},{9,10},{10,11},{11... | collective-permute-start | bytes 245768 | tf_op jit(solution)/shard_map/ppermute | solution.py:759
  10.7 1.3 %collective-permute-start.3 = (f32[20,8,128]{2,1,0:T(8,128)S(1)}, f32[20,8,128]{2,1,0:T(8,128)S(1)}, u32[]{:S(2)}, u32[]{:S(2)}) collective-permute-start(f32[20,8,128]{2,1,0:T(8,128)S(1)} %get-tuple-element.42.own_first), channel_id=1, source_target_pairs={{1,0},{2,1},{3,2},{4,3},{5,4},{6,5},{7,6},{9,8},{10,9},{11,10},{12... | collective-permute-start | bytes 245768 | tf_op jit(solution)/shard_map/ppermute | solution.py:764
  12.0 1.6 %prepare.1 = (bf16[16,128,256]{2,1,0:T(8,128)(2,1)S(1)}, bf16[16,128,256]{2,1,0:T(8,128)(2,1)S(1)}, bf16[16,128,256]{2,1,0:T(8,128)(2,1)S(1)}, bf16[16,128,256]{...) custom-call(f32[2,17,16,32,128]{4,3,2,1,0:T(8,128)S(1)} %get-tuple-e, ...), custom_call_target="tpu_custom_call" | custom-call | flops 1000000 | bytes 1000000 | tf_op jit(solution)/shard_map/prepare/pallas_call | solution.py:322
  13.6 0.0 collective-permute-done.2.west
  13.6 1.9 %collective-permute-done.3.east = f32[20,8,128]{2,1,0:T(8,128)S(1)} collective-permute-done((f32[20,8,128]{2,1,0:T(8,128)S(1)}, f32[20,8,128]{2,1,0:T(8,128)S(1)}, u32[]{:S(2)}, u32[]{:S(2)}) %collective-permute-start.3) | collective-permute-done | bytes 81952 | tf_op jit(solution)/shard_map/ppermute | solution.py:764
  15.5 14.7 %interior.1 = (bf16[16,128,256]{2,1,0:T(8,128)(2,1)S(1)}, bf16[16,128,256]{2,1,0:T(8,128)(2,1)S(1)}, f32[16,2,128,128]{3,2,1,0:T(8,128)S(1)}, f32[2,16,6,8,128]{...) custom-call(f32[2,17,16,32,128]{4,3,2,1,0:T(8,128)S(1)} %get-tuple-element.32.X, ...), custom_call_target="tpu_custom_call" | custom-call | flops 1000000 | bytes 1000000 | tf_op jit(solution)/shard_map/interior/pallas_call | solution.py:518
  30.2 0.0 collective-permute-done.below
  30.2 0.8 %collective-permute-done.1.above = f32[2,18,2,24,128]{4,3,2,1,0:T(8,128)S(1)} collective-permute-done((f32[2,18,2,24,128]{4,3,2,1,0:T(8,128)S(1)}, f32[2,18,2,24,128]{4,3,2,1,0:T(8,128)S(1)}, u32[]{:S(2)}, u32[]{:S(2)}) %collective-permute-start.1) | collective-permute-done | bytes 884768 | tf_op jit(solution)/shard_map/ppermute | solution.py:764
  31.1 3.4 %edges.1 = (bf16[16,128,256]{2,1,0:T(8,128)(2,1)S(1)}, bf16[16,128,256]{2,1,0:T(8,128)(2,1)S(1)}, f32[16,16,256]{2,1,0:T(8,128)}, f32[8,128]{1,0:T(8,128)S(1)}) custom-call(f32[2,18,2,24,128]{4,3,2,1,0:T(8,128)S(1)} %collective-permute-done.below, f32[2,18,2,24,128]{4,3,2,1,0:T(8,128)S(1)} %collective-permute-done.1.above, ...), custom_call_target="tpu_custom_call" | custom-call | flops 1000000000 | bytes 10000000 | tf_op jit(solution)/shard_map/edges/pallas_call | solution.py:638
  34.5 2.6 %collective-permute-start.4 = (f32[8,128]{1,0:T(8,128)S(1)}, f32[8,128]{1,0:T(8,128)S(1)}, u32[]{:S(2)}, u32[]{:S(2)}) collective-permute-start(f32[8,128]{1,0:T(8,128)S(1)} %get-tuple-element.50), channel_id=1, source_target_pairs={{0,1},{1,0},{2,3},{3,2},{4,5},{5,4},{6,7},{7,6},{8,9},{9,8},{10,11... | collective-permute-start | bytes 12296 | tf_op jit(solution)/shard_map/ppermute | solution.py:769
  37.1 0.8 %collective-permute-done.4 = f32[8,128]{1,0:T(8,128)S(1)} collective-permute-done((f32[8,128]{1,0:T(8,128)S(1)}, f32[8,128]{1,0:T(8,128)S(1)}, u32[]{:S(2)}, u32[]{:S(2)}) %collective-permute-start.4) | collective-permute-done | bytes 4128 | tf_op jit(solution)/shard_map/ppermute | solution.py:769
  37.9 4.7 %collective-permute-start.7 = (f32[8,128]{1,0:T(8,128)S(1)}, f32[8,128]{1,0:T(8,128)S(1)}, u32[]{:S(2)}, u32[]{:S(2)}) collective-permute-start(f32[8,128]{1,0:T(8,128)S(1)} %add.30), channel_id=1, source_target_pairs={{0,24},{1,25},{2,26},{3,27},{4,28},{5,29},{6,30},{7,31},{8,16},{9,... | collective-permute-start | bytes 12296 | tf_op jit(solution)/shard_map/ppermute | solution.py:769
  42.6 0.0 collective-permute-start.6
  42.6 0.9 %collective-permute-start.5 = (f32[8,128]{1,0:T(8,128)S(1)}, f32[8,128]{1,0:T(8,128)S(1)}, u32[]{:S(2)}, u32[]{:S(2)}) collective-permute-start(f32[8,128]{1,0:T(8,128)S(1)} %add.30), channel_id=1, source_target_pairs={{0,8},{1,9},{2,10},{3,11},{4,12},{5,13},{6,14},{7,15},{8,0},{9,1},... | collective-permute-start | bytes 12296 | tf_op jit(solution)/shard_map/ppermute | solution.py:769
  43.5 0.7 %collective-permute-done.7 = f32[8,128]{1,0:T(8,128)S(1)} collective-permute-done((f32[8,128]{1,0:T(8,128)S(1)}, f32[8,128]{1,0:T(8,128)S(1)}, u32[]{:S(2)}, u32[]{:S(2)}) %collective-permute-start.7) | collective-permute-done | bytes 4128 | tf_op jit(solution)/shard_map/ppermute | solution.py:769
  44.2 3.5 %collective-permute-done.6 = f32[8,128]{1,0:T(8,128)S(1)} collective-permute-done((f32[8,128]{1,0:T(8,128)S(1)}, f32[8,128]{1,0:T(8,128)S(1)}, u32[]{:S(2)}, u32[]{:S(2)}) %collective-permute-start.6) | collective-permute-done | bytes 4128 | tf_op jit(solution)/shard_map/ppermute | solution.py:769
  47.7 0.0 collective-permute-done.5
  47.7 2.9 %collective-permute-start.10 = (f32[8,128]{1,0:T(8,128)S(1)}, f32[8,128]{1,0:T(8,128)S(1)}, u32[]{:S(2)}, u32[]{:S(2)}) collective-permute-start(f32[8,128]{1,0:T(8,128)S(1)} %add_add_fusion.2), channel_id=1, source_target_pairs={{0,96},{1,97},{2,98},{3,99},{4,100},{5,101},{6,102},{7,103},{8,104... | collective-permute-start | bytes 12296 | tf_op jit(solution)/shard_map/ppermute | solution.py:769
  50.6 0.8 %collective-permute-start.9 = (f32[8,128]{1,0:T(8,128)S(1)}, f32[8,128]{1,0:T(8,128)S(1)}, u32[]{:S(2)}, u32[]{:S(2)}) collective-permute-start(f32[8,128]{1,0:T(8,128)S(1)} %add_add_fusion.2), channel_id=1, source_target_pairs={{0,64},{1,65},{2,66},{3,67},{4,68},{5,69},{6,70},{7,71},{8,72},{9,... | collective-permute-start | bytes 12296 | tf_op jit(solution)/shard_map/ppermute | solution.py:769
  51.4 0.5 collective-permute-start.8
  51.9 0.7 %collective-permute-done.10 = f32[8,128]{1,0:T(8,128)S(1)} collective-permute-done((f32[8,128]{1,0:T(8,128)S(1)}, f32[8,128]{1,0:T(8,128)S(1)}, u32[]{:S(2)}, u32[]{:S(2)}) %collective-permute-start.10) | collective-permute-done | bytes 4128 | tf_op jit(solution)/shard_map/ppermute | solution.py:769
  52.6 3.1 %collective-permute-done.9 = f32[8,128]{1,0:T(8,128)S(1)} collective-permute-done((f32[8,128]{1,0:T(8,128)S(1)}, f32[8,128]{1,0:T(8,128)S(1)}, u32[]{:S(2)}, u32[]{:S(2)}) %collective-permute-start.9) | collective-permute-done | bytes 4128 | tf_op jit(solution)/shard_map/ppermute | solution.py:769
  55.7 0.0 collective-permute-done.8
  55.8 1.6 %collective-permute-start.13 = (f32[8,128]{1,0:T(8,128)S(1)}, f32[8,128]{1,0:T(8,128)S(1)}, u32[]{:S(2)}, u32[]{:S(2)}) collective-permute-start(f32[8,128]{1,0:T(8,128)S(1)} %add_add_fusion.1), channel_id=1, source_target_pairs={{0,6},{1,7},{2,4},{3,5},{4,2},{5,3},{6,0},{7,1},{8,14},{9,15},{10,... | collective-permute-start | bytes 12296 | tf_op jit(solution)/shard_map/ppermute | solution.py:769
  57.3 2.3 %collective-permute-start.12 = (f32[8,128]{1,0:T(8,128)S(1)}, f32[8,128]{1,0:T(8,128)S(1)}, u32[]{:S(2)}, u32[]{:S(2)}) collective-permute-start(f32[8,128]{1,0:T(8,128)S(1)} %add_add_fusion.1), channel_id=1, source_target_pairs={{0,4},{1,5},{2,6},{3,7},{4,0},{5,1},{6,2},{7,3},{8,12},{9,13},{10,... | collective-permute-start | bytes 12296 | tf_op jit(solution)/shard_map/ppermute | solution.py:769
  59.7 0.4 collective-permute-start.11
  60.1 0.7 %collective-permute-done.13 = f32[8,128]{1,0:T(8,128)S(1)} collective-permute-done((f32[8,128]{1,0:T(8,128)S(1)}, f32[8,128]{1,0:T(8,128)S(1)}, u32[]{:S(2)}, u32[]{:S(2)}) %collective-permute-start.13) | collective-permute-done | bytes 4128 | tf_op jit(solution)/shard_map/ppermute | solution.py:769
  60.8 1.6 %collective-permute-done.12 = f32[8,128]{1,0:T(8,128)S(1)} collective-permute-done((f32[8,128]{1,0:T(8,128)S(1)}, f32[8,128]{1,0:T(8,128)S(1)}, u32[]{:S(2)}, u32[]{:S(2)}) %collective-permute-start.12) | collective-permute-done | bytes 4128 | tf_op jit(solution)/shard_map/ppermute | solution.py:769
  62.4 0.8 %collective-permute-done.11 = f32[8,128]{1,0:T(8,128)S(1)} collective-permute-done((f32[8,128]{1,0:T(8,128)S(1)}, f32[8,128]{1,0:T(8,128)S(1)}, u32[]{:S(2)}, u32[]{:S(2)}) %collective-permute-start.11) | collective-permute-done | bytes 4128 | tf_op jit(solution)/shard_map/ppermute | solution.py:769
  63.3 5.1 %apply.1 = (f32[16,16,16,256]{3,2,1,0:T(8,128)}, f32[16,16]{1,0:T(8,128)}) custom-call(f32[8,128]{1,0:T(8,128)S(1)} %add_add_fusion.sums, bf16[16,128,256]{2,1,0:T(8,128)(2,1)S(1)} %get-tuple-element.39.high_in.refs_0_, bf16[16,128,256]{2,1,0:T(8,128)(2,1)S(1)} %get-tuple-element.40.low_in.refs_1_, bf16[16,128,256]{2,1,0:T(8,128)(2,1)S(1)} %get-tuple-element.51.refs_2_, ...), custom_call_target="tpu_custom_call" | custom-call | flops 1000000000 | bytes 13000000 | tf_op jit(solution)/shard_map/apply/pallas_call | solution.py:738
  (4 shorter events, 0.0 us)
Async XLA Ops:
  4.0 26.3 %collective-permute-start = (f32[2,18,2,24,128]{4,3,2,1,0:T(8,128)S(1)}, f32[2,18,2,24,128]{4,3,2,1,0:T(8,128)S(1)}, u32[]{:S(2)}, u32[]{:S(2)}) collective-permute-start(f32[2,18,2,24,128]{4,3,2,1,0:T(8,128)S(1)} %get-tuple-element.30), channel_id=1, source_target_pairs={{0,8},{8,16},{16,24},{24,32},{32,40},{40,48},{48,56},{56,64},{64,7... | collective-permute-start | bytes 2654216 | tf_op jit(solution)/shard_map/ppermute | solution.py:759
  7.9 23.1 %collective-permute-start.1 = (f32[2,18,2,24,128]{4,3,2,1,0:T(8,128)S(1)}, f32[2,18,2,24,128]{4,3,2,1,0:T(8,128)S(1)}, u32[]{:S(2)}, u32[]{:S(2)}) collective-permute-start(f32[2,18,2,24,128]{4,3,2,1,0:T(8,128)S(1)} %get-tuple-element.31), channel_id=1, source_target_pairs={{8,0},{16,8},{24,16},{32,24},{40,32},{48,40},{56,48},{64,56},{72,6... | collective-permute-start | bytes 2654216 | tf_op jit(solution)/shard_map/ppermute | solution.py:764
  9.2 4.4 %collective-permute-start.2 = (f32[20,8,128]{2,1,0:T(8,128)S(1)}, f32[20,8,128]{2,1,0:T(8,128)S(1)}, u32[]{:S(2)}, u32[]{:S(2)}) collective-permute-start(f32[20,8,128]{2,1,0:T(8,128)S(1)} %get-tuple-element.41.own_last), channel_id=1, source_target_pairs={{0,1},{1,2},{2,3},{3,4},{4,5},{5,6},{6,7},{8,9},{9,10},{10,11},{11... | collective-permute-start | bytes 245768 | tf_op jit(solution)/shard_map/ppermute | solution.py:759
  10.7 4.8 %collective-permute-start.3 = (f32[20,8,128]{2,1,0:T(8,128)S(1)}, f32[20,8,128]{2,1,0:T(8,128)S(1)}, u32[]{:S(2)}, u32[]{:S(2)}) collective-permute-start(f32[20,8,128]{2,1,0:T(8,128)S(1)} %get-tuple-element.42.own_first), channel_id=1, source_target_pairs={{1,0},{2,1},{3,2},{4,3},{5,4},{6,5},{7,6},{9,8},{10,9},{11,10},{12... | collective-permute-start | bytes 245768 | tf_op jit(solution)/shard_map/ppermute | solution.py:764
  34.5 3.4 %collective-permute-start.4 = (f32[8,128]{1,0:T(8,128)S(1)}, f32[8,128]{1,0:T(8,128)S(1)}, u32[]{:S(2)}, u32[]{:S(2)}) collective-permute-start(f32[8,128]{1,0:T(8,128)S(1)} %get-tuple-element.50), channel_id=1, source_target_pairs={{0,1},{1,0},{2,3},{3,2},{4,5},{5,4},{6,7},{7,6},{8,9},{9,8},{10,11... | collective-permute-start | bytes 12296 | tf_op jit(solution)/shard_map/ppermute | solution.py:769
  37.9 6.3 %collective-permute-start.7 = (f32[8,128]{1,0:T(8,128)S(1)}, f32[8,128]{1,0:T(8,128)S(1)}, u32[]{:S(2)}, u32[]{:S(2)}) collective-permute-start(f32[8,128]{1,0:T(8,128)S(1)} %add.30), channel_id=1, source_target_pairs={{0,24},{1,25},{2,26},{3,27},{4,28},{5,29},{6,30},{7,31},{8,16},{9,... | collective-permute-start | bytes 12296 | tf_op jit(solution)/shard_map/ppermute | solution.py:769
  42.6 5.1 %collective-permute-start.6 = (f32[8,128]{1,0:T(8,128)S(1)}, f32[8,128]{1,0:T(8,128)S(1)}, u32[]{:S(2)}, u32[]{:S(2)}) collective-permute-start(f32[8,128]{1,0:T(8,128)S(1)} %add.30), channel_id=1, source_target_pairs={{0,16},{1,17},{2,18},{3,19},{4,20},{5,21},{6,22},{7,23},{8,24},{9,... | collective-permute-start | bytes 12296 | tf_op jit(solution)/shard_map/ppermute | solution.py:769
  42.6 5.1 %collective-permute-start.5 = (f32[8,128]{1,0:T(8,128)S(1)}, f32[8,128]{1,0:T(8,128)S(1)}, u32[]{:S(2)}, u32[]{:S(2)}) collective-permute-start(f32[8,128]{1,0:T(8,128)S(1)} %add.30), channel_id=1, source_target_pairs={{0,8},{1,9},{2,10},{3,11},{4,12},{5,13},{6,14},{7,15},{8,0},{9,1},... | collective-permute-start | bytes 12296 | tf_op jit(solution)/shard_map/ppermute | solution.py:769
  47.7 4.9 %collective-permute-start.10 = (f32[8,128]{1,0:T(8,128)S(1)}, f32[8,128]{1,0:T(8,128)S(1)}, u32[]{:S(2)}, u32[]{:S(2)}) collective-permute-start(f32[8,128]{1,0:T(8,128)S(1)} %add_add_fusion.2), channel_id=1, source_target_pairs={{0,96},{1,97},{2,98},{3,99},{4,100},{5,101},{6,102},{7,103},{8,104... | collective-permute-start | bytes 12296 | tf_op jit(solution)/shard_map/ppermute | solution.py:769
  50.6 5.1 %collective-permute-start.9 = (f32[8,128]{1,0:T(8,128)S(1)}, f32[8,128]{1,0:T(8,128)S(1)}, u32[]{:S(2)}, u32[]{:S(2)}) collective-permute-start(f32[8,128]{1,0:T(8,128)S(1)} %add_add_fusion.2), channel_id=1, source_target_pairs={{0,64},{1,65},{2,66},{3,67},{4,68},{5,69},{6,70},{7,71},{8,72},{9,... | collective-permute-start | bytes 12296 | tf_op jit(solution)/shard_map/ppermute | solution.py:769
  51.4 4.4 %collective-permute-start.8 = (f32[8,128]{1,0:T(8,128)S(1)}, f32[8,128]{1,0:T(8,128)S(1)}, u32[]{:S(2)}, u32[]{:S(2)}) collective-permute-start(f32[8,128]{1,0:T(8,128)S(1)} %add_add_fusion.2), channel_id=1, source_target_pairs={{0,32},{1,33},{2,34},{3,35},{4,36},{5,37},{6,38},{7,39},{8,40},{9,... | collective-permute-start | bytes 12296 | tf_op jit(solution)/shard_map/ppermute | solution.py:769
  55.8 5.1 %collective-permute-start.13 = (f32[8,128]{1,0:T(8,128)S(1)}, f32[8,128]{1,0:T(8,128)S(1)}, u32[]{:S(2)}, u32[]{:S(2)}) collective-permute-start(f32[8,128]{1,0:T(8,128)S(1)} %add_add_fusion.1), channel_id=1, source_target_pairs={{0,6},{1,7},{2,4},{3,5},{4,2},{5,3},{6,0},{7,1},{8,14},{9,15},{10,... | collective-permute-start | bytes 12296 | tf_op jit(solution)/shard_map/ppermute | solution.py:769
  57.3 5.1 %collective-permute-start.12 = (f32[8,128]{1,0:T(8,128)S(1)}, f32[8,128]{1,0:T(8,128)S(1)}, u32[]{:S(2)}, u32[]{:S(2)}) collective-permute-start(f32[8,128]{1,0:T(8,128)S(1)} %add_add_fusion.1), channel_id=1, source_target_pairs={{0,4},{1,5},{2,6},{3,7},{4,0},{5,1},{6,2},{7,3},{8,12},{9,13},{10,... | collective-permute-start | bytes 12296 | tf_op jit(solution)/shard_map/ppermute | solution.py:769
  59.7 3.6 %collective-permute-start.11 = (f32[8,128]{1,0:T(8,128)S(1)}, f32[8,128]{1,0:T(8,128)S(1)}, u32[]{:S(2)}, u32[]{:S(2)}) collective-permute-start(f32[8,128]{1,0:T(8,128)S(1)} %add_add_fusion.1), channel_id=1, source_target_pairs={{0,2},{1,3},{2,0},{3,1},{4,6},{5,7},{6,4},{7,5},{8,10},{9,11},{10,... | collective-permute-start | bytes 12296 | tf_op jit(solution)/shard_map/ppermute | solution.py:769
